TPU v7x, 32 devices: a whole 2x2x4 slice. The times are simulated.
32 devices in a mesh: dp: 8 (over y, x, core), mp: 4 (over z).
Axes of the slice: x: 2, y: 2, z: 4, core: 2. Of those that a mesh axis runs over, the one named last changes fastest.
Arguments:
- tokens: bfloat16 [8192, 2048], P(('dp', 'mp')), may hold values from -6 to 6
- cotangent: bfloat16 [8192, 2048], P(('dp', 'mp')), may hold values from -6 to 6
- segment: int32 [8192], P('dp'), may hold values from 0 to 31, never falling along the last dimension, each value on 1 to 1024 neighbouring positions
- counts: int32 [8], P('dp'), may hold values from 256 to 1024
- ln_gain: bfloat16 [2, 2048], replicated, may hold values from 0.25 to 1.75
- ln_bias: bfloat16 [2, 2048], replicated, may hold values from -4 to 4
- w_qkv: bfloat16 [2048, 3, 2048], P(None, None, 'mp'), may hold values from -0.125 to 0.125
- b_qv: bfloat16 [2, 2048], P(None, 'mp'), may hold values from -6 to 6
- w_out: bfloat16 [2048, 2048], P('mp'), may hold values from -1 to 1
- out_bias: bfloat16 [2, 2048], replicated, may hold values from -4 to 4
- w_up: bfloat16 [2048, 8192], P(None, 'mp'), may hold values from -0.125 to 0.125
- b_up: bfloat16 [8192], P('mp'), may hold values from -6 to 6
- w_down: bfloat16 [8192, 2048], P('mp'), may hold values from -0.09375 to 0.09375
Outputs:
- layer_out: bfloat16 [8192, 2048], P(('dp', 'mp'))
- grad_tokens: float32 [8192, 2048], P(('dp', 'mp'))
- grad_ln_gain: float32 [2, 2048], replicated
- grad_ln_bias: float32 [2, 2048], replicated
- grad_qkv: float32 [2048, 3, 2048], P('dp', None, 'mp')
- grad_bqv: float32 [2, 2048], P(None, 'mp')
- grad_out: float32 [2048, 2048], P('mp', 'dp')
- grad_out_bias: float32 [2, 2048], replicated
- grad_up: float32 [2048, 8192], P('dp', 'mp')
- grad_bup: float32 [8192], P('mp')
- grad_down: float32 [8192, 2048], P('mp', 'dp')
All inputs are finite; a program needn't handle non-finite values.
Results may differ from a plain program's by a relative error of at most 0.012.
The roundings to bfloat16 on the way count: a program that leaves them out, or rounds other values in their place, can miss the bound.
Values may be sent and summed in bfloat16 or wider, within the bound.
No kernel may reach another device: no remote copies, remote signals or barrier semaphores. Data moves between devices by JAX's collectives and lax.ppermute only.
A program may use at most 256 MiB of HBM per device.

v0:
```python
import jax
import jax.numpy as jnp
from jax import lax
from jax.sharding import PartitionSpec as P

HEAD = 128
SEQ = 1024


def norm_forward(value, gain, shift):
    mean = jnp.mean(value, axis=-1, keepdims=True)
    centered = value - mean
    inverse = lax.rsqrt(jnp.mean(centered * centered, axis=-1, keepdims=True) + 1e-05)
    scaled = centered * inverse
    return (scaled * gain + shift, scaled, inverse)


def norm_backward(grad, gain, scaled, inverse):
    inner = grad * gain
    return inverse * (
        inner
        - jnp.mean(inner, axis=-1, keepdims=True)
        - scaled * jnp.mean(inner * scaled, axis=-1, keepdims=True)
    )


def row_mask(segment_row):
    places = jnp.arange(segment_row.shape[0], dtype=jnp.int32)
    return (segment_row[:, None] == segment_row[None, :]) & (places[:, None] >= places[None, :])


def row_scores(query_row, keys_row, segment_row):
    scores = jnp.einsum(
        "qhe,khe->hqk", query_row, keys_row, preferred_element_type=jnp.float32
    ) * HEAD ** (-0.5)
    return jnp.where(row_mask(segment_row)[None], scores, -1e30)


def forward_row(item):
    query_row, keys_row, values_row, segment_row = item
    masked = row_scores(query_row, keys_row, segment_row)
    top = jnp.max(masked, axis=-1, keepdims=True)
    expo = jnp.exp(masked - top)
    total = jnp.sum(expo, axis=-1, keepdims=True)
    probs = (expo / total).astype(jnp.bfloat16)
    mixed = jnp.einsum(
        "hqk,khe->qhe", probs, values_row, preferred_element_type=jnp.float32
    ).astype(jnp.bfloat16)
    return (mixed, top[..., 0] + jnp.log(total[..., 0]))


def backward_row(item):
    query_row, keys_row, values_row, segment_row, log_total, grad_row = item
    masked = row_scores(query_row, keys_row, segment_row)
    probs = jnp.exp(masked - log_total[..., None])
    probs_low = probs.astype(jnp.bfloat16)
    grad_probs = jnp.einsum(
        "qhe,khe->hqk", grad_row, values_row, preferred_element_type=jnp.float32
    )
    delta = jnp.sum(probs * grad_probs, axis=-1, keepdims=True)
    grad_scores = (probs * (grad_probs - delta)).astype(jnp.bfloat16)
    scale = HEAD ** (-0.5)
    grad_query = (
        jnp.einsum("hqk,khe->qhe", grad_scores, keys_row, preferred_element_type=jnp.float32)
        * scale
    ).astype(jnp.bfloat16)
    grad_keys = (
        jnp.einsum("hqk,qhe->khe", grad_scores, query_row, preferred_element_type=jnp.float32)
        * scale
    ).astype(jnp.bfloat16)
    grad_values = jnp.einsum(
        "hqk,qhe->khe", probs_low, grad_row, preferred_element_type=jnp.float32
    ).astype(jnp.bfloat16)
    return (grad_query, grad_keys, grad_values)


def contract_rows(left, right):
    return lax.dot_general(
        left, right, (((0,), (0,)), ((), ())), preferred_element_type=jnp.float32
    )


def body(
    tokens,
    cotangent,
    segment,
    counts,
    ln_gain,
    ln_bias,
    w_qkv,
    b_qv,
    w_out,
    out_bias,
    w_up,
    b_up,
    w_down,
):
    f32 = jnp.float32
    bf16 = jnp.bfloat16
    gains = ln_gain.astype(f32)
    shifts = ln_bias.astype(f32)
    bias_pair = out_bias.astype(f32)
    width = tokens.shape[1]
    head_cols = w_qkv.shape[2]
    heads_here = head_cols // HEAD
    group_rows = segment.shape[0]
    row_count = group_rows // SEQ
    inputs = tokens.astype(f32)
    normed1, scaled1, inverse1 = norm_forward(inputs, gains[0], shifts[0])
    normed1_all = lax.all_gather(normed1.astype(bf16), "mp", axis=0, tiled=True)
    flat_qkv = w_qkv.reshape(width, 3 * head_cols)
    bias_rows = (
        jnp.stack([b_qv[0], jnp.zeros_like(b_qv[0]), b_qv[1]]).astype(f32).reshape(3 * head_cols)
    )
    projected = (jnp.dot(normed1_all, flat_qkv, preferred_element_type=f32) + bias_rows).astype(
        bf16
    )
    projected = projected.reshape(group_rows, 3, heads_here, HEAD)
    row_shape = (row_count, SEQ, heads_here, HEAD)
    query = projected[:, 0].reshape(row_shape)
    keys = projected[:, 1].reshape(row_shape)
    values = projected[:, 2].reshape(row_shape)
    segment_rows = segment.reshape(row_count, SEQ)
    mixed, log_totals = lax.map(forward_row, (query, keys, values, segment_rows))
    attn_out = mixed.reshape(group_rows, head_cols)
    branch = (
        lax.psum_scatter(
            jnp.dot(attn_out, w_out, preferred_element_type=f32),
            "mp",
            scatter_dimension=0,
            tiled=True,
        )
        + bias_pair[0]
    )
    middle = inputs + branch
    normed2, scaled2, inverse2 = norm_forward(middle, gains[1], shifts[1])
    normed2_all = lax.all_gather(normed2.astype(bf16), "mp", axis=0, tiled=True)
    hidden = jnp.dot(normed2_all, w_up, preferred_element_type=f32) + b_up.astype(f32)
    gelu_tanh = lambda value: jax.nn.gelu(value, approximate=True)
    activated, gelu_pull = jax.vjp(gelu_tanh, hidden)
    active = activated.astype(bf16)
    layer_out = (
        middle
        + lax.psum_scatter(
            jnp.dot(active, w_down, preferred_element_type=f32).astype(jnp.bfloat16),
            "mp",
            scatter_dimension=0,
            tiled=True,
        ).astype(jnp.float32)
        + bias_pair[1]
    ).astype(bf16)
    cot_local = cotangent.astype(f32)
    cot_all = lax.all_gather(cotangent, "mp", axis=0, tiled=True)
    grad_active = jnp.dot(cot_all, w_down.T, preferred_element_type=f32)
    grad_hidden = gelu_pull(grad_active)[0].astype(bf16)
    grad_normed2 = lax.psum_scatter(
        jnp.dot(grad_hidden, w_up.T, preferred_element_type=f32),
        "mp",
        scatter_dimension=0,
        tiled=True,
    )
    grad_middle = cot_local + norm_backward(grad_normed2, gains[1], scaled2, inverse2)
    grad_branch = grad_middle.astype(bf16)
    grad_branch_all = lax.all_gather(grad_branch, "mp", axis=0, tiled=True)
    grad_attn = jnp.dot(grad_branch_all, w_out.T, preferred_element_type=f32).astype(bf16)
    grad_q, grad_k, grad_v = lax.map(
        backward_row, (query, keys, values, segment_rows, log_totals, grad_attn.reshape(row_shape))
    )
    grad_proj = jnp.stack(
        [
            grad_q.reshape(group_rows, head_cols),
            grad_k.reshape(group_rows, head_cols),
            grad_v.reshape(group_rows, head_cols),
        ],
        axis=1,
    ).reshape(group_rows, 3 * head_cols)
    grad_normed1 = lax.psum_scatter(
        jnp.dot(grad_proj, flat_qkv.T, preferred_element_type=f32),
        "mp",
        scatter_dimension=0,
        tiled=True,
    )
    grad_input = grad_middle + norm_backward(grad_normed1, gains[0], scaled1, inverse1)
    count_here = counts.astype(f32)[0]
    total_count = lax.psum(count_here, "dp")
    factor = count_here / total_count
    grad_bqv_local = factor * jnp.stack(
        [
            jnp.sum(grad_q.reshape(group_rows, head_cols).astype(f32), axis=0),
            jnp.sum(grad_v.reshape(group_rows, head_cols).astype(f32), axis=0),
        ]
    )
    grad_bup_local = factor * jnp.sum(grad_hidden.astype(f32), axis=0)
    grad_bqv, grad_bup = lax.psum((grad_bqv_local, grad_bup_local), "dp")
    divisor = 1.0
    full_qkv = factor * contract_rows(normed1_all, grad_proj)
    full_out = factor * contract_rows(attn_out, grad_branch_all)
    full_up = factor * contract_rows(normed2_all, grad_hidden)
    full_down = factor * contract_rows(active, cot_all)
    grad_qkv, grad_wout, grad_wup, grad_wdown = (
        lax.psum_scatter(
            full_qkv.reshape(width, 3, head_cols), "dp", scatter_dimension=0, tiled=True
        ),
        lax.psum_scatter(full_out, "dp", scatter_dimension=1, tiled=True),
        lax.psum_scatter(full_up, "dp", scatter_dimension=0, tiled=True),
        lax.psum_scatter(full_down, "dp", scatter_dimension=1, tiled=True),
    )
    gain_local = factor * jnp.stack(
        [jnp.sum(grad_normed1 * scaled1, axis=0), jnp.sum(grad_normed2 * scaled2, axis=0)]
    )
    shift_local = factor * jnp.stack([jnp.sum(grad_normed1, axis=0), jnp.sum(grad_normed2, axis=0)])
    out_bias_local = factor * jnp.stack(
        [jnp.sum(grad_branch.astype(f32), axis=0), jnp.sum(cot_local, axis=0)]
    )
    grad_gain, grad_shift, grad_out_bias = lax.psum(
        (gain_local, shift_local, out_bias_local), ("dp", "mp")
    )
    return (
        layer_out,
        factor * grad_input / divisor,
        grad_gain / divisor,
        grad_shift / divisor,
        grad_qkv / divisor,
        grad_bqv / divisor,
        grad_wout / divisor,
        grad_out_bias / divisor,
        grad_wup / divisor,
        grad_bup / divisor,
        grad_wdown / divisor,
    )


def solution(mesh):
    placed = (
        P(("dp", "mp"), None),
        P(("dp", "mp"), None),
        P("dp"),
        P("dp"),
        P(),
        P(),
        P(None, None, "mp"),
        P(None, "mp"),
        P("mp", None),
        P(),
        P(None, "mp"),
        P("mp"),
        P("mp", None),
    )
    return jax.shard_map(
        body,
        mesh=mesh,
        in_specs=placed,
        out_specs=(
            P(("dp", "mp"), None),
            P(("dp", "mp"), None),
            P(),
            P(),
            P("dp", None, "mp"),
            P(None, "mp"),
            P("mp", "dp"),
            P(),
            P("dp", "mp"),
            P("mp"),
            P("mp", "dp"),
        ),
        check_vma=False,
    )
```

profile of v0, /device:TPU:0, one launch (start us, length us, event | category | flops | bytes accessed | tf_op | source)
XLA Modules:
  0.0 1411.4 jit_solution(12577962861005475201)
XLA Ops:
  7.2 1.6 convert_reduce_fusion.1
  8.9 1.6 fusion.28
  10.5 0.8 fusion.40
  11.3 0.8 fusion.41
  12.1 2.7 fusion.21
  15.0 8.8 copy.39
  23.9 1.6 fusion.13
  25.5 73.0 %all-gather.5.cloned.1.call-done = bf16[1024,2048]{1,0:T(8,128)(2,1)} async-done(((bf16[256,2048]{1,0:T(8,128)(2,1)}), bf16[1024,2048]{1,0:T(8,128)(2,1)}) %all-gather.5.cloned.1.call-update) | async-done | bytes 4194320 | tf_op jit(solution)/shard_map/all_gather | solution.py:110
  98.4 11.3 add_convert_fusion
  109.8 6.2 reshape.154
  116.0 4.2 fusion.38
  120.2 1.6 copy.64
  121.9 11.3 fusion.43
  133.2 8.0 fusion
  141.2 8.1 fusion.29
  149.3 1.0 copy-done.22
  150.3 5.6 fusion.44
  155.9 0.6 copy-done.13
  156.6 142.5 %reduce-scatter.9.cloned.1.call-done = f32[256,2048]{1,0:T(8,128)} async-done(((f32[1024,2048]{1,0:T(8,128)}), f32[256,2048]{1,0:T(8,128)}) %reduce-scatter.9.cloned.1.call-update) | async-done | bytes 2097168 | tf_op jit(solution)/shard_map/reduce_scatter | solution.py:127
  299.1 1.9 fusion.37
  301.4 0.9 copy-done.2
  302.3 1.4 add_convert_fusion.2
  304.4 81.0 %all-gather.7.cloned.1.call-done = bf16[1024,2048]{1,0:T(8,128)(2,1)} async-done(((bf16[256,2048]{1,0:T(8,128)(2,1)}), bf16[1024,2048]{1,0:T(8,128)(2,1)}) %all-gather.7.cloned.1.call-update) | async-done | bytes 4194320 | tf_op jit(solution)/shard_map/all_gather | solution.py:137
  385.4 14.4 %fusion.45 = f32[1024,2048]{1,0:T(8,128)} fusion(bf16[1024,2048]{1,0:T(8,128)(2,1)} %all-gather.7.cloned.1.call-done, bf16[2048,2048]{1,0:T(8,128)(2,1)} %param.23), kind=kOutput, calls=%fused_computation.96 | convolution fusion | flops 8589934592 | bytes 20971520 | tf_op jit(solution)/shard_map/dot_general | solution.py:138
  399.9 66.3 %all-gather.9.cloned.1.call-done = bf16[1024,2048]{1,0:T(8,128)(2,1)} async-done(((bf16[256,2048]{1,0:T(8,128)(2,1)}), bf16[1024,2048]{1,0:T(8,128)(2,1)}) %all-gather.9.cloned.1.call-update) | async-done | bytes 4194320 | tf_op jit(solution)/shard_map/all_gather | solution.py:153
  466.2 19.2 %convert_reduce_fusion = (f32[2048]{0:T(1024)}, bf16[1024,2048]{1,0:T(8,128)(2,1)S(1)}) fusion(f32[1024,2048]{1,0:T(8,128)} %fusion.45, f32[2048]{0:T(1024)S(1)} %convert_element_type.127, bf16[1024,2048]{1,0:T(8,128)(2,1)} %all-gather.9.cloned.1.call-done, bf16[2048,2048]{1,0:T(8,128)(2,1)} %param.25), kind=kOutput, calls=%fused_computation.21 | convolution fusion | flops 8638167040 | bytes 25182208 | tf_op jit(solution)/shard_map/dot_general | solution.py:154
  485.4 2.0 copy-done.24
  487.5 13.6 fusion.46
  501.1 16.1 %convolution_convert_fusion = bf16[1024,2048]{1,0:T(8,128)(2,1)} fusion(bf16[2048,2048]{1,0:T(8,128)(2,1)} %param.25, f32[1024,2048]{1,0:T(8,128)} %fusion.45, f32[2048]{0:T(1024)S(1)} %convert_element_type.127), kind=kOutput, calls=%fused_computation.29 | convolution fusion | flops 8613003264 | bytes 20979712 | tf_op jit(solution)/shard_map/dot_general | solution.py:145
  517.2 127.0 %reduce-scatter.13.cloned.1.call-done = f32[256,2048]{1,0:T(8,128)} async-done(((f32[1024,2048]{1,0:T(8,128)}), f32[256,2048]{1,0:T(8,128)}) %reduce-scatter.13.cloned.1.call-update) | async-done | bytes 2097168 | tf_op jit(solution)/shard_map/reduce_scatter | solution.py:156
  644.2 3.1 multiply_reduce_fusion.1
  647.3 76.5 %reduce-scatter.11.cloned.1.call-done = bf16[256,2048]{1,0:T(8,128)(2,1)} async-done(((bf16[1024,2048]{1,0:T(8,128)(2,1)}), bf16[256,2048]{1,0:T(8,128)(2,1)}) %reduce-scatter.11.cloned.1.call-update) | async-done | bytes 1048592 | tf_op jit(solution)/shard_map/reduce_scatter | solution.py:144
  723.9 6.1 convert_reduce_fusion.3
  730.3 81.1 %all-gather.11.cloned.1.call-done = bf16[1024,2048]{1,0:T(8,128)(2,1)} async-done(((bf16[256,2048]{1,0:T(8,128)(2,1)}), bf16[1024,2048]{1,0:T(8,128)(2,1)}) %all-gather.11.cloned.1.call-update) | async-done | bytes 4194320 | tf_op jit(solution)/shard_map/all_gather | solution.py:164
  811.4 4.5 convolution_convert_fusion.1
  816.0 8.9 convert_reduce_fusion.4
  825.0 10.7 multiply_reduce_fusion
  835.7 11.8 multiply_convert_fusion
  847.5 2.9 multiply_convert_fusion.2
  850.5 2.5 convert_reduce_fusion.5
  853.0 0.5 copy.53
  853.5 1.5 copy.51
  855.0 1.3 copy.52
  856.3 11.0 convolution_bitcast_fusion
  868.1 15.3 %psum.42 = f32[]{:T(128)} all-reduce(f32[]{:T(128)} %bitcast.12), channel_id=1, replica_groups=mesh['dp'=8,'mp'=4] {'dp'}, use_global_device_ids=true, to_apply=%region_8.9 | all-reduce | flops 1 | bytes 8 | tf_op jit(solution)/shard_map/psum | solution.py:185
  884.1 17.3 %convolution_multiply_fusion.1 = f32[2048,2048]{1,0:T(8,128)} fusion(bf16[1024,2048]{1,0:T(8,128)(2,1)} %all-gather.9.cloned.1.call-done, f32[]{:T(128)S(6)} %div.60, f32[1024,2048]{1,0:T(8,128)} %fusion.45, f32[2048]{0:T(1024)S(1)} %convert_element_type.127), kind=kOutput, calls=%fused_computation.11 | convolution fusion | flops 8615100416 | bytes 29368324 | tf_op jit(solution)/shard_map/dot_general | solution.py:78
  901.4 15.2 %convolution_multiply_fusion.2 = f32[2048,2048]{1,0:T(8,128)} fusion(bf16[1024,2048]{1,0:T(8,128)(2,1)} %all-gather.7.cloned.1.call-done, bf16[1024,2048]{1,0:T(8,128)(2,1)} %copy-done.24, f32[]{:T(128)S(6)} %div.60), kind=kOutput, calls=%fused_computation.12 | convolution fusion | flops 8594128896 | bytes 25165828 | tf_op jit(solution)/shard_map/dot_general | solution.py:78
  916.7 1.1 copy-done.23
  917.8 6.5 convolution_multiply_fusion.3
  924.4 1.1 copy-done.9
  925.5 2.0 pad_maximum_fusion
  927.5 4.8 copy.54
  932.3 12.1 convolution_multiply_fusion
  944.4 12.7 copy.55
  957.2 0.6 copy-done.19
  957.8 23.9 %all-reduce.1 = (f32[2,512]{1,0:T(2,128)}, f32[2048]{0:T(1024)}) all-reduce(f32[2,512]{1,0:T(2,128)S(1)} %maximum_multiply_fusion.3, f32[2048]{0:T(1024)S(1)} %broadcast_multiply_fusion), channel_id=1, replica_groups=mesh['dp'=8,'mp'=4] {'dp'}, use_global_device_ids=true, to_apply=%region_25.26 | all-reduce | flops 3072 | bytes 24576 | tf_op jit(solution)/shard_map/psum | solution.py:194
  981.8 28.8 %reduce-scatter.15.cloned.1.call-done = f32[256,2048]{1,0:T(8,128)} async-done(((f32[1024,2048]{1,0:T(8,128)}), f32[256,2048]{1,0:T(8,128)}) %reduce-scatter.15.cloned.1.call-update) | async-done | bytes 2097168 | tf_op jit(solution)/shard_map/reduce_scatter | solution.py:177
  1010.6 2.7 fusion.27
  1013.3 42.0 %all-reduce = (f32[2,2048]{1,0:T(2,128)}, f32[2,2048]{1,0:T(2,128)}, f32[2,2048]{1,0:T(2,128)}) all-reduce(f32[2,2048]{1,0:T(2,128)S(1)} %maximum_multiply_fusion, f32[2,2048]{1,0:T(2,128)S(1)} %maximum_multiply_fusion.1, f32[2,2048]{1,0:T(2,128)S(1)} %maximum_multiply_fusion.2), channel_id=1, replica_groups=mesh['dp'=8,'mp'=4] {'dp','mp'}, use_global_device_ids=true, to_apply=%region_18.19 | all-reduce | flops 12288 | bytes 98304 | tf_op jit(solution)/shard_map/psum | solution.py:215
  1055.3 4.4 fusion.26
  1059.7 72.3 %reduce-scatter.23.cloned.1.call-done = f32[2048,256]{1,0:T(8,128)} async-done(((f32[2048,2048]{1,0:T(8,128)}), f32[2048,256]{1,0:T(8,128)}) %reduce-scatter.23.cloned.1.call-update) | async-done | bytes 2097168 | tf_op jit(solution)/shard_map/reduce_scatter | solution.py:206
  1132.0 120.4 %reduce-scatter.21.cloned.1.call-done = f32[256,2048]{1,0:T(8,128)} async-done(((f32[2048,2048]{1,0:T(8,128)}), f32[256,2048]{1,0:T(8,128)}) %reduce-scatter.21.cloned.1.call-update) | async-done | bytes 2097168 | tf_op jit(solution)/shard_map/reduce_scatter | solution.py:205
  1252.4 55.6 %reduce-scatter.19.cloned.1.call-done = f32[512,256]{1,0:T(8,128)} async-done(((f32[512,2048]{1,0:T(8,128)}), f32[512,256]{1,0:T(8,128)}) %reduce-scatter.19.cloned.1.call-update) | async-done | bytes 524304 | tf_op jit(solution)/shard_map/reduce_scatter | solution.py:204
  1308.1 96.4 %reduce-scatter.17.cloned.1.call-done = f32[256,3,512]{2,0,1:T(8,128)} async-done(((f32[2048,3,512]{2,0,1:T(8,128)}), f32[256,3,512]{2,0,1:T(8,128)}) %reduce-scatter.17.cloned.1.call-update) | async-done | bytes 1572880 | tf_op jit(solution)/shard_map/reduce_scatter | solution.py:201
  (87 shorter events, 2.2 us)
Async XLA Ops:
  7.2 143.1 %copy-start = (bf16[512,2048]{1,0:T(8,128)(2,1)S(1)}, bf16[512,2048]{1,0:T(8,128)(2,1)}, u32[]{:S(2)}) copy-start(bf16[512,2048]{1,0:T(8,128)(2,1)} %param.21) | copy-start | bytes 6291460
  7.2 7.7 copy-start.20
  7.2 91.2 %all-gather.5.cloned.1.call-start = ((), (), s32[]{:S(2)}) async-start(), calls=%async_computation.8 | async-start | bytes 5242880 | tf_op jit(solution)/shard_map/all_gather | solution.py:110
  8.8 15.0 %copy-start.14 = (f32[256]{0:T(256)}, f32[256]{0:T(256)S(1)}, u32[]{:S(2)}) copy-start(f32[256]{0:T(256)S(1)} %broadcast_multiply_fusion.6) | copy-start | bytes 3076
  10.5 13.4 copy-start.16
  11.3 0.8 copy-start.11
  14.8 284.3 %reduce-scatter.9.cloned.1.call-start = ((), (), s32[]{:S(2)}) async-start(), calls=%async_computation.9 | async-start | bytes 10485760 | tf_op jit(solution)/shard_map/reduce_scatter | solution.py:127
  15.0 8.9 copy-start.18
  121.9 19.3 %copy-start.5 = (bf16[1024,1,4,128]{0,3,2,1:T(8,128)(2,1)}, bf16[1024,1,4,128]{0,3,2,1:T(8,128)(2,1)S(1)}, u32[]{:S(2)}) copy-start(bf16[1024,1,4,128]{0,3,2,1:T(8,128)(2,1)S(1)} %copy.64) | copy-start | bytes 3145732
  149.3 1.0 copy-start.22
  155.9 0.7 copy-start.13
  155.9 143.2 %copy-start.3 = (bf16[256,2048]{1,0:T(8,128)(2,1)S(1)}, bf16[256,2048]{1,0:T(8,128)(2,1)}, u32[]{:S(2)}) copy-start(bf16[256,2048]{1,0:T(8,128)(2,1)} %param.13) | copy-start | bytes 3145732
  155.9 229.5 %all-gather.7.cloned.1.call-start = ((), (), s32[]{:S(2)}) async-start(), calls=%async_computation.10 | async-start | bytes 5242880 | tf_op jit(solution)/shard_map/all_gather | solution.py:137
  301.0 1.3 copy-start.2
  301.0 3.4 copy-start.21
  303.8 162.4 %all-gather.9.cloned.1.call-start = ((), (), s32[]{:S(2)}) async-start(), calls=%async_computation.12 | async-start | bytes 5242880 | tf_op jit(solution)/shard_map/all_gather | solution.py:153
  304.4 339.8 %reduce-scatter.13.cloned.1.call-start = ((), (), s32[]{:S(2)}) async-start(), calls=%async_computation.13 | async-start | bytes 10485760 | tf_op jit(solution)/shard_map/reduce_scatter | solution.py:156
  485.4 2.0 copy-start.24
  501.1 222.8 %reduce-scatter.11.cloned.1.call-start = ((), (), s32[]{:S(2)}) async-start(), calls=%async_computation.11 | async-start | bytes 5242880 | tf_op jit(solution)/shard_map/reduce_scatter | solution.py:144
  517.2 206.7 %copy-start.7 = (bf16[256,2048]{1,0:T(8,128)(2,1)S(1)}, bf16[256,2048]{1,0:T(8,128)(2,1)}, u32[]{:S(2)}) copy-start(bf16[256,2048]{1,0:T(8,128)(2,1)} %param.14) | copy-start | bytes 3145732
  517.2 294.3 %all-gather.11.cloned.1.call-start = ((), (), s32[]{:S(2)}) async-start(), calls=%async_computation.14 | async-start | bytes 5242880 | tf_op jit(solution)/shard_map/all_gather | solution.py:164
  730.0 280.5 %reduce-scatter.15.cloned.1.call-start = ((), (), s32[]{:S(2)}) async-start(), calls=%async_computation.15 | async-start | bytes 10485760 | tf_op jit(solution)/shard_map/reduce_scatter | solution.py:177
  816.0 9.0 copy-start.6
  835.7 11.9 copy-start.8
  847.5 3.0 copy-start.10
  867.4 264.6 %reduce-scatter.23.cloned.1.call-start = ((), (), s32[]{:S(2)}) async-start(), calls=%async_computation.19 | async-start | bytes 18874368 | tf_op jit(solution)/shard_map/reduce_scatter | solution.py:206
  901.4 351.1 %reduce-scatter.21.cloned.1.call-start = ((), (), s32[]{:S(2)}) async-start(), calls=%async_computation.18 | async-start | bytes 18874368 | tf_op jit(solution)/shard_map/reduce_scatter | solution.py:205
  916.6 1.2 copy-start.23
  916.6 391.4 %reduce-scatter.19.cloned.1.call-start = ((), (), s32[]{:S(2)}) async-start(), calls=%async_computation.17 | async-start | bytes 4718592 | tf_op jit(solution)/shard_map/reduce_scatter | solution.py:204
  924.3 1.2 copy-start.9
  924.3 480.1 %reduce-scatter.17.cloned.1.call-start = ((), (), s32[]{:S(2)}) async-start(), calls=%async_computation.16 | async-start | bytes 14155776 | tf_op jit(solution)/shard_map/reduce_scatter | solution.py:201
  957.1 0.7 copy-start.19
  957.1 53.4 %copy-start.4 = (bf16[256,2048]{1,0:T(8,128)(2,1)S(1)}, bf16[256,2048]{1,0:T(8,128)(2,1)}, u32[]{:S(2)}) copy-start(bf16[256,2048]{1,0:T(8,128)(2,1)} %param.13) | copy-start | bytes 3145732
  957.1 53.4 %copy-start.12 = (f32[1,2048]{1,0:T(1,128)S(1)}, f32[1,2048]{1,0:T(1,128)}, u32[]{:S(2)}) copy-start(f32[1,2048]{1,0:T(1,128)} %copy-done.11) | copy-start | bytes 24580
  957.1 53.4 %copy-start.15 = (f32[256]{0:T(256)S(1)}, f32[256]{0:T(256)}, u32[]{:S(2)}) copy-start(f32[256]{0:T(256)} %copy-done.14) | copy-start | bytes 3076
  957.1 53.4 %copy-start.17 = (f32[256]{0:T(256)S(1)}, f32[256]{0:T(256)}, u32[]{:S(2)}) copy-start(f32[256]{0:T(256)} %copy-done.16) | copy-start | bytes 3076
  1010.6 393.9 %copy-start.1 = (bf16[512,2048]{1,0:T(8,128)(2,1)S(1)}, bf16[512,2048]{1,0:T(8,128)(2,1)}, u32[]{:S(2)}) copy-start(bf16[512,2048]{1,0:T(8,128)(2,1)} %param.21) | copy-start | bytes 6291460
Sparse Core Ops, SparseCore 0:
  14.9 83.4 all-gather.4
  156.0 143.0 reduce-scatter.8
  303.9 81.4 all-gather.6
  386.9 79.2 all-gather.8
  501.2 142.9 reduce-scatter.12
  646.3 77.4 reduce-scatter.10
  730.1 81.2 all-gather.10
  867.5 142.9 reduce-scatter.14
  1015.1 116.8 reduce-scatter.22
  1136.4 115.9 reduce-scatter.20
  1256.7 51.2 reduce-scatter.18
  1312.0 92.3 reduce-scatter.16
where the time goes:
time: 1420 us; the launch traced here: 1410 us
  waiting for transfers between devices  1020 us (72%)
  matrix products  191 us (13%)
  blocking collectives  81.2 us (6%)
  local copies, waits for them, and re-layouts  51.1 us (4%)
  other arithmetic  49.5 us (3%)
  between operations  16.1 us (1%)
    reduce_scatter x1, waiting for transfers between devices, body(): lax.psum_scatter(jnp.dot(attn_out, w_out, preferred_element_type=f32), 'm...  142 us
    reduce_scatter x1, waiting for transfers between devices, body(): lax.psum_scatter(jnp.dot(grad_hidden, w_up.T, preferred_element_type=f32)...  127 us
    reduce_scatter x1, waiting for transfers between devices, body(): lax.psum_scatter(full_up, 'dp', scatter_dimension=0, tiled=True)  120 us
    reduce_scatter x1, waiting for transfers between devices, body(): lax.psum_scatter(full_qkv.reshape(width, 3, head_cols), 'dp', scatter_dim...  96.4 us
    all_gather x1, waiting for transfers between devices, body(): grad_branch_all = lax.all_gather(grad_branch, 'mp', axis=0, tiled=True)  81.1 us
    all_gather x1, waiting for transfers between devices, body(): normed2_all = lax.all_gather(normed2.astype(bf16), 'mp', axis=0, tiled=True)  81 us
    reduce_scatter x1, waiting for transfers between devices, body(): lax.psum_scatter(jnp.dot(active, w_down, preferred_element_type=f32).asty...  76.5 us
    all_gather x1, waiting for transfers between devices, body(): normed1_all = lax.all_gather(normed1.astype(bf16), 'mp', axis=0, tiled=True)  73 us
  transfers between devices with their start and end apart: 12, of which 12 were waited for; matrix products, arithmetic and copies ran while one was open for 9% of the time, Pallas kernels for 0%

commit v1 on v0

v1 whole, which is shorter than its diff:
```python
import functools
import jax
import jax.numpy as jnp
from jax import lax
from jax.experimental import pallas as pl
from jax.experimental.pallas import tpu as pltpu
from jax.sharding import PartitionSpec as P

HEAD = 128
SEQ = 1024
BLOCK = 256
SCALE = HEAD ** (-0.5)
f32 = jnp.float32
bf16 = jnp.bfloat16


def dot(left, right, left_dim=1, right_dim=0):
    return lax.dot_general(
        left, right, (((left_dim,), (right_dim,)), ((), ())), preferred_element_type=f32
    )


def block_probs(q_block, k_ref, seg_col, seg_row, block, reach):
    start = block * BLOCK
    scores = dot(k_ref[:reach, :], q_block, 1, 1) * SCALE
    key_place = lax.broadcasted_iota(jnp.int32, (reach, BLOCK), 0)
    query_place = start + lax.broadcasted_iota(jnp.int32, (reach, BLOCK), 1)
    allowed = (seg_col[:reach, :] == seg_row[:, start : start + BLOCK]) & (
        key_place <= query_place
    )
    scores = jnp.where(allowed, scores, -1e30)
    expo = jnp.exp(scores - jnp.max(scores, axis=0, keepdims=True))
    return expo * (1.0 / jnp.sum(expo, axis=0, keepdims=True))


def attend_kernel(q_ref, k_ref, v_ref, seg_col, seg_row, out_ref):
    for block in range(SEQ // BLOCK):
        rows = slice(block * BLOCK, (block + 1) * BLOCK)
        reach = (block + 1) * BLOCK
        probs = block_probs(q_ref[rows, :], k_ref, seg_col, seg_row, block, reach)
        out_ref[rows, :] = dot(probs.astype(bf16), v_ref[:reach, :], 0, 0).astype(bf16)


def attend(projected, seg_col, seg_row, heads):
    tokens = projected.shape[0]
    column = lambda part: pl.BlockSpec((SEQ, HEAD), lambda r, h: (r, part * heads + h))
    return pl.pallas_call(
        attend_kernel,
        grid=(tokens // SEQ, heads),
        in_specs=[
            column(0),
            column(1),
            column(2),
            pl.BlockSpec((SEQ, 1), lambda r, h: (r, 0)),
            pl.BlockSpec((1, SEQ), lambda r, h: (0, r)),
        ],
        out_specs=pl.BlockSpec((SEQ, HEAD), lambda r, h: (r, h)),
        out_shape=jax.ShapeDtypeStruct((tokens, heads * HEAD), bf16),
        compiler_params=pltpu.CompilerParams(vmem_limit_bytes=40 * 2**20),
        cost_estimate=pl.CostEstimate(
            flops=heads * tokens * SEQ * HEAD * 4,
            bytes_accessed=tokens * heads * HEAD * 8,
            transcendentals=heads * tokens * SEQ,
        ),
        name="attend",
    )(projected, projected, projected, seg_col, seg_row)


def attend_back_kernel(
    heads, q_ref, k_ref, v_ref, grad_ref, seg_col, seg_row, out_ref, dk_ref, dv_ref
):
    head = pl.program_id(1)
    width = heads * HEAD
    column = lambda part: pl.ds(pl.multiple_of(part * width + head * HEAD, HEAD), HEAD)
    dk_ref[...] = jnp.zeros_like(dk_ref)
    dv_ref[...] = jnp.zeros_like(dv_ref)
    for block in range(SEQ // BLOCK):
        rows = slice(block * BLOCK, (block + 1) * BLOCK)
        reach = (block + 1) * BLOCK
        q_block = q_ref[rows, :]
        g_block = grad_ref[rows, :]
        probs = block_probs(q_block, k_ref, seg_col, seg_row, block, reach)
        d_probs = dot(v_ref[:reach, :], g_block, 1, 1)
        delta = jnp.sum(probs * d_probs, axis=0, keepdims=True)
        d_scores = (probs * (d_probs - delta)).astype(bf16)
        dv_ref[:reach, :] += dot(probs.astype(bf16), g_block)
        dk_ref[:reach, :] += dot(d_scores, q_block)
        out_ref[rows, column(0)] = (dot(d_scores, k_ref[:reach, :], 0, 0) * SCALE).astype(bf16)
    out_ref[:, column(1)] = (dk_ref[...] * SCALE).astype(bf16)
    out_ref[:, column(2)] = dv_ref[...].astype(bf16)


def attend_back(projected, grad_attn, seg_col, seg_row, heads):
    tokens = projected.shape[0]
    column = lambda part: pl.BlockSpec((SEQ, HEAD), lambda r, h: (r, part * heads + h))
    return pl.pallas_call(
        functools.partial(attend_back_kernel, heads),
        grid=(tokens // SEQ, heads),
        in_specs=[
            column(0),
            column(1),
            column(2),
            column(0),
            pl.BlockSpec((SEQ, 1), lambda r, h: (r, 0)),
            pl.BlockSpec((1, SEQ), lambda r, h: (0, r)),
        ],
        out_specs=pl.BlockSpec((SEQ, 3 * heads * HEAD), lambda r, h: (r, 0)),
        out_shape=jax.ShapeDtypeStruct((tokens, 3 * heads * HEAD), bf16),
        scratch_shapes=[pltpu.VMEM((SEQ, HEAD), f32), pltpu.VMEM((SEQ, HEAD), f32)],
        compiler_params=pltpu.CompilerParams(vmem_limit_bytes=40 * 2**20),
        cost_estimate=pl.CostEstimate(
            flops=heads * tokens * SEQ * HEAD * 10,
            bytes_accessed=tokens * heads * HEAD * 14,
            transcendentals=heads * tokens * SEQ,
        ),
        name="attend_back",
    )(projected, projected, projected, grad_attn, seg_col, seg_row)


def norm_parts(value):
    mean = jnp.mean(value, axis=-1, keepdims=True)
    centered = value - mean
    inverse = lax.rsqrt(jnp.mean(centered * centered, axis=-1, keepdims=True) + 1e-05)
    return centered * inverse, inverse


def norm_backward(grad, gain, scaled, inverse):
    inner = grad * gain
    return inverse * (
        inner
        - jnp.mean(inner, axis=-1, keepdims=True)
        - scaled * jnp.mean(inner * scaled, axis=-1, keepdims=True)
    )


def gelu_parts(value):
    c = 0.7978845608028654
    square = value * value
    tanh = jnp.tanh(c * value * (1.0 + 0.044715 * square))
    half = 0.5 * (1.0 + tanh)
    slope = half + 0.5 * value * (1.0 - tanh * tanh) * c * (1.0 + 3 * 0.044715 * square)
    return value * half, slope


class Line:
    def __init__(self, name, size):
        self.name, self.n = name, size
        self.me = lax.axis_index(name)
        self.low = self.me < size // 2

    def slot_index(self, k):
        n = self.n
        return jnp.where(self.low, (self.me + k) % n, (self.me + n - k) % n)

    def gather(self, block):
        n = self.n
        from_left, from_right = [block], [block]
        for k in range(1, n):
            from_left.append(
                lax.ppermute(from_left[-1], self.name, [(j, j + 1) for j in range(k - 1, n - 1)])
            )
            from_right.append(
                lax.ppermute(from_right[-1], self.name, [(j, j - 1) for j in range(1, n - k + 1)])
            )
            low_side, high_side = from_right[k], from_left[k]
            if 2 * k >= n:
                low_side = jnp.where(self.me + k < n, from_right[k], from_left[n - k])
                high_side = jnp.where(self.me >= k, from_left[k], from_right[n - k])
            yield jnp.where(self.low, low_side, high_side)

    def reduce(self, parts):
        n = self.n
        from_left = from_right = None
        for k in range(1, n):
            other = parts[n - k] if n - k < k else parts[k]
            to_right = jnp.where(self.low, parts[k], other)
            to_left = jnp.where(self.low, other, parts[k])
            if k > 1:
                to_right = to_right + from_left.astype(f32)
                to_left = to_left + from_right.astype(f32)
            from_left = lax.ppermute(
                to_right.astype(bf16), self.name, [(j, j + 1) for j in range(k)]
            )
            from_right = lax.ppermute(
                to_left.astype(bf16), self.name, [(j, j - 1) for j in range(n - k, n)]
            )
        return parts[0] + from_left.astype(f32) + from_right.astype(f32)

    def reduce_index(self, k):
        n = self.n
        return jnp.where(self.low, (self.me + n - k) % n, (self.me + k) % n)

    def shuffle(self, array, rows):
        n = self.n
        cols = array.shape[1] // n
        out = jnp.zeros((n * rows, cols), array.dtype)
        for shift in range(n):
            target = (self.me + shift) % n
            source = (self.me + n - shift) % n
            block = lax.dynamic_slice_in_dim(array, target * cols, cols, axis=1)
            if shift:
                block = lax.ppermute(block, self.name, [(j, (j + shift) % n) for j in range(n)])
            out = lax.dynamic_update_slice_in_dim(out, block, source * rows, axis=0)
        return out


def flip(value, name, size, bit):
    return lax.ppermute(value, name, [(j, j ^ bit) for j in range(size)])


def sum_over(value, name, size):
    bit = 1
    while bit < size:
        value = value + flip(value, name, size, bit)
        bit *= 2
    return value


def halve(array, axis, name, size, bit):
    mine = (lax.axis_index(name) // bit) % 2
    sent = lax.dynamic_index_in_dim(array, 1 - mine, axis, keepdims=False)
    kept = lax.dynamic_index_in_dim(array, mine, axis, keepdims=False)
    return kept.astype(f32) + flip(sent, name, size, bit).astype(f32)


def scatter_rows(full, name, size):
    rows, cols = full.shape
    bits = [1 << b for b in range(size.bit_length() - 1)]
    shape = [2] * len(bits)
    block = rows // size
    array = full.reshape(*shape, block, cols)
    first = halve(array, len(bits) - 1, name, size, 1).astype(bf16)
    rest = bits[1:]
    if not rest:
        return first.astype(f32)
    parts = []
    for order, piece in zip(
        (rest, rest[::-1]), jnp.split(first, 2, axis=-2)
    ):
        left = list(rest[::-1])
        for bit in order:
            axis = left.index(bit)
            left.pop(axis)
            piece = halve(piece, axis, name, size, bit)
            if left:
                piece = piece.astype(bf16)
        parts.append(piece)
    return jnp.concatenate(parts, axis=0)


def scatter_cols(full, name, size):
    rows, cols = full.shape
    bits = [1 << b for b in range(size.bit_length() - 1)]
    block = cols // size
    array = full.reshape(rows, *([2] * len(bits)), block)
    first = halve(array, len(bits), name, size, 1).astype(bf16)
    rest = bits[1:]
    parts = []
    for order, piece in zip((rest, rest[::-1]), jnp.split(first, 2, axis=0)):
        left = list(rest[::-1])
        for bit in order:
            axis = 1 + left.index(bit)
            left.pop(axis - 1)
            piece = halve(piece, axis, name, size, bit)
            if left:
                piece = piece.astype(bf16)
        parts.append(piece)
    return jnp.concatenate(parts, axis=0)


def after(value, *earlier):
    return lax.optimization_barrier((value, *earlier))[0]


def make_body(n_dp, n_mp):
    def body(
        tokens, cotangent, segment, counts, ln_gain, ln_bias, w_qkv, b_qv, w_out, out_bias, w_up, b_up, w_down
    ):
        line = Line("mp", n_mp)
        gains, shifts, bias_pair = ln_gain.astype(f32), ln_bias.astype(f32), out_bias.astype(f32)
        share, width = tokens.shape
        head_cols = w_qkv.shape[2]
        heads = head_cols // HEAD
        group = segment.shape[0]
        seg_col, seg_row = segment[:, None], segment[None, :]
        me = line.me
        place = lambda whole, block, index: lax.dynamic_update_slice_in_dim(
            whole, block, index * share, axis=0
        )
        own_rows = lambda whole, index: lax.dynamic_slice_in_dim(whole, index * share, share, axis=0)

        count_here = counts.astype(f32)
        factor = (count_here / sum_over(count_here, "dp", n_dp))[0]

        slice_rows = w_out.shape[0] // n_dp
        w_slice = lax.dynamic_slice_in_dim(
            w_out, lax.axis_index("dp") * slice_rows, slice_rows, axis=0
        )
        w_slices = lax.all_gather(w_slice, "mp", axis=0)
        w_out_all = lax.all_gather(w_slices, "dp", axis=1).reshape(n_mp * w_out.shape[0], width)

        flat_qkv = w_qkv.reshape(width, 3 * head_cols)
        bias_rows = (
            jnp.stack([b_qv[0], jnp.zeros_like(b_qv[0]), b_qv[1]]).astype(f32).reshape(3 * head_cols)
        )
        tokens_all = jnp.zeros((group, width), bf16)
        normed1_all = jnp.zeros((group, width), bf16)
        projected = jnp.zeros((group, 3 * head_cols), bf16)
        last = None
        for k, block in enumerate([tokens, *line.gather(tokens)]):
            index = me if k == 0 else line.slot_index(k)
            normed = (norm_parts(block.astype(f32))[0] * gains[0] + shifts[0]).astype(bf16)
            proj = (dot(normed, flat_qkv) + bias_rows).astype(bf16)
            tokens_all = place(tokens_all, block, index)
            normed1_all = place(normed1_all, normed, index)
            projected = place(projected, proj, index)
            last = block
        attn = attend(projected, seg_col, seg_row, heads)

        cot_all = lax.all_gather(after(cotangent, last), "mp", axis=0, tiled=True)

        middle_all = tokens_all.astype(f32) + bias_pair[0] + dot(attn, w_out)
        for k, block in enumerate(line.gather(attn)):
            index = line.slot_index(k + 1)
            rows = lax.dynamic_slice_in_dim(w_out_all, index * head_cols, head_cols, axis=0)
            middle_all = middle_all + dot(block, rows)
        normed2_all = (norm_parts(middle_all)[0] * gains[1] + shifts[1]).astype(bf16)
        hidden = dot(normed2_all, w_up) + b_up.astype(f32)
        active, slope = gelu_parts(hidden)
        active = active.astype(bf16)
        d_hidden = (dot(cot_all, w_down, 1, 1) * slope).astype(bf16)

        d_normed2_parts = [
            dot(own_rows(d_hidden, me if k == 0 else line.reduce_index(k)), w_up, 1, 1)
            for k in [*range(1, n_mp), 0]
        ]
        d_normed2_parts = [d_normed2_parts[-1], *d_normed2_parts[:-1]]
        d_normed2 = line.reduce(d_normed2_parts)

        middle = own_rows(middle_all, me)
        scaled2, inverse2 = norm_parts(middle)
        cot = cotangent.astype(f32)
        d_middle = cot + norm_backward(d_normed2, gains[1], scaled2, inverse2)
        d_branch = d_middle.astype(bf16)
        d_attn = line.shuffle(dot(d_branch, w_out_all, 1, 1).astype(bf16), share)

        down = dot(active, w_down).astype(bf16)
        down_sum = lax.psum_scatter(
            after(down, d_normed2), "mp", scatter_dimension=0, tiled=True
        )
        layer_out = (middle + down_sum.astype(f32) + bias_pair[1]).astype(bf16)
        d_branch_all = lax.all_gather(d_branch, "mp", axis=0, tiled=True)

        grad_proj = attend_back(projected, d_attn, seg_col, seg_row, heads)
        d_normed1_parts = [
            dot(own_rows(grad_proj, me if k == 0 else line.reduce_index(k)), flat_qkv, 1, 1)
            for k in [*range(1, n_mp), 0]
        ]
        d_normed1_parts = [d_normed1_parts[-1], *d_normed1_parts[:-1]]
        d_normed1 = line.reduce(d_normed1_parts)
        scaled1, inverse1 = norm_parts(tokens.astype(f32))
        grad_input = d_middle + norm_backward(d_normed1, gains[0], scaled1, inverse1)

        scaled = lambda left, right: (factor * dot(left, right, 0, 0)).astype(bf16)
        grad_down = scatter_cols(scaled(active, cot_all), "dp", n_dp)
        grad_up = scatter_rows(scaled(normed2_all, d_hidden), "dp", n_dp)
        grad_qkv = scatter_rows(scaled(normed1_all, grad_proj), "dp", n_dp)
        grad_out = scatter_cols(scaled(attn, d_branch_all), "dp", n_dp)

        total = lambda value: jnp.sum(value.astype(f32), axis=0)
        heads_sum = jnp.stack(
            [total(grad_proj[:, :head_cols]), total(grad_proj[:, 2 * head_cols :])]
        )
        split_sums = jnp.concatenate([heads_sum.reshape(-1), total(d_hidden)])
        full_sums = jnp.concatenate(
            [
                total(d_normed1 * scaled1),
                total(d_normed2 * scaled2),
                total(d_normed1),
                total(d_normed2),
                total(d_branch),
                total(cot),
            ]
        )
        split_sums, full_sums = factor * split_sums, factor * full_sums
        split_sums = sum_over(split_sums, "dp", n_dp)
        full_sums = sum_over(sum_over(full_sums, "dp", n_dp), "mp", n_mp).reshape(3, 2, width)
        return (
            layer_out,
            factor * grad_input,
            full_sums[0],
            full_sums[1],
            grad_qkv.reshape(-1, 3, head_cols),
            split_sums[: 2 * head_cols].reshape(2, head_cols),
            grad_out,
            full_sums[2],
            grad_up,
            split_sums[2 * head_cols :],
            grad_down,
        )

    return body


def solution(mesh):
    split = P(("dp", "mp"), None)
    return jax.shard_map(
        make_body(mesh.shape["dp"], mesh.shape["mp"]),
        mesh=mesh,
        in_specs=(
            split, split, P("dp"), P("dp"), P(), P(), P(None, None, "mp"), P(None, "mp"), P("mp", None), P(),
            P(None, "mp"), P("mp"), P("mp", None),
        ),
        out_specs=(
            split, split, P(), P(), P("dp", None, "mp"), P(None, "mp"), P("mp", "dp"), P(), P("dp", "mp"), P("mp"),
            P("mp", "dp"),
        ),
        check_vma=False,
    )
```

time: 1420 us -> 798 us (0.56)
  waiting for transfers between devices: 1020 us -> 282 us
  starting transfers between devices: 0.71 us -> 112 us
  blocking collectives: 81.2 us -> 0 us
  local copies, waits for them, and re-layouts: 51.1 us -> 102 us
  Pallas kernels: 0 us -> 24.1 us
  other arithmetic: 49.5 us -> 66.6 us
    reduce_scatter x8 -> x1, waiting for transfers between devices: 719 us -> 0.01 us  [body(): lax.psum_scatter(after(down, d_normed2), 'mp', scatter_dimension=0, tiled...]
    all_gather x4, waiting for transfers between devices: 301 us -> 42.2 us  [the longest x1 31.3 us: body(): w_slices = lax.all_gather(w_slice, 'mp', axis=0)]
    ppermute x0 -> x58, waiting for transfers between devices: none -> 240 us  [the longest x6 110 us: gather(): lax.ppermute(from_right[-1], self.name, [(j, j - 1) for j in range(1, n -...]
    ppermute x0 -> x58, starting transfers between devices: none -> 112 us  [the longest x31 46.7 us: flip(): return lax.ppermute(value, name, [(j, j ^ bit) for j in range(size)])]
    psum x3 -> x0, blocking collectives: 81.2 us -> none  [the longest x1 42 us: body(): lax.psum((gain_local, shift_local, out_bias_local), ('dp', 'mp'))]
    dynamic_slice x0 -> x8, local copies, waits for them, and re-layouts: none -> 36.9 us  [the longest x3 27.5 us: halve(): kept = lax.dynamic_index_in_dim(array, mine, axis, keepdims=False)]
    pallas_call x0 -> x2, Pallas kernels: none -> 24.1 us  [the longest x1 15.3 us: attend_back(): pl.pallas_call(functools.partial(attend_back_kernel, heads), grid=(tokens...]
    squeeze x0 -> x17, local copies, waits for them, and re-layouts: none -> 14.3 us  [halve(): sent = lax.dynamic_index_in_dim(array, 1 - mine, axis, keepdims=False)]
  transfers between devices with their start and end apart: 12 -> 63, of which waited for: 12 -> 30; matrix products, arithmetic and copies ran while one was open for 9% -> 40% of each run, Pallas kernels for 0% -> 3%
where the time goes in v1:
time: 798 us; the launch traced here: 791 us
  waiting for transfers between devices  282 us (35%)
  matrix products  185 us (23%)
  starting transfers between devices  112 us (14%)
  local copies, waits for them, and re-layouts  102 us (13%)
  other arithmetic  66.6 us (8%)
  Pallas kernels  24.1 us (3%)
  between operations  18.3 us (2%)
    dot_general x24, matrix products, dot(): lax.dot_general(left, right, (((left_dim,), (right_dim,)), ((), ())), pre...  185 us
    ppermute x6, waiting for transfers between devices, gather(): lax.ppermute(from_right[-1], self.name, [(j, j - 1) for j in range(1, n -...  110 us
    ppermute x31, waiting for transfers between devices, flip(): return lax.ppermute(value, name, [(j, j ^ bit) for j in range(size)])  64.8 us
    ppermute x31, starting transfers between devices, flip(): return lax.ppermute(value, name, [(j, j ^ bit) for j in range(size)])  46.7 us
    all_gather x1, waiting for transfers between devices, body(): w_slices = lax.all_gather(w_slice, 'mp', axis=0)  31.3 us
    ppermute x6, starting transfers between devices, reduce(): lax.ppermute(to_right.astype(bf16), self.name, [(j, j + 1) for j in range...  29.3 us
    dynamic_slice x3, local copies, waits for them, and re-layouts, halve(): kept = lax.dynamic_index_in_dim(array, mine, axis, keepdims=False)  27.5 us
    unnamed x169, local copies, waits for them, and re-layouts  26.1 us
  transfers between devices with their start and end apart: 63, of which 30 were waited for; matrix products, arithmetic and copies ran while one was open for 40% of the time, Pallas kernels for 3%

profile of v1, /device:TPU:0, one launch (start us, length us, event | category | flops | bytes accessed | tf_op | source)
XLA Modules:
  0.0 790.6 jit_solution(14205676330936642479)
XLA Ops:
  9.6 31.3 %all-gather.11.cloned.1.call-done = bf16[256,2048]{1,0:T(8,128)(2,1)} async-done(((bf16[64,2048]{1,0:T(8,128)(2,1)}), bf16[256,2048]{1,0:T(8,128)(2,1)}) %all-gather.11.cloned.1.call-update) | async-done | bytes 1048592 | tf_op jit(solution)/shard_map/all_gather | solution.py:299
  42.2 5.6 collective-permute-start.1
  47.8 9.1 %copy.31 = bf16[2048,3,512]{0,2,1:T(8,128)(2,1)} copy(bf16[2048,3,512]{2,0,1:T(8,128)(2,1)} %param.19) | data formatting | bytes 12582912 | tf_op args[6]
  65.2 3.8 collective-permute-done.1
  76.2 22.3 %collective-permute-done.2 = bf16[256,2048]{1,0:T(8,128)(2,1)S(1)} collective-permute-done((bf16[256,2048]{1,0:T(8,128)(2,1)}, bf16[256,2048]{1,0:T(8,128)(2,1)S(1)}, u32[]{:S(2)}, u32[]{:S(2)}) %collective-permute-start.2) | collective-permute-done | bytes 1048608 | tf_op jit(solution)/shard_map/ppermute | solution.py:163
  103.4 19.5 %collective-permute-done.4 = bf16[256,2048]{1,0:T(8,128)(2,1)S(1)} collective-permute-done((bf16[256,2048]{1,0:T(8,128)(2,1)S(1)}, bf16[256,2048]{1,0:T(8,128)(2,1)S(1)}, u32[]{:S(2)}, u32[]{:S(2)}) %collective-permute-start.4) | collective-permute-done | bytes 1048608 | tf_op jit(solution)/shard_map/ppermute | solution.py:163
  127.6 8.9 %attend.1 = bf16[1024,512]{1,0:T(8,128)(2,1)} custom-call(bf16[1024,1536]{1,0:T(8,128)(2,1)S(1)} %fusion.11.q_ref.k_ref.v_ref, bf16[1024,1536]{1,0:T(8,128)(2,1)S(1)} %fusion.11.q_ref.k_ref.v_ref, bf16[1024,1536]{1,0:T(8,128)(2,1)S(1)} %fusion.11.q_ref.k_ref.v_ref, s32[1024,1]{1,0:T(8,128)S(1)} %copy.32.seg_col, s32[1,1024]{1,0:T(1,128)S(1)} %bitcast.155), custom_call_target="tpu_custom_call" | custom-call | flops 2147483648 | bytes 4194304 | tf_op jit(solution)/shard_map/attend/pallas_call | solution.py:47
  140.5 17.2 %collective-permute-done.7 = bf16[1024,512]{1,0:T(8,128)(2,1)} collective-permute-done((bf16[1024,512]{1,0:T(8,128)(2,1)}, bf16[1024,512]{1,0:T(8,128)(2,1)}, u32[]{:S(2)}, u32[]{:S(2)}) %collective-permute-start.7) | collective-permute-done | bytes 1048608 | tf_op jit(solution)/shard_map/ppermute | solution.py:160
  159.4 3.4 collective-permute-done.6
  177.2 8.9 %collective-permute-done.8 = bf16[1024,512]{1,0:T(8,128)(2,1)} collective-permute-done((bf16[1024,512]{1,0:T(8,128)(2,1)}, bf16[1024,512]{1,0:T(8,128)(2,1)}, u32[]{:S(2)}, u32[]{:S(2)}) %collective-permute-start.8) | collective-permute-done | bytes 1048608 | tf_op jit(solution)/shard_map/ppermute | solution.py:163
  187.6 6.9 fusion.116
  194.5 7.9 fusion.51
  202.4 7.7 fusion.53
  210.1 55.8 %collective-permute-done.10 = bf16[1024,512]{1,0:T(8,128)(2,1)} collective-permute-done((bf16[1024,512]{1,0:T(8,128)(2,1)}, bf16[1024,512]{1,0:T(8,128)(2,1)}, u32[]{:S(2)}, u32[]{:S(2)}) %collective-permute-start.10) | collective-permute-done | bytes 1048608 | tf_op jit(solution)/shard_map/ppermute | solution.py:163
  265.9 15.9 %fusion.113 = (f32[1024]{0:T(1024)S(1)}, f32[1024,2048]{1,0:T(8,128)}) fusion(bf16[2048,2048]{1,0:T(8,128)(2,1)} %bitcast.177, s32[]{:T(128)S(6)} %select_n.443, bf16[1024,512]{1,0:T(8,128)(2,1)} %collective-permute-done.11, bf16[1024,512]{1,0:T(8,128)(2,1)} %collective-permute-done.6, bf16[1024,512]{1,0:T(8,128)(2,1)} %collective-permute-done.10, ...), kind=kOutput, calls=%fused_computation.254 | convolution fusion | flops 2163735552 | bytes 44052488 | tf_op jit(solution)/shard_map/dot_general | solution.py:18
  281.8 4.5 multiply_reduce_fusion
  287.6 13.6 %fusion.103 = f32[1024,2048]{1,0:T(8,128)} fusion(bf16[2048,2048]{1,0:T(8,128)(2,1)} %param.23, f32[1024,2048]{1,0:T(8,128)S(1)} %copy-done.7, f32[2048]{0:T(1024)S(1)} %bitcast.207, f32[2048]{0:T(1024)S(1)} %bitcast.200, f32[1024]{0:T(1024)S(1)} %add_rsqrt_fusion, f32[1024]{0:T(1024)S(1)} %broadcast_multiply_fusion.1), kind=kOutput, calls=%fused_computation.244 | convolution fusion | flops 8600420352 | bytes 25190400 | tf_op jit(solution)/shard_map/dot_general | solution.py:18
  301.2 18.5 %convert_reduce_fusion = (f32[2048]{0:T(1024)}, bf16[1024,2048]{1,0:T(8,128)(2,1)S(1)}) fusion(f32[1024,2048]{1,0:T(8,128)} %fusion.103, f32[2048]{0:T(1024)S(1)} %convert_element_type.419, bf16[1024,2048]{1,0:T(8,128)(2,1)} %all-gather.7.cloned.1.call-done, bf16[2048,2048]{1,0:T(8,128)(2,1)} %param.25), kind=kOutput, calls=%fused_computation.7 | convolution fusion | flops 8633972736 | bytes 25182208 | tf_op jit(solution)/shard_map/dot_general | solution.py:18
  319.7 8.3 %fusion.114 = (bf16[256,2048]{1,0:T(8,128)(2,1)}, f32[256,2048]{1,0:T(8,128)S(1)}) fusion(bf16[2048,2048]{1,0:T(8,128)(2,1)} %param.23, bf16[1024,2048]{1,0:T(8,128)(2,1)S(1)} %get-tuple-element.93, s32[]{:T(128)S(6)} %select_n.427), kind=kOutput, calls=%fused_computation.255 | convolution fusion | flops 2148007936 | bytes 12582916 | tf_op jit(solution)/shard_map/dot_general | solution.py:18
  332.0 16.4 %multiply_convert_fusion.1 = bf16[2048,2048]{1,0:T(8,128)(2,1)} fusion(bf16[1024,2048]{1,0:T(8,128)(2,1)S(1)} %get-tuple-element.93, f32[]{:T(128)} %bitcast.11, f32[1024,2048]{1,0:T(8,128)} %get-tuple-element.86, f32[2048]{0:T(1024)S(1)} %bitcast.208, f32[2048]{0:T(1024)S(1)} %bitcast.201, f32[1024]{0:T(1024)S(1)} %add_rsqrt_fusion, ...), kind=kOutput, calls=%fused_computation.1 | convolution fusion | flops 8608808960 | bytes 20996100 | tf_op jit(solution)/shard_map/dot_general | solution.py:18
  348.5 13.6 %convolution_convert_fusion = bf16[1024,2048]{1,0:T(8,128)(2,1)} fusion(bf16[2048,2048]{1,0:T(8,128)(2,1)S(1)} %bitcast.212, f32[1024,2048]{1,0:T(8,128)} %fusion.103, f32[2048]{0:T(1024)S(1)} %convert_element_type.419), kind=kOutput, calls=%fused_computation.21 | convolution fusion | flops 8613003264 | bytes 20979712 | tf_op jit(solution)/shard_map/dot_general | solution.py:18
  362.1 4.7 dynamic-slice_bitcast_fusion
  366.8 7.7 add_convert_fusion.9
  376.8 16.6 %multiply_convert_fusion = bf16[2048,2048]{1,0:T(8,128)(2,1)} fusion(bf16[1024,2048]{1,0:T(8,128)(2,1)} %all-gather.7.cloned.1.call-done, f32[]{:T(128)} %bitcast.11, f32[1024,2048]{1,0:T(8,128)} %fusion.103, f32[2048]{0:T(1024)S(1)} %convert_element_type.419), kind=kOutput, calls=%fused_computation | convolution fusion | flops 8619294720 | bytes 20979716 | tf_op jit(solution)/shard_map/dot_general | solution.py:18
  393.6 3.7 fusion.61
  402.8 6.7 collective-permute-start.14
  409.9 3.7 fusion.63
  413.6 14.4 %reshape.229 = bf16[2048,2,2,2,256]{4,3,2,1,0:T(2,128)(2,1)} reshape(bf16[2048,2048]{1,0:T(8,128)(2,1)} %multiply_convert_fusion) | data formatting | bytes 16777216 | tf_op jit(solution)/shard_map/reshape | solution.py:255
  431.1 4.6 multiply_reduce_fusion.1
  435.8 20.2 %constant_dynamic-slice_fusion.1 = (bf16[2048,2,2,1,256]{4,3,2,1,0:T(2,128)(2,1)}, bf16[2048,2,2,1,256]{4,3,2,1,0:T(2,128)(2,1)S(1)}) fusion(bf16[2048,2,2,2,256]{4,3,2,1,0:T(2,128)(2,1)} %reshape.229, s32[]{:T(128)S(6)} %select_n.457, s32[]{:T(128)S(6)} %select_n.458), kind=kLoop, calls=%fused_computation.188 | loop fusion | bytes 16777224 | tf_op jit(solution)/shard_map/jit(dynamic_index_in_dim)/dynamic_slice | solution.py:222
  455.9 3.4 copy.57
  464.9 5.5 fusion.1
  475.9 3.9 fusion
  483.1 15.2 %collective-permute-done.51 = bf16[2,128,2048]{2,1,0:T(8,128)(2,1)} collective-permute-done((bf16[2,128,2048]{2,1,0:T(8,128)(2,1)}, bf16[2,128,2048]{2,1,0:T(8,128)(2,1)}, u32[]{:S(2)}, u32[]{:S(2)}) %collective-permute-start.51) | collective-permute-done | bytes 1048608 | tf_op jit(solution)/shard_map/ppermute | solution.py:208
  506.6 14.1 %collective-permute-done.56 = bf16[1024,2,256]{2,0,1:T(8,128)(2,1)S(1)} collective-permute-done((bf16[1024,2,256]{2,0,1:T(8,128)(2,1)S(1)}, bf16[1024,2,256]{2,0,1:T(8,128)(2,1)S(1)}, u32[]{:S(2)}, u32[]{:S(2)}) %collective-permute-start.56) | collective-permute-done | bytes 1048608 | tf_op jit(solution)/shard_map/ppermute | solution.py:208
  521.9 5.8 convert_reduce_fusion.8
  527.7 6.1 convolution_convert_fusion.1
  545.6 8.1 %collective-permute-done.22 = bf16[256,512]{1,0:T(8,128)(2,1)S(1)} collective-permute-done((bf16[256,512]{1,0:T(8,128)(2,1)S(1)}, bf16[256,512]{1,0:T(8,128)(2,1)S(1)}, u32[]{:S(2)}, u32[]{:S(2)}) %collective-permute-start.22) | collective-permute-done | bytes 262176 | tf_op jit(solution)/shard_map/ppermute | solution.py:202
  555.3 15.3 %attend_back.1 = bf16[1024,1536]{1,0:T(8,128)(2,1)S(1)} custom-call(bf16[1024,1536]{1,0:T(8,128)(2,1)S(1)} %copy-done.3, bf16[1024,1536]{1,0:T(8,128)(2,1)S(1)} %copy-done.3, bf16[1024,1536]{1,0:T(8,128)(2,1)S(1)} %copy-done.3, bf16[1024,512]{1,0:T(8,128)(2,1)S(1)} %constant_dynamic-update-slice_fusion.4.grad_ref, s32[1024,1]{1,0:T(8,128)S(1)} %copy.32.seg_col, ...), custom_call_target="tpu_custom_call" | custom-call | flops 5368709120 | bytes 7340032 | tf_op jit(solution)/shard_map/attend_back/pallas_call | solution.py:96
  570.6 3.1 fusion.115
  573.8 7.3 collective-permute-start.24
  584.6 18.1 %collective-permute-done.24 = bf16[256,2048]{1,0:T(8,128)(2,1)S(1)} collective-permute-done((bf16[256,2048]{1,0:T(8,128)(2,1)S(1)}, bf16[256,2048]{1,0:T(8,128)(2,1)S(1)}, u32[]{:S(2)}, u32[]{:S(2)}) %collective-permute-start.24) | collective-permute-done | bytes 1048608 | tf_op jit(solution)/shard_map/ppermute | solution.py:181
  602.8 3.3 add_convert_fusion.4
  606.0 5.4 collective-permute-start.25
  613.1 7.6 multiply_convert_fusion.2
  620.7 3.0 constant_dynamic-slice_fusion.5
  623.7 4.8 copy.35
  628.5 4.7 fusion.83
  633.3 3.7 add_convert_fusion.3
  638.5 6.2 collective-permute-start.26
  654.0 4.9 copy.44
  660.1 11.8 %collective-permute-done.29 = bf16[256,2048]{1,0:T(8,128)(2,1)} collective-permute-done((bf16[256,2048]{1,0:T(8,128)(2,1)}, bf16[256,2048]{1,0:T(8,128)(2,1)}, u32[]{:S(2)}, u32[]{:S(2)}) %collective-permute-start.29) | collective-permute-done | bytes 1048608 | tf_op jit(solution)/shard_map/ppermute | solution.py:184
  672.8 6.2 fusion.43
  692.3 9.6 %collective-permute-start.33 = (f32[12288]{0:T(1024)S(1)}, f32[12288]{0:T(1024)S(1)}, u32[]{:S(2)}, u32[]{:S(2)}) collective-permute-start(f32[12288]{0:T(1024)S(1)} %add.641), channel_id=1, source_target_pairs={{0,1},{1,0},{2,3},{3,2},{4,5},{5,4},{6,7},{7,6},{8,9},{9,8},{10,11... | collective-permute-start | bytes 147464 | tf_op jit(solution)/shard_map/ppermute | solution.py:208
  704.2 3.6 collective-permute-done.33
  712.4 5.1 collective-permute-done.34
  725.0 10.9 %all-gather.9.cloned.1.call-done = bf16[1024,2048]{1,0:T(8,128)(2,1)} async-done(((bf16[256,2048]{1,0:T(8,128)(2,1)}), bf16[1024,2048]{1,0:T(8,128)(2,1)}) %all-gather.9.cloned.1.call-update) | async-done | bytes 4194320 | tf_op jit(solution)/shard_map/all_gather | solution.py:352
  735.9 6.2 multiply_convert_fusion.5
  742.1 3.5 reshape.227
  745.7 4.3 constant_dynamic-slice_fusion.3
  752.2 9.9 %collective-permute-done.37 = bf16[128,1536]{0,1:T(8,128)(2,1)S(1)} collective-permute-done((bf16[128,1536]{0,1:T(8,128)(2,1)S(1)}, bf16[128,1536]{0,1:T(8,128)(2,1)S(1)}, u32[]{:S(2)}, u32[]{:S(2)}) %collective-permute-start.37) | collective-permute-done | bytes 393248 | tf_op jit(solution)/shard_map/ppermute | solution.py:208
  765.6 3.2 copy.42
  773.4 4.4 collective-permute-done.44
  779.2 3.7 collective-permute-done.45
  (397 shorter events, 159.1 us)
Async XLA Ops:
  7.2 33.6 %all-gather.11.cloned.1.call-start = ((), (), s32[]{:S(2)}) async-start(), calls=%async_computation.4 | async-start | bytes 1310720 | tf_op jit(solution)/shard_map/all_gather | solution.py:299
  9.5 185.0 %all-gather.13.cloned.1.call-start = ((), (), s32[]{:S(2)}) async-start(), calls=%async_computation.5 | async-start | bytes 9437184 | tf_op jit(solution)/shard_map/all_gather | solution.py:300
  40.9 260.4 %all-gather.7.cloned.1.call-start = ((), (), s32[]{:S(2)}) async-start(), calls=%async_computation.1 | async-start | bytes 5242880 | tf_op jit(solution)/shard_map/all_gather | solution.py:320
  40.9 28.9 %collective-permute-start = (bf16[256,2048]{1,0:T(8,128)(2,1)}, bf16[256,2048]{1,0:T(8,128)(2,1)}, u32[]{:S(2)}, u32[]{:S(2)}) collective-permute-start(bf16[256,2048]{1,0:T(8,128)(2,1)} %param.13), channel_id=1, source_target_pairs={{1,0},{2,1},{3,2},{5,4},{6,5},{7,6},{9,8},{10,9},{11,10},{13,12},{... | collective-permute-start | bytes 3145736 | tf_op jit(solution)/shard_map/ppermute | solution.py:163
  42.2 26.9 %collective-permute-start.1 = (bf16[256,2048]{1,0:T(8,128)(2,1)}, bf16[256,2048]{1,0:T(8,128)(2,1)}, u32[]{:S(2)}, u32[]{:S(2)}) collective-permute-start(bf16[256,2048]{1,0:T(8,128)(2,1)} %param.13), channel_id=1, source_target_pairs={{0,1},{1,2},{2,3},{4,5},{5,6},{6,7},{8,9},{9,10},{10,11},{12,13},{... | collective-permute-start | bytes 3145736 | tf_op jit(solution)/shard_map/ppermute | solution.py:160
  61.2 64.3 %copy-start.44 = (f32[1,2048]{1,0:T(1,128)}, f32[1,2048]{1,0:T(1,128)S(1)}, u32[]{:S(2)}) copy-start(f32[1,2048]{1,0:T(1,128)S(1)} %get-tuple-element.82) | copy-start | bytes 24580
  69.1 6.4 collective-permute-start.3
  69.8 28.7 %collective-permute-start.2 = (bf16[256,2048]{1,0:T(8,128)(2,1)}, bf16[256,2048]{1,0:T(8,128)(2,1)S(1)}, u32[]{:S(2)}, u32[]{:S(2)}) collective-permute-start(bf16[256,2048]{1,0:T(8,128)(2,1)} %collective-permute-done), channel_id=1, source_target_pairs={{1,0},{2,1},{5,4},{6,5},{9,8},{10,9},{13,12},{14,13},{17,16},{18,1... | collective-permute-start | bytes 3145736 | tf_op jit(solution)/shard_map/ppermute | solution.py:163
  75.5 28.0 %collective-permute-start.5 = (bf16[256,2048]{1,0:T(8,128)(2,1)S(1)}, bf16[256,2048]{1,0:T(8,128)(2,1)S(1)}, u32[]{:S(2)}, u32[]{:S(2)}) collective-permute-start(bf16[256,2048]{1,0:T(8,128)(2,1)S(1)} %collective-permute-done.3), channel_id=1, source_target_pairs={{2,3},{6,7},{10,11},{14,15},{18,19},{22,23},{26,27},{30,31}} | collective-permute-start | bytes 3145736 | tf_op jit(solution)/shard_map/ppermute | solution.py:160
  98.5 24.4 %collective-permute-start.4 = (bf16[256,2048]{1,0:T(8,128)(2,1)S(1)}, bf16[256,2048]{1,0:T(8,128)(2,1)S(1)}, u32[]{:S(2)}, u32[]{:S(2)}) collective-permute-start(bf16[256,2048]{1,0:T(8,128)(2,1)S(1)} %collective-permute-done.2), channel_id=1, source_target_pairs={{1,0},{5,4},{9,8},{13,12},{17,16},{21,20},{25,24},{29,28}} | collective-permute-start | bytes 3145736 | tf_op jit(solution)/shard_map/ppermute | solution.py:163
  136.5 21.2 %collective-permute-start.7 = (bf16[1024,512]{1,0:T(8,128)(2,1)}, bf16[1024,512]{1,0:T(8,128)(2,1)}, u32[]{:S(2)}, u32[]{:S(2)}) collective-permute-start(bf16[1024,512]{1,0:T(8,128)(2,1)} %attend.1), channel_id=1, source_target_pairs={{0,1},{1,2},{2,3},{4,5},{5,6},{6,7},{8,9},{9,10},{10,11},{12,13},{... | collective-permute-start | bytes 3145736 | tf_op jit(solution)/shard_map/ppermute | solution.py:160
  139.2 23.5 %collective-permute-start.6 = (bf16[1024,512]{1,0:T(8,128)(2,1)}, bf16[1024,512]{1,0:T(8,128)(2,1)}, u32[]{:S(2)}, u32[]{:S(2)}) collective-permute-start(bf16[1024,512]{1,0:T(8,128)(2,1)} %attend.1), channel_id=1, source_target_pairs={{1,0},{2,1},{3,2},{5,4},{6,5},{7,6},{9,8},{10,9},{11,10},{13,12},{... | collective-permute-start | bytes 3145736 | tf_op jit(solution)/shard_map/ppermute | solution.py:163
  157.7 17.9 %collective-permute-start.9 = (bf16[1024,512]{1,0:T(8,128)(2,1)}, bf16[1024,512]{1,0:T(8,128)(2,1)}, u32[]{:S(2)}, u32[]{:S(2)}) collective-permute-start(bf16[1024,512]{1,0:T(8,128)(2,1)} %collective-permute-done.7), channel_id=1, source_target_pairs={{1,2},{2,3},{5,6},{6,7},{9,10},{10,11},{13,14},{14,15},{17,18},{18... | collective-permute-start | bytes 3145736 | tf_op jit(solution)/shard_map/ppermute | solution.py:160
  162.8 23.3 %collective-permute-start.8 = (bf16[1024,512]{1,0:T(8,128)(2,1)}, bf16[1024,512]{1,0:T(8,128)(2,1)}, u32[]{:S(2)}, u32[]{:S(2)}) collective-permute-start(bf16[1024,512]{1,0:T(8,128)(2,1)} %collective-permute-done.6), channel_id=1, source_target_pairs={{1,0},{2,1},{5,4},{6,5},{9,8},{10,9},{13,12},{14,13},{17,16},{18,1... | collective-permute-start | bytes 3145736 | tf_op jit(solution)/shard_map/ppermute | solution.py:163
  164.7 1.6 collective-permute-start.18
  166.9 3.7 collective-permute-start.19
  171.2 3.7 collective-permute-start.20
  175.5 346.4 %reduce-scatter.2.cloned.1.call-start = ((), (), s32[]{:S(2)}) async-start(), calls=%async_computation.2 | async-start | bytes 5242880 | tf_op jit(solution)/shard_map/reduce_scatter | solution.py:348
  175.6 34.5 %collective-permute-start.11 = (bf16[1024,512]{1,0:T(8,128)(2,1)}, bf16[1024,512]{1,0:T(8,128)(2,1)}, u32[]{:S(2)}, u32[]{:S(2)}) collective-permute-start(bf16[1024,512]{1,0:T(8,128)(2,1)} %collective-permute-done.9), channel_id=1, source_target_pairs={{2,3},{6,7},{10,11},{14,15},{18,19},{22,23},{26,27},{30,31}} | collective-permute-start | bytes 3145736 | tf_op jit(solution)/shard_map/ppermute | solution.py:160
  186.1 79.8 %collective-permute-start.10 = (bf16[1024,512]{1,0:T(8,128)(2,1)}, bf16[1024,512]{1,0:T(8,128)(2,1)}, u32[]{:S(2)}, u32[]{:S(2)}) collective-permute-start(bf16[1024,512]{1,0:T(8,128)(2,1)} %collective-permute-done.8), channel_id=1, source_target_pairs={{1,0},{5,4},{9,8},{13,12},{17,16},{21,20},{25,24},{29,28}} | collective-permute-start | bytes 3145736 | tf_op jit(solution)/shard_map/ppermute | solution.py:163
  328.0 38.8 %collective-permute-start.12 = (bf16[256,2048]{1,0:T(8,128)(2,1)}, bf16[256,2048]{1,0:T(8,128)(2,1)}, u32[]{:S(2)}, u32[]{:S(2)}) collective-permute-start(bf16[256,2048]{1,0:T(8,128)(2,1)} %get-tuple-element.87), channel_id=1, source_target_pairs={{0,1},{4,5},{8,9},{12,13},{16,17},{20,21},{24,25},{28,29}} | collective-permute-start | bytes 3145736 | tf_op jit(solution)/shard_map/ppermute | solution.py:181
  330.4 36.4 %collective-permute-start.15 = (bf16[256,2048]{1,0:T(8,128)(2,1)}, bf16[256,2048]{1,0:T(8,128)(2,1)}, u32[]{:S(2)}, u32[]{:S(2)}) collective-permute-start(bf16[256,2048]{1,0:T(8,128)(2,1)} %get-tuple-element.87), channel_id=1, source_target_pairs={{3,2},{7,6},{11,10},{15,14},{19,18},{23,22},{27,26},{31,30}} | collective-permute-start | bytes 3145736 | tf_op jit(solution)/shard_map/ppermute | solution.py:184
  366.8 98.1 %collective-permute-start.48 = (bf16[2,2,256,2048]{3,2,1,0:T(8,128)(2,1)}, bf16[2,2,256,2048]{3,2,1,0:T(8,128)(2,1)}, u32[]{:S(2)}, u32[]{:S(2)}) collective-permute-start(bf16[2,2,256,2048]{3,2,1,0:T(8,128)(2,1)} %dynamic-slice_bitcast_fusion), channel_id=1, source_target_pairs={{0,4},{4,0},{8,12},{12,8},{16,20},{20,16},{24,28},{28,24},{1,5},{5... | collective-permute-start | bytes 12582920 | tf_op jit(solution)/shard_map/ppermute | solution.py:208
  374.5 24.9 %collective-permute-start.13 = (bf16[256,2048]{1,0:T(8,128)(2,1)}, bf16[256,2048]{1,0:T(8,128)(2,1)S(1)}, u32[]{:S(2)}, u32[]{:S(2)}) collective-permute-start(bf16[256,2048]{1,0:T(8,128)(2,1)} %get-tuple-element.65), channel_id=1, source_target_pairs={{0,1},{1,2},{4,5},{5,6},{8,9},{9,10},{12,13},{13,14},{16,17},{17,1... | collective-permute-start | bytes 3145736 | tf_op jit(solution)/shard_map/ppermute | solution.py:181
  375.9 23.6 %collective-permute-start.16 = (bf16[256,2048]{1,0:T(8,128)(2,1)S(1)}, bf16[256,2048]{1,0:T(8,128)(2,1)S(1)}, u32[]{:S(2)}, u32[]{:S(2)}) collective-permute-start(bf16[256,2048]{1,0:T(8,128)(2,1)S(1)} %get-tuple-element.66), channel_id=1, source_target_pairs={{2,1},{3,2},{6,5},{7,6},{10,9},{11,10},{14,13},{15,14},{18,17},{19... | collective-permute-start | bytes 3145736 | tf_op jit(solution)/shard_map/ppermute | solution.py:184
  401.6 28.4 %collective-permute-start.17 = (bf16[256,2048]{1,0:T(8,128)(2,1)}, bf16[256,2048]{1,0:T(8,128)(2,1)}, u32[]{:S(2)}, u32[]{:S(2)}) collective-permute-start(bf16[256,2048]{1,0:T(8,128)(2,1)} %get-tuple-element.58), channel_id=1, source_target_pairs={{1,0},{2,1},{3,2},{5,4},{6,5},{7,6},{9,8},{10,9},{11,10},{13,12},{... | collective-permute-start | bytes 3145736 | tf_op jit(solution)/shard_map/ppermute | solution.py:184
  402.8 28.3 %collective-permute-start.14 = (bf16[256,2048]{1,0:T(8,128)(2,1)}, bf16[256,2048]{1,0:T(8,128)(2,1)}, u32[]{:S(2)}, u32[]{:S(2)}) collective-permute-start(bf16[256,2048]{1,0:T(8,128)(2,1)} %get-tuple-element.57), channel_id=1, source_target_pairs={{0,1},{1,2},{2,3},{4,5},{5,6},{6,7},{8,9},{9,10},{10,11},{12,13},{... | collective-permute-start | bytes 3145736 | tf_op jit(solution)/shard_map/ppermute | solution.py:181
  435.7 300.2 %all-gather.9.cloned.1.call-start = ((), (), s32[]{:S(2)}) async-start(), calls=%async_computation.3 | async-start | bytes 5242880 | tf_op jit(solution)/shard_map/all_gather | solution.py:352
  459.3 16.5 %collective-permute-start.53 = (bf16[2048,2,2,256]{3,0,2,1:T(8,128)(2,1)}, bf16[2048,2,2,256]{3,0,2,1:T(8,128)(2,1)}, u32[]{:S(2)}, u32[]{:S(2)}) collective-permute-start(bf16[2048,2,2,256]{3,0,2,1:T(8,128)(2,1)} %bitcast.152), channel_id=1, source_target_pairs={{0,4},{4,0},{8,12},{12,8},{16,20},{20,16},{24,28},{28,24},{1,5},{5... | collective-permute-start | bytes 12582920 | tf_op jit(solution)/shard_map/ppermute | solution.py:208
  471.9 26.3 %collective-permute-start.51 = (bf16[2,128,2048]{2,1,0:T(8,128)(2,1)}, bf16[2,128,2048]{2,1,0:T(8,128)(2,1)}, u32[]{:S(2)}, u32[]{:S(2)}) collective-permute-start(bf16[2,128,2048]{2,1,0:T(8,128)(2,1)} %dynamic-slice_bitcast_fusion.3), channel_id=1, source_target_pairs={{0,16},{4,20},{8,24},{12,28},{16,0},{20,4},{24,8},{28,12},{1,17},{... | collective-permute-start | bytes 3145736 | tf_op jit(solution)/shard_map/ppermute | solution.py:208
  474.5 27.8 %collective-permute-start.49 = (bf16[2,128,2048]{2,1,0:T(8,128)(2,1)}, bf16[2,128,2048]{2,1,0:T(8,128)(2,1)}, u32[]{:S(2)}, u32[]{:S(2)}) collective-permute-start(bf16[2,128,2048]{2,1,0:T(8,128)(2,1)} %dynamic-slice_bitcast_fusion.4), channel_id=1, source_target_pairs={{0,8},{4,12},{8,0},{12,4},{16,24},{20,28},{24,16},{28,20},{1,9},{5... | collective-permute-start | bytes 3145736 | tf_op jit(solution)/shard_map/ppermute | solution.py:208
  480.2 40.4 %collective-permute-start.56 = (bf16[1024,2,256]{2,0,1:T(8,128)(2,1)S(1)}, bf16[1024,2,256]{2,0,1:T(8,128)(2,1)S(1)}, u32[]{:S(2)}, u32[]{:S(2)}) collective-permute-start(bf16[1024,2,256]{2,0,1:T(8,128)(2,1)S(1)} %dynamic-slice_bitcast_fusion.1), channel_id=1, source_target_pairs={{0,16},{4,20},{8,24},{12,28},{16,0},{20,4},{24,8},{28,12},{1,17},{... | collective-permute-start | bytes 3145736 | tf_op jit(solution)/shard_map/ppermute | solution.py:208
  481.9 54.7 %collective-permute-start.54 = (bf16[1024,2,256]{2,0,1:T(8,128)(2,1)}, bf16[1024,2,256]{2,0,1:T(8,128)(2,1)}, u32[]{:S(2)}, u32[]{:S(2)}) collective-permute-start(bf16[1024,2,256]{2,0,1:T(8,128)(2,1)} %dynamic-slice_bitcast_fusion.2), channel_id=1, source_target_pairs={{0,8},{4,12},{8,0},{12,4},{16,24},{20,28},{24,16},{28,20},{1,9},{5... | collective-permute-start | bytes 3145736 | tf_op jit(solution)/shard_map/ppermute | solution.py:208
  500.8 80.2 %collective-permute-start.52 = (bf16[128,2048]{1,0:T(8,128)(2,1)}, bf16[128,2048]{1,0:T(8,128)(2,1)S(1)}, u32[]{:S(2)}, u32[]{:S(2)}) collective-permute-start(bf16[128,2048]{1,0:T(8,128)(2,1)} %dynamic-slice_bitcast_fusion.9), channel_id=1, source_target_pairs={{0,8},{4,12},{8,0},{12,4},{16,24},{20,28},{24,16},{28,20},{1,9},{5... | collective-permute-start | bytes 1572872 | tf_op jit(solution)/shard_map/ppermute | solution.py:208
  505.2 76.8 %collective-permute-start.50 = (bf16[128,2048]{1,0:T(8,128)(2,1)}, bf16[128,2048]{1,0:T(8,128)(2,1)}, u32[]{:S(2)}, u32[]{:S(2)}) collective-permute-start(bf16[128,2048]{1,0:T(8,128)(2,1)} %dynamic-slice_bitcast_fusion.10), channel_id=1, source_target_pairs={{0,16},{4,20},{8,24},{12,28},{16,0},{20,4},{24,8},{28,12},{1,17},{... | collective-permute-start | bytes 1572872 | tf_op jit(solution)/shard_map/ppermute | solution.py:208
  534.1 10.0 %collective-permute-start.21 = (bf16[256,512]{1,0:T(8,128)(2,1)S(1)}, bf16[256,512]{1,0:T(8,128)(2,1)S(1)}, u32[]{:S(2)}, u32[]{:S(2)}) collective-permute-start(bf16[256,512]{1,0:T(8,128)(2,1)S(1)} %get-tuple-element.72), channel_id=1, source_target_pairs={{0,1},{1,2},{2,3},{3,0},{4,5},{5,6},{6,7},{7,4},{8,9},{9,10},{10,1... | collective-permute-start | bytes 786440 | tf_op jit(solution)/shard_map/ppermute | solution.py:202
  538.3 15.5 %collective-permute-start.22 = (bf16[256,512]{1,0:T(8,128)(2,1)S(1)}, bf16[256,512]{1,0:T(8,128)(2,1)S(1)}, u32[]{:S(2)}, u32[]{:S(2)}) collective-permute-start(bf16[256,512]{1,0:T(8,128)(2,1)S(1)} %get-tuple-element.71), channel_id=1, source_target_pairs={{0,2},{1,3},{2,0},{3,1},{4,6},{5,7},{6,4},{7,5},{8,10},{9,11},{10,... | collective-permute-start | bytes 786440 | tf_op jit(solution)/shard_map/ppermute | solution.py:202
  541.8 13.5 %collective-permute-start.23 = (bf16[256,512]{1,0:T(8,128)(2,1)S(1)}, bf16[256,512]{1,0:T(8,128)(2,1)S(1)}, u32[]{:S(2)}, u32[]{:S(2)}) collective-permute-start(bf16[256,512]{1,0:T(8,128)(2,1)S(1)} %get-tuple-element.70), channel_id=1, source_target_pairs={{0,3},{1,0},{2,1},{3,2},{4,7},{5,4},{6,5},{7,6},{8,11},{9,8},{10,9... | collective-permute-start | bytes 786440 | tf_op jit(solution)/shard_map/ppermute | solution.py:202
  544.1 101.0 %collective-permute-start.57 = (bf16[1024,256]{1,0:T(8,128)(2,1)}, bf16[1024,256]{1,0:T(8,128)(2,1)}, u32[]{:S(2)}, u32[]{:S(2)}) collective-permute-start(bf16[1024,256]{1,0:T(8,128)(2,1)} %dynamic-slice_bitcast_fusion.7), channel_id=1, source_target_pairs={{0,8},{4,12},{8,0},{12,4},{16,24},{20,28},{24,16},{28,20},{1,9},{5... | collective-permute-start | bytes 1572872 | tf_op jit(solution)/shard_map/ppermute | solution.py:208
  553.7 94.3 %collective-permute-start.55 = (bf16[1024,256]{1,0:T(8,128)(2,1)}, bf16[1024,256]{1,0:T(8,128)(2,1)}, u32[]{:S(2)}, u32[]{:S(2)}) collective-permute-start(bf16[1024,256]{1,0:T(8,128)(2,1)} %dynamic-slice_bitcast_fusion.8), channel_id=1, source_target_pairs={{0,16},{4,20},{8,24},{12,28},{16,0},{20,4},{24,8},{28,12},{1,17},{... | collective-permute-start | bytes 1572872 | tf_op jit(solution)/shard_map/ppermute | solution.py:208
  573.8 29.0 %collective-permute-start.24 = (bf16[256,2048]{1,0:T(8,128)(2,1)S(1)}, bf16[256,2048]{1,0:T(8,128)(2,1)S(1)}, u32[]{:S(2)}, u32[]{:S(2)}) collective-permute-start(bf16[256,2048]{1,0:T(8,128)(2,1)S(1)} %get-tuple-element.89), channel_id=1, source_target_pairs={{0,1},{4,5},{8,9},{12,13},{16,17},{20,21},{24,25},{28,29}} | collective-permute-start | bytes 3145736 | tf_op jit(solution)/shard_map/ppermute | solution.py:181
  581.1 21.7 %collective-permute-start.27 = (bf16[256,2048]{1,0:T(8,128)(2,1)S(1)}, bf16[256,2048]{1,0:T(8,128)(2,1)S(1)}, u32[]{:S(2)}, u32[]{:S(2)}) collective-permute-start(bf16[256,2048]{1,0:T(8,128)(2,1)S(1)} %get-tuple-element.89), channel_id=1, source_target_pairs={{3,2},{7,6},{11,10},{15,14},{19,18},{23,22},{27,26},{31,30}} | collective-permute-start | bytes 3145736 | tf_op jit(solution)/shard_map/ppermute | solution.py:184
  606.0 27.2 %collective-permute-start.25 = (bf16[256,2048]{1,0:T(8,128)(2,1)}, bf16[256,2048]{1,0:T(8,128)(2,1)}, u32[]{:S(2)}, u32[]{:S(2)}) collective-permute-start(bf16[256,2048]{1,0:T(8,128)(2,1)} %get-tuple-element.63), channel_id=1, source_target_pairs={{0,1},{1,2},{4,5},{5,6},{8,9},{9,10},{12,13},{13,14},{16,17},{17,1... | collective-permute-start | bytes 3145736 | tf_op jit(solution)/shard_map/ppermute | solution.py:181
  611.4 21.9 %collective-permute-start.28 = (bf16[256,2048]{1,0:T(8,128)(2,1)}, bf16[256,2048]{1,0:T(8,128)(2,1)}, u32[]{:S(2)}, u32[]{:S(2)}) collective-permute-start(bf16[256,2048]{1,0:T(8,128)(2,1)} %get-tuple-element.64), channel_id=1, source_target_pairs={{2,1},{3,2},{6,5},{7,6},{10,9},{11,10},{14,13},{15,14},{18,17},{19... | collective-permute-start | bytes 3145736 | tf_op jit(solution)/shard_map/ppermute | solution.py:184
  628.5 50.7 %collective-permute-start.35 = (bf16[2,2,256,1536]{2,3,1,0:T(8,128)(2,1)}, bf16[2,2,256,1536]{2,3,1,0:T(8,128)(2,1)}, u32[]{:S(2)}, u32[]{:S(2)}) collective-permute-start(bf16[2,2,256,1536]{2,3,1,0:T(8,128)(2,1)} %bitcast.179), channel_id=1, source_target_pairs={{0,4},{4,0},{8,12},{12,8},{16,20},{20,16},{24,28},{28,24},{1,5},{5... | collective-permute-start | bytes 9437192 | tf_op jit(solution)/shard_map/ppermute | solution.py:208
  637.1 34.8 %collective-permute-start.29 = (bf16[256,2048]{1,0:T(8,128)(2,1)}, bf16[256,2048]{1,0:T(8,128)(2,1)}, u32[]{:S(2)}, u32[]{:S(2)}) collective-permute-start(bf16[256,2048]{1,0:T(8,128)(2,1)} %get-tuple-element.56), channel_id=1, source_target_pairs={{1,0},{2,1},{3,2},{5,4},{6,5},{7,6},{9,8},{10,9},{11,10},{13,12},{... | collective-permute-start | bytes 3145736 | tf_op jit(solution)/shard_map/ppermute | solution.py:184
  638.5 34.3 %collective-permute-start.26 = (bf16[256,2048]{1,0:T(8,128)(2,1)}, bf16[256,2048]{1,0:T(8,128)(2,1)}, u32[]{:S(2)}, u32[]{:S(2)}) collective-permute-start(bf16[256,2048]{1,0:T(8,128)(2,1)} %get-tuple-element.55), channel_id=1, source_target_pairs={{0,1},{1,2},{2,3},{4,5},{5,6},{6,7},{8,9},{9,10},{10,11},{12,13},{... | collective-permute-start | bytes 3145736 | tf_op jit(solution)/shard_map/ppermute | solution.py:181
  645.1 1.3 collective-permute-start.40
  646.4 3.8 collective-permute-start.41
  650.2 8.7 %collective-permute-start.42 = (f32[3072]{0:T(1024)S(1)}, f32[3072]{0:T(1024)S(1)}, u32[]{:S(2)}, u32[]{:S(2)}) collective-permute-start(f32[3072]{0:T(1024)S(1)} %add.659), channel_id=1, source_target_pairs={{0,16},{4,20},{8,24},{12,28},{16,0},{20,4},{24,8},{28,12},{1,17},{... | collective-permute-start | bytes 36872 | tf_op jit(solution)/shard_map/ppermute | solution.py:208
  679.1 4.4 collective-permute-start.30
  683.6 4.2 collective-permute-start.31
  687.8 4.5 collective-permute-start.32
  690.2 29.3 %collective-permute-start.38 = (bf16[2,128,1536]{1,2,0:T(8,128)(2,1)}, bf16[2,128,1536]{1,2,0:T(8,128)(2,1)}, u32[]{:S(2)}, u32[]{:S(2)}) collective-permute-start(bf16[2,128,1536]{1,2,0:T(8,128)(2,1)} %dynamic-slice_bitcast_fusion.5), channel_id=1, source_target_pairs={{0,16},{4,20},{8,24},{12,28},{16,0},{20,4},{24,8},{28,12},{1,17},{... | collective-permute-start | bytes 2359304 | tf_op jit(solution)/shard_map/ppermute | solution.py:208
  692.3 15.5 %collective-permute-start.33 = (f32[12288]{0:T(1024)S(1)}, f32[12288]{0:T(1024)S(1)}, u32[]{:S(2)}, u32[]{:S(2)}) collective-permute-start(f32[12288]{0:T(1024)S(1)} %add.641), channel_id=1, source_target_pairs={{0,1},{1,0},{2,3},{3,2},{4,5},{5,4},{6,7},{7,6},{8,9},{9,8},{10,11... | collective-permute-start | bytes 147464 | tf_op jit(solution)/shard_map/ppermute | solution.py:208
  702.9 20.7 %collective-permute-start.36 = (bf16[2,128,1536]{1,2,0:T(8,128)(2,1)}, bf16[2,128,1536]{1,2,0:T(8,128)(2,1)}, u32[]{:S(2)}, u32[]{:S(2)}) collective-permute-start(bf16[2,128,1536]{1,2,0:T(8,128)(2,1)} %dynamic-slice_bitcast_fusion.6), channel_id=1, source_target_pairs={{0,8},{4,12},{8,0},{12,4},{16,24},{20,28},{24,16},{28,20},{1,9},{5... | collective-permute-start | bytes 2359304 | tf_op jit(solution)/shard_map/ppermute | solution.py:208
  707.8 9.8 %collective-permute-start.34 = (f32[12288]{0:T(1024)S(1)}, f32[12288]{0:T(1024)S(1)}, u32[]{:S(2)}, u32[]{:S(2)}) collective-permute-start(f32[12288]{0:T(1024)S(1)} %add.642), channel_id=1, source_target_pairs={{0,2},{1,3},{2,0},{3,1},{4,6},{5,7},{6,4},{7,5},{8,10},{9,11},{10,... | collective-permute-start | bytes 147464 | tf_op jit(solution)/shard_map/ppermute | solution.py:208
  722.5 29.6 %collective-permute-start.39 = (bf16[128,1536]{0,1:T(8,128)(2,1)}, bf16[128,1536]{0,1:T(8,128)(2,1)S(1)}, u32[]{:S(2)}, u32[]{:S(2)}) collective-permute-start(bf16[128,1536]{0,1:T(8,128)(2,1)} %dynamic-slice_bitcast_fusion.11), channel_id=1, source_target_pairs={{0,8},{4,12},{8,0},{12,4},{16,24},{20,28},{24,16},{28,20},{1,9},{5... | collective-permute-start | bytes 1179656 | tf_op jit(solution)/shard_map/ppermute | solution.py:208
  750.4 11.8 %collective-permute-start.43 = (bf16[512,2,2,256]{3,0,2,1:T(8,128)(2,1)S(1)}, bf16[512,2,2,256]{3,0,2,1:T(8,128)(2,1)S(1)}, u32[]{:S(2)}, u32[]{:S(2)}) collective-permute-start(bf16[512,2,2,256]{3,0,2,1:T(8,128)(2,1)S(1)} %bitcast.180), channel_id=1, source_target_pairs={{0,4},{4,0},{8,12},{12,8},{16,20},{20,16},{24,28},{28,24},{1,5},{5... | collective-permute-start | bytes 3145736 | tf_op jit(solution)/shard_map/ppermute | solution.py:208
  750.5 11.5 %collective-permute-start.37 = (bf16[128,1536]{0,1:T(8,128)(2,1)S(1)}, bf16[128,1536]{0,1:T(8,128)(2,1)S(1)}, u32[]{:S(2)}, u32[]{:S(2)}) collective-permute-start(bf16[128,1536]{0,1:T(8,128)(2,1)S(1)} %dynamic-slice_bitcast_fusion.12), channel_id=1, source_target_pairs={{0,16},{4,20},{8,24},{12,28},{16,0},{20,4},{24,8},{28,12},{1,17},{... | collective-permute-start | bytes 1179656 | tf_op jit(solution)/shard_map/ppermute | solution.py:208
  762.8 8.0 %collective-permute-start.46 = (bf16[256,2,256]{2,0,1:T(8,128)(2,1)S(1)}, bf16[256,2,256]{2,0,1:T(8,128)(2,1)}, u32[]{:S(2)}, u32[]{:S(2)}) collective-permute-start(bf16[256,2,256]{2,0,1:T(8,128)(2,1)S(1)} %dynamic-slice_bitcast_fusion.13), channel_id=1, source_target_pairs={{0,16},{4,20},{8,24},{12,28},{16,0},{20,4},{24,8},{28,12},{1,17},{... | collective-permute-start | bytes 786440 | tf_op jit(solution)/shard_map/ppermute | solution.py:208
  768.8 9.0 %collective-permute-start.44 = (bf16[256,2,256]{2,0,1:T(8,128)(2,1)S(1)}, bf16[256,2,256]{2,0,1:T(8,128)(2,1)S(1)}, u32[]{:S(2)}, u32[]{:S(2)}) collective-permute-start(bf16[256,2,256]{2,0,1:T(8,128)(2,1)S(1)} %dynamic-slice_bitcast_fusion.14), channel_id=1, source_target_pairs={{0,8},{4,12},{8,0},{12,4},{16,24},{20,28},{24,16},{28,20},{1,9},{5... | collective-permute-start | bytes 786440 | tf_op jit(solution)/shard_map/ppermute | solution.py:208
  771.8 7.4 collective-permute-start.47
  777.9 5.0 collective-permute-start.45
  (79 other events, 889.7 us)
Sparse Core Ops, SparseCore 0:
  10.2 30.6 all-gather.10
  42.7 53.8 all-gather.12
  175.7 99.9 all-gather.6
  435.8 77.9 reduce-scatter.1
  654.1 81.7 all-gather.8

commit v2 on v1

v2 whole, which is shorter than its diff:
```python
import functools
import jax
import jax.numpy as jnp
from jax import lax
from jax.experimental import pallas as pl
from jax.experimental.pallas import tpu as pltpu
from jax.sharding import PartitionSpec as P

HEAD = 128
SEQ = 1024
BLOCK = 256
SCALE = HEAD ** (-0.5)
f32 = jnp.float32
bf16 = jnp.bfloat16
LIGHT = pl.CostEstimate(flops=1 << 20, bytes_accessed=1 << 16, transcendentals=0)


def dot(left, right, left_dim=1, right_dim=0):
    return lax.dot_general(
        left, right, (((left_dim,), (right_dim,)), ((), ())), preferred_element_type=f32
    )


def block_probs(q_block, k_ref, seg_col, seg_row, block, reach):
    start = block * BLOCK
    scores = dot(k_ref[:reach, :], q_block, 1, 1) * SCALE
    key_place = lax.broadcasted_iota(jnp.int32, (reach, BLOCK), 0)
    query_place = start + lax.broadcasted_iota(jnp.int32, (reach, BLOCK), 1)
    allowed = (seg_col[:reach, :] == seg_row[:, start : start + BLOCK]) & (
        key_place <= query_place
    )
    scores = jnp.where(allowed, scores, -1e30)
    expo = jnp.exp(scores - jnp.max(scores, axis=0, keepdims=True))
    return expo * (1.0 / jnp.sum(expo, axis=0, keepdims=True))


def attend_kernel(q_ref, k_ref, v_ref, seg_col, seg_row, out_ref):
    for block in range(SEQ // BLOCK):
        rows = slice(block * BLOCK, (block + 1) * BLOCK)
        reach = (block + 1) * BLOCK
        probs = block_probs(q_ref[rows, :], k_ref, seg_col, seg_row, block, reach)
        out_ref[rows, :] = dot(probs.astype(bf16), v_ref[:reach, :], 0, 0).astype(bf16)


def attend(projected, seg_col, seg_row, heads):
    tokens = projected.shape[0]
    column = lambda part: pl.BlockSpec((SEQ, HEAD), lambda r, h: (r, part * heads + h))
    return pl.pallas_call(
        attend_kernel,
        grid=(tokens // SEQ, heads),
        in_specs=[
            column(0),
            column(1),
            column(2),
            pl.BlockSpec((SEQ, 1), lambda r, h: (r, 0)),
            pl.BlockSpec((1, SEQ), lambda r, h: (0, r)),
        ],
        out_specs=pl.BlockSpec((SEQ, HEAD), lambda r, h: (r, h)),
        out_shape=jax.ShapeDtypeStruct((tokens, heads * HEAD), bf16),
        compiler_params=pltpu.CompilerParams(vmem_limit_bytes=40 * 2**20),
        cost_estimate=LIGHT,
        name="attend",
    )(projected, projected, projected, seg_col, seg_row)


def attend_back_kernel(
    heads, q_ref, k_ref, v_ref, grad_ref, seg_col, seg_row, out_ref, dk_ref, dv_ref
):
    head = pl.program_id(1)
    width = heads * HEAD
    column = lambda part: pl.ds(pl.multiple_of(part * width + head * HEAD, HEAD), HEAD)
    dk_ref[...] = jnp.zeros_like(dk_ref)
    dv_ref[...] = jnp.zeros_like(dv_ref)
    for block in range(SEQ // BLOCK):
        rows = slice(block * BLOCK, (block + 1) * BLOCK)
        reach = (block + 1) * BLOCK
        q_block = q_ref[rows, :]
        g_block = grad_ref[rows, :]
        probs = block_probs(q_block, k_ref, seg_col, seg_row, block, reach)
        d_probs = dot(v_ref[:reach, :], g_block, 1, 1)
        delta = jnp.sum(probs * d_probs, axis=0, keepdims=True)
        d_scores = (probs * (d_probs - delta)).astype(bf16)
        dv_ref[:reach, :] += dot(probs.astype(bf16), g_block)
        dk_ref[:reach, :] += dot(d_scores, q_block)
        out_ref[rows, column(0)] = (dot(d_scores, k_ref[:reach, :], 0, 0) * SCALE).astype(bf16)
    out_ref[:, column(1)] = (dk_ref[...] * SCALE).astype(bf16)
    out_ref[:, column(2)] = dv_ref[...].astype(bf16)


def attend_back(projected, grad_attn, seg_col, seg_row, heads):
    tokens = projected.shape[0]
    column = lambda part: pl.BlockSpec((SEQ, HEAD), lambda r, h: (r, part * heads + h))
    return pl.pallas_call(
        functools.partial(attend_back_kernel, heads),
        grid=(tokens // SEQ, heads),
        in_specs=[
            column(0),
            column(1),
            column(2),
            column(0),
            pl.BlockSpec((SEQ, 1), lambda r, h: (r, 0)),
            pl.BlockSpec((1, SEQ), lambda r, h: (0, r)),
        ],
        out_specs=pl.BlockSpec((SEQ, 3 * heads * HEAD), lambda r, h: (r, 0)),
        out_shape=jax.ShapeDtypeStruct((tokens, 3 * heads * HEAD), bf16),
        scratch_shapes=[pltpu.VMEM((SEQ, HEAD), f32), pltpu.VMEM((SEQ, HEAD), f32)],
        compiler_params=pltpu.CompilerParams(vmem_limit_bytes=40 * 2**20),
        cost_estimate=LIGHT,
        name="attend_back",
    )(projected, projected, projected, grad_attn, seg_col, seg_row)


def norm_parts(value):
    mean = jnp.mean(value, axis=-1, keepdims=True)
    centered = value - mean
    inverse = lax.rsqrt(jnp.mean(centered * centered, axis=-1, keepdims=True) + 1e-05)
    return centered * inverse, inverse


def norm_backward(grad, gain, scaled, inverse):
    inner = grad * gain
    return inverse * (
        inner
        - jnp.mean(inner, axis=-1, keepdims=True)
        - scaled * jnp.mean(inner * scaled, axis=-1, keepdims=True)
    )


def gelu_parts(value):
    c = 0.7978845608028654
    square = value * value
    tanh = jnp.tanh(c * value * (1.0 + 0.044715 * square))
    half = 0.5 * (1.0 + tanh)
    slope = half + 0.5 * value * (1.0 - tanh * tanh) * c * (1.0 + 3 * 0.044715 * square)
    return value * half, slope


def mix_kernel(token_ref, heads_ref, w_ref, bias_ref, gain_ref, shift_ref, middle_ref, normed_ref):
    middle = dot(heads_ref[...], w_ref[...]) + (token_ref[...].astype(f32) + bias_ref[...])
    middle_ref[...] = middle
    normed_ref[...] = (norm_parts(middle)[0] * gain_ref[...] + shift_ref[...]).astype(bf16)


def mix(tokens_all, attn_all, w_out_all, bias, gain, shift):
    tokens, width = tokens_all.shape
    cols = attn_all.shape[1]
    step = 256
    row = lambda size: pl.BlockSpec((step, size), lambda i: (i, 0))
    one = pl.BlockSpec((1, width), lambda i: (0, 0))
    return pl.pallas_call(
        mix_kernel,
        grid=(tokens // step,),
        in_specs=[row(width), row(cols), pl.BlockSpec((cols, width), lambda i: (0, 0)), one, one, one],
        out_specs=[row(width), row(width)],
        out_shape=[
            jax.ShapeDtypeStruct((tokens, width), f32),
            jax.ShapeDtypeStruct((tokens, width), bf16),
        ],
        compiler_params=pltpu.CompilerParams(vmem_limit_bytes=48 * 2**20),
        cost_estimate=LIGHT,
        name="mix",
    )(tokens_all, attn_all, w_out_all, bias[None], gain[None], shift[None])


def up_kernel(x_ref, w_ref, b_ref, hidden_ref, active_ref):
    hidden = dot(x_ref[...], w_ref[...]) + b_ref[...]
    hidden_ref[...] = hidden
    active_ref[...] = gelu_parts(hidden)[0].astype(bf16)


def feed_up(normed, w_up, b_up):
    tokens, width = normed.shape
    cols = w_up.shape[1]
    step = 256
    col = lambda rows: pl.BlockSpec((rows, step), lambda i: (0, i))
    return pl.pallas_call(
        up_kernel,
        grid=(cols // step,),
        in_specs=[pl.BlockSpec((tokens, width), lambda i: (0, 0)), col(width), col(1)],
        out_specs=[col(tokens), col(tokens)],
        out_shape=[
            jax.ShapeDtypeStruct((tokens, cols), f32),
            jax.ShapeDtypeStruct((tokens, cols), bf16),
        ],
        compiler_params=pltpu.CompilerParams(vmem_limit_bytes=48 * 2**20),
        cost_estimate=LIGHT,
        name="feed_up",
    )(normed, w_up, b_up[None])


def hidden_kernel(cot_ref, hidden_ref, w_ref, out_ref):
    slope = gelu_parts(hidden_ref[...])[1]
    out_ref[...] = (dot(cot_ref[...], w_ref[...], 1, 1) * slope).astype(bf16)


def hidden_back(cot_all, hidden, w_down):
    tokens, width = cot_all.shape
    cols, step = hidden.shape[1], 256
    return pl.pallas_call(
        hidden_kernel,
        grid=(cols // step,),
        in_specs=[
            pl.BlockSpec((tokens, width), lambda i: (0, 0)),
            pl.BlockSpec((tokens, step), lambda i: (0, i)),
            pl.BlockSpec((step, width), lambda i: (i, 0)),
        ],
        out_specs=pl.BlockSpec((tokens, step), lambda i: (0, i)),
        out_shape=jax.ShapeDtypeStruct((tokens, cols), bf16),
        compiler_params=pltpu.CompilerParams(vmem_limit_bytes=48 * 2**20),
        cost_estimate=LIGHT,
        name="hidden_back",
    )(cot_all, hidden, w_down)


def grads_kernel(bounds, factor_ref, *refs):
    count = len(bounds) - 1
    left_refs, right_refs = refs[:count], refs[count : 2 * count]
    out_ref, turned_ref = refs[2 * count :]
    i = pl.program_id(0)
    for j in range(count):

        @pl.when(i == bounds[j])
        def _():
            turned_ref[...] = left_refs[j][...].T

        @pl.when((i >= bounds[j]) & (i < bounds[j + 1]))
        def _():
            out_ref[...] = (factor_ref[0] * dot(turned_ref[...], right_refs[j][...])).astype(bf16)


def weight_grads(factor, pairs):
    tokens, width = pairs[0][0].shape
    step = 256
    bounds = [0]
    for _, right in pairs:
        bounds.append(bounds[-1] + right.shape[1] // step)

    def part(j):
        low, high = bounds[j], bounds[j + 1]
        return pl.BlockSpec((tokens, step), lambda i: (0, jnp.clip(i - low, 0, high - low - 1)))

    whole = pl.BlockSpec((tokens, width), lambda i: (0, 0))
    return pl.pallas_call(
        functools.partial(grads_kernel, tuple(bounds)),
        grid=(bounds[-1],),
        in_specs=[
            pl.BlockSpec(memory_space=pltpu.SMEM),
            *[whole] * len(pairs),
            *[part(j) for j in range(len(pairs))],
        ],
        out_specs=pl.BlockSpec((width, step), lambda i: (0, i)),
        out_shape=jax.ShapeDtypeStruct((width, step * bounds[-1]), bf16),
        scratch_shapes=[pltpu.VMEM((width, tokens), bf16)],
        compiler_params=pltpu.CompilerParams(vmem_limit_bytes=48 * 2**20),
        cost_estimate=LIGHT,
        name="weight_grads",
    )(factor[None], *[left for left, _ in pairs], *[right for _, right in pairs])


def half_kernel(index_ref, x_ref, w_ref, *refs):
    refs[-1][...] = dot(x_ref[...], w_ref[...], 1, 1).astype(bf16)


def half_product(x, weight, half, earlier=None):
    tokens, depth = x.shape
    rows = tokens // 2
    cols, step = weight.shape[0], 512
    given = [] if earlier is None else [earlier]
    return pl.pallas_call(
        half_kernel,
        grid_spec=pltpu.PrefetchScalarGridSpec(
            num_scalar_prefetch=1,
            grid=(cols // step,),
            in_specs=[
                pl.BlockSpec((rows, depth), lambda i, at: (at[0], 0)),
                pl.BlockSpec((step, depth), lambda i, at: (i, 0)),
                *[pl.BlockSpec(memory_space=pl.ANY) for _ in given],
            ],
            out_specs=pl.BlockSpec((rows, step), lambda i, at: (at[0], i)),
        ),
        out_shape=jax.ShapeDtypeStruct((tokens, cols), bf16),
        input_output_aliases={3: 0} if given else {},
        compiler_params=pltpu.CompilerParams(vmem_limit_bytes=40 * 2**20),
        cost_estimate=LIGHT,
        name="half_product",
    )(half[None], x, weight, *given)


def relay_kernel(index_ref, right_ref, left_ref, *refs):
    to_right, to_left = refs[-2:]
    if len(refs) == 2:
        to_right[...], to_left[...] = right_ref[...], left_ref[...]
    else:
        to_right[...] = (right_ref[...].astype(f32) + refs[0][...].astype(f32)).astype(bf16)
        to_left[...] = (left_ref[...].astype(f32) + refs[1][...].astype(f32)).astype(bf16)


def relay(terms, rows, index, came):
    width = terms.shape[1]
    step = min(rows, 128)
    steps = rows // step
    block = pl.BlockSpec((step, width), lambda i, at: (i, 0))
    return pl.pallas_call(
        relay_kernel,
        grid_spec=pltpu.PrefetchScalarGridSpec(
            num_scalar_prefetch=1,
            grid=(steps,),
            in_specs=[
                pl.BlockSpec((step, width), lambda i, at: (at[0] * steps + i, 0)),
                pl.BlockSpec((step, width), lambda i, at: (at[1] * steps + i, 0)),
                *[block] * len(came),
            ],
            out_specs=[block, block],
        ),
        out_shape=[jax.ShapeDtypeStruct((rows, width), bf16)] * 2,
        compiler_params=pltpu.CompilerParams(vmem_limit_bytes=40 * 2**20),
        cost_estimate=LIGHT,
        name="relay",
    )(index, terms, terms, *came)


def summed_back(term_ref, left_ref, right_ref, value_ref, gain_ref):
    grad = term_ref[...].astype(f32) + left_ref[...].astype(f32) + right_ref[...].astype(f32)
    scaled, inverse = norm_parts(value_ref[...].astype(f32))
    return grad, scaled, norm_backward(grad, gain_ref[...], scaled, inverse)


def middle_back_kernel(
    index_ref, term_ref, left_ref, right_ref, value_ref, gain_ref, cot_ref, middle_ref, branch_ref, sums_ref
):
    @pl.when(pl.program_id(0) == 0)
    def _():
        sums_ref[...] = jnp.zeros_like(sums_ref)

    grad, scaled, back = summed_back(term_ref, left_ref, right_ref, value_ref, gain_ref)
    cot = cot_ref[...].astype(f32)
    middle = cot + back
    branch = middle.astype(bf16)
    middle_ref[...], branch_ref[...] = middle, branch
    for row, value in enumerate((grad * scaled, grad, branch.astype(f32), cot)):
        sums_ref[row : row + 1, :] += jnp.sum(value, axis=0, keepdims=True)


def input_back_kernel(
    index_ref, factor_ref, term_ref, left_ref, right_ref, value_ref, gain_ref, middle_ref, out_ref
):
    back = summed_back(term_ref, left_ref, right_ref, value_ref, gain_ref)[2]
    out_ref[...] = factor_ref[0] * (middle_ref[...] + back)


def back_specs(rows, width):
    step = min(rows, 128)
    steps = rows // step
    here = pl.BlockSpec((step, width), lambda i, at: (i, 0))
    own = pl.BlockSpec((step, width), lambda i, at: (at[0] * steps + i, 0))
    return steps, here, own, pl.BlockSpec((1, width), lambda i, at: (0, 0))


def middle_back(index, terms, came, middle_all, gain, cot):
    rows, width = cot.shape
    steps, here, own, one = back_specs(rows, width)
    return pl.pallas_call(
        middle_back_kernel,
        grid_spec=pltpu.PrefetchScalarGridSpec(
            num_scalar_prefetch=1,
            grid=(steps,),
            in_specs=[own, here, here, own, one, here],
            out_specs=[here, here, pl.BlockSpec((4, width), lambda i, at: (0, 0))],
        ),
        out_shape=[
            jax.ShapeDtypeStruct((rows, width), f32),
            jax.ShapeDtypeStruct((rows, width), bf16),
            jax.ShapeDtypeStruct((4, width), f32),
        ],
        compiler_params=pltpu.CompilerParams(vmem_limit_bytes=40 * 2**20),
        cost_estimate=LIGHT,
        name="middle_back",
    )(index, terms, *came, middle_all, gain[None], cot)


def input_back(index, factor, terms, came, tokens, gain, d_middle):
    rows, width = tokens.shape
    steps, here, own, one = back_specs(rows, width)
    return pl.pallas_call(
        input_back_kernel,
        grid_spec=pltpu.PrefetchScalarGridSpec(
            num_scalar_prefetch=1,
            grid=(steps,),
            in_specs=[pl.BlockSpec(memory_space=pltpu.SMEM), own, here, here, here, one, here],
            out_specs=here,
        ),
        out_shape=jax.ShapeDtypeStruct((rows, width), f32),
        compiler_params=pltpu.CompilerParams(vmem_limit_bytes=40 * 2**20),
        cost_estimate=LIGHT,
        name="input_back",
    )(index, factor[None], terms, *came, tokens, gain[None], d_middle)


def blank_kernel(out_ref):
    pass


def blank(shape):
    return pl.pallas_call(
        blank_kernel,
        out_specs=pl.BlockSpec(memory_space=pl.ANY),
        out_shape=jax.ShapeDtypeStruct(shape, bf16),
        name="blank",
    )()


def sums_kernel(term_ref, token_ref, out_ref):
    @pl.when(pl.program_id(0) == 0)
    def _():
        out_ref[...] = jnp.zeros_like(out_ref)

    term = term_ref[...].astype(f32)
    scaled = norm_parts(token_ref[...].astype(f32))[0]
    out_ref[0:1, :] += jnp.sum(term * scaled, axis=0, keepdims=True)
    out_ref[1:2, :] += jnp.sum(term, axis=0, keepdims=True)


def gain_sums(terms, tokens_all):
    rows, width = terms.shape
    block = pl.BlockSpec((128, width), lambda i: (i, 0))
    return pl.pallas_call(
        sums_kernel,
        grid=(rows // 128,),
        in_specs=[block, block],
        out_specs=pl.BlockSpec((2, width), lambda i: (0, 0)),
        out_shape=jax.ShapeDtypeStruct((2, width), f32),
        compiler_params=pltpu.CompilerParams(vmem_limit_bytes=40 * 2**20),
        cost_estimate=LIGHT,
        name="gain_sums",
    )(terms, tokens_all)


class Phases:
    def __init__(self):
        self.marks, self.kept, self.sends = (), [], []

    def __call__(self, *values):
        gate = (*self.marks, *self.sends)
        if gate:
            values = lax.optimization_barrier((*values, *gate))[: len(values)]
        return values if len(values) > 1 else values[0]

    def early(self, *values):
        if self.marks:
            values = lax.optimization_barrier((*values, *self.marks))[: len(values)]
        return values if len(values) > 1 else values[0]

    def send(self, *values):
        self.sends += values

    def keep(self, *values):
        self.kept += values
        return values if len(values) > 1 else values[0]

    def turn(self):
        self.marks, self.kept, self.sends = tuple(self.kept), [], []


class Line:
    def __init__(self, name, size):
        self.name, self.n = name, size
        self.me = lax.axis_index(name)
        self.low = self.me < size // 2

    def slot(self, k):
        n = self.n
        return jnp.where(self.low, (self.me + k) % n, (self.me + n - k) % n)

    def shuffle(self, phase, array):
        n = self.n
        cols = array.shape[1] // n
        out = []
        for shift in range(n):
            target = (self.me + shift) % n
            block = lax.dynamic_slice_in_dim(phase.early(array), target * cols, cols, axis=1)
            if shift:
                phase.send(block)
                block = lax.ppermute(block, self.name, [(j, (j + shift) % n) for j in range(n)])
            out.append(phase.keep(block))
        return out

    def shuffle_rows(self, phase, array, rows):
        n = self.n
        out = []
        for shift in range(1, n):
            target = (self.me + shift) % n
            block = lax.dynamic_slice_in_dim(phase.early(array), target * rows, rows, axis=0)
            out.append(lax.ppermute(block, self.name, [(j, (j + shift) % n) for j in range(n)]))
        return out

    def stack(self, blocks):
        n = self.n
        rows, cols = blocks[0].shape
        out = blank((n * rows, cols))
        for shift, block in enumerate(blocks):
            source = (self.me + n - shift) % n
            out = lax.dynamic_update_slice_in_dim(out, block, source * rows, axis=0)
        return out


class Gather:
    def __init__(self, line, block):
        self.line, self.left, self.right = line, [block], [block]

    def step(self, phase):
        line, n, k = self.line, self.line.n, len(self.left)
        left, right = phase.early(self.left[-1], self.right[-1])
        phase.send(left, right)
        self.left.append(lax.ppermute(left, line.name, [(j, j + 1) for j in range(k - 1, n - 1)]))
        self.right.append(lax.ppermute(right, line.name, [(j, j - 1) for j in range(1, n - k + 1)]))
        phase.keep(self.left[k], self.right[k])
        low_side, high_side = self.right[k], self.left[k]
        if 2 * k >= n:
            low_side = jnp.where(line.me + k < n, self.right[k], self.left[n - k])
            high_side = jnp.where(line.me >= k, self.left[k], self.right[n - k])
        return jnp.where(line.low, low_side, high_side)


class Reduce:
    def __init__(self, line, rows):
        self.line, self.rows, self.k, self.came, self.terms = line, rows, 1, (), None

    def step(self, phase):
        line, n, k = self.line, self.line.n, self.k
        blocks = [jnp.clip(line.me + n - k, 0, n - 1), jnp.clip(line.me - n + k, 0, n - 1)]
        self.terms = phase.early(self.terms)
        sent = relay(self.terms, self.rows, jnp.stack(blocks).astype(jnp.int32), self.came)
        phase.send(*sent)
        self.came = (
            lax.ppermute(sent[0], line.name, [(j, j + 1) for j in range(k)]),
            lax.ppermute(sent[1], line.name, [(j, j - 1) for j in range(n - k, n)]),
        )
        phase.keep(*self.came)
        self.k += 1


def flip(value, name, size, bit):
    return lax.ppermute(value, name, [(j, j ^ bit) for j in range(size)])


def sum_over(value, name, size):
    bit = 1
    while bit < size:
        value = value + flip(value, name, size, bit)
        bit *= 2
    return value


class Spread:
    def __init__(self, name, size, moved, still, moved_left, factor):
        self.name, self.size, self.factor, self.moved_left = name, size, factor, moved_left
        self.moved, self.still = moved, still
        self.bits = [1 << b for b in range(1, size.bit_length() - 1)]
        self.orders = [self.bits, self.bits[::-1]]
        self.block_cols = moved.shape[1] // size

    def blocks(self, moved, wanted):
        cols, index = self.block_cols, lax.axis_index(self.name)
        return jnp.concatenate(
            [lax.dynamic_slice_in_dim(moved, (index ^ r) * cols, cols, axis=1) for r in wanted], axis=1
        )

    def product(self, moved, still):
        left, right = (moved, still) if self.moved_left else (still, moved)
        return self.factor * dot(left, right, 0, 0)

    def listed(self, order, fixed):
        out = [sum(bit for bit, on in fixed.items() if on)]
        for bit in order[::-1]:
            if bit not in fixed:
                out = [*out, *[r + bit for r in out]]
        return out

    def cut(self, array, low, high):
        return array[low:high] if self.moved_left else array[:, low:high]

    def start(self, phase):
        moved = phase(self.moved)
        self.sent = self.product(self.blocks(moved, self.listed(self.bits, {1: True})), self.still).astype(bf16)
        return self.sent

    def cross(self, phase):
        sent = phase.early(self.sent)
        phase.send(sent)
        self.brought = flip(sent, self.name, self.size, 1)
        return self.brought

    def second(self, phase):
        moved, brought = phase(self.moved, self.brought)
        cols, along = self.block_cols, 0 if self.moved_left else 1
        half = self.still.shape[1] // 2
        first_list = self.listed(self.bits, {1: True})
        self.sent, self.kept = [], []
        for which, order in enumerate(self.orders):
            still = self.still[:, which * half : (which + 1) * half]
            part = lax.slice_in_dim(brought, which * half, (which + 1) * half, axis=1 - along)
            for on in (True, False):
                wanted = self.listed(order, {1: False, order[0]: on})
                places = [first_list.index(r + 1) for r in wanted]
                added = jnp.concatenate(
                    [self.cut(part, p * cols, (p + 1) * cols) for p in places], axis=along
                )
                value = (self.product(self.blocks(moved, wanted), still) + added.astype(f32)).astype(bf16)
                (self.sent if on else self.kept).append(value)
        self.done, self.air, self.result = 0, False, None
        return (*self.sent, *self.kept)

    def fly(self, phase):
        sent = phase.early(*self.sent)
        phase.send(*sent)
        self.flying = tuple(
            flip(value, self.name, self.size, order[self.done]) for value, order in zip(sent, self.orders)
        )
        self.done, self.air = self.done + 1, True
        return self.flying

    def land(self, phase):
        along, self.air = 0 if self.moved_left else 1, False
        flying = phase.early(*self.flying)
        totals = [k.astype(f32) + f.astype(f32) for k, f in zip(self.kept, flying)]
        if self.done == len(self.bits):
            self.result = jnp.concatenate(totals, axis=1 - along)
            return (self.result,)
        size = totals[0].shape[along]
        self.sent = [self.cut(t, size // 2, size).astype(bf16) for t in totals]
        self.kept = [self.cut(t, 0, size // 2).astype(bf16) for t in totals]
        return (*self.sent, *self.kept)

    def finish(self, phase):
        while self.result is None:
            (self.land if self.air else self.fly)(phase)
        return self.result


def after(value, *earlier):
    return lax.optimization_barrier((value, *earlier))[0]


def make_body(n_dp, n_mp):
    def body(
        tokens, cotangent, segment, counts, ln_gain, ln_bias, w_qkv, b_qv, w_out, out_bias, w_up, b_up, w_down
    ):
        line, phase = Line("mp", n_mp), Phases()
        keep, turn = phase.keep, phase.turn
        gains, shifts, bias_pair = ln_gain.astype(f32), ln_bias.astype(f32), out_bias.astype(f32)
        share, width = tokens.shape
        head_cols = w_qkv.shape[2]
        heads = head_cols // HEAD
        group = segment.shape[0]
        seg_col, seg_row = segment[:, None], segment[None, :]
        me = line.me
        place = lambda whole, block, index: lax.dynamic_update_slice_in_dim(
            whole, block, index * share, axis=0
        )
        rows_of = lambda whole, index: lax.dynamic_slice_in_dim(whole, index * share, share, axis=0)
        total = lambda value: jnp.sum(value.astype(f32), axis=0)
        slots, last = range(1, n_mp), n_mp - 1

        flat_qkv = jnp.concatenate([w_qkv[:, j] for j in range(3)], axis=1)
        bias_rows = (
            jnp.stack([b_qv[0], jnp.zeros_like(b_qv[0]), b_qv[1]]).astype(f32).reshape(3 * head_cols)
        )
        state = [blank((group, width)), blank((group, width)), blank((group, 3 * head_cols))]

        def project(k, block):
            block = phase(block)
            normed = (norm_parts(block.astype(f32))[0] * gains[0] + shifts[0]).astype(bf16)
            proj = (dot(normed, flat_qkv) + bias_rows).astype(bf16)
            for j, value in enumerate((block, normed, proj)):
                state[j] = keep(place(state[j], value, line.slot(k)))

        slice_rows = w_out.shape[0] // n_dp
        w_slice = lax.dynamic_slice_in_dim(
            w_out, lax.axis_index("dp") * slice_rows, slice_rows, axis=0
        )

        gather = Gather(line, tokens)
        token_slots = [tokens]
        for k in slots:
            token_slots.append(gather.step(phase))
            if k == 2:
                w_slices = lax.all_gather(phase(w_slice), "mp", axis=0)
            project(k - 1, token_slots[k - 1])
            turn()
        cot_gather = Gather(line, cotangent)
        cot_slots = [cotangent, cot_gather.step(phase)]
        w_out_all = lax.all_gather(phase(w_slices), "dp", axis=1).reshape(n_mp * w_out.shape[0], width)
        project(last, token_slots[last])
        tokens_all, normed1_all, projected = state
        attn = keep(attend(projected, seg_col, seg_row, heads))
        turn()

        set_heads = lambda whole, block, index: lax.dynamic_update_slice_in_dim(
            whole, block, index * head_cols, axis=1
        )
        attn_all = blank((group, n_mp * head_cols))
        attn_gather, attn_slots = Gather(line, attn), [attn]
        for k in slots:
            attn_slots.append(attn_gather.step(phase))
            attn_all = keep(set_heads(attn_all, phase(attn_slots[k - 1]), line.slot(k - 1)))
            if k == 2:
                cot_all = blank((group, width))
                for j in range(2):
                    cot_all = place(cot_all, phase(cot_slots[j]), line.slot(j))
                keep(cot_all)
            if k == 1:
                count_here = phase(counts.astype(f32))
                factor = keep((count_here / sum_over(count_here, "dp", n_dp))[0])
            turn()
        reduce_down, reduce2, reduce1 = (Reduce(line, share) for _ in range(3))
        for k in slots[1:]:
            cot_slots.append(cot_gather.step(phase))
            if k == 2:
                attn_all = set_heads(attn_all, phase(attn_slots[last]), line.slot(last))
                middle_all, normed2_all = mix(
                    tokens_all, attn_all, w_out_all, bias_pair[0], gains[1], shifts[1]
                )
                hidden, active = keep(*feed_up(normed2_all, w_up, b_up.astype(f32)))
                keep(middle_all, normed2_all)
            if k == 3:
                reduce_down.terms = keep(dot(phase(active), w_down).astype(bf16))
            if k > 2:
                cot_all = keep(place(cot_all, phase(cot_slots[k - 1]), line.slot(k - 1)))
            turn()

        reduce_down.step(phase)
        cot_all = place(cot_all, phase(cot_slots[last]), line.slot(last))
        d_hidden_all = keep(hidden_back(cot_all, hidden, w_down))
        reduce2.terms = keep(dot(d_hidden_all, w_up, 1, 1).astype(bf16))
        turn()
        for k in slots:
            reduce2.step(phase)
            if k == 1:
                feed_full = keep(
                    weight_grads(factor, [(phase(normed2_all), d_hidden_all), (cot_all, active)])
                )
            if k == 2:
                grad_feed = lax.psum_scatter(phase(feed_full), "dp", scatter_dimension=0, tiled=True)
                split_sums = keep(factor * total(phase(d_hidden_all)))
            turn()
        own = me[None].astype(jnp.int32)
        reduce_down.step(phase)
        d_middle, d_branch, own_sums = keep(
            *middle_back(own, phase(reduce2.terms), reduce2.came, middle_all, gains[1], cotangent)
        )
        d_attn_own = keep(dot(d_branch, w_out_all, 1, 1).astype(bf16))
        spread_out = Spread("dp", n_dp, after(d_branch, d_attn_own), rows_of(attn_all, me), False, factor)
        keep(spread_out.start(phase))
        turn()
        d_attn_blocks = line.shuffle(phase, d_attn_own)
        spread_out.cross(phase)
        keep(*spread_out.second(phase))
        turn()
        reduce_down.step(phase)
        keep(*spread_out.fly(phase))
        d_attn = line.stack(phase(*d_attn_blocks))
        grad_proj = keep(attend_back(projected, d_attn, seg_col, seg_row, heads))
        half = line.low.astype(jnp.int32)
        reduce1.terms = keep(half_product(grad_proj, flat_qkv, half))
        turn()
        for k in slots:
            reduce1.step(phase)
            if k == 1:
                keep(*spread_out.land(phase))
                keep(*spread_out.fly(phase))
                reduce1.terms = keep(half_product(phase(grad_proj), flat_qkv, 1 - half, reduce1.terms))
                qkv_full = weight_grads(factor, [(after(normed1_all, reduce1.terms), grad_proj)])
                grad_qkv = lax.psum_scatter(qkv_full, "dp", scatter_dimension=0, tiled=True)
                keep(qkv_full, grad_feed)
            if k == 2:
                out_rows = keep(spread_out.finish(phase))
                heads_sum = [total(phase(grad_proj)[:, :head_cols]), total(grad_proj[:, 2 * head_cols :])]
                gain1 = gain_sums(phase(reduce1.terms), tokens_all)
                full_sums = jnp.concatenate([gain1, own_sums], axis=0).reshape(-1)
                sums = keep(
                    jnp.concatenate(
                        [
                            sum_over(factor * full_sums, "mp", n_mp),
                            *[factor * s for s in heads_sum],
                            split_sums,
                        ]
                    )
                )
            if k == 3:
                sums = jnp.sum(lax.all_gather(phase(sums).reshape(1, 8, -1), "dp", axis=0, tiled=True), axis=0).reshape(-1)
                grad_feed = phase(grad_feed).astype(f32)
                feed_cols = grad_feed.shape[1] // 2
                grad_up, grad_down = keep(grad_feed[:, :feed_cols], grad_feed[:, feed_cols:].T)
                keep(grad_qkv)
                for _ in slots[3:]:
                    reduce_down.step(phase)
                down_sum = sum(
                    value.astype(f32)
                    for value in (rows_of(phase(reduce_down.terms), me), *reduce_down.came)
                )
                layer_out = keep((rows_of(middle_all, me) + down_sum + bias_pair[1]).astype(bf16))
            turn()
        out_blocks = line.shuffle_rows(phase, out_rows.astype(bf16), head_cols)
        grad_input = input_back(
            own, factor, phase(reduce1.terms), reduce1.came, tokens, gains[0], d_middle
        )
        full_sums = sums[: 6 * width].reshape(6, width)
        split_sums = sums[6 * width :]
        own_block = lax.dynamic_slice_in_dim(out_rows, me * head_cols, head_cols, axis=0)
        for block in out_blocks:
            own_block = own_block + block.astype(f32)
        grad_out = own_block
        grad_qkv = phase(grad_qkv).astype(f32)
        return (
            layer_out,
            grad_input,
            jnp.stack([full_sums[0], full_sums[2]]),
            jnp.stack([full_sums[1], full_sums[3]]),
            jnp.stack([grad_qkv[:, j * head_cols : (j + 1) * head_cols] for j in range(3)], axis=1),
            split_sums[: 2 * head_cols].reshape(2, head_cols),
            grad_out,
            full_sums[4:],
            grad_up,
            split_sums[2 * head_cols :],
            grad_down,
        )

    return body


def solution(mesh):
    split = P(("dp", "mp"), None)
    return jax.shard_map(
        make_body(mesh.shape["dp"], mesh.shape["mp"]),
        mesh=mesh,
        in_specs=(
            split, split, P("dp"), P("dp"), P(), P(), P(None, None, "mp"), P(None, "mp"), P("mp", None), P(),
            P(None, "mp"), P("mp"), P("mp", None),
        ),
        out_specs=(
            split, split, P(), P(), P("dp", None, "mp"), P(None, "mp"), P("mp", "dp"), P(), P("dp", "mp"), P("mp"),
            P("mp", "dp"),
        ),
        check_vma=False,
    )
```

time: 798 us -> 662 us (0.83)
  Pallas kernels: 24.1 us -> 154 us
  matrix products: 185 us -> 63.3 us
  waiting for transfers between devices: 282 us -> 175 us
  local copies, waits for them, and re-layouts: 102 us -> 69.8 us
  other arithmetic: 66.6 us -> 49.3 us
  blocking collectives: 0 us -> 10.2 us
    pallas_call x0 -> x25, Pallas kernels: none -> 129 us  [the longest x2 39.8 us: weight_grads(): pl.pallas_call(functools.partial(grads_kernel, tuple(bounds)), grid=(boun...]
    dot_general x24 -> x12, matrix products: 185 us -> 63.3 us  [dot(): lax.dot_general(left, right, (((left_dim,), (right_dim,)), ((), ())), pre...]
    all_gather x4 -> x2, waiting for transfers between devices: 42.2 us -> 0.01 us  [the longest x1 0.01 us: body(): w_slices = lax.all_gather(phase(w_slice), 'mp', axis=0)]
    ppermute x31 -> x10, waiting for transfers between devices: 64.8 us -> 29.4 us  [flip(): return lax.ppermute(value, name, [(j, j ^ bit) for j in range(size)])]
    dynamic_slice x7 -> x4, local copies, waits for them, and re-layouts: 36.1 us -> 1.48 us  [the longest x1 1.24 us: shuffle_rows(): lax.dynamic_slice_in_dim(phase.early(array), target * rows, rows, axis=0)]
    ppermute x31 -> x10, starting transfers between devices: 46.7 us -> 15.2 us  [flip(): return lax.ppermute(value, name, [(j, j ^ bit) for j in range(size)])]
    ppermute x24 -> x39, starting transfers between devices: 58.4 us -> 88.5 us  [the longest x9 35.4 us: step(): lax.ppermute(sent[0], line.name, [(j, j + 1) for j in range(k)])]
    ppermute x24 -> x39, waiting for transfers between devices: 167 us -> 144 us  [the longest x9 100 us: step(): lax.ppermute(right, line.name, [(j, j - 1) for j in range(1, n - k + 1)])]
  transfers between devices with their start and end apart: 63 -> 56, of which waited for: 30 -> 25; matrix products, arithmetic and copies ran while one was open for 40% -> 21% of each run, Pallas kernels for 3% -> 23%
where the time goes in v2:
time: 662 us; the launch traced here: 650 us
  waiting for transfers between devices  175 us (26%)
  Pallas kernels  154 us (23%)
  starting transfers between devices  109 us (16%)
  local copies, waits for them, and re-layouts  69.8 us (11%)
  matrix products  63.3 us (10%)
  other arithmetic  49.3 us (7%)
  between operations  18.2 us (3%)
  blocking collectives  10.2 us (2%)
    ppermute x9, waiting for transfers between devices, step(): lax.ppermute(right, line.name, [(j, j - 1) for j in range(1, n - k + 1)])  100 us
    dot_general x12, matrix products, dot(): lax.dot_general(left, right, (((left_dim,), (right_dim,)), ((), ())), pre...  63.3 us
    unnamed x175, local copies, waits for them, and re-layouts  40.4 us
    pallas_call x2, Pallas kernels, weight_grads(): pl.pallas_call(functools.partial(grads_kernel, tuple(bounds)), grid=(boun...  39.8 us
    ppermute x9, starting transfers between devices, step(): lax.ppermute(sent[0], line.name, [(j, j + 1) for j in range(k)])  35.4 us
    ppermute x10, waiting for transfers between devices, flip(): return lax.ppermute(value, name, [(j, j ^ bit) for j in range(size)])  29.4 us
    ppermute x9, waiting for transfers between devices, step(): lax.ppermute(sent[0], line.name, [(j, j + 1) for j in range(k)])  28.3 us
    ppermute x9, starting transfers between devices, step(): lax.ppermute(left, line.name, [(j, j + 1) for j in range(k - 1, n - 1)])  21.9 us
  transfers between devices with their start and end apart: 56, of which 25 were waited for; matrix products, arithmetic and copies ran while one was open for 21% of the time, Pallas kernels for 23%

profile of v2, /device:TPU:0, one launch (start us, length us, event | category | flops | bytes accessed | tf_op | source)
XLA Modules:
  0.0 649.5 jit_solution(3437698042489437718)
XLA Ops:
  8.7 6.5 %collective-permute-start.1 = (bf16[256,2048]{1,0:T(8,128)(2,1)}, bf16[256,2048]{1,0:T(8,128)(2,1)}, u32[]{:S(2)}, u32[]{:S(2)}) collective-permute-start(bf16[256,2048]{1,0:T(8,128)(2,1)} %value_ref.1), channel_id=1, source_target_pairs={{0,1},{1,2},{2,3},{4,5},{5,6},{6,7},{8,9},{9,10},{10,11},{12,13},{... | collective-permute-start | bytes 3145736 | tf_op jit(solution)/shard_map/ppermute | solution.py:514
  17.2 5.7 slice_bitcast_fusion.3
  25.7 5.0 fusion.1
  30.7 5.1 collective-permute-done
  43.9 5.0 fusion.3
  48.9 30.4 %collective-permute-done.2 = bf16[256,2048]{1,0:T(8,128)(2,1)S(1)} collective-permute-done((bf16[256,2048]{1,0:T(8,128)(2,1)}, bf16[256,2048]{1,0:T(8,128)(2,1)S(1)}, u32[]{:S(2)}, u32[]{:S(2)}) %collective-permute-start.2) | collective-permute-done | bytes 1048608 | tf_op jit(solution)/shard_map/ppermute | solution.py:515
  85.6 2.8 fusion.5
  88.4 17.7 %collective-permute-done.4 = bf16[256,2048]{1,0:T(8,128)(2,1)S(1)} collective-permute-done((bf16[256,2048]{1,0:T(8,128)(2,1)S(1)}, bf16[256,2048]{1,0:T(8,128)(2,1)S(1)}, u32[]{:S(2)}, u32[]{:S(2)}) %collective-permute-start.4) | collective-permute-done | bytes 1048608 | tf_op jit(solution)/shard_map/ppermute | solution.py:515
  114.9 2.8 fusion.7.q_ref.k_ref.v_ref
  117.6 9.0 %attend.1 = bf16[1024,512]{1,0:T(8,128)(2,1)S(1)} custom-call(bf16[1024,1536]{1,0:T(8,128)(2,1)} %fusion.7.q_ref.k_ref.v_ref, bf16[1024,1536]{1,0:T(8,128)(2,1)} %fusion.7.q_ref.k_ref.v_ref, bf16[1024,1536]{1,0:T(8,128)(2,1)} %fusion.7.q_ref.k_ref.v_ref, s32[1024,1]{1,0:T(8,128)S(1)} %copy.29.seg_col, s32[1,1024]{1,0:T(1,128)S(1)} %bitcast.54), custom_call_target="tpu_custom_call" | custom-call | flops 1048576 | bytes 65536 | tf_op jit(solution)/shard_map/attend/pallas_call | solution.py:48
  130.0 4.2 collective-permute-done.7
  135.5 5.7 collective-permute-start.9
  152.9 3.8 collective-permute-done.8
  164.7 2.3 constant_dynamic-update-slice_fusion.9
  168.1 12.7 %collective-permute-done.13 = bf16[1024,512]{1,0:T(8,128)(2,1)} collective-permute-done((bf16[1024,512]{1,0:T(8,128)(2,1)}, bf16[1024,512]{1,0:T(8,128)(2,1)}, u32[]{:S(2)}, u32[]{:S(2)}) %collective-permute-start.13) | collective-permute-done | bytes 1048608 | tf_op jit(solution)/shard_map/ppermute | solution.py:515
  186.6 16.0 %collective-permute-done.15 = bf16[1024,512]{1,0:T(8,128)(2,1)} collective-permute-done((bf16[1024,512]{1,0:T(8,128)(2,1)}, bf16[1024,512]{1,0:T(8,128)(2,1)}, u32[]{:S(2)}, u32[]{:S(2)}) %collective-permute-start.15) | collective-permute-done | bytes 1048608 | tf_op jit(solution)/shard_map/ppermute | solution.py:515
  209.2 16.9 %mix.1 = (f32[1024,2048]{1,0:T(8,128)}, bf16[1024,2048]{1,0:T(8,128)(2,1)S(1)}) custom-call(bf16[1024,2048]{1,0:T(8,128)(2,1)} %get-tuple-element.272.token_ref, bf16[1024,2048]{1,0:T(8,128)(2,1)} %constant_dynamic-update-slice_fusion.6.heads_ref, bf16[2048,2048]{1,0:T(8,128)(2,1)} %bitcast.57, f32[1,2048]{1,0:T(1,128)S(1)} %get-tuple-element.285.bias_ref, ...), custom_call_target="tpu_custom_call" | custom-call | flops 1048576 | bytes 65536 | tf_op jit(solution)/shard_map/mix/pallas_call | solution.py:150
  228.1 15.5 %feed_up.1 = (f32[1024,2048]{1,0:T(8,128)}, bf16[1024,2048]{1,0:T(8,128)(2,1)S(1)}) custom-call(bf16[1024,2048]{1,0:T(8,128)(2,1)} %copy-done.17, bf16[2048,2048]{1,0:T(8,128)(2,1)} %w_ref.2, f32[1,2048]{1,0:T(1,128)S(1)} %bitcast.56), custom_call_target="tpu_custom_call" | custom-call | flops 1048576 | bytes 65536 | tf_op jit(solution)/shard_map/feed_up/pallas_call | solution.py:176
  246.1 11.2 %convolution_convert_fusion.1.right_ref.left_ref = bf16[1024,2048]{1,0:T(8,128)(2,1)S(1)} fusion(bf16[1024,2048]{1,0:T(8,128)(2,1)S(1)} %get-tuple-element.142.refs_3_, bf16[2048,2048]{1,0:T(8,128)(2,1)} %w_ref.3), kind=kOutput, calls=%fused_computation.4 | convolution fusion | flops 8592031744 | bytes 16777216 | tf_op jit(solution)/shard_map/dot_general | solution.py:19
  257.3 10.3 %collective-permute-done.20 = bf16[256,2048]{1,0:T(8,128)(2,1)S(1)} collective-permute-done((bf16[256,2048]{1,0:T(8,128)(2,1)}, bf16[256,2048]{1,0:T(8,128)(2,1)S(1)}, u32[]{:S(2)}, u32[]{:S(2)}) %collective-permute-start.20) | collective-permute-done | bytes 1048608 | tf_op jit(solution)/shard_map/ppermute | solution.py:515
  275.5 16.5 %hidden_back.1.refs_2_ = bf16[1024,2048]{1,0:T(8,128)(2,1)S(1)} custom-call(bf16[1024,2048]{1,0:T(8,128)(2,1)} %constant_dynamic-update-slice_fusion.4.cot_ref.refs_1_, f32[1024,2048]{1,0:T(8,128)} %get-tuple-element.139.hidden_ref, bf16[2048,2048]{1,0:T(8,128)(2,1)} %w_ref.3), custom_call_target="tpu_custom_call" | custom-call | flops 1048576 | bytes 65536 | tf_op jit(solution)/shard_map/hidden_back/pallas_call | solution.py:199
  291.9 12.8 %convolution_convert_fusion.right_ref.left_ref.term_ref = bf16[1024,2048]{1,0:T(8,128)(2,1)S(1)} fusion(bf16[1024,2048]{1,0:T(8,128)(2,1)S(1)} %hidden_back.1.refs_2_, bf16[2048,2048]{1,0:T(8,128)(2,1)} %w_ref.2), kind=kOutput, calls=%fused_computation.3 | convolution fusion | flops 8592031744 | bytes 16777216 | tf_op jit(solution)/shard_map/dot_general | solution.py:19
  314.8 27.5 %weight_grads.2 = bf16[2048,4096]{1,0:T(8,128)(2,1)} custom-call(f32[1]{0:T(128)} %div.35.factor_ref, bf16[1024,2048]{1,0:T(8,128)(2,1)S(1)} %copy-done.18, bf16[1024,2048]{1,0:T(8,128)(2,1)} %constant_dynamic-update-slice_fusion.4.cot_ref.refs_1_, bf16[1024,2048]{1,0:T(8,128)(2,1)} %copy-done.16, bf16[1024,2048]{1,0:T(8,128)(2,1)} %copy-done.22), custom_call_target="tpu_custom_call" | custom-call | flops 1048576 | bytes 65536 | tf_op jit(solution)/shard_map/weight_grads/pallas_call | solution.py:243
  346.7 2.8 relay.11
  352.7 3.0 convert_reduce_fusion
  355.7 10.1 %collective-permute-done.25.refs_0_ = bf16[256,2048]{1,0:T(8,128)(2,1)S(1)} collective-permute-done((bf16[256,2048]{1,0:T(8,128)(2,1)}, bf16[256,2048]{1,0:T(8,128)(2,1)S(1)}, u32[]{:S(2)}, u32[]{:S(2)}) %collective-permute-start.25) | collective-permute-done | bytes 1048608 | tf_op jit(solution)/shard_map/ppermute | solution.py:535
  367.9 10.4 %collective-permute-start.27 = (bf16[256,2048]{1,0:T(8,128)(2,1)}, bf16[256,2048]{1,0:T(8,128)(2,1)S(1)}, u32[]{:S(2)}, u32[]{:S(2)}) collective-permute-start(bf16[256,2048]{1,0:T(8,128)(2,1)} %get-tuple-element.157), channel_id=1, source_target_pairs={{0,1},{1,2},{2,3},{4,5},{5,6},{6,7},{8,9},{9,10},{10,11},{12,13},{... | collective-permute-start | bytes 3145736 | tf_op jit(solution)/shard_map/ppermute | solution.py:535
  379.6 11.2 %collective-permute-done.27.left_ref = bf16[256,2048]{1,0:T(8,128)(2,1)S(1)} collective-permute-done((bf16[256,2048]{1,0:T(8,128)(2,1)}, bf16[256,2048]{1,0:T(8,128)(2,1)S(1)}, u32[]{:S(2)}, u32[]{:S(2)}) %collective-permute-start.27) | collective-permute-done | bytes 1048608 | tf_op jit(solution)/shard_map/ppermute | solution.py:535
  391.8 3.4 collective-permute-done.28.right_ref
  402.0 2.3 collective-permute-start.29
  406.5 4.6 middle_back.1
  411.2 8.0 %convolution_convert_fusion.2 = bf16[256,2048]{1,0:T(8,128)(2,1)} fusion(bf16[256,2048]{1,0:T(8,128)(2,1)S(1)} %get-tuple-element.170, bf16[2048,2048]{1,0:T(8,128)(2,1)} %bitcast.58), kind=kOutput, calls=%fused_computation.25 | convolution fusion | flops 2148007936 | bytes 10485760 | tf_op jit(solution)/shard_map/dot_general | solution.py:19
  419.3 4.6 multiply_convert_fusion
  428.6 2.8 collective-permute-start.33
  435.0 2.5 add_convert_fusion.3
  437.6 2.5 add_convert_fusion.5
  440.1 3.2 add_convert_fusion.4
  443.3 3.0 add_convert_fusion.6
  449.1 7.7 %collective-permute-start.35 = (bf16[256,2048]{1,0:T(8,128)(2,1)S(1)}, bf16[256,2048]{1,0:T(8,128)(2,1)S(1)}, u32[]{:S(2)}, u32[]{:S(2)}) collective-permute-start(bf16[256,2048]{1,0:T(8,128)(2,1)S(1)} %get-tuple-element.173), channel_id=1, source_target_pairs={{0,1},{1,2},{2,3},{4,5},{5,6},{6,7},{8,9},{9,10},{10,11},{12,13},{... | collective-permute-start | bytes 3145736 | tf_op jit(solution)/shard_map/ppermute | solution.py:535
  460.6 16.4 %attend_back.1.x_ref.refs_1_ = bf16[1024,1536]{1,0:T(8,128)(2,1)S(1)} custom-call(bf16[1024,1536]{1,0:T(8,128)(2,1)} %fusion.7.q_ref.k_ref.v_ref, bf16[1024,1536]{1,0:T(8,128)(2,1)} %fusion.7.q_ref.k_ref.v_ref, bf16[1024,1536]{1,0:T(8,128)(2,1)} %fusion.7.q_ref.k_ref.v_ref, bf16[1024,512]{1,0:T(8,128)(2,1)S(1)} %constant_dynamic-update-slice_fusion.grad_ref, ...), custom_call_target="tpu_custom_call" | custom-call | flops 1048576 | bytes 65536 | tf_op jit(solution)/shard_map/attend_back/pallas_call | solution.py:93
  477.0 4.2 half_product.2.right_ref.left_ref.refs_0_
  481.2 6.3 collective-permute-done.37
  487.5 2.3 add_convert_fusion.1
  495.8 4.2 half_product.3.right_ref.left_ref.term_ref
  502.0 12.3 %weight_grads.3 = bf16[2048,1536]{1,0:T(8,128)(2,1)} custom-call(f32[1]{0:T(128)} %div.35.factor_ref, bf16[1024,2048]{1,0:T(8,128)(2,1)} %get-tuple-element.189.refs_0_, bf16[1024,1536]{1,0:T(8,128)(2,1)S(1)} %attend_back.1.x_ref.refs_1_), custom_call_target="tpu_custom_call" | custom-call | flops 1048576 | bytes 65536 | tf_op jit(solution)/shard_map/weight_grads/pallas_call | solution.py:243
  514.4 3.5 collective-permute-start.39
  522.1 10.0 %collective-permute-done.41 = bf16[1024,256]{1,0:T(8,128)(2,1)} collective-permute-done((bf16[1024,256]{1,0:T(8,128)(2,1)}, bf16[1024,256]{1,0:T(8,128)(2,1)}, u32[]{:S(2)}, u32[]{:S(2)}) %collective-permute-start.41) | collective-permute-done | bytes 524320 | tf_op jit(solution)/shard_map/ppermute | solution.py:543
  533.3 6.9 %collective-permute-done.39.refs_0_ = bf16[256,2048]{1,0:T(8,128)(2,1)S(1)} collective-permute-done((bf16[256,2048]{1,0:T(8,128)(2,1)}, bf16[256,2048]{1,0:T(8,128)(2,1)S(1)}, u32[]{:S(2)}, u32[]{:S(2)}) %collective-permute-start.39) | collective-permute-done | bytes 1048608 | tf_op jit(solution)/shard_map/ppermute | solution.py:535
  544.5 4.3 collective-permute-start.43
  550.5 6.9 %gain_sums.1 = f32[2,2048]{1,0:T(2,128)S(1)} custom-call(bf16[1024,2048]{1,0:T(8,128)(2,1)S(1)} %copy-done.4, bf16[1024,2048]{1,0:T(8,128)(2,1)} %get-tuple-element.272.token_ref), custom_call_target="tpu_custom_call" | custom-call | flops 1048576 | bytes 65536 | tf_op jit(solution)/shard_map/gain_sums/pallas_call | solution.py:426
  563.6 2.7 convert_reduce_fusion.6
  566.3 5.1 collective-permute-done.45
  571.4 6.0 collective-permute-start.46
  581.6 3.2 relay.17
  584.8 2.4 collective-permute-start.47
  588.5 2.5 convert_element_type.211
  591.0 10.2 %all_gather.19 = f32[8,8,1920]{2,1,0:T(8,128)S(1)} all-gather(f32[1,8,1920]{2,1,0:T(8,128)S(1)} %reshape.101), channel_id=1, replica_groups=mesh['dp'=8,'mp'=4] {'dp'}, dimensions={0}, use_global_device_ids=true | all-gather | bytes 552960 | tf_op jit(solution)/shard_map/all_gather | solution.py:790
  601.3 3.3 slice_bitcast_fusion
  608.0 2.9 copy.31
  612.2 4.3 add_convert_fusion
  617.7 3.7 collective-permute-start.49
  621.4 2.4 collective-permute-start.50
  627.9 3.9 input_back.1
  633.2 8.2 %collective-permute-done.50 = bf16[512,256]{1,0:T(8,128)(2,1)S(1)} collective-permute-done((bf16[512,256]{1,0:T(8,128)(2,1)S(1)}, bf16[512,256]{1,0:T(8,128)(2,1)S(1)}, u32[]{:S(2)}, u32[]{:S(2)}) %collective-permute-start.50) | collective-permute-done | bytes 262176 | tf_op jit(solution)/shard_map/ppermute | solution.py:493
  (364 shorter events, 165.8 us)
Async XLA Ops:
  7.2 17.8 %copy-start = (bf16[512,2048]{1,0:T(8,128)(2,1)S(1)}, bf16[512,2048]{1,0:T(8,128)(2,1)}, u32[]{:S(2)}) copy-start(bf16[512,2048]{1,0:T(8,128)(2,1)} %param.21) | copy-start | bytes 6291460
  7.2 100.9 %all-gather.5.cloned.1.call-start = ((), (), s32[]{:S(2)}) async-start(), calls=%async_computation.4 | async-start | bytes 1310720 | tf_op jit(solution)/shard_map/all_gather | solution.py:687
  7.2 28.5 %collective-permute-start = (bf16[256,2048]{1,0:T(8,128)(2,1)}, bf16[256,2048]{1,0:T(8,128)(2,1)}, u32[]{:S(2)}, u32[]{:S(2)}) collective-permute-start(bf16[256,2048]{1,0:T(8,128)(2,1)} %value_ref.1), channel_id=1, source_target_pairs={{1,0},{2,1},{3,2},{5,4},{6,5},{7,6},{9,8},{10,9},{11,10},{13,12},{... | collective-permute-start | bytes 3145736 | tf_op jit(solution)/shard_map/ppermute | solution.py:515
  8.7 28.3 %collective-permute-start.1 = (bf16[256,2048]{1,0:T(8,128)(2,1)}, bf16[256,2048]{1,0:T(8,128)(2,1)}, u32[]{:S(2)}, u32[]{:S(2)}) collective-permute-start(bf16[256,2048]{1,0:T(8,128)(2,1)} %value_ref.1), channel_id=1, source_target_pairs={{0,1},{1,2},{2,3},{4,5},{5,6},{6,7},{8,9},{9,10},{10,11},{12,13},{... | collective-permute-start | bytes 3145736 | tf_op jit(solution)/shard_map/ppermute | solution.py:514
  37.0 42.3 %collective-permute-start.2 = (bf16[256,2048]{1,0:T(8,128)(2,1)}, bf16[256,2048]{1,0:T(8,128)(2,1)S(1)}, u32[]{:S(2)}, u32[]{:S(2)}) collective-permute-start(bf16[256,2048]{1,0:T(8,128)(2,1)} %collective-permute-done), channel_id=1, source_target_pairs={{1,0},{2,1},{5,4},{6,5},{9,8},{10,9},{13,12},{14,13},{17,16},{18,1... | collective-permute-start | bytes 3145736 | tf_op jit(solution)/shard_map/ppermute | solution.py:515
  38.2 41.0 %collective-permute-start.3 = (bf16[256,2048]{1,0:T(8,128)(2,1)}, bf16[256,2048]{1,0:T(8,128)(2,1)}, u32[]{:S(2)}, u32[]{:S(2)}) collective-permute-start(bf16[256,2048]{1,0:T(8,128)(2,1)} %collective-permute-done.1), channel_id=1, source_target_pairs={{1,2},{2,3},{5,6},{6,7},{9,10},{10,11},{13,14},{14,15},{17,18},{18... | collective-permute-start | bytes 3145736 | tf_op jit(solution)/shard_map/ppermute | solution.py:514
  41.9 167.3 %all-gather.7.cloned.1.call-start = ((), (), s32[]{:S(2)}) async-start(), calls=%async_computation.5 | async-start | bytes 9437184 | tf_op jit(solution)/shard_map/all_gather | solution.py:692
  79.3 26.8 %collective-permute-start.4 = (bf16[256,2048]{1,0:T(8,128)(2,1)S(1)}, bf16[256,2048]{1,0:T(8,128)(2,1)S(1)}, u32[]{:S(2)}, u32[]{:S(2)}) collective-permute-start(bf16[256,2048]{1,0:T(8,128)(2,1)S(1)} %collective-permute-done.2), channel_id=1, source_target_pairs={{1,0},{5,4},{9,8},{13,12},{17,16},{21,20},{25,24},{29,28}} | collective-permute-start | bytes 3145736 | tf_op jit(solution)/shard_map/ppermute | solution.py:515
  80.6 26.5 %collective-permute-start.5 = (bf16[256,2048]{1,0:T(8,128)(2,1)}, bf16[256,2048]{1,0:T(8,128)(2,1)S(1)}, u32[]{:S(2)}, u32[]{:S(2)}) collective-permute-start(bf16[256,2048]{1,0:T(8,128)(2,1)} %collective-permute-done.3), channel_id=1, source_target_pairs={{2,3},{6,7},{10,11},{14,15},{18,19},{22,23},{26,27},{30,31}} | collective-permute-start | bytes 3145736 | tf_op jit(solution)/shard_map/ppermute | solution.py:514
  85.6 22.5 %copy-start.44 = (s32[1024]{0:T(1024)S(1)}, s32[1024]{0:T(1024)}, u32[]{:S(2)}) copy-start(s32[1024]{0:T(1024)} %param.15) | copy-start | bytes 12292
  108.1 432.2 %reduce-scatter.3.cloned.1.call-start = ((), (), s32[]{:S(2)}) async-start(), calls=%async_computation.2 | async-start | bytes 18874368 | tf_op jit(solution)/shard_map/reduce_scatter | solution.py:743
  108.4 21.6 %collective-permute-start.6 = (bf16[256,2048]{1,0:T(8,128)(2,1)}, bf16[256,2048]{1,0:T(8,128)(2,1)S(1)}, u32[]{:S(2)}, u32[]{:S(2)}) collective-permute-start(bf16[256,2048]{1,0:T(8,128)(2,1)} %cot_ref.1), channel_id=1, source_target_pairs={{0,1},{1,2},{2,3},{4,5},{5,6},{6,7},{8,9},{9,10},{10,11},{12,13},{... | collective-permute-start | bytes 3145736 | tf_op jit(solution)/shard_map/ppermute | solution.py:514
  109.9 24.2 %collective-permute-start.7 = (bf16[256,2048]{1,0:T(8,128)(2,1)}, bf16[256,2048]{1,0:T(8,128)(2,1)}, u32[]{:S(2)}, u32[]{:S(2)}) collective-permute-start(bf16[256,2048]{1,0:T(8,128)(2,1)} %cot_ref.1), channel_id=1, source_target_pairs={{1,0},{2,1},{3,2},{5,4},{6,5},{7,6},{9,8},{10,9},{11,10},{13,12},{... | collective-permute-start | bytes 3145736 | tf_op jit(solution)/shard_map/ppermute | solution.py:515
  134.2 22.6 %collective-permute-start.8 = (bf16[1024,512]{1,0:T(8,128)(2,1)S(1)}, bf16[1024,512]{1,0:T(8,128)(2,1)}, u32[]{:S(2)}, u32[]{:S(2)}) collective-permute-start(bf16[1024,512]{1,0:T(8,128)(2,1)S(1)} %attend.1), channel_id=1, source_target_pairs={{1,0},{2,1},{3,2},{5,4},{6,5},{7,6},{9,8},{10,9},{11,10},{13,12},{... | collective-permute-start | bytes 3145736 | tf_op jit(solution)/shard_map/ppermute | solution.py:515
  135.5 22.4 %collective-permute-start.9 = (bf16[1024,512]{1,0:T(8,128)(2,1)S(1)}, bf16[1024,512]{1,0:T(8,128)(2,1)}, u32[]{:S(2)}, u32[]{:S(2)}) collective-permute-start(bf16[1024,512]{1,0:T(8,128)(2,1)S(1)} %attend.1), channel_id=1, source_target_pairs={{0,1},{1,2},{2,3},{4,5},{5,6},{6,7},{8,9},{9,10},{10,11},{12,13},{... | collective-permute-start | bytes 3145736 | tf_op jit(solution)/shard_map/ppermute | solution.py:514
  141.2 19.7 %copy-start.63 = (bf16[256,2048]{1,0:T(8,128)(2,1)S(1)}, bf16[256,2048]{1,0:T(8,128)(2,1)}, u32[]{:S(2)}) copy-start(bf16[256,2048]{1,0:T(8,128)(2,1)} %copy-done.62) | copy-start | bytes 3145732
  141.9 2.0 collective-permute-start.10
  144.6 3.6 collective-permute-start.11
  148.7 3.6 collective-permute-start.12
  157.9 22.9 %collective-permute-start.13 = (bf16[1024,512]{1,0:T(8,128)(2,1)}, bf16[1024,512]{1,0:T(8,128)(2,1)}, u32[]{:S(2)}, u32[]{:S(2)}) collective-permute-start(bf16[1024,512]{1,0:T(8,128)(2,1)} %collective-permute-done.8), channel_id=1, source_target_pairs={{1,0},{2,1},{5,4},{6,5},{9,8},{10,9},{13,12},{14,13},{17,16},{18,1... | collective-permute-start | bytes 3145736 | tf_op jit(solution)/shard_map/ppermute | solution.py:515
  159.1 21.7 %collective-permute-start.14 = (bf16[1024,512]{1,0:T(8,128)(2,1)}, bf16[1024,512]{1,0:T(8,128)(2,1)}, u32[]{:S(2)}, u32[]{:S(2)}) collective-permute-start(bf16[1024,512]{1,0:T(8,128)(2,1)} %collective-permute-done.9), channel_id=1, source_target_pairs={{1,2},{2,3},{5,6},{6,7},{9,10},{10,11},{13,14},{14,15},{17,18},{18... | collective-permute-start | bytes 3145736 | tf_op jit(solution)/shard_map/ppermute | solution.py:514
  164.7 19.1 %copy-start.84 = (bf16[2048]{0:T(1024)(128)(2,1)S(1)}, bf16[2048]{0:T(1024)(128)(2,1)}, u32[]{:S(2)}) copy-start(bf16[2048]{0:T(1024)(128)(2,1)} %param.24) | copy-start | bytes 12292
  180.8 21.8 %collective-permute-start.15 = (bf16[1024,512]{1,0:T(8,128)(2,1)}, bf16[1024,512]{1,0:T(8,128)(2,1)}, u32[]{:S(2)}, u32[]{:S(2)}) collective-permute-start(bf16[1024,512]{1,0:T(8,128)(2,1)} %collective-permute-done.13), channel_id=1, source_target_pairs={{1,0},{5,4},{9,8},{13,12},{17,16},{21,20},{25,24},{29,28}} | collective-permute-start | bytes 3145736 | tf_op jit(solution)/shard_map/ppermute | solution.py:515
  182.1 20.6 %collective-permute-start.16 = (bf16[1024,512]{1,0:T(8,128)(2,1)}, bf16[1024,512]{1,0:T(8,128)(2,1)}, u32[]{:S(2)}, u32[]{:S(2)}) collective-permute-start(bf16[1024,512]{1,0:T(8,128)(2,1)} %collective-permute-done.14), channel_id=1, source_target_pairs={{2,3},{6,7},{10,11},{14,15},{18,19},{22,23},{26,27},{30,31}} | collective-permute-start | bytes 3145736 | tf_op jit(solution)/shard_map/ppermute | solution.py:514
  183.8 21.9 %copy-start.82 = (bf16[2,2048]{1,0:T(2,128)(2,1)S(1)}, bf16[2,2048]{1,0:T(2,128)(2,1)}, u32[]{:S(2)}) copy-start(bf16[2,2048]{1,0:T(2,128)(2,1)} %param.22) | copy-start | bytes 24580
  202.6 41.0 %collective-permute-start.17 = (bf16[256,2048]{1,0:T(8,128)(2,1)S(1)}, bf16[256,2048]{1,0:T(8,128)(2,1)}, u32[]{:S(2)}, u32[]{:S(2)}) collective-permute-start(bf16[256,2048]{1,0:T(8,128)(2,1)S(1)} %copy-done.63), channel_id=1, source_target_pairs={{1,2},{2,3},{5,6},{6,7},{9,10},{10,11},{13,14},{14,15},{17,18},{18... | collective-permute-start | bytes 3145736 | tf_op jit(solution)/shard_map/ppermute | solution.py:514
  204.3 39.3 %collective-permute-start.18 = (bf16[256,2048]{1,0:T(8,128)(2,1)}, bf16[256,2048]{1,0:T(8,128)(2,1)}, u32[]{:S(2)}, u32[]{:S(2)}) collective-permute-start(bf16[256,2048]{1,0:T(8,128)(2,1)} %collective-permute-done.7), channel_id=1, source_target_pairs={{1,0},{2,1},{5,4},{6,5},{9,8},{10,9},{13,12},{14,13},{17,16},{18,1... | collective-permute-start | bytes 3145736 | tf_op jit(solution)/shard_map/ppermute | solution.py:515
  243.6 13.7 %collective-permute-start.19 = (bf16[256,2048]{1,0:T(8,128)(2,1)}, bf16[256,2048]{1,0:T(8,128)(2,1)S(1)}, u32[]{:S(2)}, u32[]{:S(2)}) collective-permute-start(bf16[256,2048]{1,0:T(8,128)(2,1)} %collective-permute-done.17), channel_id=1, source_target_pairs={{2,3},{6,7},{10,11},{14,15},{18,19},{22,23},{26,27},{30,31}} | collective-permute-start | bytes 3145736 | tf_op jit(solution)/shard_map/ppermute | solution.py:514
  244.4 23.2 %collective-permute-start.20 = (bf16[256,2048]{1,0:T(8,128)(2,1)}, bf16[256,2048]{1,0:T(8,128)(2,1)S(1)}, u32[]{:S(2)}, u32[]{:S(2)}) collective-permute-start(bf16[256,2048]{1,0:T(8,128)(2,1)} %collective-permute-done.18), channel_id=1, source_target_pairs={{1,0},{5,4},{9,8},{13,12},{17,16},{21,20},{25,24},{29,28}} | collective-permute-start | bytes 3145736 | tf_op jit(solution)/shard_map/ppermute | solution.py:515
  271.6 33.2 %collective-permute-start.21 = (bf16[256,2048]{1,0:T(8,128)(2,1)S(1)}, bf16[256,2048]{1,0:T(8,128)(2,1)S(1)}, u32[]{:S(2)}, u32[]{:S(2)}) collective-permute-start(bf16[256,2048]{1,0:T(8,128)(2,1)S(1)} %get-tuple-element.145), channel_id=1, source_target_pairs={{0,1},{4,5},{8,9},{12,13},{16,17},{20,21},{24,25},{28,29}} | collective-permute-start | bytes 3145736 | tf_op jit(solution)/shard_map/ppermute | solution.py:535
  273.7 32.2 %collective-permute-start.22 = (bf16[256,2048]{1,0:T(8,128)(2,1)S(1)}, bf16[256,2048]{1,0:T(8,128)(2,1)S(1)}, u32[]{:S(2)}, u32[]{:S(2)}) collective-permute-start(bf16[256,2048]{1,0:T(8,128)(2,1)S(1)} %get-tuple-element.146), channel_id=1, source_target_pairs={{3,2},{7,6},{11,10},{15,14},{19,18},{23,22},{27,26},{31,30}} | collective-permute-start | bytes 3145736 | tf_op jit(solution)/shard_map/ppermute | solution.py:536
  309.3 33.0 %collective-permute-start.23 = (bf16[256,2048]{1,0:T(8,128)(2,1)}, bf16[256,2048]{1,0:T(8,128)(2,1)S(1)}, u32[]{:S(2)}, u32[]{:S(2)}) collective-permute-start(bf16[256,2048]{1,0:T(8,128)(2,1)} %get-tuple-element.149), channel_id=1, source_target_pairs={{0,1},{4,5},{8,9},{12,13},{16,17},{20,21},{24,25},{28,29}} | collective-permute-start | bytes 3145736 | tf_op jit(solution)/shard_map/ppermute | solution.py:535
  310.6 32.6 %collective-permute-start.24 = (bf16[256,2048]{1,0:T(8,128)(2,1)}, bf16[256,2048]{1,0:T(8,128)(2,1)}, u32[]{:S(2)}, u32[]{:S(2)}) collective-permute-start(bf16[256,2048]{1,0:T(8,128)(2,1)} %get-tuple-element.150), channel_id=1, source_target_pairs={{3,2},{7,6},{11,10},{15,14},{19,18},{23,22},{27,26},{31,30}} | collective-permute-start | bytes 3145736 | tf_op jit(solution)/shard_map/ppermute | solution.py:536
  350.5 265.9 %reduce-scatter.5.cloned.1.call-start = ((), (), s32[]{:S(2)}) async-start(), calls=%async_computation.3 | async-start | bytes 7077888 | tf_op jit(solution)/shard_map/reduce_scatter | solution.py:773
  350.6 15.3 %collective-permute-start.25 = (bf16[256,2048]{1,0:T(8,128)(2,1)}, bf16[256,2048]{1,0:T(8,128)(2,1)S(1)}, u32[]{:S(2)}, u32[]{:S(2)}) collective-permute-start(bf16[256,2048]{1,0:T(8,128)(2,1)} %get-tuple-element.153), channel_id=1, source_target_pairs={{0,1},{1,2},{4,5},{5,6},{8,9},{9,10},{12,13},{13,14},{16,17},{17,1... | collective-permute-start | bytes 3145736 | tf_op jit(solution)/shard_map/ppermute | solution.py:535
  351.9 13.9 %collective-permute-start.26 = (bf16[256,2048]{1,0:T(8,128)(2,1)}, bf16[256,2048]{1,0:T(8,128)(2,1)S(1)}, u32[]{:S(2)}, u32[]{:S(2)}) collective-permute-start(bf16[256,2048]{1,0:T(8,128)(2,1)} %copy-done.46), channel_id=1, source_target_pairs={{2,1},{3,2},{6,5},{7,6},{10,9},{11,10},{14,13},{15,14},{18,17},{19... | collective-permute-start | bytes 3145736 | tf_op jit(solution)/shard_map/ppermute | solution.py:536
  367.9 23.0 %collective-permute-start.27 = (bf16[256,2048]{1,0:T(8,128)(2,1)}, bf16[256,2048]{1,0:T(8,128)(2,1)S(1)}, u32[]{:S(2)}, u32[]{:S(2)}) collective-permute-start(bf16[256,2048]{1,0:T(8,128)(2,1)} %get-tuple-element.157), channel_id=1, source_target_pairs={{0,1},{1,2},{2,3},{4,5},{5,6},{6,7},{8,9},{9,10},{10,11},{12,13},{... | collective-permute-start | bytes 3145736 | tf_op jit(solution)/shard_map/ppermute | solution.py:535
  378.3 16.9 %collective-permute-start.28 = (bf16[256,2048]{1,0:T(8,128)(2,1)}, bf16[256,2048]{1,0:T(8,128)(2,1)S(1)}, u32[]{:S(2)}, u32[]{:S(2)}) collective-permute-start(bf16[256,2048]{1,0:T(8,128)(2,1)} %get-tuple-element.158), channel_id=1, source_target_pairs={{1,0},{2,1},{3,2},{5,4},{6,5},{7,6},{9,8},{10,9},{11,10},{13,12},{... | collective-permute-start | bytes 3145736 | tf_op jit(solution)/shard_map/ppermute | solution.py:536
  402.0 21.8 %collective-permute-start.29 = (bf16[256,2048]{1,0:T(8,128)(2,1)S(1)}, bf16[256,2048]{1,0:T(8,128)(2,1)S(1)}, u32[]{:S(2)}, u32[]{:S(2)}) collective-permute-start(bf16[256,2048]{1,0:T(8,128)(2,1)S(1)} %get-tuple-element.160), channel_id=1, source_target_pairs={{0,1},{1,2},{4,5},{5,6},{8,9},{9,10},{12,13},{13,14},{16,17},{17,1... | collective-permute-start | bytes 3145736 | tf_op jit(solution)/shard_map/ppermute | solution.py:535
  404.3 20.5 %collective-permute-start.30 = (bf16[256,2048]{1,0:T(8,128)(2,1)S(1)}, bf16[256,2048]{1,0:T(8,128)(2,1)S(1)}, u32[]{:S(2)}, u32[]{:S(2)}) collective-permute-start(bf16[256,2048]{1,0:T(8,128)(2,1)S(1)} %get-tuple-element.161), channel_id=1, source_target_pairs={{2,1},{3,2},{6,5},{7,6},{10,9},{11,10},{14,13},{15,14},{18,17},{19... | collective-permute-start | bytes 3145736 | tf_op jit(solution)/shard_map/ppermute | solution.py:536
  425.8 7.5 %collective-permute-start.34 = (bf16[2048,1024]{1,0:T(8,128)(2,1)}, bf16[2048,1024]{1,0:T(8,128)(2,1)}, u32[]{:S(2)}, u32[]{:S(2)}) collective-permute-start(bf16[2048,1024]{1,0:T(8,128)(2,1)} %multiply_convert_fusion), channel_id=1, source_target_pairs={{0,4},{4,0},{8,12},{12,8},{16,20},{20,16},{24,28},{28,24},{1,5},{5... | collective-permute-start | bytes 12582920 | tf_op jit(solution)/shard_map/ppermute | solution.py:543
  425.9 20.4 %collective-permute-start.31 = (bf16[256,512]{1,0:T(8,128)(2,1)S(1)}, bf16[256,512]{1,0:T(8,128)(2,1)S(1)}, u32[]{:S(2)}, u32[]{:S(2)}) collective-permute-start(bf16[256,512]{1,0:T(8,128)(2,1)S(1)} %get-tuple-element.265), channel_id=1, source_target_pairs={{0,1},{1,2},{2,3},{3,0},{4,5},{5,6},{6,7},{7,4},{8,9},{9,10},{10,1... | collective-permute-start | bytes 786440 | tf_op jit(solution)/shard_map/ppermute | solution.py:483
  426.5 21.3 %collective-permute-start.32 = (bf16[256,512]{1,0:T(8,128)(2,1)S(1)}, bf16[256,512]{1,0:T(8,128)(2,1)S(1)}, u32[]{:S(2)}, u32[]{:S(2)}) collective-permute-start(bf16[256,512]{1,0:T(8,128)(2,1)S(1)} %get-tuple-element.264), channel_id=1, source_target_pairs={{0,2},{1,3},{2,0},{3,1},{4,6},{5,7},{6,4},{7,5},{8,10},{9,11},{10,... | collective-permute-start | bytes 786440 | tf_op jit(solution)/shard_map/ppermute | solution.py:483
  428.6 19.2 %collective-permute-start.33 = (bf16[256,512]{1,0:T(8,128)(2,1)S(1)}, bf16[256,512]{1,0:T(8,128)(2,1)S(1)}, u32[]{:S(2)}, u32[]{:S(2)}) collective-permute-start(bf16[256,512]{1,0:T(8,128)(2,1)S(1)} %get-tuple-element.263), channel_id=1, source_target_pairs={{0,3},{1,0},{2,1},{3,2},{4,7},{5,4},{6,5},{7,6},{8,11},{9,8},{10,9... | collective-permute-start | bytes 786440 | tf_op jit(solution)/shard_map/ppermute | solution.py:483
  447.8 39.7 %collective-permute-start.37 = (bf16[1024,512]{1,0:T(8,128)(2,1)}, bf16[1024,512]{1,0:T(8,128)(2,1)}, u32[]{:S(2)}, u32[]{:S(2)}) collective-permute-start(bf16[1024,512]{1,0:T(8,128)(2,1)} %add_convert_fusion.6), channel_id=1, source_target_pairs={{0,8},{4,12},{8,0},{12,4},{16,24},{20,28},{24,16},{28,20},{1,9},{5... | collective-permute-start | bytes 3145736 | tf_op jit(solution)/shard_map/ppermute | solution.py:543
  447.9 39.6 %collective-permute-start.38 = (bf16[1024,512]{1,0:T(8,128)(2,1)}, bf16[1024,512]{1,0:T(8,128)(2,1)}, u32[]{:S(2)}, u32[]{:S(2)}) collective-permute-start(bf16[1024,512]{1,0:T(8,128)(2,1)} %add_convert_fusion.5), channel_id=1, source_target_pairs={{0,16},{4,20},{8,24},{12,28},{16,0},{20,4},{24,8},{28,12},{1,17},{... | collective-permute-start | bytes 3145736 | tf_op jit(solution)/shard_map/ppermute | solution.py:543
  449.1 38.4 %collective-permute-start.35 = (bf16[256,2048]{1,0:T(8,128)(2,1)S(1)}, bf16[256,2048]{1,0:T(8,128)(2,1)S(1)}, u32[]{:S(2)}, u32[]{:S(2)}) collective-permute-start(bf16[256,2048]{1,0:T(8,128)(2,1)S(1)} %get-tuple-element.173), channel_id=1, source_target_pairs={{0,1},{1,2},{2,3},{4,5},{5,6},{6,7},{8,9},{9,10},{10,11},{12,13},{... | collective-permute-start | bytes 3145736 | tf_op jit(solution)/shard_map/ppermute | solution.py:535
  456.8 30.7 %collective-permute-start.36 = (bf16[256,2048]{1,0:T(8,128)(2,1)S(1)}, bf16[256,2048]{1,0:T(8,128)(2,1)S(1)}, u32[]{:S(2)}, u32[]{:S(2)}) collective-permute-start(bf16[256,2048]{1,0:T(8,128)(2,1)S(1)} %get-tuple-element.174), channel_id=1, source_target_pairs={{1,0},{2,1},{3,2},{5,4},{6,5},{7,6},{9,8},{10,9},{11,10},{13,12},{... | collective-permute-start | bytes 3145736 | tf_op jit(solution)/shard_map/ppermute | solution.py:536
  459.1 17.9 %copy-start.15 = (bf16[2048,1536]{1,0:T(8,128)(2,1)}, bf16[2048,1536]{1,0:T(8,128)(2,1)S(1)}, u32[]{:S(2)}) copy-start(bf16[2048,1536]{1,0:T(8,128)(2,1)S(1)} %pad_maximum_fusion.w_ref) | copy-start | bytes 18874372
  477.0 23.0 %copy-start.14 = (bf16[1024,1536]{1,0:T(8,128)(2,1)}, bf16[1024,1536]{1,0:T(8,128)(2,1)S(1)}, u32[]{:S(2)}) copy-start(bf16[1024,1536]{1,0:T(8,128)(2,1)S(1)} %attend_back.1.x_ref.refs_1_) | copy-start | bytes 9437188
  514.4 25.9 %collective-permute-start.39 = (bf16[256,2048]{1,0:T(8,128)(2,1)}, bf16[256,2048]{1,0:T(8,128)(2,1)S(1)}, u32[]{:S(2)}, u32[]{:S(2)}) collective-permute-start(bf16[256,2048]{1,0:T(8,128)(2,1)} %get-tuple-element.182), channel_id=1, source_target_pairs={{0,1},{4,5},{8,9},{12,13},{16,17},{20,21},{24,25},{28,29}} | collective-permute-start | bytes 3145736 | tf_op jit(solution)/shard_map/ppermute | solution.py:535
  517.8 22.4 %collective-permute-start.40 = (bf16[256,2048]{1,0:T(8,128)(2,1)}, bf16[256,2048]{1,0:T(8,128)(2,1)S(1)}, u32[]{:S(2)}, u32[]{:S(2)}) collective-permute-start(bf16[256,2048]{1,0:T(8,128)(2,1)} %copy-done.45), channel_id=1, source_target_pairs={{3,2},{7,6},{11,10},{15,14},{19,18},{23,22},{27,26},{31,30}} | collective-permute-start | bytes 3145736 | tf_op jit(solution)/shard_map/ppermute | solution.py:536
  518.6 13.6 %collective-permute-start.41 = (bf16[1024,256]{1,0:T(8,128)(2,1)}, bf16[1024,256]{1,0:T(8,128)(2,1)}, u32[]{:S(2)}, u32[]{:S(2)}) collective-permute-start(bf16[1024,256]{1,0:T(8,128)(2,1)} %fusion.76), channel_id=1, source_target_pairs={{0,16},{4,20},{8,24},{12,28},{16,0},{20,4},{24,8},{28,12},{1,17},{... | collective-permute-start | bytes 1572872 | tf_op jit(solution)/shard_map/ppermute | solution.py:543
  520.1 13.2 %collective-permute-start.42 = (bf16[1024,256]{1,0:T(8,128)(2,1)}, bf16[1024,256]{1,0:T(8,128)(2,1)}, u32[]{:S(2)}, u32[]{:S(2)}) collective-permute-start(bf16[1024,256]{1,0:T(8,128)(2,1)} %fusion.75), channel_id=1, source_target_pairs={{0,8},{4,12},{8,0},{12,4},{16,24},{20,28},{24,16},{28,20},{1,9},{5... | collective-permute-start | bytes 1572872 | tf_op jit(solution)/shard_map/ppermute | solution.py:543
  544.5 34.9 %collective-permute-start.43 = (bf16[256,2048]{1,0:T(8,128)(2,1)}, bf16[256,2048]{1,0:T(8,128)(2,1)S(1)}, u32[]{:S(2)}, u32[]{:S(2)}) collective-permute-start(bf16[256,2048]{1,0:T(8,128)(2,1)} %get-tuple-element.192), channel_id=1, source_target_pairs={{0,1},{1,2},{4,5},{5,6},{8,9},{9,10},{12,13},{13,14},{16,17},{17,1... | collective-permute-start | bytes 3145736 | tf_op jit(solution)/shard_map/ppermute | solution.py:535
  548.9 31.5 %collective-permute-start.44 = (bf16[256,2048]{1,0:T(8,128)(2,1)}, bf16[256,2048]{1,0:T(8,128)(2,1)}, u32[]{:S(2)}, u32[]{:S(2)}) collective-permute-start(bf16[256,2048]{1,0:T(8,128)(2,1)} %get-tuple-element.193), channel_id=1, source_target_pairs={{2,1},{3,2},{6,5},{7,6},{10,9},{11,10},{14,13},{15,14},{18,17},{19... | collective-permute-start | bytes 3145736 | tf_op jit(solution)/shard_map/ppermute | solution.py:536
  557.5 13.9 %collective-permute-start.45 = (f32[12288]{0:T(1024)S(1)}, f32[12288]{0:T(1024)S(1)}, u32[]{:S(2)}, u32[]{:S(2)}) collective-permute-start(f32[12288]{0:T(1024)S(1)} %mul.272), channel_id=1, source_target_pairs={{0,1},{1,0},{2,3},{3,2},{4,5},{5,4},{6,7},{7,6},{8,9},{9,8},{10,11... | collective-permute-start | bytes 147464 | tf_op jit(solution)/shard_map/ppermute | solution.py:543
  562.5 17.9 %copy-start.5 = (bf16[1024,2048]{1,0:T(8,128)(2,1)S(1)}, bf16[1024,2048]{1,0:T(8,128)(2,1)}, u32[]{:S(2)}) copy-start(bf16[1024,2048]{1,0:T(8,128)(2,1)} %copy-done.2) | copy-start | bytes 12582916
  571.4 8.0 %collective-permute-start.46 = (f32[12288]{0:T(1024)S(1)}, f32[12288]{0:T(1024)S(1)}, u32[]{:S(2)}, u32[]{:S(2)}) collective-permute-start(f32[12288]{0:T(1024)S(1)} %add.475), channel_id=1, source_target_pairs={{0,2},{1,3},{2,0},{3,1},{4,6},{5,7},{6,4},{7,5},{8,10},{9,11},{10,... | collective-permute-start | bytes 147464 | tf_op jit(solution)/shard_map/ppermute | solution.py:543
  584.8 31.6 %collective-permute-start.47 = (bf16[256,2048]{1,0:T(8,128)(2,1)}, bf16[256,2048]{1,0:T(8,128)(2,1)}, u32[]{:S(2)}, u32[]{:S(2)}) collective-permute-start(bf16[256,2048]{1,0:T(8,128)(2,1)} %get-tuple-element.199), channel_id=1, source_target_pairs={{0,1},{1,2},{2,3},{4,5},{5,6},{6,7},{8,9},{9,10},{10,11},{12,13},{... | collective-permute-start | bytes 3145736 | tf_op jit(solution)/shard_map/ppermute | solution.py:535
  587.2 29.2 %collective-permute-start.48 = (bf16[256,2048]{1,0:T(8,128)(2,1)}, bf16[256,2048]{1,0:T(8,128)(2,1)}, u32[]{:S(2)}, u32[]{:S(2)}) collective-permute-start(bf16[256,2048]{1,0:T(8,128)(2,1)} %get-tuple-element.200), channel_id=1, source_target_pairs={{1,0},{2,1},{3,2},{5,4},{6,5},{7,6},{9,8},{10,9},{11,10},{13,12},{... | collective-permute-start | bytes 3145736 | tf_op jit(solution)/shard_map/ppermute | solution.py:536
  617.7 15.5 %collective-permute-start.49 = (bf16[512,256]{1,0:T(8,128)(2,1)S(1)}, bf16[512,256]{1,0:T(8,128)(2,1)S(1)}, u32[]{:S(2)}, u32[]{:S(2)}) collective-permute-start(bf16[512,256]{1,0:T(8,128)(2,1)S(1)} %get-tuple-element.252), channel_id=1, source_target_pairs={{0,1},{1,2},{2,3},{3,0},{4,5},{5,6},{6,7},{7,4},{8,9},{9,10},{10,1... | collective-permute-start | bytes 786440 | tf_op jit(solution)/shard_map/ppermute | solution.py:493
  621.4 20.0 %collective-permute-start.50 = (bf16[512,256]{1,0:T(8,128)(2,1)S(1)}, bf16[512,256]{1,0:T(8,128)(2,1)S(1)}, u32[]{:S(2)}, u32[]{:S(2)}) collective-permute-start(bf16[512,256]{1,0:T(8,128)(2,1)S(1)} %get-tuple-element.254), channel_id=1, source_target_pairs={{0,2},{1,3},{2,0},{3,1},{4,6},{5,7},{6,4},{7,5},{8,10},{9,11},{10,... | collective-permute-start | bytes 786440 | tf_op jit(solution)/shard_map/ppermute | solution.py:493
  623.8 17.6 %collective-permute-start.51 = (bf16[512,256]{1,0:T(8,128)(2,1)S(1)}, bf16[512,256]{1,0:T(8,128)(2,1)S(1)}, u32[]{:S(2)}, u32[]{:S(2)}) collective-permute-start(bf16[512,256]{1,0:T(8,128)(2,1)S(1)} %get-tuple-element.253), channel_id=1, source_target_pairs={{0,3},{1,0},{2,1},{3,2},{4,7},{5,4},{6,5},{7,6},{8,11},{9,8},{10,9... | collective-permute-start | bytes 786440 | tf_op jit(solution)/shard_map/ppermute | solution.py:493
  (79 other events, 355.1 us)
Sparse Core Ops, SparseCore 0:
  42.0 39.6 all-gather.4
  108.2 54.7 all-gather.6
  350.6 130.5 reduce-scatter.2
  514.5 61.7 reduce-scatter.4

commit v3 on v2

--- a/solution.py
+++ b/solution.py
@@ -12,7 +12,8 @@
 SCALE = HEAD ** (-0.5)
 f32 = jnp.float32
 bf16 = jnp.bfloat16
-LIGHT = pl.CostEstimate(flops=1 << 20, bytes_accessed=1 << 16, transcendentals=0)
+MIB = 2**20
+COST = pl.CostEstimate(flops=1 << 20, bytes_accessed=1 << 16, transcendentals=0)
 
 
 def dot(left, right, left_dim=1, right_dim=0):
@@ -57,8 +58,8 @@
         ],
         out_specs=pl.BlockSpec((SEQ, HEAD), lambda r, h: (r, h)),
         out_shape=jax.ShapeDtypeStruct((tokens, heads * HEAD), bf16),
-        compiler_params=pltpu.CompilerParams(vmem_limit_bytes=40 * 2**20),
-        cost_estimate=LIGHT,
+        compiler_params=pltpu.CompilerParams(vmem_limit_bytes=24 * MIB),
+        cost_estimate=COST,
         name="attend",
     )(projected, projected, projected, seg_col, seg_row)
 
@@ -104,8 +105,8 @@
         out_specs=pl.BlockSpec((SEQ, 3 * heads * HEAD), lambda r, h: (r, 0)),
         out_shape=jax.ShapeDtypeStruct((tokens, 3 * heads * HEAD), bf16),
         scratch_shapes=[pltpu.VMEM((SEQ, HEAD), f32), pltpu.VMEM((SEQ, HEAD), f32)],
-        compiler_params=pltpu.CompilerParams(vmem_limit_bytes=40 * 2**20),
-        cost_estimate=LIGHT,
+        compiler_params=pltpu.CompilerParams(vmem_limit_bytes=32 * MIB),
+        cost_estimate=COST,
         name="attend_back",
     )(projected, projected, projected, grad_attn, seg_col, seg_row)
 
@@ -135,31 +136,34 @@
     return value * half, slope
 
 
-def mix_kernel(token_ref, heads_ref, w_ref, bias_ref, gain_ref, shift_ref, middle_ref, normed_ref):
-    middle = dot(heads_ref[...], w_ref[...]) + (token_ref[...].astype(f32) + bias_ref[...])
+def mix_kernel(index_ref, sum_ref, heads_ref, w_ref, gain_ref, shift_ref, middle_ref, normed_ref):
+    middle = sum_ref[...] + dot(heads_ref[...], w_ref[...])
     middle_ref[...] = middle
     normed_ref[...] = (norm_parts(middle)[0] * gain_ref[...] + shift_ref[...]).astype(bf16)
 
 
-def mix(tokens_all, attn_all, w_out_all, bias, gain, shift):
-    tokens, width = tokens_all.shape
-    cols = attn_all.shape[1]
+def mix(summed, heads_block, w_out_all, index, gain, shift):
+    tokens, width = summed.shape
+    cols = heads_block.shape[1]
     step = 256
-    row = lambda size: pl.BlockSpec((step, size), lambda i: (i, 0))
-    one = pl.BlockSpec((1, width), lambda i: (0, 0))
+    row = lambda size: pl.BlockSpec((step, size), lambda i, at: (i, 0))
+    one = pl.BlockSpec((1, width), lambda i, at: (0, 0))
     return pl.pallas_call(
         mix_kernel,
-        grid=(tokens // step,),
-        in_specs=[row(width), row(cols), pl.BlockSpec((cols, width), lambda i: (0, 0)), one, one, one],
-        out_specs=[row(width), row(width)],
+        grid_spec=pltpu.PrefetchScalarGridSpec(
+            num_scalar_prefetch=1,
+            grid=(tokens // step,),
+            in_specs=[row(width), row(cols), pl.BlockSpec((cols, width), lambda i, at: (at[0], 0)), one, one],
+            out_specs=[row(width), row(width)],
+        ),
         out_shape=[
             jax.ShapeDtypeStruct((tokens, width), f32),
             jax.ShapeDtypeStruct((tokens, width), bf16),
         ],
-        compiler_params=pltpu.CompilerParams(vmem_limit_bytes=48 * 2**20),
-        cost_estimate=LIGHT,
+        compiler_params=pltpu.CompilerParams(vmem_limit_bytes=48 * MIB),
+        cost_estimate=COST,
         name="mix",
-    )(tokens_all, attn_all, w_out_all, bias[None], gain[None], shift[None])
+    )(index[None].astype(jnp.int32), summed, heads_block, w_out_all, gain[None], shift[None])
 
 
 def up_kernel(x_ref, w_ref, b_ref, hidden_ref, active_ref):
@@ -182,79 +186,99 @@
             jax.ShapeDtypeStruct((tokens, cols), f32),
             jax.ShapeDtypeStruct((tokens, cols), bf16),
         ],
-        compiler_params=pltpu.CompilerParams(vmem_limit_bytes=48 * 2**20),
-        cost_estimate=LIGHT,
+        compiler_params=pltpu.CompilerParams(vmem_limit_bytes=48 * MIB),
+        cost_estimate=COST,
         name="feed_up",
     )(normed, w_up, b_up[None])
 
 
-def hidden_kernel(cot_ref, hidden_ref, w_ref, out_ref):
+def hidden_kernel(index_ref, cot_ref, hidden_ref, w_ref, *refs):
     slope = gelu_parts(hidden_ref[...])[1]
-    out_ref[...] = (dot(cot_ref[...], w_ref[...], 1, 1) * slope).astype(bf16)
-
-
-def hidden_back(cot_all, hidden, w_down):
+    refs[-1][...] = (dot(cot_ref[...], w_ref[...], 1, 1) * slope).astype(bf16)
+
+
+def hidden_back(cot_all, hidden, w_down, half, earlier=None):
     tokens, width = cot_all.shape
-    cols, step = hidden.shape[1], 256
+    rows = tokens // 2
+    cols, step = hidden.shape[1], 512
+    given = [] if earlier is None else [earlier]
     return pl.pallas_call(
         hidden_kernel,
-        grid=(cols // step,),
+        grid_spec=pltpu.PrefetchScalarGridSpec(
+            num_scalar_prefetch=1,
+            grid=(cols // step,),
+            in_specs=[
+                pl.BlockSpec((rows, width), lambda i, at: (at[0], 0)),
+                pl.BlockSpec((rows, step), lambda i, at: (at[0], i)),
+                pl.BlockSpec((step, width), lambda i, at: (i, 0)),
+                *[pl.BlockSpec(memory_space=pl.ANY) for _ in given],
+            ],
+            out_specs=pl.BlockSpec((rows, step), lambda i, at: (at[0], i)),
+        ),
+        out_shape=jax.ShapeDtypeStruct((tokens, cols), bf16),
+        input_output_aliases={4: 0} if given else {},
+        compiler_params=pltpu.CompilerParams(vmem_limit_bytes=20 * MIB),
+        cost_estimate=COST,
+        name="hidden_back",
+    )(half[None], cot_all, hidden, w_down, *given)
+
+
+def slope_kernel(index_ref, grad_ref, hidden_ref, out_ref):
+    out_ref[...] = (grad_ref[...] * gelu_parts(hidden_ref[...])[1]).astype(bf16)
+
+
+def slope_back(d_active, hidden, half):
+    tokens, cols = hidden.shape
+    step = 64
+    steps = tokens // 2 // step
+    place = pl.BlockSpec((step, cols), lambda i, at: (at[0] * steps + i, 0))
+    return pl.pallas_call(
+        slope_kernel,
+        grid_spec=pltpu.PrefetchScalarGridSpec(
+            num_scalar_prefetch=1,
+            grid=(steps,),
+            in_specs=[pl.BlockSpec((step, cols), lambda i, at: (i, 0)), place],
+            out_specs=place,
+        ),
+        out_shape=jax.ShapeDtypeStruct((tokens, cols), bf16),
+        compiler_params=pltpu.CompilerParams(vmem_limit_bytes=12 * MIB),
+        cost_estimate=COST,
+        name="slope_back",
+    )(half[None], d_active, hidden)
+
+
+def grads_kernel(factor_ref, left_ref, right_ref, *refs):
+    out_ref, turned_ref = refs[-2:]
+
+    @pl.when(pl.program_id(0) == 0)
+    def _():
+        turned_ref[...] = left_ref[...].T
+
+    out_ref[...] = (factor_ref[0] * dot(turned_ref[...], right_ref[...])).astype(bf16)
+
+
+def weight_grads(factor, left, right, parts=1, part=0, earlier=None):
+    tokens, width = left.shape
+    cols, step = right.shape[1], 256
+    steps = cols // step
+    given = [] if earlier is None else [earlier]
+    return pl.pallas_call(
+        grads_kernel,
+        grid=(steps,),
         in_specs=[
+            pl.BlockSpec(memory_space=pltpu.SMEM),
             pl.BlockSpec((tokens, width), lambda i: (0, 0)),
             pl.BlockSpec((tokens, step), lambda i: (0, i)),
-            pl.BlockSpec((step, width), lambda i: (i, 0)),
+            *[pl.BlockSpec(memory_space=pl.ANY) for _ in given],
         ],
-        out_specs=pl.BlockSpec((tokens, step), lambda i: (0, i)),
-        out_shape=jax.ShapeDtypeStruct((tokens, cols), bf16),
-        compiler_params=pltpu.CompilerParams(vmem_limit_bytes=48 * 2**20),
-        cost_estimate=LIGHT,
-        name="hidden_back",
-    )(cot_all, hidden, w_down)
-
-
-def grads_kernel(bounds, factor_ref, *refs):
-    count = len(bounds) - 1
-    left_refs, right_refs = refs[:count], refs[count : 2 * count]
-    out_ref, turned_ref = refs[2 * count :]
-    i = pl.program_id(0)
-    for j in range(count):
-
-        @pl.when(i == bounds[j])
-        def _():
-            turned_ref[...] = left_refs[j][...].T
-
-        @pl.when((i >= bounds[j]) & (i < bounds[j + 1]))
-        def _():
-            out_ref[...] = (factor_ref[0] * dot(turned_ref[...], right_refs[j][...])).astype(bf16)
-
-
-def weight_grads(factor, pairs):
-    tokens, width = pairs[0][0].shape
-    step = 256
-    bounds = [0]
-    for _, right in pairs:
-        bounds.append(bounds[-1] + right.shape[1] // step)
-
-    def part(j):
-        low, high = bounds[j], bounds[j + 1]
-        return pl.BlockSpec((tokens, step), lambda i: (0, jnp.clip(i - low, 0, high - low - 1)))
-
-    whole = pl.BlockSpec((tokens, width), lambda i: (0, 0))
-    return pl.pallas_call(
-        functools.partial(grads_kernel, tuple(bounds)),
-        grid=(bounds[-1],),
-        in_specs=[
-            pl.BlockSpec(memory_space=pltpu.SMEM),
-            *[whole] * len(pairs),
-            *[part(j) for j in range(len(pairs))],
-        ],
-        out_specs=pl.BlockSpec((width, step), lambda i: (0, i)),
-        out_shape=jax.ShapeDtypeStruct((width, step * bounds[-1]), bf16),
+        out_specs=pl.BlockSpec((width, step), lambda i: (0, part * steps + i)),
+        out_shape=jax.ShapeDtypeStruct((width, parts * cols), bf16),
+        input_output_aliases={3: 0} if given else {},
         scratch_shapes=[pltpu.VMEM((width, tokens), bf16)],
-        compiler_params=pltpu.CompilerParams(vmem_limit_bytes=48 * 2**20),
-        cost_estimate=LIGHT,
+        compiler_params=pltpu.CompilerParams(vmem_limit_bytes=48 * MIB),
+        cost_estimate=COST,
         name="weight_grads",
-    )(factor[None], *[left for left, _ in pairs], *[right for _, right in pairs])
+    )(factor[None], left, right, *given)
 
 
 def half_kernel(index_ref, x_ref, w_ref, *refs):
@@ -280,8 +304,8 @@
         ),
         out_shape=jax.ShapeDtypeStruct((tokens, cols), bf16),
         input_output_aliases={3: 0} if given else {},
-        compiler_params=pltpu.CompilerParams(vmem_limit_bytes=40 * 2**20),
-        cost_estimate=LIGHT,
+        compiler_params=pltpu.CompilerParams(vmem_limit_bytes=40 * MIB),
+        cost_estimate=COST,
         name="half_product",
     )(half[None], x, weight, *given)
 
@@ -313,8 +337,8 @@
             out_specs=[block, block],
         ),
         out_shape=[jax.ShapeDtypeStruct((rows, width), bf16)] * 2,
-        compiler_params=pltpu.CompilerParams(vmem_limit_bytes=40 * 2**20),
-        cost_estimate=LIGHT,
+        compiler_params=pltpu.CompilerParams(vmem_limit_bytes=12 * MIB),
+        cost_estimate=COST,
         name="relay",
     )(index, terms, terms, *came)
 
@@ -372,8 +396,8 @@
             jax.ShapeDtypeStruct((rows, width), bf16),
             jax.ShapeDtypeStruct((4, width), f32),
         ],
-        compiler_params=pltpu.CompilerParams(vmem_limit_bytes=40 * 2**20),
-        cost_estimate=LIGHT,
+        compiler_params=pltpu.CompilerParams(vmem_limit_bytes=16 * MIB),
+        cost_estimate=COST,
         name="middle_back",
     )(index, terms, *came, middle_all, gain[None], cot)
 
@@ -390,8 +414,8 @@
             out_specs=here,
         ),
         out_shape=jax.ShapeDtypeStruct((rows, width), f32),
-        compiler_params=pltpu.CompilerParams(vmem_limit_bytes=40 * 2**20),
-        cost_estimate=LIGHT,
+        compiler_params=pltpu.CompilerParams(vmem_limit_bytes=16 * MIB),
+        cost_estimate=COST,
         name="input_back",
     )(index, factor[None], terms, *came, tokens, gain[None], d_middle)
 
@@ -429,8 +453,8 @@
         in_specs=[block, block],
         out_specs=pl.BlockSpec((2, width), lambda i: (0, 0)),
         out_shape=jax.ShapeDtypeStruct((2, width), f32),
-        compiler_params=pltpu.CompilerParams(vmem_limit_bytes=40 * 2**20),
-        cost_estimate=LIGHT,
+        compiler_params=pltpu.CompilerParams(vmem_limit_bytes=12 * MIB),
+        cost_estimate=COST,
         name="gain_sums",
     )(terms, tokens_all)
 
@@ -505,7 +529,7 @@
 
 class Gather:
     def __init__(self, line, block):
-        self.line, self.left, self.right = line, [block], [block]
+        self.line, self.left, self.right, self.slots = line, [block], [block], {0: block}
 
     def step(self, phase):
         line, n, k = self.line, self.line.n, len(self.left)
@@ -514,11 +538,22 @@
         self.left.append(lax.ppermute(left, line.name, [(j, j + 1) for j in range(k - 1, n - 1)]))
         self.right.append(lax.ppermute(right, line.name, [(j, j - 1) for j in range(1, n - k + 1)]))
         phase.keep(self.left[k], self.right[k])
-        low_side, high_side = self.right[k], self.left[k]
-        if 2 * k >= n:
-            low_side = jnp.where(line.me + k < n, self.right[k], self.left[n - k])
-            high_side = jnp.where(line.me >= k, self.left[k], self.right[n - k])
-        return jnp.where(line.low, low_side, high_side)
+
+    def slot(self, phase, k):
+        if k not in self.slots:
+            line, n = self.line, self.line.n
+            if 2 * k < n:
+                left, right = phase(self.left[k], self.right[k])
+                value = jnp.where(line.low, right, left)
+            else:
+                left, right, left_far, right_far = phase(
+                    self.left[n - k], self.right[n - k], self.left[k], self.right[k]
+                )
+                low_side = jnp.where(line.me + k < n, right_far, left)
+                high_side = jnp.where(line.me >= k, left_far, right)
+                value = jnp.where(line.low, low_side, high_side)
+            self.slots[k] = value
+        return self.slots[k]
 
 
 class Reduce:
@@ -667,8 +702,8 @@
         )
         state = [blank((group, width)), blank((group, width)), blank((group, 3 * head_cols))]
 
-        def project(k, block):
-            block = phase(block)
+        def project(k):
+            block = phase(gather.slot(phase, k))
             normed = (norm_parts(block.astype(f32))[0] * gains[0] + shifts[0]).astype(bf16)
             proj = (dot(normed, flat_qkv) + bias_rows).astype(bf16)
             for j, value in enumerate((block, normed, proj)):
@@ -680,17 +715,16 @@
         )
 
         gather = Gather(line, tokens)
-        token_slots = [tokens]
         for k in slots:
-            token_slots.append(gather.step(phase))
+            gather.step(phase)
             if k == 2:
                 w_slices = lax.all_gather(phase(w_slice), "mp", axis=0)
-            project(k - 1, token_slots[k - 1])
+            project(k - 1)
             turn()
         cot_gather = Gather(line, cotangent)
-        cot_slots = [cotangent, cot_gather.step(phase)]
+        cot_gather.step(phase)
         w_out_all = lax.all_gather(phase(w_slices), "dp", axis=1).reshape(n_mp * w_out.shape[0], width)
-        project(last, token_slots[last])
+        project(last)
         tokens_all, normed1_all, projected = state
         attn = keep(attend(projected, seg_col, seg_row, heads))
         turn()
@@ -698,48 +732,77 @@
         set_heads = lambda whole, block, index: lax.dynamic_update_slice_in_dim(
             whole, block, index * head_cols, axis=1
         )
+        w_rows = lambda k: lax.dynamic_slice_in_dim(w_out_all, line.slot(k) * head_cols, head_cols, axis=0)
+        half = line.low.astype(jnp.int32)
         attn_all = blank((group, n_mp * head_cols))
-        attn_gather, attn_slots = Gather(line, attn), [attn]
+        cot_all = place(blank((group, width)), phase(cotangent), me)
+
+        def place_near():
+            nonlocal cot_all
+            for j in range(1, n_mp // 2):
+                for came, index in ((cot_gather.left[j], me - j), (cot_gather.right[j], me + j)):
+                    here = (index >= 0) & (index < n_mp) & ((index < n_mp // 2) == line.low)
+                    came = phase(came)
+                    cot_all = place(cot_all, jnp.where(here, came, cotangent), jnp.where(here, index, me))
+            cot_all = keep(phase(cot_all))
+
+        attn_gather = Gather(line, attn)
         for k in slots:
-            attn_slots.append(attn_gather.step(phase))
-            attn_all = keep(set_heads(attn_all, phase(attn_slots[k - 1]), line.slot(k - 1)))
-            if k == 2:
-                cot_all = blank((group, width))
-                for j in range(2):
-                    cot_all = place(cot_all, phase(cot_slots[j]), line.slot(j))
-                keep(cot_all)
+            attn_gather.step(phase)
+            attn_all = keep(set_heads(attn_all, phase(attn_gather.slot(phase, k - 1)), line.slot(k - 1)))
             if k == 1:
+                middle_sum = keep(tokens_all.astype(f32) + bias_pair[0] + dot(phase(attn), w_out))
                 count_here = phase(counts.astype(f32))
                 factor = keep((count_here / sum_over(count_here, "dp", n_dp))[0])
+            if k == 2 and n_mp == 4:
+                place_near()
+                near_rows = lax.dynamic_slice_in_dim(cot_all, (1 - half) * (group // 2), group // 2, axis=0)
+                near_active = keep(dot(near_rows, w_down, 1, 1))
+            if k == last:
+                for j in range(1, last):
+                    middle_sum = keep(middle_sum + dot(phase(attn_gather.slot(phase, j)), w_rows(j)))
             turn()
         reduce_down, reduce2, reduce1 = (Reduce(line, share) for _ in range(3))
         for k in slots[1:]:
-            cot_slots.append(cot_gather.step(phase))
+            cot_gather.step(phase)
             if k == 2:
-                attn_all = set_heads(attn_all, phase(attn_slots[last]), line.slot(last))
+                heads_last = attn_gather.slot(phase, last)
                 middle_all, normed2_all = mix(
-                    tokens_all, attn_all, w_out_all, bias_pair[0], gains[1], shifts[1]
+                    middle_sum, heads_last, w_out_all, line.slot(last), gains[1], shifts[1]
                 )
                 hidden, active = keep(*feed_up(normed2_all, w_up, b_up.astype(f32)))
                 keep(middle_all, normed2_all)
             if k == 3:
+                attn_all = keep(set_heads(attn_all, heads_last, line.slot(last)))
                 reduce_down.terms = keep(dot(phase(active), w_down).astype(bf16))
-            if k > 2:
-                cot_all = keep(place(cot_all, phase(cot_slots[k - 1]), line.slot(k - 1)))
+            if k == max(3, n_mp // 2):
+                if n_mp == 4:
+                    cot_all = keep(place(cot_all, cot_gather.slot(phase, 2), line.slot(2)))
+                    d_hidden_all = keep(slope_back(phase(near_active), hidden, 1 - half))
+                else:
+                    place_near()
+                    d_hidden_all = keep(hidden_back(cot_all, hidden, w_down, 1 - half))
             turn()
 
         reduce_down.step(phase)
-        cot_all = place(cot_all, phase(cot_slots[last]), line.slot(last))
-        d_hidden_all = keep(hidden_back(cot_all, hidden, w_down))
+        if n_mp == 4:
+            edge = (me == 0) | (me == last)
+            came = [phase(side[1], side[3]) for side in (cot_gather.left, cot_gather.right)]
+            block = jnp.where(line.low, jnp.where(edge, came[1][1], came[1][0]), jnp.where(edge, came[0][1], came[0][0]))
+            cot_all = place(cot_all, block, jnp.where(edge, line.slot(3), line.slot(1)))
+        else:
+            for k in slots:
+                cot_all = place(cot_all, cot_gather.slot(phase, k), line.slot(k))
+        d_hidden_all = keep(hidden_back(cot_all, hidden, w_down, half, d_hidden_all))
         reduce2.terms = keep(dot(d_hidden_all, w_up, 1, 1).astype(bf16))
         turn()
         for k in slots:
             reduce2.step(phase)
             if k == 1:
-                feed_full = keep(
-                    weight_grads(factor, [(phase(normed2_all), d_hidden_all), (cot_all, active)])
-                )
+                feed_up_grad = keep(weight_grads(factor, phase(normed2_all), d_hidden_all, 2, 0))
             if k == 2:
+                feed_full = keep(weight_grads(factor, phase(cot_all), active, 2, 1, feed_up_grad))
+            if k == 3:
                 grad_feed = lax.psum_scatter(phase(feed_full), "dp", scatter_dimension=0, tiled=True)
                 split_sums = keep(factor * total(phase(d_hidden_all)))
             turn()
@@ -760,8 +823,8 @@
         keep(*spread_out.fly(phase))
         d_attn = line.stack(phase(*d_attn_blocks))
         grad_proj = keep(attend_back(projected, d_attn, seg_col, seg_row, heads))
-        half = line.low.astype(jnp.int32)
         reduce1.terms = keep(half_product(grad_proj, flat_qkv, half))
+        qkv_full = keep(weight_grads(factor, after(normed1_all, reduce1.terms), grad_proj))
         turn()
         for k in slots:
             reduce1.step(phase)
@@ -769,44 +832,40 @@
                 keep(*spread_out.land(phase))
                 keep(*spread_out.fly(phase))
                 reduce1.terms = keep(half_product(phase(grad_proj), flat_qkv, 1 - half, reduce1.terms))
-                qkv_full = weight_grads(factor, [(after(normed1_all, reduce1.terms), grad_proj)])
-                grad_qkv = lax.psum_scatter(qkv_full, "dp", scatter_dimension=0, tiled=True)
-                keep(qkv_full, grad_feed)
+                gain1 = gain_sums(reduce1.terms, tokens_all)
+                full_sums = keep(factor * jnp.concatenate([gain1, own_sums], axis=0).reshape(-1))
+                grad_qkv = lax.psum_scatter(phase(qkv_full), "dp", scatter_dimension=0, tiled=True)
+                keep(grad_feed)
             if k == 2:
                 out_rows = keep(spread_out.finish(phase))
                 heads_sum = [total(phase(grad_proj)[:, :head_cols]), total(grad_proj[:, 2 * head_cols :])]
-                gain1 = gain_sums(phase(reduce1.terms), tokens_all)
-                full_sums = jnp.concatenate([gain1, own_sums], axis=0).reshape(-1)
-                sums = keep(
-                    jnp.concatenate(
-                        [
-                            sum_over(factor * full_sums, "mp", n_mp),
-                            *[factor * s for s in heads_sum],
-                            split_sums,
-                        ]
-                    )
-                )
+                split_sums = keep(jnp.concatenate([*[factor * s for s in heads_sum], split_sums]))
+                full_sums = phase.early(full_sums)
+                phase.send(full_sums)
+                full_sums = keep(sum_over(full_sums, "mp", n_mp))
             if k == 3:
-                sums = jnp.sum(lax.all_gather(phase(sums).reshape(1, 8, -1), "dp", axis=0, tiled=True), axis=0).reshape(-1)
-                grad_feed = phase(grad_feed).astype(f32)
-                feed_cols = grad_feed.shape[1] // 2
-                grad_up, grad_down = keep(grad_feed[:, :feed_cols], grad_feed[:, feed_cols:].T)
                 keep(grad_qkv)
+                sums = phase(jnp.concatenate([full_sums, split_sums])).reshape(1, 8, -1)
+                sums = keep(lax.all_gather(sums, "dp", axis=0, tiled=True))
                 for _ in slots[3:]:
                     reduce_down.step(phase)
-                down_sum = sum(
-                    value.astype(f32)
-                    for value in (rows_of(phase(reduce_down.terms), me), *reduce_down.came)
-                )
-                layer_out = keep((rows_of(middle_all, me) + down_sum + bias_pair[1]).astype(bf16))
             turn()
         out_blocks = line.shuffle_rows(phase, out_rows.astype(bf16), head_cols)
         grad_input = input_back(
             own, factor, phase(reduce1.terms), reduce1.came, tokens, gains[0], d_middle
         )
+        sums = jnp.sum(sums, axis=0).reshape(-1)
+        grad_feed = phase(grad_feed).astype(f32)
+        feed_cols = grad_feed.shape[1] // 2
+        grad_up, grad_down = grad_feed[:, :feed_cols], grad_feed[:, feed_cols:].T
+        down_sum = sum(
+            value.astype(f32) for value in (rows_of(phase(reduce_down.terms), me), *reduce_down.came)
+        )
+        layer_out = (rows_of(middle_all, me) + down_sum + bias_pair[1]).astype(bf16)
         full_sums = sums[: 6 * width].reshape(6, width)
         split_sums = sums[6 * width :]
         own_block = lax.dynamic_slice_in_dim(out_rows, me * head_cols, head_cols, axis=0)
+        out_blocks = lax.optimization_barrier((*out_blocks, grad_input, layer_out, grad_up, grad_down))[:-4]
         for block in out_blocks:
             own_block = own_block + block.astype(f32)
         grad_out = own_block

time: 662 us -> 632 us (0.955)
  waiting for transfers between devices: 175 us -> 133 us
  matrix products: 63.3 us -> 86.8 us
  Pallas kernels: 154 us -> 136 us
    dot_general x12 -> x16, matrix products: 63.3 us -> 86.8 us  [dot(): lax.dot_general(left, right, (((left_dim,), (right_dim,)), ((), ())), pre...]
    ppermute x9, waiting for transfers between devices: 28.3 us -> 11.6 us  [step(): lax.ppermute(sent[0], line.name, [(j, j + 1) for j in range(k)])]
    ppermute x9, waiting for transfers between devices: 100 us -> 85.5 us  [step(): lax.ppermute(right, line.name, [(j, j - 1) for j in range(1, n - k + 1)])]
    pallas_call x4 -> x6, Pallas kernels: 73.2 us -> 60.2 us  [the longest x3 40.7 us: weight_grads(): pl.pallas_call(grads_kernel, grid=(steps,), in_specs=[pl.BlockSpec(memory...]
    unnamed x175 -> x187, local copies, waits for them, and re-layouts: 40.4 us -> 49.8 us
    ppermute x3, waiting for transfers between devices: 8.22 us -> 0.01 us  [shuffle_rows(): lax.ppermute(block, self.name, [(j, (j + shift) % n) for j in range(n)])]
    dynamic_update_slice x4 -> x8, other arithmetic: 7.61 us -> 13.4 us  [body(): lax.dynamic_update_slice_in_dim(whole, block, index * share, axis=0)]
  transfers between devices with their start and end apart: 56 -> 56, of which waited for: 25 -> 22; matrix products, arithmetic and copies ran while one was open for 21% -> 25% of each run, Pallas kernels for 23% -> 20%
where the time goes in v3:
time: 632 us; the launch traced here: 622 us
  Pallas kernels  136 us (22%)
  waiting for transfers between devices  133 us (21%)
  starting transfers between devices  111 us (18%)
  matrix products  86.8 us (14%)
  local copies, waits for them, and re-layouts  73.4 us (12%)
  other arithmetic  50.9 us (8%)
  between operations  18.3 us (3%)
  blocking collectives  12.9 us (2%)
    dot_general x16, matrix products, dot(): lax.dot_general(left, right, (((left_dim,), (right_dim,)), ((), ())), pre...  86.8 us
    ppermute x9, waiting for transfers between devices, step(): lax.ppermute(right, line.name, [(j, j - 1) for j in range(1, n - k + 1)])  85.5 us
    unnamed x187, local copies, waits for them, and re-layouts  49.8 us
    pallas_call x3, Pallas kernels, weight_grads(): pl.pallas_call(grads_kernel, grid=(steps,), in_specs=[pl.BlockSpec(memory...  40.7 us
    ppermute x9, starting transfers between devices, step(): lax.ppermute(sent[0], line.name, [(j, j + 1) for j in range(k)])  37.4 us
    ppermute x10, waiting for transfers between devices, flip(): return lax.ppermute(value, name, [(j, j ^ bit) for j in range(size)])  24.8 us
    ppermute x9, starting transfers between devices, step(): lax.ppermute(left, line.name, [(j, j + 1) for j in range(k - 1, n - 1)])  18.7 us
    ppermute x10, starting transfers between devices, flip(): return lax.ppermute(value, name, [(j, j ^ bit) for j in range(size)])  18.6 us
  transfers between devices with their start and end apart: 56, of which 22 were waited for; matrix products, arithmetic and copies ran while one was open for 25% of the time, Pallas kernels for 20%

profile of v3, /device:TPU:0, one launch (start us, length us, event | category | flops | bytes accessed | tf_op | source)
XLA Modules:
  0.0 622.4 jit_solution(14226067904022325234)
XLA Ops:
  7.2 6.0 collective-permute-start
  16.5 5.7 slice_bitcast_fusion.3
  25.1 5.1 fusion.1
  30.1 4.9 collective-permute-done
  35.0 5.1 collective-permute-done.1
  47.7 2.7 fusion.3
  50.4 35.5 %collective-permute-done.3 = bf16[256,2048]{1,0:T(8,128)(2,1)} collective-permute-done((bf16[256,2048]{1,0:T(8,128)(2,1)}, bf16[256,2048]{1,0:T(8,128)(2,1)}, u32[]{:S(2)}, u32[]{:S(2)}) %collective-permute-start.3) | collective-permute-done | bytes 1048608 | tf_op jit(solution)/shard_map/ppermute | solution.py:539
  93.1 2.7 fusion.5
  95.9 16.1 %collective-permute-done.5 = bf16[256,2048]{1,0:T(8,128)(2,1)} collective-permute-done((bf16[256,2048]{1,0:T(8,128)(2,1)}, bf16[256,2048]{1,0:T(8,128)(2,1)}, u32[]{:S(2)}, u32[]{:S(2)}) %collective-permute-start.5) | collective-permute-done | bytes 1048608 | tf_op jit(solution)/shard_map/ppermute | solution.py:539
  123.1 2.8 fusion.7.q_ref.k_ref.v_ref
  125.9 9.1 %attend.1 = bf16[1024,512]{1,0:T(8,128)(2,1)S(1)} custom-call(bf16[1024,1536]{1,0:T(8,128)(2,1)} %fusion.7.q_ref.k_ref.v_ref, bf16[1024,1536]{1,0:T(8,128)(2,1)} %fusion.7.q_ref.k_ref.v_ref, bf16[1024,1536]{1,0:T(8,128)(2,1)} %fusion.7.q_ref.k_ref.v_ref, s32[1024,1]{1,0:T(8,128)S(1)} %copy-done.34, s32[1,1024]{1,0:T(1,128)S(1)} %bitcast.63), custom_call_target="tpu_custom_call" | custom-call | flops 1048576 | bytes 65536 | tf_op jit(solution)/shard_map/attend/pallas_call | solution.py:49
  136.6 3.9 collective-permute-done.7
  145.3 5.8 add_add_fusion
  151.8 2.9 collective-permute-start.11
  156.0 3.0 collective-permute-start.12
  160.2 3.9 collective-permute-done.9
  171.4 6.1 fusion.34.grad_ref
  177.5 12.6 %collective-permute-done.14 = bf16[1024,512]{1,0:T(8,128)(2,1)} collective-permute-done((bf16[1024,512]{1,0:T(8,128)(2,1)S(1)}, bf16[1024,512]{1,0:T(8,128)(2,1)}, u32[]{:S(2)}, u32[]{:S(2)}) %collective-permute-start.14) | collective-permute-done | bytes 1048608 | tf_op jit(solution)/shard_map/ppermute | solution.py:539
  196.3 6.4 %convolution_add_fusion.1 = f32[1024,2048]{1,0:T(8,128)S(1)} fusion(f32[1024,2048]{1,0:T(8,128)} %add_add_fusion, bf16[1024,512]{1,0:T(8,128)(2,1)S(1)} %broadcast_select_fusion, bf16[2048,2048]{1,0:T(8,128)(2,1)} %bitcast.66, s32[]{:T(128)S(6)} %select_n.415), kind=kOutput, calls=%fused_computation.5 | convolution fusion | flops 2149580800 | bytes 19922948 | tf_op jit(solution)/shard_map/dot_general | solution.py:20
  202.7 7.3 %convolution_add_fusion.sum_ref = f32[1024,2048]{1,0:T(8,128)} fusion(f32[1024,2048]{1,0:T(8,128)S(1)} %convolution_add_fusion.1, bf16[1024,512]{1,0:T(8,128)(2,1)S(1)} %select_select_fusion.1, bf16[2048,2048]{1,0:T(8,128)(2,1)} %bitcast.67, s32[]{:T(128)S(6)} %select_n.432), kind=kOutput, calls=%fused_computation.4 | convolution fusion | flops 2149580800 | bytes 19922948 | tf_op jit(solution)/shard_map/dot_general | solution.py:20
  210.0 5.3 collective-permute-done.16
  217.5 3.1 constant_dynamic-update-slice_fusion.4
  220.6 9.5 %mix.1 = (f32[1024,2048]{1,0:T(8,128)}, bf16[1024,2048]{1,0:T(8,128)(2,1)S(1)}) custom-call(s32[1]{0:T(128)} %bitcast.index_ref, f32[1024,2048]{1,0:T(8,128)} %convolution_add_fusion.sum_ref, bf16[1024,512]{1,0:T(8,128)(2,1)S(1)} %get-tuple-element.309.heads_ref, bf16[2048,2048]{1,0:T(8,128)(2,1)} %bitcast.68, f32[1,2048]{1,0:T(1,128)S(1)} %get-tuple-element.363.gain_ref, ...), custom_call_target="tpu_custom_call" | custom-call | flops 1048576 | bytes 65536 | tf_op jit(solution)/shard_map/mix/pallas_call | solution.py:151
  232.1 15.6 %feed_up.1 = (f32[1024,2048]{1,0:T(8,128)}, bf16[1024,2048]{1,0:T(8,128)(2,1)S(1)}) custom-call(bf16[1024,2048]{1,0:T(8,128)(2,1)} %copy-done.31, bf16[2048,2048]{1,0:T(8,128)(2,1)} %w_ref.2, f32[1,2048]{1,0:T(1,128)S(1)} %bitcast.65), custom_call_target="tpu_custom_call" | custom-call | flops 1048576 | bytes 65536 | tf_op jit(solution)/shard_map/feed_up/pallas_call | solution.py:180
  252.6 12.6 %convolution_convert_fusion.1.right_ref.left_ref = bf16[1024,2048]{1,0:T(8,128)(2,1)S(1)} fusion(bf16[1024,2048]{1,0:T(8,128)(2,1)} %copy-done.38, bf16[2048,2048]{1,0:T(8,128)(2,1)} %w_ref.3), kind=kOutput, calls=%fused_computation.7 | convolution fusion | flops 8592031744 | bytes 16777216 | tf_op jit(solution)/shard_map/dot_general | solution.py:20
  265.3 2.7 slope_back.1.refs_0_
  271.0 3.1 collective-permute-done.20
  281.7 7.3 %hidden_back.1.right_ref = bf16[1024,2048]{1,0:T(8,128)(2,1)S(1)} custom-call(s32[1]{0:T(128)} %bitcast.16.index_ref, bf16[1024,2048]{1,0:T(8,128)(2,1)S(1)} %select_dynamic-update-slice_fusion.cot_ref.left_ref, f32[1024,2048]{1,0:T(8,128)S(1)} %copy-done.24, bf16[2048,2048]{1,0:T(8,128)(2,1)S(1)} %bitcast.53, ...), custom_call_target="tpu_custom_call", output_to_operand_aliasing={{}: (4, {})} | custom-call | flops 1048576 | bytes 65536 | tf_op jit(solution)/shard_map/hidden_back/pallas_call | solution.py:205
  289.1 13.0 %convolution_convert_fusion.right_ref.left_ref.term_ref = bf16[1024,2048]{1,0:T(8,128)(2,1)S(1)} fusion(bf16[1024,2048]{1,0:T(8,128)(2,1)S(1)} %hidden_back.1.right_ref, bf16[2048,2048]{1,0:T(8,128)(2,1)} %w_ref.2), kind=kOutput, calls=%fused_computation.6 | convolution fusion | flops 8592031744 | bytes 16777216 | tf_op jit(solution)/shard_map/dot_general | solution.py:20
  309.7 14.2 %weight_grads.3.refs_0_ = bf16[2048,4096]{1,0:T(8,128)(2,1)} custom-call(f32[1]{0:T(128)} %div.35.factor_ref, bf16[1024,2048]{1,0:T(8,128)(2,1)S(1)} %copy-done.32, bf16[1024,2048]{1,0:T(8,128)(2,1)} %copy-done.16), custom_call_target="tpu_custom_call" | custom-call | flops 1048576 | bytes 65536 | tf_op jit(solution)/shard_map/weight_grads/pallas_call | solution.py:265
  326.8 4.3 collective-permute-start.25
  334.1 14.0 %weight_grads.4 = bf16[2048,4096]{1,0:T(8,128)(2,1)} custom-call(f32[1]{0:T(128)} %div.35.factor_ref, bf16[1024,2048]{1,0:T(8,128)(2,1)S(1)} %copy-done.23, bf16[1024,2048]{1,0:T(8,128)(2,1)} %copy-done.38, bf16[2048,4096]{1,0:T(8,128)(2,1)} %weight_grads.3.refs_0_), custom_call_target="tpu_custom_call", output_to_operand_aliasing={{}: (3, {})} | custom-call | flops 1048576 | bytes 65536 | tf_op jit(solution)/shard_map/weight_grads/pallas_call | solution.py:265
  353.2 7.8 %collective-permute-start.27 = (bf16[256,2048]{1,0:T(8,128)(2,1)}, bf16[256,2048]{1,0:T(8,128)(2,1)S(1)}, u32[]{:S(2)}, u32[]{:S(2)}) collective-permute-start(bf16[256,2048]{1,0:T(8,128)(2,1)} %get-tuple-element.220), channel_id=1, source_target_pairs={{0,1},{1,2},{2,3},{4,5},{5,6},{6,7},{8,9},{9,10},{10,11},{12,13},{... | collective-permute-start | bytes 3145736 | tf_op jit(solution)/shard_map/ppermute | solution.py:570
  362.5 3.6 convert_reduce_fusion
  366.1 10.7 %collective-permute-done.27.left_ref = bf16[256,2048]{1,0:T(8,128)(2,1)S(1)} collective-permute-done((bf16[256,2048]{1,0:T(8,128)(2,1)}, bf16[256,2048]{1,0:T(8,128)(2,1)S(1)}, u32[]{:S(2)}, u32[]{:S(2)}) %collective-permute-start.27) | collective-permute-done | bytes 1048608 | tf_op jit(solution)/shard_map/ppermute | solution.py:570
  376.8 4.1 collective-permute-done.28.right_ref
  388.0 3.4 copy-done.33
  391.4 3.0 middle_back.1
  395.7 6.4 %convolution_convert_fusion.2 = bf16[256,2048]{1,0:T(8,128)(2,1)S(1)} fusion(bf16[256,2048]{1,0:T(8,128)(2,1)S(1)} %get-tuple-element.234, bf16[2048,2048]{1,0:T(8,128)(2,1)} %bitcast.69), kind=kOutput, calls=%fused_computation.28 | convolution fusion | flops 2148007936 | bytes 10485760 | tf_op jit(solution)/shard_map/dot_general | solution.py:20
  402.2 4.5 multiply_convert_fusion
  411.5 2.8 collective-permute-start.33
  417.9 2.5 add_convert_fusion.5
  420.4 2.6 add_convert_fusion.3
  423.0 3.1 add_convert_fusion.6
  426.1 3.2 add_convert_fusion.4
  434.1 9.6 %collective-permute-start.35 = (bf16[256,2048]{1,0:T(8,128)(2,1)}, bf16[256,2048]{1,0:T(8,128)(2,1)}, u32[]{:S(2)}, u32[]{:S(2)}) collective-permute-start(bf16[256,2048]{1,0:T(8,128)(2,1)} %get-tuple-element.237), channel_id=1, source_target_pairs={{0,1},{1,2},{2,3},{4,5},{5,6},{6,7},{8,9},{9,10},{10,11},{12,13},{... | collective-permute-start | bytes 3145736 | tf_op jit(solution)/shard_map/ppermute | solution.py:570
  448.0 16.4 %attend_back.1.x_ref.right_ref = bf16[1024,1536]{1,0:T(8,128)(2,1)S(1)} custom-call(bf16[1024,1536]{1,0:T(8,128)(2,1)} %fusion.7.q_ref.k_ref.v_ref, bf16[1024,1536]{1,0:T(8,128)(2,1)} %fusion.7.q_ref.k_ref.v_ref, bf16[1024,1536]{1,0:T(8,128)(2,1)} %fusion.7.q_ref.k_ref.v_ref, bf16[1024,512]{1,0:T(8,128)(2,1)S(1)} %constant_dynamic-update-slice_fusion.grad_ref, ...), custom_call_target="tpu_custom_call" | custom-call | flops 1048576 | bytes 65536 | tf_op jit(solution)/shard_map/attend_back/pallas_call | solution.py:94
  464.5 4.2 half_product.2.right_ref.left_ref.refs_0_
  470.6 12.5 %weight_grads.5 = bf16[2048,1536]{1,0:T(8,128)(2,1)} custom-call(f32[1]{0:T(128)} %div.35.factor_ref, bf16[1024,2048]{1,0:T(8,128)(2,1)} %get-tuple-element.245.left_ref, bf16[1024,1536]{1,0:T(8,128)(2,1)S(1)} %attend_back.1.x_ref.right_ref), custom_call_target="tpu_custom_call" | custom-call | flops 1048576 | bytes 65536 | tf_op jit(solution)/shard_map/weight_grads/pallas_call | solution.py:265
  483.1 7.0 %collective-permute-done.37 = bf16[1024,512]{1,0:T(8,128)(2,1)} collective-permute-done((bf16[1024,512]{1,0:T(8,128)(2,1)}, bf16[1024,512]{1,0:T(8,128)(2,1)}, u32[]{:S(2)}, u32[]{:S(2)}) %collective-permute-start.37) | collective-permute-done | bytes 1048608 | tf_op jit(solution)/shard_map/ppermute | solution.py:578
  500.5 3.6 collective-permute-start.39
  507.9 2.8 copy-done.4
  510.7 3.5 copy-done.18
  514.2 4.2 half_product.3.term_ref.right_ref.left_ref
  518.4 4.2 gain_sums.1
  527.5 3.8 collective-permute-start.43
  538.2 10.7 %collective-permute-done.45 = f32[12288]{0:T(1024)S(1)} collective-permute-done((f32[12288]{0:T(1024)S(1)}, f32[12288]{0:T(1024)S(1)}, u32[]{:S(2)}, u32[]{:S(2)}) %collective-permute-start.45) | collective-permute-done | bytes 49184 | tf_op jit(solution)/shard_map/ppermute | solution.py:578
  548.9 5.1 collective-permute-start.46
  561.6 12.9 %all_gather.19 = f32[8,8,1920]{2,1,0:T(8,128)} all-gather(f32[1,8,1920]{2,1,0:T(8,128)S(1)} %reshape.101), channel_id=1, replica_groups=mesh['dp'=8,'mp'=4] {'dp'}, dimensions={0}, use_global_device_ids=true | all-gather | bytes 552960 | tf_op jit(solution)/shard_map/all_gather | solution.py:849
  583.3 4.5 collective-permute-start.49
  589.3 2.9 collective-permute-start.51
  594.1 4.1 add_convert_fusion
  601.0 3.0 copy.33
  608.7 2.8 input_back.1
  (380 shorter events, 176.5 us)
Async XLA Ops:
  7.2 17.1 %copy-start = (bf16[512,2048]{1,0:T(8,128)(2,1)S(1)}, bf16[512,2048]{1,0:T(8,128)(2,1)}, u32[]{:S(2)}) copy-start(bf16[512,2048]{1,0:T(8,128)(2,1)} %param.21) | copy-start | bytes 6291460
  7.2 104.8 %all-gather.5.cloned.1.call-start = ((), (), s32[]{:S(2)}) async-start(), calls=%async_computation.4 | async-start | bytes 1310720 | tf_op jit(solution)/shard_map/all_gather | solution.py:721
  7.2 27.8 %collective-permute-start = (bf16[256,2048]{1,0:T(8,128)(2,1)}, bf16[256,2048]{1,0:T(8,128)(2,1)}, u32[]{:S(2)}, u32[]{:S(2)}) collective-permute-start(bf16[256,2048]{1,0:T(8,128)(2,1)} %value_ref.1), channel_id=1, source_target_pairs={{0,1},{1,2},{2,3},{4,5},{5,6},{6,7},{8,9},{9,10},{10,11},{12,13},{... | collective-permute-start | bytes 3145736 | tf_op jit(solution)/shard_map/ppermute | solution.py:538
  13.3 26.8 %collective-permute-start.1 = (bf16[256,2048]{1,0:T(8,128)(2,1)}, bf16[256,2048]{1,0:T(8,128)(2,1)}, u32[]{:S(2)}, u32[]{:S(2)}) collective-permute-start(bf16[256,2048]{1,0:T(8,128)(2,1)} %value_ref.1), channel_id=1, source_target_pairs={{1,0},{2,1},{3,2},{5,4},{6,5},{7,6},{9,8},{10,9},{11,10},{13,12},{... | collective-permute-start | bytes 3145736 | tf_op jit(solution)/shard_map/ppermute | solution.py:539
  40.1 10.3 %collective-permute-start.2 = (bf16[256,2048]{1,0:T(8,128)(2,1)}, bf16[256,2048]{1,0:T(8,128)(2,1)}, u32[]{:S(2)}, u32[]{:S(2)}) collective-permute-start(bf16[256,2048]{1,0:T(8,128)(2,1)} %collective-permute-done), channel_id=1, source_target_pairs={{1,2},{2,3},{5,6},{6,7},{9,10},{10,11},{13,14},{14,15},{17,18},{18... | collective-permute-start | bytes 3145736 | tf_op jit(solution)/shard_map/ppermute | solution.py:538
  41.7 44.2 %collective-permute-start.3 = (bf16[256,2048]{1,0:T(8,128)(2,1)}, bf16[256,2048]{1,0:T(8,128)(2,1)}, u32[]{:S(2)}, u32[]{:S(2)}) collective-permute-start(bf16[256,2048]{1,0:T(8,128)(2,1)} %collective-permute-done.1), channel_id=1, source_target_pairs={{1,0},{2,1},{5,4},{6,5},{9,8},{10,9},{13,12},{14,13},{17,16},{18,1... | collective-permute-start | bytes 3145736 | tf_op jit(solution)/shard_map/ppermute | solution.py:539
  43.1 153.3 %all-gather.7.cloned.1.call-start = ((), (), s32[]{:S(2)}) async-start(), calls=%async_computation.5 | async-start | bytes 9437184 | tf_op jit(solution)/shard_map/all_gather | solution.py:726
  85.9 10.0 %collective-permute-start.4 = (bf16[256,2048]{1,0:T(8,128)(2,1)}, bf16[256,2048]{1,0:T(8,128)(2,1)}, u32[]{:S(2)}, u32[]{:S(2)}) collective-permute-start(bf16[256,2048]{1,0:T(8,128)(2,1)} %collective-permute-done.2), channel_id=1, source_target_pairs={{2,3},{6,7},{10,11},{14,15},{18,19},{22,23},{26,27},{30,31}} | collective-permute-start | bytes 3145736 | tf_op jit(solution)/shard_map/ppermute | solution.py:538
  87.6 24.3 %collective-permute-start.5 = (bf16[256,2048]{1,0:T(8,128)(2,1)}, bf16[256,2048]{1,0:T(8,128)(2,1)}, u32[]{:S(2)}, u32[]{:S(2)}) collective-permute-start(bf16[256,2048]{1,0:T(8,128)(2,1)} %collective-permute-done.3), channel_id=1, source_target_pairs={{1,0},{5,4},{9,8},{13,12},{17,16},{21,20},{25,24},{29,28}} | collective-permute-start | bytes 3145736 | tf_op jit(solution)/shard_map/ppermute | solution.py:539
  112.0 410.7 %reduce-scatter.3.cloned.1.call-start = ((), (), s32[]{:S(2)}) async-start(), calls=%async_computation.2 | async-start | bytes 18874368 | tf_op jit(solution)/shard_map/reduce_scatter | solution.py:806
  115.1 21.5 %collective-permute-start.6 = (bf16[256,2048]{1,0:T(8,128)(2,1)S(1)}, bf16[256,2048]{1,0:T(8,128)(2,1)}, u32[]{:S(2)}, u32[]{:S(2)}) collective-permute-start(bf16[256,2048]{1,0:T(8,128)(2,1)S(1)} %copy-done.25), channel_id=1, source_target_pairs={{0,1},{1,2},{2,3},{4,5},{5,6},{6,7},{8,9},{9,10},{10,11},{12,13},{... | collective-permute-start | bytes 3145736 | tf_op jit(solution)/shard_map/ppermute | solution.py:538
  117.5 23.0 %collective-permute-start.7 = (bf16[256,2048]{1,0:T(8,128)(2,1)S(1)}, bf16[256,2048]{1,0:T(8,128)(2,1)}, u32[]{:S(2)}, u32[]{:S(2)}) collective-permute-start(bf16[256,2048]{1,0:T(8,128)(2,1)S(1)} %copy-done.25), channel_id=1, source_target_pairs={{1,0},{2,1},{3,2},{5,4},{6,5},{7,6},{9,8},{10,9},{11,10},{13,12},{... | collective-permute-start | bytes 3145736 | tf_op jit(solution)/shard_map/ppermute | solution.py:539
  140.5 19.7 %collective-permute-start.8 = (bf16[1024,512]{1,0:T(8,128)(2,1)S(1)}, bf16[1024,512]{1,0:T(8,128)(2,1)S(1)}, u32[]{:S(2)}, u32[]{:S(2)}) collective-permute-start(bf16[1024,512]{1,0:T(8,128)(2,1)S(1)} %attend.1), channel_id=1, source_target_pairs={{0,1},{1,2},{2,3},{4,5},{5,6},{6,7},{8,9},{9,10},{10,11},{12,13},{... | collective-permute-start | bytes 3145736 | tf_op jit(solution)/shard_map/ppermute | solution.py:538
  141.9 22.2 %collective-permute-start.9 = (bf16[1024,512]{1,0:T(8,128)(2,1)S(1)}, bf16[1024,512]{1,0:T(8,128)(2,1)S(1)}, u32[]{:S(2)}, u32[]{:S(2)}) collective-permute-start(bf16[1024,512]{1,0:T(8,128)(2,1)S(1)} %attend.1), channel_id=1, source_target_pairs={{1,0},{2,1},{3,2},{5,4},{6,5},{7,6},{9,8},{10,9},{11,10},{13,12},{... | collective-permute-start | bytes 3145736 | tf_op jit(solution)/shard_map/ppermute | solution.py:539
  143.2 7.9 %collective-permute-start.10 = (f32[1]{0:T(128)}, f32[1]{0:T(128)}, u32[]{:S(2)}, u32[]{:S(2)}) collective-permute-start(f32[1]{0:T(128)} %convert_element_type.186), channel_id=1, source_target_pairs={{0,4},{4,0},{8,12},{12,8},{16,20},{20,16},{24,28},{28,24},{1,5},{5... | collective-permute-start | bytes 20 | tf_op jit(solution)/shard_map/ppermute | solution.py:578
  144.1 27.3 %slice-start = ((s8[8388608]{0:T(1024)(128)(4,1)}), s8[4194304]{0:T(1024)(128)(4,1)S(1)}, s32[]{:S(2)}) async-start(s8[8388608]{0:T(1024)(128)(4,1)} %bitcast.50), calls=%async_computation.6 | async-start | bytes 8388608
  145.3 26.1 %slice-start.1 = ((s8[8388608]{0:T(1024)(128)(4,1)}), s8[4194304]{0:T(1024)(128)(4,1)S(1)}, s32[]{:S(2)}) async-start(s8[8388608]{0:T(1024)(128)(4,1)} %bitcast.50), calls=%async_computation.7 | async-start | bytes 8388608
  151.8 3.6 collective-permute-start.11
  156.0 3.6 collective-permute-start.12
  164.1 13.4 %collective-permute-start.13 = (bf16[1024,512]{1,0:T(8,128)(2,1)S(1)}, bf16[1024,512]{1,0:T(8,128)(2,1)}, u32[]{:S(2)}, u32[]{:S(2)}) collective-permute-start(bf16[1024,512]{1,0:T(8,128)(2,1)S(1)} %collective-permute-done.8), channel_id=1, source_target_pairs={{1,2},{2,3},{5,6},{6,7},{9,10},{10,11},{13,14},{14,15},{17,18},{18... | collective-permute-start | bytes 3145736 | tf_op jit(solution)/shard_map/ppermute | solution.py:538
  165.8 24.3 %collective-permute-start.14 = (bf16[1024,512]{1,0:T(8,128)(2,1)S(1)}, bf16[1024,512]{1,0:T(8,128)(2,1)}, u32[]{:S(2)}, u32[]{:S(2)}) collective-permute-start(bf16[1024,512]{1,0:T(8,128)(2,1)S(1)} %collective-permute-done.9), channel_id=1, source_target_pairs={{1,0},{2,1},{5,4},{6,5},{9,8},{10,9},{13,12},{14,13},{17,16},{18,1... | collective-permute-start | bytes 3145736 | tf_op jit(solution)/shard_map/ppermute | solution.py:539
  190.1 19.9 %collective-permute-start.15 = (bf16[1024,512]{1,0:T(8,128)(2,1)}, bf16[1024,512]{1,0:T(8,128)(2,1)}, u32[]{:S(2)}, u32[]{:S(2)}) collective-permute-start(bf16[1024,512]{1,0:T(8,128)(2,1)} %collective-permute-done.13), channel_id=1, source_target_pairs={{2,3},{6,7},{10,11},{14,15},{18,19},{22,23},{26,27},{30,31}} | collective-permute-start | bytes 3145736 | tf_op jit(solution)/shard_map/ppermute | solution.py:538
  191.7 23.6 %collective-permute-start.16 = (bf16[1024,512]{1,0:T(8,128)(2,1)}, bf16[1024,512]{1,0:T(8,128)(2,1)}, u32[]{:S(2)}, u32[]{:S(2)}) collective-permute-start(bf16[1024,512]{1,0:T(8,128)(2,1)} %collective-permute-done.14), channel_id=1, source_target_pairs={{1,0},{5,4},{9,8},{13,12},{17,16},{21,20},{25,24},{29,28}} | collective-permute-start | bytes 3145736 | tf_op jit(solution)/shard_map/ppermute | solution.py:539
  215.3 34.4 %collective-permute-start.17 = (bf16[256,2048]{1,0:T(8,128)(2,1)}, bf16[256,2048]{1,0:T(8,128)(2,1)S(1)}, u32[]{:S(2)}, u32[]{:S(2)}) collective-permute-start(bf16[256,2048]{1,0:T(8,128)(2,1)} %collective-permute-done.6), channel_id=1, source_target_pairs={{1,2},{2,3},{5,6},{6,7},{9,10},{10,11},{13,14},{14,15},{17,18},{18... | collective-permute-start | bytes 3145736 | tf_op jit(solution)/shard_map/ppermute | solution.py:538
  216.1 33.7 %collective-permute-start.18 = (bf16[256,2048]{1,0:T(8,128)(2,1)}, bf16[256,2048]{1,0:T(8,128)(2,1)}, u32[]{:S(2)}, u32[]{:S(2)}) collective-permute-start(bf16[256,2048]{1,0:T(8,128)(2,1)} %collective-permute-done.7), channel_id=1, source_target_pairs={{1,0},{2,1},{5,4},{6,5},{9,8},{10,9},{13,12},{14,13},{17,16},{18,1... | collective-permute-start | bytes 3145736 | tf_op jit(solution)/shard_map/ppermute | solution.py:539
  249.7 21.2 %collective-permute-start.19 = (bf16[256,2048]{1,0:T(8,128)(2,1)S(1)}, bf16[256,2048]{1,0:T(8,128)(2,1)}, u32[]{:S(2)}, u32[]{:S(2)}) collective-permute-start(bf16[256,2048]{1,0:T(8,128)(2,1)S(1)} %collective-permute-done.17), channel_id=1, source_target_pairs={{2,3},{6,7},{10,11},{14,15},{18,19},{22,23},{26,27},{30,31}} | collective-permute-start | bytes 3145736 | tf_op jit(solution)/shard_map/ppermute | solution.py:538
  251.3 22.7 %collective-permute-start.20 = (bf16[256,2048]{1,0:T(8,128)(2,1)}, bf16[256,2048]{1,0:T(8,128)(2,1)}, u32[]{:S(2)}, u32[]{:S(2)}) collective-permute-start(bf16[256,2048]{1,0:T(8,128)(2,1)} %collective-permute-done.18), channel_id=1, source_target_pairs={{1,0},{5,4},{9,8},{13,12},{17,16},{21,20},{25,24},{29,28}} | collective-permute-start | bytes 3145736 | tf_op jit(solution)/shard_map/ppermute | solution.py:539
  265.3 16.4 %slice-start.2 = ((s8[8388608]{0:T(1024)(128)(4,1)}), s8[4194304]{0:T(1024)(128)(4,1)S(1)}, s32[]{:S(2)}) async-start(s8[8388608]{0:T(1024)(128)(4,1)} %bitcast.52), calls=%async_computation.8 | async-start | bytes 8388608
  276.0 26.1 %collective-permute-start.21 = (bf16[256,2048]{1,0:T(8,128)(2,1)}, bf16[256,2048]{1,0:T(8,128)(2,1)S(1)}, u32[]{:S(2)}, u32[]{:S(2)}) collective-permute-start(bf16[256,2048]{1,0:T(8,128)(2,1)} %get-tuple-element.205), channel_id=1, source_target_pairs={{0,1},{4,5},{8,9},{12,13},{16,17},{20,21},{24,25},{28,29}} | collective-permute-start | bytes 3145736 | tf_op jit(solution)/shard_map/ppermute | solution.py:570
  278.5 23.6 %collective-permute-start.22 = (bf16[256,2048]{1,0:T(8,128)(2,1)}, bf16[256,2048]{1,0:T(8,128)(2,1)S(1)}, u32[]{:S(2)}, u32[]{:S(2)}) collective-permute-start(bf16[256,2048]{1,0:T(8,128)(2,1)} %get-tuple-element.206), channel_id=1, source_target_pairs={{3,2},{7,6},{11,10},{15,14},{19,18},{23,22},{27,26},{31,30}} | collective-permute-start | bytes 3145736 | tf_op jit(solution)/shard_map/ppermute | solution.py:571
  305.4 19.3 %collective-permute-start.23 = (bf16[256,2048]{1,0:T(8,128)(2,1)}, bf16[256,2048]{1,0:T(8,128)(2,1)S(1)}, u32[]{:S(2)}, u32[]{:S(2)}) collective-permute-start(bf16[256,2048]{1,0:T(8,128)(2,1)} %get-tuple-element.212), channel_id=1, source_target_pairs={{0,1},{4,5},{8,9},{12,13},{16,17},{20,21},{24,25},{28,29}} | collective-permute-start | bytes 3145736 | tf_op jit(solution)/shard_map/ppermute | solution.py:570
  306.7 18.0 %collective-permute-start.24 = (bf16[256,2048]{1,0:T(8,128)(2,1)}, bf16[256,2048]{1,0:T(8,128)(2,1)S(1)}, u32[]{:S(2)}, u32[]{:S(2)}) collective-permute-start(bf16[256,2048]{1,0:T(8,128)(2,1)} %get-tuple-element.213), channel_id=1, source_target_pairs={{3,2},{7,6},{11,10},{15,14},{19,18},{23,22},{27,26},{31,30}} | collective-permute-start | bytes 3145736 | tf_op jit(solution)/shard_map/ppermute | solution.py:571
  326.8 21.4 %collective-permute-start.25 = (bf16[256,2048]{1,0:T(8,128)(2,1)}, bf16[256,2048]{1,0:T(8,128)(2,1)S(1)}, u32[]{:S(2)}, u32[]{:S(2)}) collective-permute-start(bf16[256,2048]{1,0:T(8,128)(2,1)} %get-tuple-element.216), channel_id=1, source_target_pairs={{0,1},{1,2},{4,5},{5,6},{8,9},{9,10},{12,13},{13,14},{16,17},{17,1... | collective-permute-start | bytes 3145736 | tf_op jit(solution)/shard_map/ppermute | solution.py:570
  331.1 17.1 %collective-permute-start.26 = (bf16[256,2048]{1,0:T(8,128)(2,1)}, bf16[256,2048]{1,0:T(8,128)(2,1)S(1)}, u32[]{:S(2)}, u32[]{:S(2)}) collective-permute-start(bf16[256,2048]{1,0:T(8,128)(2,1)} %get-tuple-element.217), channel_id=1, source_target_pairs={{2,1},{3,2},{6,5},{7,6},{10,9},{11,10},{14,13},{15,14},{18,17},{19... | collective-permute-start | bytes 3145736 | tf_op jit(solution)/shard_map/ppermute | solution.py:571
  353.1 225.6 %reduce-scatter.5.cloned.1.call-start = ((), (), s32[]{:S(2)}) async-start(), calls=%async_computation.3 | async-start | bytes 7077888 | tf_op jit(solution)/shard_map/reduce_scatter | solution.py:837
  353.2 23.7 %collective-permute-start.27 = (bf16[256,2048]{1,0:T(8,128)(2,1)}, bf16[256,2048]{1,0:T(8,128)(2,1)S(1)}, u32[]{:S(2)}, u32[]{:S(2)}) collective-permute-start(bf16[256,2048]{1,0:T(8,128)(2,1)} %get-tuple-element.220), channel_id=1, source_target_pairs={{0,1},{1,2},{2,3},{4,5},{5,6},{6,7},{8,9},{9,10},{10,11},{12,13},{... | collective-permute-start | bytes 3145736 | tf_op jit(solution)/shard_map/ppermute | solution.py:570
  361.0 19.9 %collective-permute-start.28 = (bf16[256,2048]{1,0:T(8,128)(2,1)}, bf16[256,2048]{1,0:T(8,128)(2,1)S(1)}, u32[]{:S(2)}, u32[]{:S(2)}) collective-permute-start(bf16[256,2048]{1,0:T(8,128)(2,1)} %copy-done.56), channel_id=1, source_target_pairs={{1,0},{2,1},{3,2},{5,4},{6,5},{7,6},{9,8},{10,9},{11,10},{13,12},{... | collective-permute-start | bytes 3145736 | tf_op jit(solution)/shard_map/ppermute | solution.py:571
  362.5 18.4 %copy-start.14 = (bf16[1024,2048]{1,0:T(8,128)(2,1)S(1)}, bf16[1024,2048]{1,0:T(8,128)(2,1)}, u32[]{:S(2)}) copy-start(bf16[1024,2048]{1,0:T(8,128)(2,1)} %copy-done.13) | copy-start | bytes 12582916
  384.7 22.0 %collective-permute-start.29 = (bf16[256,2048]{1,0:T(8,128)(2,1)S(1)}, bf16[256,2048]{1,0:T(8,128)(2,1)S(1)}, u32[]{:S(2)}, u32[]{:S(2)}) collective-permute-start(bf16[256,2048]{1,0:T(8,128)(2,1)S(1)} %get-tuple-element.224), channel_id=1, source_target_pairs={{0,1},{1,2},{4,5},{5,6},{8,9},{9,10},{12,13},{13,14},{16,17},{17,1... | collective-permute-start | bytes 3145736 | tf_op jit(solution)/shard_map/ppermute | solution.py:570
  387.2 20.4 %collective-permute-start.30 = (bf16[256,2048]{1,0:T(8,128)(2,1)S(1)}, bf16[256,2048]{1,0:T(8,128)(2,1)S(1)}, u32[]{:S(2)}, u32[]{:S(2)}) collective-permute-start(bf16[256,2048]{1,0:T(8,128)(2,1)S(1)} %get-tuple-element.225), channel_id=1, source_target_pairs={{2,1},{3,2},{6,5},{7,6},{10,9},{11,10},{14,13},{15,14},{18,17},{19... | collective-permute-start | bytes 3145736 | tf_op jit(solution)/shard_map/ppermute | solution.py:571
  408.6 7.5 %collective-permute-start.34 = (bf16[2048,1024]{1,0:T(8,128)(2,1)}, bf16[2048,1024]{1,0:T(8,128)(2,1)}, u32[]{:S(2)}, u32[]{:S(2)}) collective-permute-start(bf16[2048,1024]{1,0:T(8,128)(2,1)} %multiply_convert_fusion), channel_id=1, source_target_pairs={{0,4},{4,0},{8,12},{12,8},{16,20},{20,16},{24,28},{28,24},{1,5},{5... | collective-permute-start | bytes 12582920 | tf_op jit(solution)/shard_map/ppermute | solution.py:578
  408.7 20.6 %collective-permute-start.31 = (bf16[256,512]{1,0:T(8,128)(2,1)S(1)}, bf16[256,512]{1,0:T(8,128)(2,1)S(1)}, u32[]{:S(2)}, u32[]{:S(2)}) collective-permute-start(bf16[256,512]{1,0:T(8,128)(2,1)S(1)} %get-tuple-element.335), channel_id=1, source_target_pairs={{0,1},{1,2},{2,3},{3,0},{4,5},{5,6},{6,7},{7,4},{8,9},{9,10},{10,1... | collective-permute-start | bytes 786440 | tf_op jit(solution)/shard_map/ppermute | solution.py:507
  409.2 21.3 %collective-permute-start.32 = (bf16[256,512]{1,0:T(8,128)(2,1)S(1)}, bf16[256,512]{1,0:T(8,128)(2,1)S(1)}, u32[]{:S(2)}, u32[]{:S(2)}) collective-permute-start(bf16[256,512]{1,0:T(8,128)(2,1)S(1)} %get-tuple-element.334), channel_id=1, source_target_pairs={{0,2},{1,3},{2,0},{3,1},{4,6},{5,7},{6,4},{7,5},{8,10},{9,11},{10,... | collective-permute-start | bytes 786440 | tf_op jit(solution)/shard_map/ppermute | solution.py:507
  411.5 19.0 %collective-permute-start.33 = (bf16[256,512]{1,0:T(8,128)(2,1)S(1)}, bf16[256,512]{1,0:T(8,128)(2,1)S(1)}, u32[]{:S(2)}, u32[]{:S(2)}) collective-permute-start(bf16[256,512]{1,0:T(8,128)(2,1)S(1)} %get-tuple-element.333), channel_id=1, source_target_pairs={{0,3},{1,0},{2,1},{3,2},{4,7},{5,4},{6,5},{7,6},{8,11},{9,8},{10,9... | collective-permute-start | bytes 786440 | tf_op jit(solution)/shard_map/ppermute | solution.py:507
  432.6 50.5 %collective-permute-start.36 = (bf16[256,2048]{1,0:T(8,128)(2,1)}, bf16[256,2048]{1,0:T(8,128)(2,1)}, u32[]{:S(2)}, u32[]{:S(2)}) collective-permute-start(bf16[256,2048]{1,0:T(8,128)(2,1)} %get-tuple-element.238), channel_id=1, source_target_pairs={{1,0},{2,1},{3,2},{5,4},{6,5},{7,6},{9,8},{10,9},{11,10},{13,12},{... | collective-permute-start | bytes 3145736 | tf_op jit(solution)/shard_map/ppermute | solution.py:571
  434.1 49.1 %collective-permute-start.35 = (bf16[256,2048]{1,0:T(8,128)(2,1)}, bf16[256,2048]{1,0:T(8,128)(2,1)}, u32[]{:S(2)}, u32[]{:S(2)}) collective-permute-start(bf16[256,2048]{1,0:T(8,128)(2,1)} %get-tuple-element.237), channel_id=1, source_target_pairs={{0,1},{1,2},{2,3},{4,5},{5,6},{6,7},{8,9},{9,10},{10,11},{12,13},{... | collective-permute-start | bytes 3145736 | tf_op jit(solution)/shard_map/ppermute | solution.py:570
  443.6 46.5 %collective-permute-start.37 = (bf16[1024,512]{1,0:T(8,128)(2,1)}, bf16[1024,512]{1,0:T(8,128)(2,1)}, u32[]{:S(2)}, u32[]{:S(2)}) collective-permute-start(bf16[1024,512]{1,0:T(8,128)(2,1)} %add_convert_fusion.6), channel_id=1, source_target_pairs={{0,8},{4,12},{8,0},{12,4},{16,24},{20,28},{24,16},{28,20},{1,9},{5... | collective-permute-start | bytes 3145736 | tf_op jit(solution)/shard_map/ppermute | solution.py:578
  445.0 46.8 %collective-permute-start.38 = (bf16[1024,512]{1,0:T(8,128)(2,1)}, bf16[1024,512]{1,0:T(8,128)(2,1)}, u32[]{:S(2)}, u32[]{:S(2)}) collective-permute-start(bf16[1024,512]{1,0:T(8,128)(2,1)} %add_convert_fusion.5), channel_id=1, source_target_pairs={{0,16},{4,20},{8,24},{12,28},{16,0},{20,4},{24,8},{28,12},{1,17},{... | collective-permute-start | bytes 3145736 | tf_op jit(solution)/shard_map/ppermute | solution.py:578
  446.6 17.9 %copy-start.17 = (bf16[2048,1536]{1,0:T(8,128)(2,1)}, bf16[2048,1536]{1,0:T(8,128)(2,1)S(1)}, u32[]{:S(2)}) copy-start(bf16[2048,1536]{1,0:T(8,128)(2,1)S(1)} %pad_maximum_fusion.w_ref) | copy-start | bytes 18874372
  500.5 22.2 %collective-permute-start.39 = (bf16[256,2048]{1,0:T(8,128)(2,1)}, bf16[256,2048]{1,0:T(8,128)(2,1)}, u32[]{:S(2)}, u32[]{:S(2)}) collective-permute-start(bf16[256,2048]{1,0:T(8,128)(2,1)} %copy-done.58), channel_id=1, source_target_pairs={{0,1},{4,5},{8,9},{12,13},{16,17},{20,21},{24,25},{28,29}} | collective-permute-start | bytes 3145736 | tf_op jit(solution)/shard_map/ppermute | solution.py:570
  504.1 18.6 %collective-permute-start.40 = (bf16[256,2048]{1,0:T(8,128)(2,1)}, bf16[256,2048]{1,0:T(8,128)(2,1)}, u32[]{:S(2)}, u32[]{:S(2)}) collective-permute-start(bf16[256,2048]{1,0:T(8,128)(2,1)} %copy-done.57), channel_id=1, source_target_pairs={{3,2},{7,6},{11,10},{15,14},{19,18},{23,22},{27,26},{31,30}} | collective-permute-start | bytes 3145736 | tf_op jit(solution)/shard_map/ppermute | solution.py:571
  505.7 17.0 %collective-permute-start.41 = (bf16[1024,256]{1,0:T(8,128)(2,1)}, bf16[1024,256]{1,0:T(8,128)(2,1)}, u32[]{:S(2)}, u32[]{:S(2)}) collective-permute-start(bf16[1024,256]{1,0:T(8,128)(2,1)} %fusion.83), channel_id=1, source_target_pairs={{0,16},{4,20},{8,24},{12,28},{16,0},{20,4},{24,8},{28,12},{1,17},{... | collective-permute-start | bytes 1572872 | tf_op jit(solution)/shard_map/ppermute | solution.py:578
  506.7 15.9 %collective-permute-start.42 = (bf16[1024,256]{1,0:T(8,128)(2,1)}, bf16[1024,256]{1,0:T(8,128)(2,1)}, u32[]{:S(2)}, u32[]{:S(2)}) collective-permute-start(bf16[1024,256]{1,0:T(8,128)(2,1)} %fusion.82), channel_id=1, source_target_pairs={{0,8},{4,12},{8,0},{12,4},{16,24},{20,28},{24,16},{28,20},{1,9},{5... | collective-permute-start | bytes 1572872 | tf_op jit(solution)/shard_map/ppermute | solution.py:578
  527.5 28.8 %collective-permute-start.43 = (bf16[256,2048]{1,0:T(8,128)(2,1)S(1)}, bf16[256,2048]{1,0:T(8,128)(2,1)S(1)}, u32[]{:S(2)}, u32[]{:S(2)}) collective-permute-start(bf16[256,2048]{1,0:T(8,128)(2,1)S(1)} %get-tuple-element.256), channel_id=1, source_target_pairs={{0,1},{1,2},{4,5},{5,6},{8,9},{9,10},{12,13},{13,14},{16,17},{17,1... | collective-permute-start | bytes 3145736 | tf_op jit(solution)/shard_map/ppermute | solution.py:570
  531.4 25.0 %collective-permute-start.44 = (bf16[256,2048]{1,0:T(8,128)(2,1)S(1)}, bf16[256,2048]{1,0:T(8,128)(2,1)S(1)}, u32[]{:S(2)}, u32[]{:S(2)}) collective-permute-start(bf16[256,2048]{1,0:T(8,128)(2,1)S(1)} %get-tuple-element.257), channel_id=1, source_target_pairs={{2,1},{3,2},{6,5},{7,6},{10,9},{11,10},{14,13},{15,14},{18,17},{19... | collective-permute-start | bytes 3145736 | tf_op jit(solution)/shard_map/ppermute | solution.py:571
  533.3 15.6 %collective-permute-start.45 = (f32[12288]{0:T(1024)S(1)}, f32[12288]{0:T(1024)S(1)}, u32[]{:S(2)}, u32[]{:S(2)}) collective-permute-start(f32[12288]{0:T(1024)S(1)} %mul.288), channel_id=1, source_target_pairs={{0,1},{1,0},{2,3},{3,2},{4,5},{5,4},{6,7},{7,6},{8,9},{9,8},{10,11... | collective-permute-start | bytes 147464 | tf_op jit(solution)/shard_map/ppermute | solution.py:578
  535.8 20.6 %copy-start.7 = (bf16[1024,2048]{1,0:T(8,128)(2,1)S(1)}, bf16[1024,2048]{1,0:T(8,128)(2,1)}, u32[]{:S(2)}) copy-start(bf16[1024,2048]{1,0:T(8,128)(2,1)} %copy-done.5) | copy-start | bytes 12582916
  537.1 21.1 %copy-start.61 = (f32[1024,256]{1,0:T(8,128)}, f32[1024,256]{1,0:T(8,128)S(1)}, u32[]{:S(2)}) copy-start(f32[1024,256]{1,0:T(8,128)S(1)} %convert_add_fusion.1) | copy-start | bytes 3145732
  548.9 7.5 %collective-permute-start.46 = (f32[12288]{0:T(1024)S(1)}, f32[12288]{0:T(1024)S(1)}, u32[]{:S(2)}, u32[]{:S(2)}) collective-permute-start(f32[12288]{0:T(1024)S(1)} %add.523), channel_id=1, source_target_pairs={{0,2},{1,3},{2,0},{3,1},{4,6},{5,7},{6,4},{7,5},{8,10},{9,11},{10,... | collective-permute-start | bytes 147464 | tf_op jit(solution)/shard_map/ppermute | solution.py:578
  558.2 20.5 %collective-permute-start.47 = (bf16[256,2048]{1,0:T(8,128)(2,1)}, bf16[256,2048]{1,0:T(8,128)(2,1)S(1)}, u32[]{:S(2)}, u32[]{:S(2)}) collective-permute-start(bf16[256,2048]{1,0:T(8,128)(2,1)} %get-tuple-element.263), channel_id=1, source_target_pairs={{0,1},{1,2},{2,3},{4,5},{5,6},{6,7},{8,9},{9,10},{10,11},{12,13},{... | collective-permute-start | bytes 3145736 | tf_op jit(solution)/shard_map/ppermute | solution.py:570
  560.2 19.4 %collective-permute-start.48 = (bf16[256,2048]{1,0:T(8,128)(2,1)S(1)}, bf16[256,2048]{1,0:T(8,128)(2,1)S(1)}, u32[]{:S(2)}, u32[]{:S(2)}) collective-permute-start(bf16[256,2048]{1,0:T(8,128)(2,1)S(1)} %get-tuple-element.264), channel_id=1, source_target_pairs={{1,0},{2,1},{3,2},{5,4},{6,5},{7,6},{9,8},{10,9},{11,10},{13,12},{... | collective-permute-start | bytes 3145736 | tf_op jit(solution)/shard_map/ppermute | solution.py:571
  583.3 29.4 %collective-permute-start.49 = (bf16[512,256]{1,0:T(8,128)(2,1)}, bf16[512,256]{1,0:T(8,128)(2,1)}, u32[]{:S(2)}, u32[]{:S(2)}) collective-permute-start(bf16[512,256]{1,0:T(8,128)(2,1)} %get-tuple-element.324), channel_id=1, source_target_pairs={{0,1},{1,2},{2,3},{3,0},{4,5},{5,6},{6,7},{7,4},{8,9},{9,10},{10,1... | collective-permute-start | bytes 786440 | tf_op jit(solution)/shard_map/ppermute | solution.py:517
  587.8 25.0 %collective-permute-start.50 = (bf16[512,256]{1,0:T(8,128)(2,1)}, bf16[512,256]{1,0:T(8,128)(2,1)}, u32[]{:S(2)}, u32[]{:S(2)}) collective-permute-start(bf16[512,256]{1,0:T(8,128)(2,1)} %get-tuple-element.323), channel_id=1, source_target_pairs={{0,2},{1,3},{2,0},{3,1},{4,6},{5,7},{6,4},{7,5},{8,10},{9,11},{10,... | collective-permute-start | bytes 786440 | tf_op jit(solution)/shard_map/ppermute | solution.py:517
  589.3 23.4 %collective-permute-start.51 = (bf16[512,256]{1,0:T(8,128)(2,1)S(1)}, bf16[512,256]{1,0:T(8,128)(2,1)}, u32[]{:S(2)}, u32[]{:S(2)}) collective-permute-start(bf16[512,256]{1,0:T(8,128)(2,1)S(1)} %get-tuple-element.322), channel_id=1, source_target_pairs={{0,3},{1,0},{2,1},{3,2},{4,7},{5,4},{6,5},{7,6},{8,11},{9,8},{10,9... | collective-permute-start | bytes 786440 | tf_op jit(solution)/shard_map/ppermute | solution.py:517
  (85 other events, 447.9 us)
Sparse Core Ops, SparseCore 0:
  43.2 41.2 all-gather.4
  112.1 52.7 all-gather.6
  353.2 139.8 reduce-scatter.2
  500.6 59.9 reduce-scatter.4

commit v4 on v3

--- a/solution.py
+++ b/solution.py
@@ -396,7 +396,7 @@
             jax.ShapeDtypeStruct((rows, width), bf16),
             jax.ShapeDtypeStruct((4, width), f32),
         ],
-        compiler_params=pltpu.CompilerParams(vmem_limit_bytes=16 * MIB),
+        compiler_params=pltpu.CompilerParams(vmem_limit_bytes=48 * MIB),
         cost_estimate=COST,
         name="middle_back",
     )(index, terms, *came, middle_all, gain[None], cot)
@@ -414,10 +414,43 @@
             out_specs=here,
         ),
         out_shape=jax.ShapeDtypeStruct((rows, width), f32),
-        compiler_params=pltpu.CompilerParams(vmem_limit_bytes=16 * MIB),
+        compiler_params=pltpu.CompilerParams(vmem_limit_bytes=48 * MIB),
         cost_estimate=COST,
         name="input_back",
     )(index, factor[None], terms, *came, tokens, gain[None], d_middle)
+
+
+def present_kernel(qkv_ref, up_ref, down_ref, qkv_out, up_out, down_out):
+    cols = qkv_out.shape[2]
+    for j in range(3):
+        qkv_out[j] = qkv_ref[:, j * cols : (j + 1) * cols].astype(f32)
+    up_out[...] = up_ref[...].astype(f32)
+    down_out[...] = down_ref[...].astype(f32).T
+
+
+def present(qkv, up, down):
+    rows, cols = up.shape
+    head_cols = qkv.shape[1] // 3
+    step = min(rows, 128)
+    row = lambda size: pl.BlockSpec((step, size), lambda i: (i, 0))
+    return pl.pallas_call(
+        present_kernel,
+        grid=(rows // step,),
+        in_specs=[row(3 * head_cols), row(cols), row(cols)],
+        out_specs=[
+            pl.BlockSpec((3, step, head_cols), lambda i: (0, i, 0)),
+            row(cols),
+            pl.BlockSpec((cols, step), lambda i: (0, i)),
+        ],
+        out_shape=[
+            jax.ShapeDtypeStruct((3, rows, head_cols), f32),
+            jax.ShapeDtypeStruct((rows, cols), f32),
+            jax.ShapeDtypeStruct((cols, rows), f32),
+        ],
+        compiler_params=pltpu.CompilerParams(vmem_limit_bytes=48 * MIB),
+        cost_estimate=COST,
+        name="present",
+    )(qkv, up, down)
 
 
 def blank_kernel(out_ref):
@@ -514,6 +547,7 @@
         for shift in range(1, n):
             target = (self.me + shift) % n
             block = lax.dynamic_slice_in_dim(phase.early(array), target * rows, rows, axis=0)
+            phase.send(block)
             out.append(lax.ppermute(block, self.name, [(j, (j + shift) % n) for j in range(n)]))
         return out
 
@@ -578,8 +612,7 @@
     return lax.ppermute(value, name, [(j, j ^ bit) for j in range(size)])
 
 
-def sum_over(value, name, size):
-    bit = 1
+def sum_over(value, name, size, bit=1):
     while bit < size:
         value = value + flip(value, name, size, bit)
         bit *= 2
@@ -656,7 +689,7 @@
 
     def land(self, phase):
         along, self.air = 0 if self.moved_left else 1, False
-        flying = phase.early(*self.flying)
+        flying = phase(*self.flying)
         totals = [k.astype(f32) + f.astype(f32) for k, f in zip(self.kept, flying)]
         if self.done == len(self.bits):
             self.result = jnp.concatenate(totals, axis=1 - along)
@@ -773,7 +806,7 @@
                 hidden, active = keep(*feed_up(normed2_all, w_up, b_up.astype(f32)))
                 keep(middle_all, normed2_all)
             if k == 3:
-                attn_all = keep(set_heads(attn_all, heads_last, line.slot(last)))
+                attn_all = keep(set_heads(attn_all, phase(heads_last), line.slot(last)))
                 reduce_down.terms = keep(dot(phase(active), w_down).astype(bf16))
             if k == max(3, n_mp // 2):
                 if n_mp == 4:
@@ -783,6 +816,8 @@
                     place_near()
                     d_hidden_all = keep(hidden_back(cot_all, hidden, w_down, 1 - half))
             turn()
+
+        scatter = lambda full: lax.psum_scatter(phase(full), "dp", scatter_dimension=0, tiled=True)
 
         reduce_down.step(phase)
         if n_mp == 4:
@@ -799,11 +834,12 @@
         for k in slots:
             reduce2.step(phase)
             if k == 1:
-                feed_up_grad = keep(weight_grads(factor, phase(normed2_all), d_hidden_all, 2, 0))
+                up_full = keep(weight_grads(factor, phase(normed2_all), d_hidden_all))
             if k == 2:
-                feed_full = keep(weight_grads(factor, phase(cot_all), active, 2, 1, feed_up_grad))
+                grad_up = scatter(up_full)
+                down_full = keep(weight_grads(factor, phase(cot_all), active))
             if k == 3:
-                grad_feed = lax.psum_scatter(phase(feed_full), "dp", scatter_dimension=0, tiled=True)
+                grad_down = scatter(down_full)
                 split_sums = keep(factor * total(phase(d_hidden_all)))
             turn()
         own = me[None].astype(jnp.int32)
@@ -818,64 +854,60 @@
         d_attn_blocks = line.shuffle(phase, d_attn_own)
         spread_out.cross(phase)
         keep(*spread_out.second(phase))
+        keep(grad_up)
         turn()
         reduce_down.step(phase)
-        keep(*spread_out.fly(phase))
         d_attn = line.stack(phase(*d_attn_blocks))
         grad_proj = keep(attend_back(projected, d_attn, seg_col, seg_row, heads))
         reduce1.terms = keep(half_product(grad_proj, flat_qkv, half))
-        qkv_full = keep(weight_grads(factor, after(normed1_all, reduce1.terms), grad_proj))
         turn()
         for k in slots:
             reduce1.step(phase)
             if k == 1:
-                keep(*spread_out.land(phase))
                 keep(*spread_out.fly(phase))
                 reduce1.terms = keep(half_product(phase(grad_proj), flat_qkv, 1 - half, reduce1.terms))
                 gain1 = gain_sums(reduce1.terms, tokens_all)
-                full_sums = keep(factor * jnp.concatenate([gain1, own_sums], axis=0).reshape(-1))
-                grad_qkv = lax.psum_scatter(phase(qkv_full), "dp", scatter_dimension=0, tiled=True)
-                keep(grad_feed)
+                full_sums = factor * jnp.concatenate([gain1, own_sums], axis=0).reshape(-1)
+                full_sums = keep(full_sums + keep(flip(full_sums, "mp", n_mp, 1)))
+                qkv_full = keep(weight_grads(factor, after(normed1_all, gain1), grad_proj))
+                keep(grad_down)
             if k == 2:
-                out_rows = keep(spread_out.finish(phase))
+                grad_qkv = scatter(qkv_full)
+                keep(*spread_out.land(phase))
                 heads_sum = [total(phase(grad_proj)[:, :head_cols]), total(grad_proj[:, 2 * head_cols :])]
                 split_sums = keep(jnp.concatenate([*[factor * s for s in heads_sum], split_sums]))
-                full_sums = phase.early(full_sums)
-                phase.send(full_sums)
-                full_sums = keep(sum_over(full_sums, "mp", n_mp))
             if k == 3:
-                keep(grad_qkv)
-                sums = phase(jnp.concatenate([full_sums, split_sums])).reshape(1, 8, -1)
-                sums = keep(lax.all_gather(sums, "dp", axis=0, tiled=True))
+                keep(*spread_out.fly(phase))
                 for _ in slots[3:]:
                     reduce_down.step(phase)
+                down_sum = sum(
+                    value.astype(f32)
+                    for value in (rows_of(phase(reduce_down.terms), me), *reduce_down.came)
+                )
+                layer_out = keep((rows_of(middle_all, me) + down_sum + bias_pair[1]).astype(bf16))
+                full_sums = keep(sum_over(phase(full_sums), "mp", n_mp, 2))
             turn()
+        out_rows = spread_out.finish(phase)
         out_blocks = line.shuffle_rows(phase, out_rows.astype(bf16), head_cols)
         grad_input = input_back(
             own, factor, phase(reduce1.terms), reduce1.came, tokens, gains[0], d_middle
         )
+        grad_qkv, grad_up, grad_down = present(*phase(grad_qkv, grad_up, grad_down))
+        sums = after(jnp.concatenate([full_sums, split_sums]), grad_input).reshape(1, 8, -1)
+        sums = lax.all_gather(sums, "dp", axis=0, tiled=True)
+        sums, grad_qkv, *out_blocks = lax.optimization_barrier((sums, grad_qkv, *out_blocks))
+        grad_out = lax.dynamic_slice_in_dim(out_rows, me * head_cols, head_cols, axis=0)
+        for block in out_blocks:
+            grad_out = grad_out + block.astype(f32)
         sums = jnp.sum(sums, axis=0).reshape(-1)
-        grad_feed = phase(grad_feed).astype(f32)
-        feed_cols = grad_feed.shape[1] // 2
-        grad_up, grad_down = grad_feed[:, :feed_cols], grad_feed[:, feed_cols:].T
-        down_sum = sum(
-            value.astype(f32) for value in (rows_of(phase(reduce_down.terms), me), *reduce_down.came)
-        )
-        layer_out = (rows_of(middle_all, me) + down_sum + bias_pair[1]).astype(bf16)
         full_sums = sums[: 6 * width].reshape(6, width)
         split_sums = sums[6 * width :]
-        own_block = lax.dynamic_slice_in_dim(out_rows, me * head_cols, head_cols, axis=0)
-        out_blocks = lax.optimization_barrier((*out_blocks, grad_input, layer_out, grad_up, grad_down))[:-4]
-        for block in out_blocks:
-            own_block = own_block + block.astype(f32)
-        grad_out = own_block
-        grad_qkv = phase(grad_qkv).astype(f32)
         return (
             layer_out,
             grad_input,
             jnp.stack([full_sums[0], full_sums[2]]),
             jnp.stack([full_sums[1], full_sums[3]]),
-            jnp.stack([grad_qkv[:, j * head_cols : (j + 1) * head_cols] for j in range(3)], axis=1),
+            grad_qkv.transpose(1, 0, 2),
             split_sums[: 2 * head_cols].reshape(2, head_cols),
             grad_out,
             full_sums[4:],

time: 632 us -> 624 us (0.987)
  waiting for transfers between devices: 133 us -> 147 us
  starting transfers between devices: 111 us -> 98.6 us
    ppermute x9, waiting for transfers between devices: 11.6 us -> 22.5 us  [step(): lax.ppermute(sent[0], line.name, [(j, j + 1) for j in range(k)])]
    ppermute x3, starting transfers between devices: 8.83 us -> 2.03 us  [shuffle_rows(): lax.ppermute(block, self.name, [(j, (j + shift) % n) for j in range(n)])]
    unnamed x187 -> x196, local copies, waits for them, and re-layouts: 49.8 us -> 47.3 us
  transfers between devices with their start and end apart: 56 -> 57, of which waited for: 22 -> 20; matrix products, arithmetic and copies ran while one was open for 25% -> 24% of each run, Pallas kernels for 20% -> 22%
where the time goes in v4:
time: 624 us; the launch traced here: 614 us
  waiting for transfers between devices  147 us (24%)
  Pallas kernels  142 us (23%)
  starting transfers between devices  98.6 us (16%)
  matrix products  84.7 us (14%)
  local copies, waits for them, and re-layouts  68 us (11%)
  other arithmetic  45.4 us (7%)
  between operations  18.2 us (3%)
  blocking collectives  10.3 us (2%)
    ppermute x9, waiting for transfers between devices, step(): lax.ppermute(right, line.name, [(j, j - 1) for j in range(1, n - k + 1)])  85.4 us
    dot_general x16, matrix products, dot(): lax.dot_general(left, right, (((left_dim,), (right_dim,)), ((), ())), pre...  84.7 us
    unnamed x196, local copies, waits for them, and re-layouts  47.3 us
    pallas_call x3, Pallas kernels, weight_grads(): pl.pallas_call(grads_kernel, grid=(steps,), in_specs=[pl.BlockSpec(memory...  40.6 us
    ppermute x9, starting transfers between devices, step(): lax.ppermute(sent[0], line.name, [(j, j + 1) for j in range(k)])  34.5 us
    ppermute x9, waiting for transfers between devices, step(): lax.ppermute(sent[0], line.name, [(j, j + 1) for j in range(k)])  22.5 us
    ppermute x10, waiting for transfers between devices, flip(): return lax.ppermute(value, name, [(j, j ^ bit) for j in range(size)])  21.9 us
    ppermute x9, starting transfers between devices, step(): lax.ppermute(left, line.name, [(j, j + 1) for j in range(k - 1, n - 1)])  18.8 us
  transfers between devices with their start and end apart: 57, of which 20 were waited for; matrix products, arithmetic and copies ran while one was open for 24% of the time, Pallas kernels for 22%

profile of v4, /device:TPU:0, one launch (start us, length us, event | category | flops | bytes accessed | tf_op | source)
XLA Modules:
  0.0 614.0 jit_solution(10940733708854774873)
XLA Ops:
  7.2 6.0 collective-permute-start
  16.5 5.7 slice_bitcast_fusion.2
  25.0 5.1 fusion.1
  30.1 5.0 collective-permute-done
  35.0 5.1 collective-permute-done.1
  46.3 2.8 fusion.3
  49.1 36.0 %collective-permute-done.3 = bf16[256,2048]{1,0:T(8,128)(2,1)} collective-permute-done((bf16[256,2048]{1,0:T(8,128)(2,1)}, bf16[256,2048]{1,0:T(8,128)(2,1)}, u32[]{:S(2)}, u32[]{:S(2)}) %collective-permute-start.3) | collective-permute-done | bytes 1048608 | tf_op jit(solution)/shard_map/ppermute | solution.py:573
  90.9 2.8 fusion.5
  94.6 15.4 %collective-permute-done.5 = bf16[256,2048]{1,0:T(8,128)(2,1)S(1)} collective-permute-done((bf16[256,2048]{1,0:T(8,128)(2,1)}, bf16[256,2048]{1,0:T(8,128)(2,1)S(1)}, u32[]{:S(2)}, u32[]{:S(2)}) %collective-permute-start.5) | collective-permute-done | bytes 1048608 | tf_op jit(solution)/shard_map/ppermute | solution.py:573
  119.9 2.8 fusion.7.q_ref.k_ref.v_ref
  122.8 9.1 %attend.1 = bf16[1024,512]{1,0:T(8,128)(2,1)S(1)} custom-call(bf16[1024,1536]{1,0:T(8,128)(2,1)} %fusion.7.q_ref.k_ref.v_ref, bf16[1024,1536]{1,0:T(8,128)(2,1)} %fusion.7.q_ref.k_ref.v_ref, bf16[1024,1536]{1,0:T(8,128)(2,1)} %fusion.7.q_ref.k_ref.v_ref, s32[1024,1]{1,0:T(8,128)S(1)} %copy-done.28, s32[1,1024]{1,0:T(1,128)S(1)} %bitcast.56), custom_call_target="tpu_custom_call" | custom-call | flops 1048576 | bytes 65536 | tf_op jit(solution)/shard_map/attend/pallas_call | solution.py:49
  134.3 4.4 collective-permute-done.7
  144.5 5.8 add_add_fusion
  150.8 2.9 collective-permute-start.11
  155.1 2.9 collective-permute-start.12
  159.5 3.7 collective-permute-done.9
  169.5 6.1 fusion.35.grad_ref
  175.6 15.0 %collective-permute-done.14 = bf16[1024,512]{1,0:T(8,128)(2,1)} collective-permute-done((bf16[1024,512]{1,0:T(8,128)(2,1)S(1)}, bf16[1024,512]{1,0:T(8,128)(2,1)}, u32[]{:S(2)}, u32[]{:S(2)}) %collective-permute-start.14) | collective-permute-done | bytes 1048608 | tf_op jit(solution)/shard_map/ppermute | solution.py:573
  196.8 6.4 %convolution_add_fusion.1 = f32[1024,2048]{1,0:T(8,128)S(1)} fusion(f32[1024,2048]{1,0:T(8,128)} %add_add_fusion, bf16[1024,512]{1,0:T(8,128)(2,1)S(1)} %broadcast_select_fusion, bf16[2048,2048]{1,0:T(8,128)(2,1)} %bitcast.59, s32[]{:T(128)S(6)} %select_n.415), kind=kOutput, calls=%fused_computation.5 | convolution fusion | flops 2149580800 | bytes 19922948 | tf_op jit(solution)/shard_map/dot_general | solution.py:20
  203.2 7.4 %convolution_add_fusion.sum_ref = f32[1024,2048]{1,0:T(8,128)} fusion(f32[1024,2048]{1,0:T(8,128)S(1)} %convolution_add_fusion.1, bf16[1024,512]{1,0:T(8,128)(2,1)S(1)} %select_select_fusion.1, bf16[2048,2048]{1,0:T(8,128)(2,1)} %bitcast.60, s32[]{:T(128)S(6)} %select_n.432), kind=kOutput, calls=%fused_computation.4 | convolution fusion | flops 2149580800 | bytes 19922948 | tf_op jit(solution)/shard_map/dot_general | solution.py:20
  210.6 5.4 collective-permute-done.16
  220.9 9.5 %mix.1 = (f32[1024,2048]{1,0:T(8,128)}, bf16[1024,2048]{1,0:T(8,128)(2,1)S(1)}) custom-call(s32[1]{0:T(128)} %bitcast.index_ref, f32[1024,2048]{1,0:T(8,128)} %convolution_add_fusion.sum_ref, bf16[1024,512]{1,0:T(8,128)(2,1)S(1)} %select_select_fusion.heads_ref, bf16[2048,2048]{1,0:T(8,128)(2,1)} %bitcast.61, f32[1,2048]{1,0:T(1,128)S(1)} %get-tuple-element.339.gain_ref, ...), custom_call_target="tpu_custom_call" | custom-call | flops 1048576 | bytes 65536 | tf_op jit(solution)/shard_map/mix/pallas_call | solution.py:151
  232.2 15.7 %feed_up.1 = (f32[1024,2048]{1,0:T(8,128)}, bf16[1024,2048]{1,0:T(8,128)(2,1)S(1)}) custom-call(bf16[1024,2048]{1,0:T(8,128)(2,1)} %copy-done.21, bf16[2048,2048]{1,0:T(8,128)(2,1)} %w_ref.2, f32[1,2048]{1,0:T(1,128)S(1)} %bitcast.58), custom_call_target="tpu_custom_call" | custom-call | flops 1048576 | bytes 65536 | tf_op jit(solution)/shard_map/feed_up/pallas_call | solution.py:180
  251.4 11.4 %convolution_convert_fusion.1.right_ref.left_ref = bf16[1024,2048]{1,0:T(8,128)(2,1)S(1)} fusion(bf16[1024,2048]{1,0:T(8,128)(2,1)S(1)} %get-tuple-element.206.right_ref, bf16[2048,2048]{1,0:T(8,128)(2,1)} %w_ref.3), kind=kOutput, calls=%fused_computation.7 | convolution fusion | flops 8592031744 | bytes 16777216 | tf_op jit(solution)/shard_map/dot_general | solution.py:20
  262.8 3.7 copy-done.31
  266.5 2.7 slope_back.1.refs_0_
  274.9 5.2 collective-permute-start.21
  284.3 7.3 %hidden_back.1.right_ref = bf16[1024,2048]{1,0:T(8,128)(2,1)S(1)} custom-call(s32[1]{0:T(128)} %bitcast.16.index_ref, bf16[1024,2048]{1,0:T(8,128)(2,1)S(1)} %select_dynamic-update-slice_fusion.cot_ref.left_ref, f32[1024,2048]{1,0:T(8,128)S(1)} %copy-done.19, bf16[2048,2048]{1,0:T(8,128)(2,1)S(1)} %bitcast.46, ...), custom_call_target="tpu_custom_call", output_to_operand_aliasing={{}: (4, {})} | custom-call | flops 1048576 | bytes 65536 | tf_op jit(solution)/shard_map/hidden_back/pallas_call | solution.py:205
  291.6 12.8 %convolution_convert_fusion.right_ref.left_ref.term_ref = bf16[1024,2048]{1,0:T(8,128)(2,1)S(1)} fusion(bf16[1024,2048]{1,0:T(8,128)(2,1)S(1)} %hidden_back.1.right_ref, bf16[2048,2048]{1,0:T(8,128)(2,1)} %w_ref.2), kind=kOutput, calls=%fused_computation.6 | convolution fusion | flops 8592031744 | bytes 16777216 | tf_op jit(solution)/shard_map/dot_general | solution.py:20
  312.7 14.1 %weight_grads.3 = bf16[2048,2048]{1,0:T(8,128)(2,1)} custom-call(f32[1]{0:T(128)} %div.35.factor_ref, bf16[1024,2048]{1,0:T(8,128)(2,1)S(1)} %copy-done.22, bf16[1024,2048]{1,0:T(8,128)(2,1)} %copy-done.13), custom_call_target="tpu_custom_call" | custom-call | flops 1048576 | bytes 65536 | tf_op jit(solution)/shard_map/weight_grads/pallas_call | solution.py:265
  335.5 4.3 collective-permute-start.25
  344.1 14.2 %weight_grads.4 = bf16[2048,2048]{1,0:T(8,128)(2,1)} custom-call(f32[1]{0:T(128)} %div.35.factor_ref, bf16[1024,2048]{1,0:T(8,128)(2,1)S(1)} %copy-done.18, bf16[1024,2048]{1,0:T(8,128)(2,1)} %copy-done.30), custom_call_target="tpu_custom_call" | custom-call | flops 1048576 | bytes 65536 | tf_op jit(solution)/shard_map/weight_grads/pallas_call | solution.py:265
  359.3 2.9 copy-done.7
  363.4 2.8 relay.12
  367.2 4.3 collective-permute-start.27
  373.1 3.0 convert_reduce_fusion
  376.1 10.9 %collective-permute-done.27.left_ref = bf16[256,2048]{1,0:T(8,128)(2,1)S(1)} collective-permute-done((bf16[256,2048]{1,0:T(8,128)(2,1)}, bf16[256,2048]{1,0:T(8,128)(2,1)S(1)}, u32[]{:S(2)}, u32[]{:S(2)}) %collective-permute-start.27) | collective-permute-done | bytes 1048608 | tf_op jit(solution)/shard_map/ppermute | solution.py:604
  387.9 3.1 collective-permute-done.28.right_ref
  395.4 2.7 collective-permute-start.29
  400.1 5.0 middle_back.1
  405.1 5.8 convolution_convert_fusion.2
  411.1 4.6 multiply_convert_fusion
  423.2 4.0 collective-permute-done.34
  429.4 2.6 add_convert_fusion.3
  434.5 3.1 add_convert_fusion.4
  437.5 2.9 add_convert_fusion.6
  440.4 4.7 collective-permute-done.32
  449.3 2.5 collective-permute-start.35
  455.4 15.8 %attend_back.1.x_ref.right_ref = bf16[1024,1536]{1,0:T(8,128)(2,1)S(1)} custom-call(bf16[1024,1536]{1,0:T(8,128)(2,1)} %fusion.7.q_ref.k_ref.v_ref, bf16[1024,1536]{1,0:T(8,128)(2,1)} %fusion.7.q_ref.k_ref.v_ref, bf16[1024,1536]{1,0:T(8,128)(2,1)} %fusion.7.q_ref.k_ref.v_ref, bf16[1024,512]{1,0:T(8,128)(2,1)S(1)} %constant_dynamic-update-slice_fusion.grad_ref, ...), custom_call_target="tpu_custom_call" | custom-call | flops 1048576 | bytes 65536 | tf_op jit(solution)/shard_map/attend_back/pallas_call | solution.py:94
  471.2 4.2 half_product.2.right_ref.left_ref.refs_0_
  475.4 3.5 collective-permute-done.36
  483.7 3.3 collective-permute-start.37
  487.9 4.2 half_product.3.term_ref.right_ref.left_ref
  492.1 4.1 gain_sums.1
  498.3 12.3 %weight_grads.5 = bf16[2048,1536]{1,0:T(8,128)(2,1)} custom-call(f32[1]{0:T(128)} %div.35.factor_ref, bf16[1024,2048]{1,0:T(8,128)(2,1)} %get-tuple-element.259.left_ref, bf16[1024,1536]{1,0:T(8,128)(2,1)S(1)} %copy-done.12), custom_call_target="tpu_custom_call" | custom-call | flops 1048576 | bytes 65536 | tf_op jit(solution)/shard_map/weight_grads/pallas_call | solution.py:265
  517.4 4.0 collective-permute-start.42
  526.8 2.7 add_convert_fusion.2
  530.4 11.4 %collective-permute-done.42.refs_0_ = bf16[256,2048]{1,0:T(8,128)(2,1)S(1)} collective-permute-done((bf16[256,2048]{1,0:T(8,128)(2,1)S(1)}, bf16[256,2048]{1,0:T(8,128)(2,1)S(1)}, u32[]{:S(2)}, u32[]{:S(2)}) %collective-permute-start.42) | collective-permute-done | bytes 1048608 | tf_op jit(solution)/shard_map/ppermute | solution.py:604
  543.6 6.8 %collective-permute-start.44 = (bf16[256,2048]{1,0:T(8,128)(2,1)}, bf16[256,2048]{1,0:T(8,128)(2,1)S(1)}, u32[]{:S(2)}, u32[]{:S(2)}) collective-permute-start(bf16[256,2048]{1,0:T(8,128)(2,1)} %get-tuple-element.268), channel_id=1, source_target_pairs={{0,1},{1,2},{2,3},{4,5},{5,6},{6,7},{8,9},{9,10},{10,11},{12,13},{... | collective-permute-start | bytes 3145736 | tf_op jit(solution)/shard_map/ppermute | solution.py:604
  555.2 4.3 add_convert_fusion
  559.5 16.2 %collective-permute-done.48 = f32[12288]{0:T(1024)S(1)} collective-permute-done((f32[12288]{0:T(1024)S(1)}, f32[12288]{0:T(1024)S(1)}, u32[]{:S(2)}, u32[]{:S(2)}) %collective-permute-start.48) | collective-permute-done | bytes 49184 | tf_op jit(solution)/shard_map/ppermute | solution.py:612
  581.4 3.9 input_back.1
  585.3 10.3 %all_gather.19 = f32[8,8,1920]{2,1,0:T(8,128)} all-gather(f32[1,8,1920]{2,1,0:T(8,128)S(1)} %reshape.101), channel_id=1, replica_groups=mesh['dp'=8,'mp'=4] {'dp'}, dimensions={0}, use_global_device_ids=true | all-gather | bytes 552960 | tf_op jit(solution)/shard_map/all_gather | solution.py:897
  598.0 2.8 present.1
  (388 shorter events, 164.8 us)
Async XLA Ops:
  7.2 103.8 %all-gather.5.cloned.1.call-start = ((), (), s32[]{:S(2)}) async-start(), calls=%async_computation.6 | async-start | bytes 1310720 | tf_op jit(solution)/shard_map/all_gather | solution.py:754
  7.2 27.8 %collective-permute-start = (bf16[256,2048]{1,0:T(8,128)(2,1)}, bf16[256,2048]{1,0:T(8,128)(2,1)}, u32[]{:S(2)}, u32[]{:S(2)}) collective-permute-start(bf16[256,2048]{1,0:T(8,128)(2,1)} %value_ref.1), channel_id=1, source_target_pairs={{0,1},{1,2},{2,3},{4,5},{5,6},{6,7},{8,9},{9,10},{10,11},{12,13},{... | collective-permute-start | bytes 3145736 | tf_op jit(solution)/shard_map/ppermute | solution.py:572
  13.3 26.8 %collective-permute-start.1 = (bf16[256,2048]{1,0:T(8,128)(2,1)}, bf16[256,2048]{1,0:T(8,128)(2,1)}, u32[]{:S(2)}, u32[]{:S(2)}) collective-permute-start(bf16[256,2048]{1,0:T(8,128)(2,1)} %value_ref.1), channel_id=1, source_target_pairs={{1,0},{2,1},{3,2},{5,4},{6,5},{7,6},{9,8},{10,9},{11,10},{13,12},{... | collective-permute-start | bytes 3145736 | tf_op jit(solution)/shard_map/ppermute | solution.py:573
  40.1 9.0 %collective-permute-start.2 = (bf16[256,2048]{1,0:T(8,128)(2,1)}, bf16[256,2048]{1,0:T(8,128)(2,1)S(1)}, u32[]{:S(2)}, u32[]{:S(2)}) collective-permute-start(bf16[256,2048]{1,0:T(8,128)(2,1)} %collective-permute-done), channel_id=1, source_target_pairs={{1,2},{2,3},{5,6},{6,7},{9,10},{10,11},{13,14},{14,15},{17,18},{18... | collective-permute-start | bytes 3145736 | tf_op jit(solution)/shard_map/ppermute | solution.py:572
  40.8 44.2 %collective-permute-start.3 = (bf16[256,2048]{1,0:T(8,128)(2,1)}, bf16[256,2048]{1,0:T(8,128)(2,1)}, u32[]{:S(2)}, u32[]{:S(2)}) collective-permute-start(bf16[256,2048]{1,0:T(8,128)(2,1)} %collective-permute-done.1), channel_id=1, source_target_pairs={{1,0},{2,1},{5,4},{6,5},{9,8},{10,9},{13,12},{14,13},{17,16},{18,1... | collective-permute-start | bytes 3145736 | tf_op jit(solution)/shard_map/ppermute | solution.py:573
  42.1 154.6 %all-gather.7.cloned.1.call-start = ((), (), s32[]{:S(2)}) async-start(), calls=%async_computation.7 | async-start | bytes 9437184 | tf_op jit(solution)/shard_map/all_gather | solution.py:759
  85.0 8.6 %collective-permute-start.4 = (bf16[256,2048]{1,0:T(8,128)(2,1)S(1)}, bf16[256,2048]{1,0:T(8,128)(2,1)S(1)}, u32[]{:S(2)}, u32[]{:S(2)}) collective-permute-start(bf16[256,2048]{1,0:T(8,128)(2,1)S(1)} %collective-permute-done.2), channel_id=1, source_target_pairs={{2,3},{6,7},{10,11},{14,15},{18,19},{22,23},{26,27},{30,31}} | collective-permute-start | bytes 3145736 | tf_op jit(solution)/shard_map/ppermute | solution.py:572
  85.7 24.3 %collective-permute-start.5 = (bf16[256,2048]{1,0:T(8,128)(2,1)}, bf16[256,2048]{1,0:T(8,128)(2,1)S(1)}, u32[]{:S(2)}, u32[]{:S(2)}) collective-permute-start(bf16[256,2048]{1,0:T(8,128)(2,1)} %collective-permute-done.3), channel_id=1, source_target_pairs={{1,0},{5,4},{9,8},{13,12},{17,16},{21,20},{25,24},{29,28}} | collective-permute-start | bytes 3145736 | tf_op jit(solution)/shard_map/ppermute | solution.py:573
  111.0 334.7 %reduce-scatter.4.cloned.1.call-start = ((), (), s32[]{:S(2)}) async-start(), calls=%async_computation.3 | async-start | bytes 9437184 | tf_op jit(solution)/shard_map/reduce_scatter | solution.py:820
  113.6 20.7 %collective-permute-start.6 = (bf16[256,2048]{1,0:T(8,128)(2,1)S(1)}, bf16[256,2048]{1,0:T(8,128)(2,1)S(1)}, u32[]{:S(2)}, u32[]{:S(2)}) collective-permute-start(bf16[256,2048]{1,0:T(8,128)(2,1)S(1)} %copy-done.20), channel_id=1, source_target_pairs={{0,1},{1,2},{2,3},{4,5},{5,6},{6,7},{8,9},{9,10},{10,11},{12,13},{... | collective-permute-start | bytes 3145736 | tf_op jit(solution)/shard_map/ppermute | solution.py:572
  115.6 23.1 %collective-permute-start.7 = (bf16[256,2048]{1,0:T(8,128)(2,1)S(1)}, bf16[256,2048]{1,0:T(8,128)(2,1)}, u32[]{:S(2)}, u32[]{:S(2)}) collective-permute-start(bf16[256,2048]{1,0:T(8,128)(2,1)S(1)} %copy-done.20), channel_id=1, source_target_pairs={{1,0},{2,1},{3,2},{5,4},{6,5},{7,6},{9,8},{10,9},{11,10},{13,12},{... | collective-permute-start | bytes 3145736 | tf_op jit(solution)/shard_map/ppermute | solution.py:573
  134.3 31.7 %copy-start.78 = (bf16[256,2048]{1,0:T(8,128)(2,1)}, bf16[256,2048]{1,0:T(8,128)(2,1)S(1)}, u32[]{:S(2)}) copy-start(bf16[256,2048]{1,0:T(8,128)(2,1)S(1)} %collective-permute-done.6) | copy-start | bytes 3145732
  138.7 20.7 %collective-permute-start.8 = (bf16[1024,512]{1,0:T(8,128)(2,1)S(1)}, bf16[1024,512]{1,0:T(8,128)(2,1)S(1)}, u32[]{:S(2)}, u32[]{:S(2)}) collective-permute-start(bf16[1024,512]{1,0:T(8,128)(2,1)S(1)} %attend.1), channel_id=1, source_target_pairs={{0,1},{1,2},{2,3},{4,5},{5,6},{6,7},{8,9},{9,10},{10,11},{12,13},{... | collective-permute-start | bytes 3145736 | tf_op jit(solution)/shard_map/ppermute | solution.py:572
  140.9 22.2 %collective-permute-start.9 = (bf16[1024,512]{1,0:T(8,128)(2,1)S(1)}, bf16[1024,512]{1,0:T(8,128)(2,1)S(1)}, u32[]{:S(2)}, u32[]{:S(2)}) collective-permute-start(bf16[1024,512]{1,0:T(8,128)(2,1)S(1)} %attend.1), channel_id=1, source_target_pairs={{1,0},{2,1},{3,2},{5,4},{6,5},{7,6},{9,8},{10,9},{11,10},{13,12},{... | collective-permute-start | bytes 3145736 | tf_op jit(solution)/shard_map/ppermute | solution.py:573
  142.2 8.0 %collective-permute-start.10 = (f32[1]{0:T(128)}, f32[1]{0:T(128)}, u32[]{:S(2)}, u32[]{:S(2)}) collective-permute-start(f32[1]{0:T(128)} %convert_element_type.180), channel_id=1, source_target_pairs={{0,4},{4,0},{8,12},{12,8},{16,20},{20,16},{24,28},{28,24},{1,5},{5... | collective-permute-start | bytes 20 | tf_op jit(solution)/shard_map/ppermute | solution.py:612
  143.2 26.2 %slice-start = ((s8[8388608]{0:T(1024)(128)(4,1)}), s8[4194304]{0:T(1024)(128)(4,1)S(1)}, s32[]{:S(2)}) async-start(s8[8388608]{0:T(1024)(128)(4,1)} %bitcast.43), calls=%async_computation.8 | async-start | bytes 8388608
  144.4 25.0 %slice-start.1 = ((s8[8388608]{0:T(1024)(128)(4,1)}), s8[4194304]{0:T(1024)(128)(4,1)S(1)}, s32[]{:S(2)}) async-start(s8[8388608]{0:T(1024)(128)(4,1)} %bitcast.43), calls=%async_computation.9 | async-start | bytes 8388608
  150.8 3.7 collective-permute-start.11
  155.1 3.7 collective-permute-start.12
  163.1 12.5 %collective-permute-start.13 = (bf16[1024,512]{1,0:T(8,128)(2,1)S(1)}, bf16[1024,512]{1,0:T(8,128)(2,1)}, u32[]{:S(2)}, u32[]{:S(2)}) collective-permute-start(bf16[1024,512]{1,0:T(8,128)(2,1)S(1)} %collective-permute-done.8), channel_id=1, source_target_pairs={{1,2},{2,3},{5,6},{6,7},{9,10},{10,11},{13,14},{14,15},{17,18},{18... | collective-permute-start | bytes 3145736 | tf_op jit(solution)/shard_map/ppermute | solution.py:572
  164.8 25.8 %collective-permute-start.14 = (bf16[1024,512]{1,0:T(8,128)(2,1)S(1)}, bf16[1024,512]{1,0:T(8,128)(2,1)}, u32[]{:S(2)}, u32[]{:S(2)}) collective-permute-start(bf16[1024,512]{1,0:T(8,128)(2,1)S(1)} %collective-permute-done.9), channel_id=1, source_target_pairs={{1,0},{2,1},{5,4},{6,5},{9,8},{10,9},{13,12},{14,13},{17,16},{18,1... | collective-permute-start | bytes 3145736 | tf_op jit(solution)/shard_map/ppermute | solution.py:573
  190.5 20.1 %collective-permute-start.15 = (bf16[1024,512]{1,0:T(8,128)(2,1)}, bf16[1024,512]{1,0:T(8,128)(2,1)}, u32[]{:S(2)}, u32[]{:S(2)}) collective-permute-start(bf16[1024,512]{1,0:T(8,128)(2,1)} %collective-permute-done.13), channel_id=1, source_target_pairs={{2,3},{6,7},{10,11},{14,15},{18,19},{22,23},{26,27},{30,31}} | collective-permute-start | bytes 3145736 | tf_op jit(solution)/shard_map/ppermute | solution.py:572
  192.2 23.8 %collective-permute-start.16 = (bf16[1024,512]{1,0:T(8,128)(2,1)}, bf16[1024,512]{1,0:T(8,128)(2,1)}, u32[]{:S(2)}, u32[]{:S(2)}) collective-permute-start(bf16[1024,512]{1,0:T(8,128)(2,1)} %collective-permute-done.14), channel_id=1, source_target_pairs={{1,0},{5,4},{9,8},{13,12},{17,16},{21,20},{25,24},{29,28}} | collective-permute-start | bytes 3145736 | tf_op jit(solution)/shard_map/ppermute | solution.py:573
  216.0 31.9 %collective-permute-start.17 = (bf16[256,2048]{1,0:T(8,128)(2,1)S(1)}, bf16[256,2048]{1,0:T(8,128)(2,1)}, u32[]{:S(2)}, u32[]{:S(2)}) collective-permute-start(bf16[256,2048]{1,0:T(8,128)(2,1)S(1)} %copy-done.79), channel_id=1, source_target_pairs={{1,2},{2,3},{5,6},{6,7},{9,10},{10,11},{13,14},{14,15},{17,18},{18... | collective-permute-start | bytes 3145736 | tf_op jit(solution)/shard_map/ppermute | solution.py:572
  217.7 30.2 %collective-permute-start.18 = (bf16[256,2048]{1,0:T(8,128)(2,1)}, bf16[256,2048]{1,0:T(8,128)(2,1)}, u32[]{:S(2)}, u32[]{:S(2)}) collective-permute-start(bf16[256,2048]{1,0:T(8,128)(2,1)} %collective-permute-done.7), channel_id=1, source_target_pairs={{1,0},{2,1},{5,4},{6,5},{9,8},{10,9},{13,12},{14,13},{17,16},{18,1... | collective-permute-start | bytes 3145736 | tf_op jit(solution)/shard_map/ppermute | solution.py:573
  247.9 24.5 %collective-permute-start.19 = (bf16[256,2048]{1,0:T(8,128)(2,1)}, bf16[256,2048]{1,0:T(8,128)(2,1)}, u32[]{:S(2)}, u32[]{:S(2)}) collective-permute-start(bf16[256,2048]{1,0:T(8,128)(2,1)} %collective-permute-done.17), channel_id=1, source_target_pairs={{2,3},{6,7},{10,11},{14,15},{18,19},{22,23},{26,27},{30,31}} | collective-permute-start | bytes 3145736 | tf_op jit(solution)/shard_map/ppermute | solution.py:572
  250.1 22.9 %collective-permute-start.20 = (bf16[256,2048]{1,0:T(8,128)(2,1)}, bf16[256,2048]{1,0:T(8,128)(2,1)}, u32[]{:S(2)}, u32[]{:S(2)}) collective-permute-start(bf16[256,2048]{1,0:T(8,128)(2,1)} %collective-permute-done.18), channel_id=1, source_target_pairs={{1,0},{5,4},{9,8},{13,12},{17,16},{21,20},{25,24},{29,28}} | collective-permute-start | bytes 3145736 | tf_op jit(solution)/shard_map/ppermute | solution.py:573
  274.9 29.5 %collective-permute-start.21 = (bf16[256,2048]{1,0:T(8,128)(2,1)}, bf16[256,2048]{1,0:T(8,128)(2,1)S(1)}, u32[]{:S(2)}, u32[]{:S(2)}) collective-permute-start(bf16[256,2048]{1,0:T(8,128)(2,1)} %get-tuple-element.214), channel_id=1, source_target_pairs={{0,1},{4,5},{8,9},{12,13},{16,17},{20,21},{24,25},{28,29}} | collective-permute-start | bytes 3145736 | tf_op jit(solution)/shard_map/ppermute | solution.py:604
  280.1 25.3 %collective-permute-start.22 = (bf16[256,2048]{1,0:T(8,128)(2,1)}, bf16[256,2048]{1,0:T(8,128)(2,1)}, u32[]{:S(2)}, u32[]{:S(2)}) collective-permute-start(bf16[256,2048]{1,0:T(8,128)(2,1)} %get-tuple-element.215), channel_id=1, source_target_pairs={{3,2},{7,6},{11,10},{15,14},{19,18},{23,22},{27,26},{31,30}} | collective-permute-start | bytes 3145736 | tf_op jit(solution)/shard_map/ppermute | solution.py:605
  307.5 19.5 %collective-permute-start.23 = (bf16[256,2048]{1,0:T(8,128)(2,1)}, bf16[256,2048]{1,0:T(8,128)(2,1)S(1)}, u32[]{:S(2)}, u32[]{:S(2)}) collective-permute-start(bf16[256,2048]{1,0:T(8,128)(2,1)} %get-tuple-element.221), channel_id=1, source_target_pairs={{0,1},{4,5},{8,9},{12,13},{16,17},{20,21},{24,25},{28,29}} | collective-permute-start | bytes 3145736 | tf_op jit(solution)/shard_map/ppermute | solution.py:604
  308.8 19.1 %collective-permute-start.24 = (bf16[256,2048]{1,0:T(8,128)(2,1)}, bf16[256,2048]{1,0:T(8,128)(2,1)}, u32[]{:S(2)}, u32[]{:S(2)}) collective-permute-start(bf16[256,2048]{1,0:T(8,128)(2,1)} %get-tuple-element.222), channel_id=1, source_target_pairs={{3,2},{7,6},{11,10},{15,14},{19,18},{23,22},{27,26},{31,30}} | collective-permute-start | bytes 3145736 | tf_op jit(solution)/shard_map/ppermute | solution.py:605
  335.4 175.1 %reduce-scatter.6.cloned.1.call-start = ((), (), s32[]{:S(2)}) async-start(), calls=%async_computation.4 | async-start | bytes 9437184 | tf_op jit(solution)/shard_map/reduce_scatter | solution.py:820
  335.5 22.9 %collective-permute-start.25 = (bf16[256,2048]{1,0:T(8,128)(2,1)}, bf16[256,2048]{1,0:T(8,128)(2,1)S(1)}, u32[]{:S(2)}, u32[]{:S(2)}) collective-permute-start(bf16[256,2048]{1,0:T(8,128)(2,1)} %copy-done.60), channel_id=1, source_target_pairs={{0,1},{1,2},{4,5},{5,6},{8,9},{9,10},{12,13},{13,14},{16,17},{17,1... | collective-permute-start | bytes 3145736 | tf_op jit(solution)/shard_map/ppermute | solution.py:604
  339.8 19.5 %collective-permute-start.26 = (bf16[256,2048]{1,0:T(8,128)(2,1)}, bf16[256,2048]{1,0:T(8,128)(2,1)}, u32[]{:S(2)}, u32[]{:S(2)}) collective-permute-start(bf16[256,2048]{1,0:T(8,128)(2,1)} %copy-done.57), channel_id=1, source_target_pairs={{2,1},{3,2},{6,5},{7,6},{10,9},{11,10},{14,13},{15,14},{18,17},{19... | collective-permute-start | bytes 3145736 | tf_op jit(solution)/shard_map/ppermute | solution.py:605
  367.2 228.4 %reduce-scatter.8.cloned.1.call-start = ((), (), s32[]{:S(2)}) async-start(), calls=%async_computation.5 | async-start | bytes 7077888 | tf_op jit(solution)/shard_map/reduce_scatter | solution.py:820
  367.2 19.7 %collective-permute-start.27 = (bf16[256,2048]{1,0:T(8,128)(2,1)}, bf16[256,2048]{1,0:T(8,128)(2,1)S(1)}, u32[]{:S(2)}, u32[]{:S(2)}) collective-permute-start(bf16[256,2048]{1,0:T(8,128)(2,1)} %get-tuple-element.229), channel_id=1, source_target_pairs={{0,1},{1,2},{2,3},{4,5},{5,6},{6,7},{8,9},{9,10},{10,11},{12,13},{... | collective-permute-start | bytes 3145736 | tf_op jit(solution)/shard_map/ppermute | solution.py:604
  371.6 19.5 %collective-permute-start.28 = (bf16[256,2048]{1,0:T(8,128)(2,1)}, bf16[256,2048]{1,0:T(8,128)(2,1)S(1)}, u32[]{:S(2)}, u32[]{:S(2)}) collective-permute-start(bf16[256,2048]{1,0:T(8,128)(2,1)} %copy-done.56), channel_id=1, source_target_pairs={{1,0},{2,1},{3,2},{5,4},{6,5},{7,6},{9,8},{10,9},{11,10},{13,12},{... | collective-permute-start | bytes 3145736 | tf_op jit(solution)/shard_map/ppermute | solution.py:605
  395.4 20.2 %collective-permute-start.29 = (bf16[256,2048]{1,0:T(8,128)(2,1)S(1)}, bf16[256,2048]{1,0:T(8,128)(2,1)S(1)}, u32[]{:S(2)}, u32[]{:S(2)}) collective-permute-start(bf16[256,2048]{1,0:T(8,128)(2,1)S(1)} %get-tuple-element.233), channel_id=1, source_target_pairs={{0,1},{1,2},{4,5},{5,6},{8,9},{9,10},{12,13},{13,14},{16,17},{17,1... | collective-permute-start | bytes 3145736 | tf_op jit(solution)/shard_map/ppermute | solution.py:604
  398.1 18.5 %collective-permute-start.30 = (bf16[256,2048]{1,0:T(8,128)(2,1)S(1)}, bf16[256,2048]{1,0:T(8,128)(2,1)S(1)}, u32[]{:S(2)}, u32[]{:S(2)}) collective-permute-start(bf16[256,2048]{1,0:T(8,128)(2,1)S(1)} %get-tuple-element.234), channel_id=1, source_target_pairs={{2,1},{3,2},{6,5},{7,6},{10,9},{11,10},{14,13},{15,14},{18,17},{19... | collective-permute-start | bytes 3145736 | tf_op jit(solution)/shard_map/ppermute | solution.py:605
  417.6 9.7 %collective-permute-start.34 = (bf16[2048,1024]{1,0:T(8,128)(2,1)}, bf16[2048,1024]{1,0:T(8,128)(2,1)}, u32[]{:S(2)}, u32[]{:S(2)}) collective-permute-start(bf16[2048,1024]{1,0:T(8,128)(2,1)} %multiply_convert_fusion), channel_id=1, source_target_pairs={{0,4},{4,0},{8,12},{12,8},{16,20},{20,16},{24,28},{28,24},{1,5},{5... | collective-permute-start | bytes 12582920 | tf_op jit(solution)/shard_map/ppermute | solution.py:612
  417.7 22.7 %collective-permute-start.33 = (bf16[256,512]{1,0:T(8,128)(2,1)S(1)}, bf16[256,512]{1,0:T(8,128)(2,1)S(1)}, u32[]{:S(2)}, u32[]{:S(2)}) collective-permute-start(bf16[256,512]{1,0:T(8,128)(2,1)S(1)} %get-tuple-element.309), channel_id=1, source_target_pairs={{0,3},{1,0},{2,1},{3,2},{4,7},{5,4},{6,5},{7,6},{8,11},{9,8},{10,9... | collective-permute-start | bytes 786440 | tf_op jit(solution)/shard_map/ppermute | solution.py:540
  420.2 24.9 %collective-permute-start.32 = (bf16[256,512]{1,0:T(8,128)(2,1)S(1)}, bf16[256,512]{1,0:T(8,128)(2,1)S(1)}, u32[]{:S(2)}, u32[]{:S(2)}) collective-permute-start(bf16[256,512]{1,0:T(8,128)(2,1)S(1)} %get-tuple-element.310), channel_id=1, source_target_pairs={{0,2},{1,3},{2,0},{3,1},{4,6},{5,7},{6,4},{7,5},{8,10},{9,11},{10,... | collective-permute-start | bytes 786440 | tf_op jit(solution)/shard_map/ppermute | solution.py:540
  421.3 24.5 %collective-permute-start.31 = (bf16[256,512]{1,0:T(8,128)(2,1)S(1)}, bf16[256,512]{1,0:T(8,128)(2,1)}, u32[]{:S(2)}, u32[]{:S(2)}) collective-permute-start(bf16[256,512]{1,0:T(8,128)(2,1)S(1)} %get-tuple-element.311), channel_id=1, source_target_pairs={{0,1},{1,2},{2,3},{3,0},{4,5},{5,6},{6,7},{7,4},{8,9},{9,10},{10,1... | collective-permute-start | bytes 786440 | tf_op jit(solution)/shard_map/ppermute | solution.py:540
  449.3 26.1 %collective-permute-start.35 = (bf16[256,2048]{1,0:T(8,128)(2,1)S(1)}, bf16[256,2048]{1,0:T(8,128)(2,1)}, u32[]{:S(2)}, u32[]{:S(2)}) collective-permute-start(bf16[256,2048]{1,0:T(8,128)(2,1)S(1)} %get-tuple-element.247), channel_id=1, source_target_pairs={{0,1},{1,2},{2,3},{4,5},{5,6},{6,7},{8,9},{9,10},{10,11},{12,13},{... | collective-permute-start | bytes 3145736 | tf_op jit(solution)/shard_map/ppermute | solution.py:604
  451.9 27.1 %collective-permute-start.36 = (bf16[256,2048]{1,0:T(8,128)(2,1)S(1)}, bf16[256,2048]{1,0:T(8,128)(2,1)}, u32[]{:S(2)}, u32[]{:S(2)}) collective-permute-start(bf16[256,2048]{1,0:T(8,128)(2,1)S(1)} %get-tuple-element.248), channel_id=1, source_target_pairs={{1,0},{2,1},{3,2},{5,4},{6,5},{7,6},{9,8},{10,9},{11,10},{13,12},{... | collective-permute-start | bytes 3145736 | tf_op jit(solution)/shard_map/ppermute | solution.py:605
  479.0 31.6 %collective-permute-start.39 = (bf16[1024,512]{1,0:T(8,128)(2,1)}, bf16[1024,512]{1,0:T(8,128)(2,1)}, u32[]{:S(2)}, u32[]{:S(2)}) collective-permute-start(bf16[1024,512]{1,0:T(8,128)(2,1)} %add_convert_fusion.6), channel_id=1, source_target_pairs={{0,8},{4,12},{8,0},{12,4},{16,24},{20,28},{24,16},{28,20},{1,9},{5... | collective-permute-start | bytes 3145736 | tf_op jit(solution)/shard_map/ppermute | solution.py:612
  480.5 30.1 %collective-permute-start.40 = (bf16[1024,512]{1,0:T(8,128)(2,1)}, bf16[1024,512]{1,0:T(8,128)(2,1)}, u32[]{:S(2)}, u32[]{:S(2)}) collective-permute-start(bf16[1024,512]{1,0:T(8,128)(2,1)} %add_convert_fusion.5), channel_id=1, source_target_pairs={{0,16},{4,20},{8,24},{12,28},{16,0},{20,4},{24,8},{28,12},{1,17},{... | collective-permute-start | bytes 3145736 | tf_op jit(solution)/shard_map/ppermute | solution.py:612
  483.7 26.9 %collective-permute-start.37 = (bf16[256,2048]{1,0:T(8,128)(2,1)}, bf16[256,2048]{1,0:T(8,128)(2,1)S(1)}, u32[]{:S(2)}, u32[]{:S(2)}) collective-permute-start(bf16[256,2048]{1,0:T(8,128)(2,1)} %get-tuple-element.254), channel_id=1, source_target_pairs={{0,1},{4,5},{8,9},{12,13},{16,17},{20,21},{24,25},{28,29}} | collective-permute-start | bytes 3145736 | tf_op jit(solution)/shard_map/ppermute | solution.py:604
  487.0 23.6 %collective-permute-start.38 = (bf16[256,2048]{1,0:T(8,128)(2,1)}, bf16[256,2048]{1,0:T(8,128)(2,1)S(1)}, u32[]{:S(2)}, u32[]{:S(2)}) collective-permute-start(bf16[256,2048]{1,0:T(8,128)(2,1)} %get-tuple-element.255), channel_id=1, source_target_pairs={{3,2},{7,6},{11,10},{15,14},{19,18},{23,22},{27,26},{31,30}} | collective-permute-start | bytes 3145736 | tf_op jit(solution)/shard_map/ppermute | solution.py:605
  496.3 14.2 %collective-permute-start.41 = (f32[12288]{0:T(1024)S(1)}, f32[12288]{0:T(1024)S(1)}, u32[]{:S(2)}, u32[]{:S(2)}) collective-permute-start(f32[12288]{0:T(1024)S(1)} %mul.288), channel_id=1, source_target_pairs={{0,1},{1,0},{2,3},{3,2},{4,5},{5,4},{6,7},{7,6},{8,9},{9,8},{10,11... | collective-permute-start | bytes 147464 | tf_op jit(solution)/shard_map/ppermute | solution.py:612
  517.4 24.4 %collective-permute-start.42 = (bf16[256,2048]{1,0:T(8,128)(2,1)S(1)}, bf16[256,2048]{1,0:T(8,128)(2,1)S(1)}, u32[]{:S(2)}, u32[]{:S(2)}) collective-permute-start(bf16[256,2048]{1,0:T(8,128)(2,1)S(1)} %copy-done.62), channel_id=1, source_target_pairs={{0,1},{1,2},{4,5},{5,6},{8,9},{9,10},{12,13},{13,14},{16,17},{17,1... | collective-permute-start | bytes 3145736 | tf_op jit(solution)/shard_map/ppermute | solution.py:604
  521.4 20.4 %collective-permute-start.43 = (bf16[256,2048]{1,0:T(8,128)(2,1)S(1)}, bf16[256,2048]{1,0:T(8,128)(2,1)S(1)}, u32[]{:S(2)}, u32[]{:S(2)}) collective-permute-start(bf16[256,2048]{1,0:T(8,128)(2,1)S(1)} %copy-done.59), channel_id=1, source_target_pairs={{2,1},{3,2},{6,5},{7,6},{10,9},{11,10},{14,13},{15,14},{18,17},{19... | collective-permute-start | bytes 3145736 | tf_op jit(solution)/shard_map/ppermute | solution.py:605
  530.4 24.8 %copy-start.88 = (f32[1,2048]{1,0:T(1,128)S(1)}, f32[1,2048]{1,0:T(1,128)}, u32[]{:S(2)}) copy-start(f32[1,2048]{1,0:T(1,128)} %get-tuple-element.330) | copy-start | bytes 24580
  543.6 32.1 %collective-permute-start.44 = (bf16[256,2048]{1,0:T(8,128)(2,1)}, bf16[256,2048]{1,0:T(8,128)(2,1)S(1)}, u32[]{:S(2)}, u32[]{:S(2)}) collective-permute-start(bf16[256,2048]{1,0:T(8,128)(2,1)} %get-tuple-element.268), channel_id=1, source_target_pairs={{0,1},{1,2},{2,3},{4,5},{5,6},{6,7},{8,9},{9,10},{10,11},{12,13},{... | collective-permute-start | bytes 3145736 | tf_op jit(solution)/shard_map/ppermute | solution.py:604
  550.5 26.2 %collective-permute-start.45 = (bf16[256,2048]{1,0:T(8,128)(2,1)S(1)}, bf16[256,2048]{1,0:T(8,128)(2,1)S(1)}, u32[]{:S(2)}, u32[]{:S(2)}) collective-permute-start(bf16[256,2048]{1,0:T(8,128)(2,1)S(1)} %get-tuple-element.269), channel_id=1, source_target_pairs={{1,0},{2,1},{3,2},{5,4},{6,5},{7,6},{9,8},{10,9},{11,10},{13,12},{... | collective-permute-start | bytes 3145736 | tf_op jit(solution)/shard_map/ppermute | solution.py:605
  551.9 23.8 %collective-permute-start.46 = (bf16[1024,256]{1,0:T(8,128)(2,1)}, bf16[1024,256]{1,0:T(8,128)(2,1)S(1)}, u32[]{:S(2)}, u32[]{:S(2)}) collective-permute-start(bf16[1024,256]{1,0:T(8,128)(2,1)} %fusion.83), channel_id=1, source_target_pairs={{0,16},{4,20},{8,24},{12,28},{16,0},{20,4},{24,8},{28,12},{1,17},{... | collective-permute-start | bytes 1572872 | tf_op jit(solution)/shard_map/ppermute | solution.py:612
  552.6 23.1 %collective-permute-start.47 = (bf16[1024,256]{1,0:T(8,128)(2,1)}, bf16[1024,256]{1,0:T(8,128)(2,1)S(1)}, u32[]{:S(2)}, u32[]{:S(2)}) collective-permute-start(bf16[1024,256]{1,0:T(8,128)(2,1)} %fusion.82), channel_id=1, source_target_pairs={{0,8},{4,12},{8,0},{12,4},{16,24},{20,28},{24,16},{28,20},{1,9},{5... | collective-permute-start | bytes 1572872 | tf_op jit(solution)/shard_map/ppermute | solution.py:612
  553.2 22.5 %collective-permute-start.48 = (f32[12288]{0:T(1024)S(1)}, f32[12288]{0:T(1024)S(1)}, u32[]{:S(2)}, u32[]{:S(2)}) collective-permute-start(f32[12288]{0:T(1024)S(1)} %add.521), channel_id=1, source_target_pairs={{0,2},{1,3},{2,0},{3,1},{4,6},{5,7},{6,4},{7,5},{8,10},{9,11},{10,... | collective-permute-start | bytes 147464 | tf_op jit(solution)/shard_map/ppermute | solution.py:612
  555.2 22.5 %copy-start.77 = (bf16[1024,512]{1,0:T(8,128)(2,1)S(1)}, bf16[1024,512]{1,0:T(8,128)(2,1)}, u32[]{:S(2)}) copy-start(bf16[1024,512]{1,0:T(8,128)(2,1)} %copy-done.76) | copy-start | bytes 3145732
  555.2 22.6 %copy-start.75 = (bf16[1024,512]{1,0:T(8,128)(2,1)S(1)}, bf16[1024,512]{1,0:T(8,128)(2,1)}, u32[]{:S(2)}) copy-start(bf16[1024,512]{1,0:T(8,128)(2,1)} %copy-done.74) | copy-start | bytes 3145732
  579.0 21.8 %collective-permute-start.51 = (bf16[512,256]{1,0:T(8,128)(2,1)}, bf16[512,256]{1,0:T(8,128)(2,1)S(1)}, u32[]{:S(2)}, u32[]{:S(2)}) collective-permute-start(bf16[512,256]{1,0:T(8,128)(2,1)} %get-tuple-element.298), channel_id=1, source_target_pairs={{0,3},{1,0},{2,1},{3,2},{4,7},{5,4},{6,5},{7,6},{8,11},{9,8},{10,9... | collective-permute-start | bytes 786440 | tf_op jit(solution)/shard_map/ppermute | solution.py:551
  579.0 21.8 %collective-permute-start.50 = (bf16[512,256]{1,0:T(8,128)(2,1)}, bf16[512,256]{1,0:T(8,128)(2,1)}, u32[]{:S(2)}, u32[]{:S(2)}) collective-permute-start(bf16[512,256]{1,0:T(8,128)(2,1)} %get-tuple-element.299), channel_id=1, source_target_pairs={{0,2},{1,3},{2,0},{3,1},{4,6},{5,7},{6,4},{7,5},{8,10},{9,11},{10,... | collective-permute-start | bytes 786440 | tf_op jit(solution)/shard_map/ppermute | solution.py:551
  579.5 21.3 %collective-permute-start.49 = (bf16[512,256]{1,0:T(8,128)(2,1)}, bf16[512,256]{1,0:T(8,128)(2,1)}, u32[]{:S(2)}, u32[]{:S(2)}) collective-permute-start(bf16[512,256]{1,0:T(8,128)(2,1)} %get-tuple-element.300), channel_id=1, source_target_pairs={{0,1},{1,2},{2,3},{3,0},{4,5},{5,6},{6,7},{7,4},{8,9},{9,10},{10,1... | collective-permute-start | bytes 786440 | tf_op jit(solution)/shard_map/ppermute | solution.py:551
  585.3 22.0 %copy-start.1 = (bf16[512,2048]{1,0:T(8,128)(2,1)S(1)}, bf16[512,2048]{1,0:T(8,128)(2,1)}, u32[]{:S(2)}) copy-start(bf16[512,2048]{1,0:T(8,128)(2,1)} %param.21) | copy-start | bytes 6291460
  (91 other events, 496.8 us)
Sparse Core Ops, SparseCore 0:
  42.3 41.1 all-gather.4
  111.1 52.6 all-gather.6
  335.6 71.2 reduce-scatter.3
  410.6 80.0 reduce-scatter.5
  516.0 66.6 reduce-scatter.7

commit v5 on v4

--- a/solution.py
+++ b/solution.py
@@ -310,37 +310,11 @@
     )(half[None], x, weight, *given)
 
 
-def relay_kernel(index_ref, right_ref, left_ref, *refs):
-    to_right, to_left = refs[-2:]
-    if len(refs) == 2:
-        to_right[...], to_left[...] = right_ref[...], left_ref[...]
-    else:
-        to_right[...] = (right_ref[...].astype(f32) + refs[0][...].astype(f32)).astype(bf16)
-        to_left[...] = (left_ref[...].astype(f32) + refs[1][...].astype(f32)).astype(bf16)
-
-
 def relay(terms, rows, index, came):
-    width = terms.shape[1]
-    step = min(rows, 128)
-    steps = rows // step
-    block = pl.BlockSpec((step, width), lambda i, at: (i, 0))
-    return pl.pallas_call(
-        relay_kernel,
-        grid_spec=pltpu.PrefetchScalarGridSpec(
-            num_scalar_prefetch=1,
-            grid=(steps,),
-            in_specs=[
-                pl.BlockSpec((step, width), lambda i, at: (at[0] * steps + i, 0)),
-                pl.BlockSpec((step, width), lambda i, at: (at[1] * steps + i, 0)),
-                *[block] * len(came),
-            ],
-            out_specs=[block, block],
-        ),
-        out_shape=[jax.ShapeDtypeStruct((rows, width), bf16)] * 2,
-        compiler_params=pltpu.CompilerParams(vmem_limit_bytes=12 * MIB),
-        cost_estimate=COST,
-        name="relay",
-    )(index, terms, terms, *came)
+    sent = [lax.dynamic_slice_in_dim(terms, index[j] * rows, rows, axis=0) for j in range(2)]
+    if came:
+        sent = [(term.astype(f32) + value.astype(f32)).astype(bf16) for term, value in zip(sent, came)]
+    return sent
 
 
 def summed_back(term_ref, left_ref, right_ref, value_ref, gain_ref):

time: 624 us -> 614 us (0.984)
  other arithmetic: 45.4 us -> 63 us
  Pallas kernels: 142 us -> 125 us
  local copies, waits for them, and re-layouts: 68 us -> 54.3 us
  starting transfers between devices: 98.6 us -> 105 us
    convert_element_type x0 -> x6, other arithmetic: none -> 22.9 us  [relay(): (term.astype(f32) + value.astype(f32)).astype(bf16)]
    pallas_call x9 -> x0, Pallas kernels: 16.8 us -> none  [relay(): pl.pallas_call(relay_kernel, grid_spec=pltpu.PrefetchScalarGridSpec(num_s...]
    unnamed x196 -> x168, local copies, waits for them, and re-layouts: 47.3 us -> 30.9 us
    ppermute x9, waiting for transfers between devices: 6.65 us -> 15.1 us  [step(): lax.ppermute(sent[1], line.name, [(j, j - 1) for j in range(n - k, n)])]
  transfers between devices with their start and end apart: 57 -> 57, of which waited for: 20 -> 19; matrix products, arithmetic and copies ran while one was open for 24% -> 24% of each run, Pallas kernels for 22% -> 21%
where the time goes in v5:
time: 614 us; the launch traced here: 605 us
  waiting for transfers between devices  148 us (24%)
  Pallas kernels  125 us (20%)
  starting transfers between devices  105 us (17%)
  matrix products  79.2 us (13%)
  other arithmetic  63 us (10%)
  local copies, waits for them, and re-layouts  54.3 us (9%)
  between operations  18.9 us (3%)
  blocking collectives  11.6 us (2%)
    ppermute x9, waiting for transfers between devices, step(): lax.ppermute(right, line.name, [(j, j - 1) for j in range(1, n - k + 1)])  85.9 us
    dot_general x16, matrix products, dot(): lax.dot_general(left, right, (((left_dim,), (right_dim,)), ((), ())), pre...  79.2 us
    pallas_call x3, Pallas kernels, weight_grads(): pl.pallas_call(grads_kernel, grid=(steps,), in_specs=[pl.BlockSpec(memory...  40.6 us
    ppermute x9, starting transfers between devices, step(): lax.ppermute(sent[0], line.name, [(j, j + 1) for j in range(k)])  36.6 us
    unnamed x168, local copies, waits for them, and re-layouts  30.9 us
    convert_element_type x6, other arithmetic, relay(): (term.astype(f32) + value.astype(f32)).astype(bf16)  22.9 us
    ppermute x9, waiting for transfers between devices, step(): lax.ppermute(sent[0], line.name, [(j, j + 1) for j in range(k)])  18.6 us
    ppermute x9, starting transfers between devices, step(): lax.ppermute(left, line.name, [(j, j + 1) for j in range(k - 1, n - 1)])  17.2 us
  transfers between devices with their start and end apart: 57, of which 19 were waited for; matrix products, arithmetic and copies ran while one was open for 24% of the time, Pallas kernels for 21%

profile of v5, /device:TPU:0, one launch (start us, length us, event | category | flops | bytes accessed | tf_op | source)
XLA Modules:
  0.0 604.6 jit_solution(14386646061344479213)
XLA Ops:
  7.2 6.1 %collective-permute-start = (bf16[256,2048]{1,0:T(8,128)(2,1)}, bf16[256,2048]{1,0:T(8,128)(2,1)}, u32[]{:S(2)}, u32[]{:S(2)}) collective-permute-start(bf16[256,2048]{1,0:T(8,128)(2,1)} %value_ref.1), channel_id=1, source_target_pairs={{0,1},{1,2},{2,3},{4,5},{5,6},{6,7},{8,9},{9,10},{10,11},{12,13},{... | collective-permute-start | bytes 3145736 | tf_op jit(solution)/shard_map/ppermute | solution.py:546
  16.6 5.7 slice_bitcast_fusion.2
  25.1 5.0 fusion.1
  30.1 4.9 collective-permute-done
  35.0 5.1 collective-permute-done.1
  46.8 2.7 fusion.3
  49.5 35.5 %collective-permute-done.3 = bf16[256,2048]{1,0:T(8,128)(2,1)} collective-permute-done((bf16[256,2048]{1,0:T(8,128)(2,1)}, bf16[256,2048]{1,0:T(8,128)(2,1)}, u32[]{:S(2)}, u32[]{:S(2)}) %collective-permute-start.3) | collective-permute-done | bytes 1048608 | tf_op jit(solution)/shard_map/ppermute | solution.py:547
  90.9 2.8 fusion.5
  94.7 15.3 %collective-permute-done.5 = bf16[256,2048]{1,0:T(8,128)(2,1)S(1)} collective-permute-done((bf16[256,2048]{1,0:T(8,128)(2,1)}, bf16[256,2048]{1,0:T(8,128)(2,1)S(1)}, u32[]{:S(2)}, u32[]{:S(2)}) %collective-permute-start.5) | collective-permute-done | bytes 1048608 | tf_op jit(solution)/shard_map/ppermute | solution.py:547
  120.9 2.9 fusion.7.q_ref.k_ref.v_ref
  123.8 9.1 %attend.1 = bf16[1024,512]{1,0:T(8,128)(2,1)S(1)} custom-call(bf16[1024,1536]{1,0:T(8,128)(2,1)} %fusion.7.q_ref.k_ref.v_ref, bf16[1024,1536]{1,0:T(8,128)(2,1)} %fusion.7.q_ref.k_ref.v_ref, bf16[1024,1536]{1,0:T(8,128)(2,1)} %fusion.7.q_ref.k_ref.v_ref, s32[1024,1]{1,0:T(8,128)S(1)} %copy-done.22, s32[1,1024]{1,0:T(1,128)S(1)} %bitcast.48), custom_call_target="tpu_custom_call" | custom-call | flops 1048576 | bytes 65536 | tf_op jit(solution)/shard_map/attend/pallas_call | solution.py:49
  134.5 3.7 collective-permute-done.7
  144.1 5.7 add_add_fusion
  150.5 2.9 collective-permute-start.11
  154.7 2.9 collective-permute-start.12
  159.1 3.8 collective-permute-done.9
  170.2 6.1 %fusion.35.grad_ref = f32[512,2048]{1,0:T(8,128)} fusion(bf16[2048,2048]{1,0:T(8,128)(2,1)S(1)} %bitcast.38, bf16[1024,2048]{1,0:T(8,128)(2,1)S(1)} %select_dynamic-update-slice_fusion.2, s32[]{:T(128)S(6)} %select_n.455), kind=kOutput, calls=%fused_computation.80 | convolution fusion | flops 4294967296 | bytes 14680068 | tf_op jit(solution)/shard_map/dot_general | solution.py:20
  176.2 14.1 %collective-permute-done.14 = bf16[1024,512]{1,0:T(8,128)(2,1)} collective-permute-done((bf16[1024,512]{1,0:T(8,128)(2,1)S(1)}, bf16[1024,512]{1,0:T(8,128)(2,1)}, u32[]{:S(2)}, u32[]{:S(2)}) %collective-permute-start.14) | collective-permute-done | bytes 1048608 | tf_op jit(solution)/shard_map/ppermute | solution.py:547
  196.2 6.4 %convolution_add_fusion.1 = f32[1024,2048]{1,0:T(8,128)S(1)} fusion(f32[1024,2048]{1,0:T(8,128)} %add_add_fusion, bf16[1024,512]{1,0:T(8,128)(2,1)S(1)} %broadcast_select_fusion, bf16[2048,2048]{1,0:T(8,128)(2,1)} %bitcast.51, s32[]{:T(128)S(6)} %select_n.445), kind=kOutput, calls=%fused_computation.5 | convolution fusion | flops 2149580800 | bytes 19922948 | tf_op jit(solution)/shard_map/dot_general | solution.py:20
  202.6 7.4 %convolution_add_fusion.sum_ref = f32[1024,2048]{1,0:T(8,128)} fusion(f32[1024,2048]{1,0:T(8,128)S(1)} %convolution_add_fusion.1, bf16[1024,512]{1,0:T(8,128)(2,1)S(1)} %select_select_fusion.1, bf16[2048,2048]{1,0:T(8,128)(2,1)} %bitcast.52, s32[]{:T(128)S(6)} %select_n.462), kind=kOutput, calls=%fused_computation.4 | convolution fusion | flops 2149580800 | bytes 19922948 | tf_op jit(solution)/shard_map/dot_general | solution.py:20
  210.0 5.9 collective-permute-done.16
  220.7 9.4 %mix.1 = (f32[1024,2048]{1,0:T(8,128)}, bf16[1024,2048]{1,0:T(8,128)(2,1)S(1)}) custom-call(s32[1]{0:T(128)} %bitcast.index_ref, f32[1024,2048]{1,0:T(8,128)} %convolution_add_fusion.sum_ref, bf16[1024,512]{1,0:T(8,128)(2,1)S(1)} %select_select_fusion.heads_ref, bf16[2048,2048]{1,0:T(8,128)(2,1)} %bitcast.53, f32[1,2048]{1,0:T(1,128)S(1)} %get-tuple-element.321.gain_ref, ...), custom_call_target="tpu_custom_call" | custom-call | flops 1048576 | bytes 65536 | tf_op jit(solution)/shard_map/mix/pallas_call | solution.py:151
  232.1 15.6 %feed_up.1 = (f32[1024,2048]{1,0:T(8,128)}, bf16[1024,2048]{1,0:T(8,128)(2,1)S(1)}) custom-call(bf16[1024,2048]{1,0:T(8,128)(2,1)} %copy-done.14, bf16[2048,2048]{1,0:T(8,128)(2,1)} %w_ref.2, f32[1,2048]{1,0:T(1,128)S(1)} %bitcast.50), custom_call_target="tpu_custom_call" | custom-call | flops 1048576 | bytes 65536 | tf_op jit(solution)/shard_map/feed_up/pallas_call | solution.py:180
  249.8 12.7 %convolution_convert_fusion.1 = bf16[1024,2048]{1,0:T(8,128)(2,1)} fusion(bf16[1024,2048]{1,0:T(8,128)(2,1)S(1)} %get-tuple-element.188.right_ref, bf16[2048,2048]{1,0:T(8,128)(2,1)} %w_ref.3), kind=kOutput, calls=%fused_computation.7 | convolution fusion | flops 8592031744 | bytes 16777216 | tf_op jit(solution)/shard_map/dot_general | solution.py:20
  262.5 2.7 slope_back.1.refs_0_
  272.5 3.2 collective-permute-start.21
  278.5 4.9 copy-done.21
  283.4 7.3 %hidden_back.1.right_ref = bf16[1024,2048]{1,0:T(8,128)(2,1)S(1)} custom-call(s32[1]{0:T(128)} %bitcast.14.index_ref, bf16[1024,2048]{1,0:T(8,128)(2,1)S(1)} %select_dynamic-update-slice_fusion.cot_ref.left_ref, f32[1024,2048]{1,0:T(8,128)S(1)} %copy-done.12, bf16[2048,2048]{1,0:T(8,128)(2,1)S(1)} %copy-done.21, ...), custom_call_target="tpu_custom_call", output_to_operand_aliasing={{}: (4, {})} | custom-call | flops 1048576 | bytes 65536 | tf_op jit(solution)/shard_map/hidden_back/pallas_call | solution.py:205
  290.7 9.1 %convolution_convert_fusion.term_ref = bf16[1024,2048]{1,0:T(8,128)(2,1)S(1)} fusion(bf16[1024,2048]{1,0:T(8,128)(2,1)S(1)} %hidden_back.1.right_ref, bf16[2048,2048]{1,0:T(8,128)(2,1)S(1)} %bitcast.58), kind=kOutput, calls=%fused_computation.6 | convolution fusion | flops 8592031744 | bytes 16777216 | tf_op jit(solution)/shard_map/dot_general | solution.py:20
  308.4 14.0 %weight_grads.3 = bf16[2048,2048]{1,0:T(8,128)(2,1)} custom-call(f32[1]{0:T(128)} %div.35.factor_ref, bf16[1024,2048]{1,0:T(8,128)(2,1)S(1)} %copy-done.15, bf16[1024,2048]{1,0:T(8,128)(2,1)} %copy-done.6), custom_call_target="tpu_custom_call" | custom-call | flops 1048576 | bytes 65536 | tf_op jit(solution)/shard_map/weight_grads/pallas_call | solution.py:265
  323.3 4.0 add_convert_fusion.17
  329.0 5.3 collective-permute-start.25
  334.3 3.0 copy-done.11
  337.3 14.2 %weight_grads.4 = bf16[2048,2048]{1,0:T(8,128)(2,1)} custom-call(f32[1]{0:T(128)} %div.35.factor_ref, bf16[1024,2048]{1,0:T(8,128)(2,1)S(1)} %copy-done.11, bf16[1024,2048]{1,0:T(8,128)(2,1)} %copy-done.24), custom_call_target="tpu_custom_call" | custom-call | flops 1048576 | bytes 65536 | tf_op jit(solution)/shard_map/weight_grads/pallas_call | solution.py:265
  351.5 5.1 add_convert_fusion.15
  358.0 4.6 collective-permute-start.27
  362.6 3.0 convert_reduce_fusion
  365.6 11.0 %collective-permute-done.28.right_ref = bf16[256,2048]{1,0:T(8,128)(2,1)S(1)} collective-permute-done((bf16[256,2048]{1,0:T(8,128)(2,1)}, bf16[256,2048]{1,0:T(8,128)(2,1)S(1)}, u32[]{:S(2)}, u32[]{:S(2)}) %collective-permute-start.28) | collective-permute-done | bytes 1048608 | tf_op jit(solution)/shard_map/ppermute | solution.py:579
  378.3 3.3 add_convert_fusion.14
  381.7 5.2 collective-permute-start.29
  391.0 5.2 middle_back.1
  398.8 4.5 multiply_convert_fusion
  418.0 3.2 add_convert_fusion.10
  421.2 2.9 add_convert_fusion.12
  424.1 7.1 %collective-permute-done.32 = bf16[256,512]{1,0:T(8,128)(2,1)S(1)} collective-permute-done((bf16[256,512]{1,0:T(8,128)(2,1)S(1)}, bf16[256,512]{1,0:T(8,128)(2,1)S(1)}, u32[]{:S(2)}, u32[]{:S(2)}) %collective-permute-start.32) | collective-permute-done | bytes 262176 | tf_op jit(solution)/shard_map/ppermute | solution.py:514
  431.2 3.2 add_convert_fusion.8
  439.0 15.7 %attend_back.1.x_ref.right_ref = bf16[1024,1536]{1,0:T(8,128)(2,1)S(1)} custom-call(bf16[1024,1536]{1,0:T(8,128)(2,1)} %fusion.7.q_ref.k_ref.v_ref, bf16[1024,1536]{1,0:T(8,128)(2,1)} %fusion.7.q_ref.k_ref.v_ref, bf16[1024,1536]{1,0:T(8,128)(2,1)} %fusion.7.q_ref.k_ref.v_ref, bf16[1024,512]{1,0:T(8,128)(2,1)S(1)} %constant_dynamic-update-slice_fusion.grad_ref, ...), custom_call_target="tpu_custom_call" | custom-call | flops 1048576 | bytes 65536 | tf_op jit(solution)/shard_map/attend_back/pallas_call | solution.py:94
  454.8 4.2 half_product.2.refs_0_
  459.0 4.1 collective-permute-done.36
  469.3 4.9 collective-permute-start.37
  474.2 4.2 half_product.3.term_ref
  478.4 4.1 gain_sums.1
  484.6 12.3 %weight_grads.5 = bf16[2048,1536]{1,0:T(8,128)(2,1)} custom-call(f32[1]{0:T(128)} %div.35.factor_ref, bf16[1024,2048]{1,0:T(8,128)(2,1)} %get-tuple-element.227.left_ref, bf16[1024,1536]{1,0:T(8,128)(2,1)S(1)} %copy-done.5), custom_call_target="tpu_custom_call" | custom-call | flops 1048576 | bytes 65536 | tf_op jit(solution)/shard_map/weight_grads/pallas_call | solution.py:265
  497.1 5.1 add_convert_fusion.5
  504.6 4.5 collective-permute-start.42
  513.8 16.1 %collective-permute-done.42 = bf16[256,2048]{1,0:T(8,128)(2,1)S(1)} collective-permute-done((bf16[256,2048]{1,0:T(8,128)(2,1)}, bf16[256,2048]{1,0:T(8,128)(2,1)S(1)}, u32[]{:S(2)}, u32[]{:S(2)}) %collective-permute-start.42) | collective-permute-done | bytes 1048608 | tf_op jit(solution)/shard_map/ppermute | solution.py:578
  533.4 5.0 collective-permute-start.44
  540.4 3.8 collective-permute-start.48
  544.2 4.2 add_convert_fusion
  548.4 11.8 %collective-permute-done.48 = f32[12288]{0:T(1024)S(1)} collective-permute-done((f32[12288]{0:T(1024)S(1)}, f32[12288]{0:T(1024)S(1)}, u32[]{:S(2)}, u32[]{:S(2)}) %collective-permute-start.48) | collective-permute-done | bytes 49184 | tf_op jit(solution)/shard_map/ppermute | solution.py:586
  563.4 5.1 collective-permute-start.51
  570.3 3.9 input_back.1
  574.2 11.6 %all_gather.19 = f32[8,8,1920]{2,1,0:T(8,128)} all-gather(f32[1,8,1920]{2,1,0:T(8,128)S(1)} %reshape.101), channel_id=1, replica_groups=mesh['dp'=8,'mp'=4] {'dp'}, dimensions={0}, use_global_device_ids=true | all-gather | bytes 552960 | tf_op jit(solution)/shard_map/all_gather | solution.py:871
  588.2 2.8 present.1
  (358 shorter events, 144.5 us)
Async XLA Ops:
  7.2 103.8 %all-gather.5.cloned.1.call-start = ((), (), s32[]{:S(2)}) async-start(), calls=%async_computation.6 | async-start | bytes 1310720 | tf_op jit(solution)/shard_map/all_gather | solution.py:728
  7.2 27.8 %collective-permute-start = (bf16[256,2048]{1,0:T(8,128)(2,1)}, bf16[256,2048]{1,0:T(8,128)(2,1)}, u32[]{:S(2)}, u32[]{:S(2)}) collective-permute-start(bf16[256,2048]{1,0:T(8,128)(2,1)} %value_ref.1), channel_id=1, source_target_pairs={{0,1},{1,2},{2,3},{4,5},{5,6},{6,7},{8,9},{9,10},{10,11},{12,13},{... | collective-permute-start | bytes 3145736 | tf_op jit(solution)/shard_map/ppermute | solution.py:546
  13.3 26.8 %collective-permute-start.1 = (bf16[256,2048]{1,0:T(8,128)(2,1)}, bf16[256,2048]{1,0:T(8,128)(2,1)}, u32[]{:S(2)}, u32[]{:S(2)}) collective-permute-start(bf16[256,2048]{1,0:T(8,128)(2,1)} %value_ref.1), channel_id=1, source_target_pairs={{1,0},{2,1},{3,2},{5,4},{6,5},{7,6},{9,8},{10,9},{11,10},{13,12},{... | collective-permute-start | bytes 3145736 | tf_op jit(solution)/shard_map/ppermute | solution.py:547
  40.1 9.4 %collective-permute-start.2 = (bf16[256,2048]{1,0:T(8,128)(2,1)}, bf16[256,2048]{1,0:T(8,128)(2,1)S(1)}, u32[]{:S(2)}, u32[]{:S(2)}) collective-permute-start(bf16[256,2048]{1,0:T(8,128)(2,1)} %collective-permute-done), channel_id=1, source_target_pairs={{1,2},{2,3},{5,6},{6,7},{9,10},{10,11},{13,14},{14,15},{17,18},{18... | collective-permute-start | bytes 3145736 | tf_op jit(solution)/shard_map/ppermute | solution.py:546
  40.9 44.2 %collective-permute-start.3 = (bf16[256,2048]{1,0:T(8,128)(2,1)}, bf16[256,2048]{1,0:T(8,128)(2,1)}, u32[]{:S(2)}, u32[]{:S(2)}) collective-permute-start(bf16[256,2048]{1,0:T(8,128)(2,1)} %collective-permute-done.1), channel_id=1, source_target_pairs={{1,0},{2,1},{5,4},{6,5},{9,8},{10,9},{13,12},{14,13},{17,16},{18,1... | collective-permute-start | bytes 3145736 | tf_op jit(solution)/shard_map/ppermute | solution.py:547
  42.2 154.0 %all-gather.7.cloned.1.call-start = ((), (), s32[]{:S(2)}) async-start(), calls=%async_computation.7 | async-start | bytes 9437184 | tf_op jit(solution)/shard_map/all_gather | solution.py:733
  85.0 8.7 %collective-permute-start.4 = (bf16[256,2048]{1,0:T(8,128)(2,1)S(1)}, bf16[256,2048]{1,0:T(8,128)(2,1)S(1)}, u32[]{:S(2)}, u32[]{:S(2)}) collective-permute-start(bf16[256,2048]{1,0:T(8,128)(2,1)S(1)} %collective-permute-done.2), channel_id=1, source_target_pairs={{2,3},{6,7},{10,11},{14,15},{18,19},{22,23},{26,27},{30,31}} | collective-permute-start | bytes 3145736 | tf_op jit(solution)/shard_map/ppermute | solution.py:546
  85.7 24.3 %collective-permute-start.5 = (bf16[256,2048]{1,0:T(8,128)(2,1)}, bf16[256,2048]{1,0:T(8,128)(2,1)S(1)}, u32[]{:S(2)}, u32[]{:S(2)}) collective-permute-start(bf16[256,2048]{1,0:T(8,128)(2,1)} %collective-permute-done.3), channel_id=1, source_target_pairs={{1,0},{5,4},{9,8},{13,12},{17,16},{21,20},{25,24},{29,28}} | collective-permute-start | bytes 3145736 | tf_op jit(solution)/shard_map/ppermute | solution.py:547
  111.0 320.1 %reduce-scatter.4.cloned.1.call-start = ((), (), s32[]{:S(2)}) async-start(), calls=%async_computation.3 | async-start | bytes 9437184 | tf_op jit(solution)/shard_map/reduce_scatter | solution.py:794
  113.6 20.9 %collective-permute-start.6 = (bf16[256,2048]{1,0:T(8,128)(2,1)S(1)}, bf16[256,2048]{1,0:T(8,128)(2,1)S(1)}, u32[]{:S(2)}, u32[]{:S(2)}) collective-permute-start(bf16[256,2048]{1,0:T(8,128)(2,1)S(1)} %copy-done.13), channel_id=1, source_target_pairs={{0,1},{1,2},{2,3},{4,5},{5,6},{6,7},{8,9},{9,10},{10,11},{12,13},{... | collective-permute-start | bytes 3145736 | tf_op jit(solution)/shard_map/ppermute | solution.py:546
  115.2 23.0 %collective-permute-start.7 = (bf16[256,2048]{1,0:T(8,128)(2,1)S(1)}, bf16[256,2048]{1,0:T(8,128)(2,1)}, u32[]{:S(2)}, u32[]{:S(2)}) collective-permute-start(bf16[256,2048]{1,0:T(8,128)(2,1)S(1)} %copy-done.13), channel_id=1, source_target_pairs={{1,0},{2,1},{3,2},{5,4},{6,5},{7,6},{9,8},{10,9},{11,10},{13,12},{... | collective-permute-start | bytes 3145736 | tf_op jit(solution)/shard_map/ppermute | solution.py:547
  134.5 31.2 %copy-start.57 = (bf16[256,2048]{1,0:T(8,128)(2,1)}, bf16[256,2048]{1,0:T(8,128)(2,1)S(1)}, u32[]{:S(2)}) copy-start(bf16[256,2048]{1,0:T(8,128)(2,1)S(1)} %collective-permute-done.6) | copy-start | bytes 3145732
  138.2 20.8 %collective-permute-start.8 = (bf16[1024,512]{1,0:T(8,128)(2,1)S(1)}, bf16[1024,512]{1,0:T(8,128)(2,1)S(1)}, u32[]{:S(2)}, u32[]{:S(2)}) collective-permute-start(bf16[1024,512]{1,0:T(8,128)(2,1)S(1)} %attend.1), channel_id=1, source_target_pairs={{0,1},{1,2},{2,3},{4,5},{5,6},{6,7},{8,9},{9,10},{10,11},{12,13},{... | collective-permute-start | bytes 3145736 | tf_op jit(solution)/shard_map/ppermute | solution.py:546
  140.6 22.2 %collective-permute-start.9 = (bf16[1024,512]{1,0:T(8,128)(2,1)S(1)}, bf16[1024,512]{1,0:T(8,128)(2,1)S(1)}, u32[]{:S(2)}, u32[]{:S(2)}) collective-permute-start(bf16[1024,512]{1,0:T(8,128)(2,1)S(1)} %attend.1), channel_id=1, source_target_pairs={{1,0},{2,1},{3,2},{5,4},{6,5},{7,6},{9,8},{10,9},{11,10},{13,12},{... | collective-permute-start | bytes 3145736 | tf_op jit(solution)/shard_map/ppermute | solution.py:547
  141.9 7.9 %collective-permute-start.10 = (f32[1]{0:T(128)}, f32[1]{0:T(128)}, u32[]{:S(2)}, u32[]{:S(2)}) collective-permute-start(f32[1]{0:T(128)} %convert_element_type.288), channel_id=1, source_target_pairs={{0,4},{4,0},{8,12},{12,8},{16,20},{20,16},{24,28},{28,24},{1,5},{5... | collective-permute-start | bytes 20 | tf_op jit(solution)/shard_map/ppermute | solution.py:586
  142.8 27.4 %slice-start = ((s8[8388608]{0:T(1024)(128)(4,1)}), s8[4194304]{0:T(1024)(128)(4,1)S(1)}, s32[]{:S(2)}) async-start(s8[8388608]{0:T(1024)(128)(4,1)} %bitcast.37), calls=%async_computation.8 | async-start | bytes 8388608
  144.1 26.1 %slice-start.1 = ((s8[8388608]{0:T(1024)(128)(4,1)}), s8[4194304]{0:T(1024)(128)(4,1)S(1)}, s32[]{:S(2)}) async-start(s8[8388608]{0:T(1024)(128)(4,1)} %bitcast.37), calls=%async_computation.9 | async-start | bytes 8388608
  150.5 3.6 collective-permute-start.11
  154.7 3.6 collective-permute-start.12
  162.8 13.4 %collective-permute-start.13 = (bf16[1024,512]{1,0:T(8,128)(2,1)S(1)}, bf16[1024,512]{1,0:T(8,128)(2,1)}, u32[]{:S(2)}, u32[]{:S(2)}) collective-permute-start(bf16[1024,512]{1,0:T(8,128)(2,1)S(1)} %collective-permute-done.8), channel_id=1, source_target_pairs={{1,2},{2,3},{5,6},{6,7},{9,10},{10,11},{13,14},{14,15},{17,18},{18... | collective-permute-start | bytes 3145736 | tf_op jit(solution)/shard_map/ppermute | solution.py:546
  164.5 25.9 %collective-permute-start.14 = (bf16[1024,512]{1,0:T(8,128)(2,1)S(1)}, bf16[1024,512]{1,0:T(8,128)(2,1)}, u32[]{:S(2)}, u32[]{:S(2)}) collective-permute-start(bf16[1024,512]{1,0:T(8,128)(2,1)S(1)} %collective-permute-done.9), channel_id=1, source_target_pairs={{1,0},{2,1},{5,4},{6,5},{9,8},{10,9},{13,12},{14,13},{17,16},{18,1... | collective-permute-start | bytes 3145736 | tf_op jit(solution)/shard_map/ppermute | solution.py:547
  190.3 19.6 %collective-permute-start.15 = (bf16[1024,512]{1,0:T(8,128)(2,1)}, bf16[1024,512]{1,0:T(8,128)(2,1)}, u32[]{:S(2)}, u32[]{:S(2)}) collective-permute-start(bf16[1024,512]{1,0:T(8,128)(2,1)} %collective-permute-done.13), channel_id=1, source_target_pairs={{2,3},{6,7},{10,11},{14,15},{18,19},{22,23},{26,27},{30,31}} | collective-permute-start | bytes 3145736 | tf_op jit(solution)/shard_map/ppermute | solution.py:546
  192.0 23.9 %collective-permute-start.16 = (bf16[1024,512]{1,0:T(8,128)(2,1)}, bf16[1024,512]{1,0:T(8,128)(2,1)}, u32[]{:S(2)}, u32[]{:S(2)}) collective-permute-start(bf16[1024,512]{1,0:T(8,128)(2,1)} %collective-permute-done.14), channel_id=1, source_target_pairs={{1,0},{5,4},{9,8},{13,12},{17,16},{21,20},{25,24},{29,28}} | collective-permute-start | bytes 3145736 | tf_op jit(solution)/shard_map/ppermute | solution.py:547
  215.9 31.8 %collective-permute-start.17 = (bf16[256,2048]{1,0:T(8,128)(2,1)S(1)}, bf16[256,2048]{1,0:T(8,128)(2,1)}, u32[]{:S(2)}, u32[]{:S(2)}) collective-permute-start(bf16[256,2048]{1,0:T(8,128)(2,1)S(1)} %copy-done.58), channel_id=1, source_target_pairs={{1,2},{2,3},{5,6},{6,7},{9,10},{10,11},{13,14},{14,15},{17,18},{18... | collective-permute-start | bytes 3145736 | tf_op jit(solution)/shard_map/ppermute | solution.py:546
  217.6 30.1 %collective-permute-start.18 = (bf16[256,2048]{1,0:T(8,128)(2,1)}, bf16[256,2048]{1,0:T(8,128)(2,1)}, u32[]{:S(2)}, u32[]{:S(2)}) collective-permute-start(bf16[256,2048]{1,0:T(8,128)(2,1)} %collective-permute-done.7), channel_id=1, source_target_pairs={{1,0},{2,1},{5,4},{6,5},{9,8},{10,9},{13,12},{14,13},{17,16},{18,1... | collective-permute-start | bytes 3145736 | tf_op jit(solution)/shard_map/ppermute | solution.py:547
  247.7 21.2 %collective-permute-start.19 = (bf16[256,2048]{1,0:T(8,128)(2,1)}, bf16[256,2048]{1,0:T(8,128)(2,1)S(1)}, u32[]{:S(2)}, u32[]{:S(2)}) collective-permute-start(bf16[256,2048]{1,0:T(8,128)(2,1)} %collective-permute-done.17), channel_id=1, source_target_pairs={{2,3},{6,7},{10,11},{14,15},{18,19},{22,23},{26,27},{30,31}} | collective-permute-start | bytes 3145736 | tf_op jit(solution)/shard_map/ppermute | solution.py:546
  248.5 22.9 %collective-permute-start.20 = (bf16[256,2048]{1,0:T(8,128)(2,1)}, bf16[256,2048]{1,0:T(8,128)(2,1)S(1)}, u32[]{:S(2)}, u32[]{:S(2)}) collective-permute-start(bf16[256,2048]{1,0:T(8,128)(2,1)} %collective-permute-done.18), channel_id=1, source_target_pairs={{1,0},{5,4},{9,8},{13,12},{17,16},{21,20},{25,24},{29,28}} | collective-permute-start | bytes 3145736 | tf_op jit(solution)/shard_map/ppermute | solution.py:547
  266.4 24.3 %slice-start.4 = ((s8[8388608]{0:T(1024)(128)(4,1)}), s8[4194304]{0:T(1024)(128)(4,1)S(1)}, s32[]{:S(2)}) async-start(s8[8388608]{0:T(1024)(128)(4,1)} %bitcast.57), calls=%async_computation.12 | async-start | bytes 8388608
  272.5 27.4 %collective-permute-start.21 = (bf16[256,2048]{1,0:T(8,128)(2,1)}, bf16[256,2048]{1,0:T(8,128)(2,1)}, u32[]{:S(2)}, u32[]{:S(2)}) collective-permute-start(bf16[256,2048]{1,0:T(8,128)(2,1)} %get-tuple-element.278), channel_id=1, source_target_pairs={{0,1},{4,5},{8,9},{12,13},{16,17},{20,21},{24,25},{28,29}} | collective-permute-start | bytes 3145736 | tf_op jit(solution)/shard_map/ppermute | solution.py:578
  275.7 24.2 %collective-permute-start.22 = (bf16[256,2048]{1,0:T(8,128)(2,1)S(1)}, bf16[256,2048]{1,0:T(8,128)(2,1)}, u32[]{:S(2)}, u32[]{:S(2)}) collective-permute-start(bf16[256,2048]{1,0:T(8,128)(2,1)S(1)} %get-tuple-element.279), channel_id=1, source_target_pairs={{3,2},{7,6},{11,10},{15,14},{19,18},{23,22},{27,26},{31,30}} | collective-permute-start | bytes 3145736 | tf_op jit(solution)/shard_map/ppermute | solution.py:579
  302.1 20.3 %collective-permute-start.24 = (bf16[256,2048]{1,0:T(8,128)(2,1)}, bf16[256,2048]{1,0:T(8,128)(2,1)}, u32[]{:S(2)}, u32[]{:S(2)}) collective-permute-start(bf16[256,2048]{1,0:T(8,128)(2,1)} %get-tuple-element.276), channel_id=1, source_target_pairs={{3,2},{7,6},{11,10},{15,14},{19,18},{23,22},{27,26},{31,30}} | collective-permute-start | bytes 3145736 | tf_op jit(solution)/shard_map/ppermute | solution.py:579
  303.7 19.5 %collective-permute-start.23 = (bf16[256,2048]{1,0:T(8,128)(2,1)S(1)}, bf16[256,2048]{1,0:T(8,128)(2,1)}, u32[]{:S(2)}, u32[]{:S(2)}) collective-permute-start(bf16[256,2048]{1,0:T(8,128)(2,1)S(1)} %get-tuple-element.277), channel_id=1, source_target_pairs={{0,1},{4,5},{8,9},{12,13},{16,17},{20,21},{24,25},{28,29}} | collective-permute-start | bytes 3145736 | tf_op jit(solution)/shard_map/ppermute | solution.py:578
  327.2 169.8 %reduce-scatter.6.cloned.1.call-start = ((), (), s32[]{:S(2)}) async-start(), calls=%async_computation.4 | async-start | bytes 9437184 | tf_op jit(solution)/shard_map/reduce_scatter | solution.py:794
  327.3 24.2 %collective-permute-start.26 = (bf16[256,2048]{1,0:T(8,128)(2,1)}, bf16[256,2048]{1,0:T(8,128)(2,1)}, u32[]{:S(2)}, u32[]{:S(2)}) collective-permute-start(bf16[256,2048]{1,0:T(8,128)(2,1)} %get-tuple-element.274), channel_id=1, source_target_pairs={{2,1},{3,2},{6,5},{7,6},{10,9},{11,10},{14,13},{15,14},{18,17},{19... | collective-permute-start | bytes 3145736 | tf_op jit(solution)/shard_map/ppermute | solution.py:579
  329.0 22.6 %collective-permute-start.25 = (bf16[256,2048]{1,0:T(8,128)(2,1)S(1)}, bf16[256,2048]{1,0:T(8,128)(2,1)}, u32[]{:S(2)}, u32[]{:S(2)}) collective-permute-start(bf16[256,2048]{1,0:T(8,128)(2,1)S(1)} %get-tuple-element.275), channel_id=1, source_target_pairs={{0,1},{1,2},{4,5},{5,6},{8,9},{9,10},{12,13},{13,14},{16,17},{17,1... | collective-permute-start | bytes 3145736 | tf_op jit(solution)/shard_map/ppermute | solution.py:578
  356.6 229.2 %reduce-scatter.8.cloned.1.call-start = ((), (), s32[]{:S(2)}) async-start(), calls=%async_computation.5 | async-start | bytes 7077888 | tf_op jit(solution)/shard_map/reduce_scatter | solution.py:794
  356.7 20.0 %collective-permute-start.28 = (bf16[256,2048]{1,0:T(8,128)(2,1)}, bf16[256,2048]{1,0:T(8,128)(2,1)S(1)}, u32[]{:S(2)}, u32[]{:S(2)}) collective-permute-start(bf16[256,2048]{1,0:T(8,128)(2,1)} %get-tuple-element.272), channel_id=1, source_target_pairs={{1,0},{2,1},{3,2},{5,4},{6,5},{7,6},{9,8},{10,9},{11,10},{13,12},{... | collective-permute-start | bytes 3145736 | tf_op jit(solution)/shard_map/ppermute | solution.py:579
  358.0 20.3 %collective-permute-start.27 = (bf16[256,2048]{1,0:T(8,128)(2,1)}, bf16[256,2048]{1,0:T(8,128)(2,1)S(1)}, u32[]{:S(2)}, u32[]{:S(2)}) collective-permute-start(bf16[256,2048]{1,0:T(8,128)(2,1)} %get-tuple-element.273), channel_id=1, source_target_pairs={{0,1},{1,2},{2,3},{4,5},{5,6},{6,7},{8,9},{9,10},{10,11},{12,13},{... | collective-permute-start | bytes 3145736 | tf_op jit(solution)/shard_map/ppermute | solution.py:578
  362.6 33.6 %slice-start.2 = ((s8[8388608]{0:T(1024)(128)(4,1)}), s8[4194304]{0:T(1024)(128)(4,1)S(1)}, s32[]{:S(2)}) async-start(s8[8388608]{0:T(1024)(128)(4,1)} %bitcast.54), calls=%async_computation.10 | async-start | bytes 8388608
  381.7 21.7 %collective-permute-start.29 = (bf16[256,2048]{1,0:T(8,128)(2,1)S(1)}, bf16[256,2048]{1,0:T(8,128)(2,1)}, u32[]{:S(2)}, u32[]{:S(2)}) collective-permute-start(bf16[256,2048]{1,0:T(8,128)(2,1)S(1)} %get-tuple-element.270), channel_id=1, source_target_pairs={{0,1},{1,2},{4,5},{5,6},{8,9},{9,10},{12,13},{13,14},{16,17},{17,1... | collective-permute-start | bytes 3145736 | tf_op jit(solution)/shard_map/ppermute | solution.py:578
  386.9 16.4 %collective-permute-start.30 = (bf16[256,2048]{1,0:T(8,128)(2,1)S(1)}, bf16[256,2048]{1,0:T(8,128)(2,1)}, u32[]{:S(2)}, u32[]{:S(2)}) collective-permute-start(bf16[256,2048]{1,0:T(8,128)(2,1)S(1)} %get-tuple-element.271), channel_id=1, source_target_pairs={{2,1},{3,2},{6,5},{7,6},{10,9},{11,10},{14,13},{15,14},{18,17},{19... | collective-permute-start | bytes 3145736 | tf_op jit(solution)/shard_map/ppermute | solution.py:579
  403.3 7.6 %collective-permute-start.34 = (bf16[2048,1024]{1,0:T(8,128)(2,1)}, bf16[2048,1024]{1,0:T(8,128)(2,1)}, u32[]{:S(2)}, u32[]{:S(2)}) collective-permute-start(bf16[2048,1024]{1,0:T(8,128)(2,1)} %multiply_convert_fusion), channel_id=1, source_target_pairs={{0,4},{4,0},{8,12},{12,8},{16,20},{20,16},{24,28},{28,24},{1,5},{5... | collective-permute-start | bytes 12582920 | tf_op jit(solution)/shard_map/ppermute | solution.py:586
  403.7 20.4 %collective-permute-start.33 = (bf16[256,512]{1,0:T(8,128)(2,1)S(1)}, bf16[256,512]{1,0:T(8,128)(2,1)S(1)}, u32[]{:S(2)}, u32[]{:S(2)}) collective-permute-start(bf16[256,512]{1,0:T(8,128)(2,1)S(1)} %get-tuple-element.291), channel_id=1, source_target_pairs={{0,3},{1,0},{2,1},{3,2},{4,7},{5,4},{6,5},{7,6},{8,11},{9,8},{10,9... | collective-permute-start | bytes 786440 | tf_op jit(solution)/shard_map/ppermute | solution.py:514
  405.8 25.3 %collective-permute-start.32 = (bf16[256,512]{1,0:T(8,128)(2,1)S(1)}, bf16[256,512]{1,0:T(8,128)(2,1)S(1)}, u32[]{:S(2)}, u32[]{:S(2)}) collective-permute-start(bf16[256,512]{1,0:T(8,128)(2,1)S(1)} %get-tuple-element.292), channel_id=1, source_target_pairs={{0,2},{1,3},{2,0},{3,1},{4,6},{5,7},{6,4},{7,5},{8,10},{9,11},{10,... | collective-permute-start | bytes 786440 | tf_op jit(solution)/shard_map/ppermute | solution.py:514
  407.6 23.5 %collective-permute-start.31 = (bf16[256,512]{1,0:T(8,128)(2,1)S(1)}, bf16[256,512]{1,0:T(8,128)(2,1)S(1)}, u32[]{:S(2)}, u32[]{:S(2)}) collective-permute-start(bf16[256,512]{1,0:T(8,128)(2,1)S(1)} %get-tuple-element.293), channel_id=1, source_target_pairs={{0,1},{1,2},{2,3},{3,0},{4,5},{5,6},{6,7},{7,4},{8,9},{9,10},{10,1... | collective-permute-start | bytes 786440 | tf_op jit(solution)/shard_map/ppermute | solution.py:514
  434.4 24.5 %collective-permute-start.35 = (bf16[256,2048]{1,0:T(8,128)(2,1)S(1)}, bf16[256,2048]{1,0:T(8,128)(2,1)S(1)}, u32[]{:S(2)}, u32[]{:S(2)}) collective-permute-start(bf16[256,2048]{1,0:T(8,128)(2,1)S(1)} %get-tuple-element.264), channel_id=1, source_target_pairs={{0,1},{1,2},{2,3},{4,5},{5,6},{6,7},{8,9},{9,10},{10,11},{12,13},{... | collective-permute-start | bytes 3145736 | tf_op jit(solution)/shard_map/ppermute | solution.py:578
  435.9 27.2 %collective-permute-start.36 = (bf16[256,2048]{1,0:T(8,128)(2,1)S(1)}, bf16[256,2048]{1,0:T(8,128)(2,1)S(1)}, u32[]{:S(2)}, u32[]{:S(2)}) collective-permute-start(bf16[256,2048]{1,0:T(8,128)(2,1)S(1)} %get-tuple-element.265), channel_id=1, source_target_pairs={{1,0},{2,1},{3,2},{5,4},{6,5},{7,6},{9,8},{10,9},{11,10},{13,12},{... | collective-permute-start | bytes 3145736 | tf_op jit(solution)/shard_map/ppermute | solution.py:579
  454.8 19.4 %copy-start.4 = (bf16[1024,1536]{1,0:T(8,128)(2,1)}, bf16[1024,1536]{1,0:T(8,128)(2,1)S(1)}, u32[]{:S(2)}) copy-start(bf16[1024,1536]{1,0:T(8,128)(2,1)S(1)} %attend_back.1.x_ref.right_ref) | copy-start | bytes 9437188
  463.1 33.9 %collective-permute-start.39 = (bf16[1024,512]{1,0:T(8,128)(2,1)}, bf16[1024,512]{1,0:T(8,128)(2,1)S(1)}, u32[]{:S(2)}, u32[]{:S(2)}) collective-permute-start(bf16[1024,512]{1,0:T(8,128)(2,1)} %add_convert_fusion.12), channel_id=1, source_target_pairs={{0,8},{4,12},{8,0},{12,4},{16,24},{20,28},{24,16},{28,20},{1,9},{5... | collective-permute-start | bytes 3145736 | tf_op jit(solution)/shard_map/ppermute | solution.py:586
  464.6 32.4 %collective-permute-start.40 = (bf16[1024,512]{1,0:T(8,128)(2,1)}, bf16[1024,512]{1,0:T(8,128)(2,1)S(1)}, u32[]{:S(2)}, u32[]{:S(2)}) collective-permute-start(bf16[1024,512]{1,0:T(8,128)(2,1)} %add_convert_fusion.11), channel_id=1, source_target_pairs={{0,16},{4,20},{8,24},{12,28},{16,0},{20,4},{24,8},{28,12},{1,17},{... | collective-permute-start | bytes 3145736 | tf_op jit(solution)/shard_map/ppermute | solution.py:586
  467.7 29.3 %collective-permute-start.38 = (bf16[256,2048]{1,0:T(8,128)(2,1)}, bf16[256,2048]{1,0:T(8,128)(2,1)}, u32[]{:S(2)}, u32[]{:S(2)}) collective-permute-start(bf16[256,2048]{1,0:T(8,128)(2,1)} %get-tuple-element.262), channel_id=1, source_target_pairs={{3,2},{7,6},{11,10},{15,14},{19,18},{23,22},{27,26},{31,30}} | collective-permute-start | bytes 3145736 | tf_op jit(solution)/shard_map/ppermute | solution.py:579
  469.3 27.7 %collective-permute-start.37 = (bf16[256,2048]{1,0:T(8,128)(2,1)}, bf16[256,2048]{1,0:T(8,128)(2,1)}, u32[]{:S(2)}, u32[]{:S(2)}) collective-permute-start(bf16[256,2048]{1,0:T(8,128)(2,1)} %get-tuple-element.263), channel_id=1, source_target_pairs={{0,1},{4,5},{8,9},{12,13},{16,17},{20,21},{24,25},{28,29}} | collective-permute-start | bytes 3145736 | tf_op jit(solution)/shard_map/ppermute | solution.py:578
  482.6 14.3 %collective-permute-start.41 = (f32[12288]{0:T(1024)S(1)}, f32[12288]{0:T(1024)S(1)}, u32[]{:S(2)}, u32[]{:S(2)}) collective-permute-start(f32[12288]{0:T(1024)S(1)} %mul.324), channel_id=1, source_target_pairs={{0,1},{1,0},{2,3},{3,2},{4,5},{5,4},{6,7},{7,6},{8,9},{9,8},{10,11... | collective-permute-start | bytes 147464 | tf_op jit(solution)/shard_map/ppermute | solution.py:586
  503.8 10.0 %collective-permute-start.43 = (bf16[256,2048]{1,0:T(8,128)(2,1)}, bf16[256,2048]{1,0:T(8,128)(2,1)S(1)}, u32[]{:S(2)}, u32[]{:S(2)}) collective-permute-start(bf16[256,2048]{1,0:T(8,128)(2,1)} %get-tuple-element.260), channel_id=1, source_target_pairs={{2,1},{3,2},{6,5},{7,6},{10,9},{11,10},{14,13},{15,14},{18,17},{19... | collective-permute-start | bytes 3145736 | tf_op jit(solution)/shard_map/ppermute | solution.py:579
  504.6 25.4 %collective-permute-start.42 = (bf16[256,2048]{1,0:T(8,128)(2,1)}, bf16[256,2048]{1,0:T(8,128)(2,1)S(1)}, u32[]{:S(2)}, u32[]{:S(2)}) collective-permute-start(bf16[256,2048]{1,0:T(8,128)(2,1)} %get-tuple-element.261), channel_id=1, source_target_pairs={{0,1},{1,2},{4,5},{5,6},{8,9},{9,10},{12,13},{13,14},{16,17},{17,1... | collective-permute-start | bytes 3145736 | tf_op jit(solution)/shard_map/ppermute | solution.py:578
  513.8 30.4 %copy-start.72 = (f32[1,2048]{1,0:T(1,128)S(1)}, f32[1,2048]{1,0:T(1,128)}, u32[]{:S(2)}) copy-start(f32[1,2048]{1,0:T(1,128)} %get-tuple-element.312) | copy-start | bytes 24580
  532.1 28.2 %collective-permute-start.45 = (bf16[256,2048]{1,0:T(8,128)(2,1)}, bf16[256,2048]{1,0:T(8,128)(2,1)S(1)}, u32[]{:S(2)}, u32[]{:S(2)}) collective-permute-start(bf16[256,2048]{1,0:T(8,128)(2,1)} %get-tuple-element.258), channel_id=1, source_target_pairs={{1,0},{2,1},{3,2},{5,4},{6,5},{7,6},{9,8},{10,9},{11,10},{13,12},{... | collective-permute-start | bytes 3145736 | tf_op jit(solution)/shard_map/ppermute | solution.py:579
  533.4 26.9 %collective-permute-start.44 = (bf16[256,2048]{1,0:T(8,128)(2,1)}, bf16[256,2048]{1,0:T(8,128)(2,1)S(1)}, u32[]{:S(2)}, u32[]{:S(2)}) collective-permute-start(bf16[256,2048]{1,0:T(8,128)(2,1)} %get-tuple-element.259), channel_id=1, source_target_pairs={{0,1},{1,2},{2,3},{4,5},{5,6},{6,7},{8,9},{9,10},{10,11},{12,13},{... | collective-permute-start | bytes 3145736 | tf_op jit(solution)/shard_map/ppermute | solution.py:578
  538.3 21.9 %collective-permute-start.46 = (bf16[1024,256]{1,0:T(8,128)(2,1)}, bf16[1024,256]{1,0:T(8,128)(2,1)S(1)}, u32[]{:S(2)}, u32[]{:S(2)}) collective-permute-start(bf16[1024,256]{1,0:T(8,128)(2,1)} %fusion.83), channel_id=1, source_target_pairs={{0,16},{4,20},{8,24},{12,28},{16,0},{20,4},{24,8},{28,12},{1,17},{... | collective-permute-start | bytes 1572872 | tf_op jit(solution)/shard_map/ppermute | solution.py:586
  539.8 20.4 %collective-permute-start.47 = (bf16[1024,256]{1,0:T(8,128)(2,1)}, bf16[1024,256]{1,0:T(8,128)(2,1)S(1)}, u32[]{:S(2)}, u32[]{:S(2)}) collective-permute-start(bf16[1024,256]{1,0:T(8,128)(2,1)} %fusion.82), channel_id=1, source_target_pairs={{0,8},{4,12},{8,0},{12,4},{16,24},{20,28},{24,16},{28,20},{1,9},{5... | collective-permute-start | bytes 1572872 | tf_op jit(solution)/shard_map/ppermute | solution.py:586
  540.4 19.8 %collective-permute-start.48 = (f32[12288]{0:T(1024)S(1)}, f32[12288]{0:T(1024)S(1)}, u32[]{:S(2)}, u32[]{:S(2)}) collective-permute-start(f32[12288]{0:T(1024)S(1)} %add.601), channel_id=1, source_target_pairs={{0,2},{1,3},{2,0},{3,1},{4,6},{5,7},{6,4},{7,5},{8,10},{9,11},{10,... | collective-permute-start | bytes 147464 | tf_op jit(solution)/shard_map/ppermute | solution.py:586
  563.4 27.6 %collective-permute-start.51 = (bf16[512,256]{1,0:T(8,128)(2,1)}, bf16[512,256]{1,0:T(8,128)(2,1)S(1)}, u32[]{:S(2)}, u32[]{:S(2)}) collective-permute-start(bf16[512,256]{1,0:T(8,128)(2,1)} %get-tuple-element.280), channel_id=1, source_target_pairs={{0,3},{1,0},{2,1},{3,2},{4,7},{5,4},{6,5},{7,6},{8,11},{9,8},{10,9... | collective-permute-start | bytes 786440 | tf_op jit(solution)/shard_map/ppermute | solution.py:525
  568.5 22.5 %collective-permute-start.50 = (bf16[512,256]{1,0:T(8,128)(2,1)}, bf16[512,256]{1,0:T(8,128)(2,1)}, u32[]{:S(2)}, u32[]{:S(2)}) collective-permute-start(bf16[512,256]{1,0:T(8,128)(2,1)} %get-tuple-element.281), channel_id=1, source_target_pairs={{0,2},{1,3},{2,0},{3,1},{4,6},{5,7},{6,4},{7,5},{8,10},{9,11},{10,... | collective-permute-start | bytes 786440 | tf_op jit(solution)/shard_map/ppermute | solution.py:525
  568.5 22.5 %collective-permute-start.49 = (bf16[512,256]{1,0:T(8,128)(2,1)}, bf16[512,256]{1,0:T(8,128)(2,1)}, u32[]{:S(2)}, u32[]{:S(2)}) collective-permute-start(bf16[512,256]{1,0:T(8,128)(2,1)} %get-tuple-element.282), channel_id=1, source_target_pairs={{0,1},{1,2},{2,3},{3,0},{4,5},{5,6},{6,7},{7,4},{8,9},{9,10},{10,1... | collective-permute-start | bytes 786440 | tf_op jit(solution)/shard_map/ppermute | solution.py:525
  (77 other events, 445.6 us)
Sparse Core Ops, SparseCore 0:
  42.3 41.1 all-gather.4
  111.2 52.6 all-gather.6
  327.4 71.4 reduce-scatter.3
  402.6 80.5 reduce-scatter.5
  502.3 66.7 reduce-scatter.7

commit v6 on v5

--- a/solution.py
+++ b/solution.py
@@ -217,7 +217,7 @@
         ),
         out_shape=jax.ShapeDtypeStruct((tokens, cols), bf16),
         input_output_aliases={4: 0} if given else {},
-        compiler_params=pltpu.CompilerParams(vmem_limit_bytes=20 * MIB),
+        compiler_params=pltpu.CompilerParams(vmem_limit_bytes=48 * MIB),
         cost_estimate=COST,
         name="hidden_back",
     )(half[None], cot_all, hidden, w_down, *given)
@@ -304,7 +304,7 @@
         ),
         out_shape=jax.ShapeDtypeStruct((tokens, cols), bf16),
         input_output_aliases={3: 0} if given else {},
-        compiler_params=pltpu.CompilerParams(vmem_limit_bytes=40 * MIB),
+        compiler_params=pltpu.CompilerParams(vmem_limit_bytes=24 * MIB),
         cost_estimate=COST,
         name="half_product",
     )(half[None], x, weight, *given)
@@ -860,13 +860,15 @@
                 )
                 layer_out = keep((rows_of(middle_all, me) + down_sum + bias_pair[1]).astype(bf16))
                 full_sums = keep(sum_over(phase(full_sums), "mp", n_mp, 2))
+                grad_up, grad_down = keep(phase(grad_up).astype(f32), phase(grad_down).astype(f32).T)
             turn()
         out_rows = spread_out.finish(phase)
         out_blocks = line.shuffle_rows(phase, out_rows.astype(bf16), head_cols)
         grad_input = input_back(
             own, factor, phase(reduce1.terms), reduce1.came, tokens, gains[0], d_middle
         )
-        grad_qkv, grad_up, grad_down = present(*phase(grad_qkv, grad_up, grad_down))
+        grad_qkv = phase(grad_qkv).astype(f32)
+        grad_qkv = jnp.stack([grad_qkv[:, j * head_cols : (j + 1) * head_cols] for j in range(3)])
         sums = after(jnp.concatenate([full_sums, split_sums]), grad_input).reshape(1, 8, -1)
         sums = lax.all_gather(sums, "dp", axis=0, tiled=True)
         sums, grad_qkv, *out_blocks = lax.optimization_barrier((sums, grad_qkv, *out_blocks))

time: 614 us -> 614 us (level)
  other arithmetic: 63 us -> 73.4 us
  local copies, waits for them, and re-layouts: 54.3 us -> 46.4 us
    unnamed x168 -> x161, local copies, waits for them, and re-layouts: 30.9 us -> 21.3 us
  transfers between devices with their start and end apart: 57 -> 57, of which waited for: 19 -> 20; matrix products, arithmetic and copies ran while one was open for 24% -> 27% of each run, Pallas kernels for 21% -> 21%
where the time goes in v6:
time: 614 us; the launch traced here: 604 us
  waiting for transfers between devices  146 us (24%)
  Pallas kernels  125 us (20%)
  starting transfers between devices  104 us (17%)
  matrix products  80.4 us (13%)
  other arithmetic  73.4 us (12%)
  local copies, waits for them, and re-layouts  46.4 us (8%)
  between operations  18.5 us (3%)
  blocking collectives  10.4 us (2%)
    ppermute x9, waiting for transfers between devices, step(): lax.ppermute(right, line.name, [(j, j - 1) for j in range(1, n - k + 1)])  87 us
    dot_general x16, matrix products, dot(): lax.dot_general(left, right, (((left_dim,), (right_dim,)), ((), ())), pre...  80.4 us
    pallas_call x3, Pallas kernels, weight_grads(): pl.pallas_call(grads_kernel, grid=(steps,), in_specs=[pl.BlockSpec(memory...  40.6 us
    ppermute x9, starting transfers between devices, step(): lax.ppermute(sent[0], line.name, [(j, j + 1) for j in range(k)])  36.6 us
    convert_element_type x6, other arithmetic, relay(): (term.astype(f32) + value.astype(f32)).astype(bf16)  22.5 us
    unnamed x161, local copies, waits for them, and re-layouts  21.3 us
    ppermute x9, waiting for transfers between devices, step(): lax.ppermute(sent[0], line.name, [(j, j + 1) for j in range(k)])  17.7 us
    ppermute x9, starting transfers between devices, step(): lax.ppermute(left, line.name, [(j, j + 1) for j in range(k - 1, n - 1)])  17.2 us
  transfers between devices with their start and end apart: 57, of which 20 were waited for; matrix products, arithmetic and copies ran while one was open for 27% of the time, Pallas kernels for 21%

profile of v6, /device:TPU:0, one launch (start us, length us, event | category | flops | bytes accessed | tf_op | source)
XLA Modules:
  0.0 604.5 jit_solution(550637234978214990)
XLA Ops:
  7.2 6.1 %collective-permute-start = (bf16[256,2048]{1,0:T(8,128)(2,1)}, bf16[256,2048]{1,0:T(8,128)(2,1)}, u32[]{:S(2)}, u32[]{:S(2)}) collective-permute-start(bf16[256,2048]{1,0:T(8,128)(2,1)} %value_ref.1), channel_id=1, source_target_pairs={{0,1},{1,2},{2,3},{4,5},{5,6},{6,7},{8,9},{9,10},{10,11},{12,13},{... | collective-permute-start | bytes 3145736 | tf_op jit(solution)/shard_map/ppermute | solution.py:546
  16.6 5.7 slice_bitcast_fusion.2
  25.1 5.0 fusion.1
  30.1 4.9 collective-permute-done
  35.0 5.1 collective-permute-done.1
  49.5 35.5 %collective-permute-done.3 = bf16[256,2048]{1,0:T(8,128)(2,1)} collective-permute-done((bf16[256,2048]{1,0:T(8,128)(2,1)}, bf16[256,2048]{1,0:T(8,128)(2,1)}, u32[]{:S(2)}, u32[]{:S(2)}) %collective-permute-start.3) | collective-permute-done | bytes 1048608 | tf_op jit(solution)/shard_map/ppermute | solution.py:547
  90.9 2.8 fusion.5
  94.7 15.3 %collective-permute-done.5 = bf16[256,2048]{1,0:T(8,128)(2,1)S(1)} collective-permute-done((bf16[256,2048]{1,0:T(8,128)(2,1)}, bf16[256,2048]{1,0:T(8,128)(2,1)S(1)}, u32[]{:S(2)}, u32[]{:S(2)}) %collective-permute-start.5) | collective-permute-done | bytes 1048608 | tf_op jit(solution)/shard_map/ppermute | solution.py:547
  121.6 2.9 fusion.7.q_ref.k_ref.v_ref
  124.5 9.1 %attend.1 = bf16[1024,512]{1,0:T(8,128)(2,1)S(1)} custom-call(bf16[1024,1536]{1,0:T(8,128)(2,1)} %fusion.7.q_ref.k_ref.v_ref, bf16[1024,1536]{1,0:T(8,128)(2,1)} %fusion.7.q_ref.k_ref.v_ref, bf16[1024,1536]{1,0:T(8,128)(2,1)} %fusion.7.q_ref.k_ref.v_ref, s32[1024,1]{1,0:T(8,128)S(1)} %copy-done.21, s32[1,1024]{1,0:T(1,128)S(1)} %bitcast.54), custom_call_target="tpu_custom_call" | custom-call | flops 1048576 | bytes 65536 | tf_op jit(solution)/shard_map/attend/pallas_call | solution.py:49
  135.2 3.9 collective-permute-done.7
  144.2 5.7 add_add_fusion
  150.5 2.9 collective-permute-start.11
  154.7 2.9 collective-permute-start.12
  159.1 3.8 collective-permute-done.9
  169.2 6.1 %fusion.35.grad_ref = f32[512,2048]{1,0:T(8,128)} fusion(bf16[2048,2048]{1,0:T(8,128)(2,1)S(1)} %bitcast.64, bf16[1024,2048]{1,0:T(8,128)(2,1)S(1)} %select_dynamic-update-slice_fusion.2, s32[]{:T(128)S(6)} %select_n.455), kind=kOutput, calls=%fused_computation.81 | convolution fusion | flops 4294967296 | bytes 14680068 | tf_op jit(solution)/shard_map/dot_general | solution.py:20
  175.3 14.7 %collective-permute-done.14 = bf16[1024,512]{1,0:T(8,128)(2,1)} collective-permute-done((bf16[1024,512]{1,0:T(8,128)(2,1)S(1)}, bf16[1024,512]{1,0:T(8,128)(2,1)}, u32[]{:S(2)}, u32[]{:S(2)}) %collective-permute-start.14) | collective-permute-done | bytes 1048608 | tf_op jit(solution)/shard_map/ppermute | solution.py:547
  195.9 6.4 %convolution_add_fusion.1 = f32[1024,2048]{1,0:T(8,128)S(1)} fusion(f32[1024,2048]{1,0:T(8,128)} %add_add_fusion, bf16[1024,512]{1,0:T(8,128)(2,1)S(1)} %broadcast_select_fusion, bf16[2048,2048]{1,0:T(8,128)(2,1)} %bitcast.57, s32[]{:T(128)S(6)} %select_n.445), kind=kOutput, calls=%fused_computation.5 | convolution fusion | flops 2149580800 | bytes 19922948 | tf_op jit(solution)/shard_map/dot_general | solution.py:20
  202.3 7.3 %convolution_add_fusion.sum_ref = f32[1024,2048]{1,0:T(8,128)} fusion(f32[1024,2048]{1,0:T(8,128)S(1)} %convolution_add_fusion.1, bf16[1024,512]{1,0:T(8,128)(2,1)S(1)} %select_select_fusion.1, bf16[2048,2048]{1,0:T(8,128)(2,1)} %bitcast.58, s32[]{:T(128)S(6)} %select_n.462), kind=kOutput, calls=%fused_computation.4 | convolution fusion | flops 2149580800 | bytes 19922948 | tf_op jit(solution)/shard_map/dot_general | solution.py:20
  209.5 5.7 collective-permute-done.16
  220.1 9.8 %mix.1 = (f32[1024,2048]{1,0:T(8,128)}, bf16[1024,2048]{1,0:T(8,128)(2,1)S(1)}) custom-call(s32[1]{0:T(128)} %bitcast.index_ref, f32[1024,2048]{1,0:T(8,128)} %convolution_add_fusion.sum_ref, bf16[1024,512]{1,0:T(8,128)(2,1)S(1)} %select_select_fusion.heads_ref, bf16[2048,2048]{1,0:T(8,128)(2,1)} %bitcast.59, f32[1,2048]{1,0:T(1,128)S(1)} %get-tuple-element.351.gain_ref, ...), custom_call_target="tpu_custom_call" | custom-call | flops 1048576 | bytes 65536 | tf_op jit(solution)/shard_map/mix/pallas_call | solution.py:151
  231.8 15.6 %feed_up.1 = (f32[1024,2048]{1,0:T(8,128)}, bf16[1024,2048]{1,0:T(8,128)(2,1)S(1)}) custom-call(bf16[1024,2048]{1,0:T(8,128)(2,1)} %copy-done.12, bf16[2048,2048]{1,0:T(8,128)(2,1)} %w_ref.2, f32[1,2048]{1,0:T(1,128)S(1)} %bitcast.56), custom_call_target="tpu_custom_call" | custom-call | flops 1048576 | bytes 65536 | tf_op jit(solution)/shard_map/feed_up/pallas_call | solution.py:180
  249.5 11.4 %convolution_convert_fusion.1 = bf16[1024,2048]{1,0:T(8,128)(2,1)S(1)} fusion(bf16[1024,2048]{1,0:T(8,128)(2,1)S(1)} %get-tuple-element.185.right_ref, bf16[2048,2048]{1,0:T(8,128)(2,1)} %w_ref.3), kind=kOutput, calls=%fused_computation.7 | convolution fusion | flops 8592031744 | bytes 16777216 | tf_op jit(solution)/shard_map/dot_general | solution.py:20
  264.7 3.0 select_dynamic-update-slice_fusion.1
  267.8 3.0 collective-permute-done.20
  275.4 9.8 %hidden_back.1.right_ref = bf16[1024,2048]{1,0:T(8,128)(2,1)S(1)} custom-call(s32[1]{0:T(128)} %bitcast.14.index_ref, bf16[1024,2048]{1,0:T(8,128)(2,1)} %select_dynamic-update-slice_fusion.cot_ref.left_ref, f32[1024,2048]{1,0:T(8,128)} %get-tuple-element.182.hidden_ref, bf16[2048,2048]{1,0:T(8,128)(2,1)} %w_ref.3, ...), custom_call_target="tpu_custom_call", output_to_operand_aliasing={{}: (4, {})} | custom-call | flops 1048576 | bytes 65536 | tf_op jit(solution)/shard_map/hidden_back/pallas_call | solution.py:205
  285.2 12.8 %convolution_convert_fusion.term_ref = bf16[1024,2048]{1,0:T(8,128)(2,1)S(1)} fusion(bf16[1024,2048]{1,0:T(8,128)(2,1)S(1)} %hidden_back.1.right_ref, bf16[2048,2048]{1,0:T(8,128)(2,1)} %w_ref.2), kind=kOutput, calls=%fused_computation.6 | convolution fusion | flops 8592031744 | bytes 16777216 | tf_op jit(solution)/shard_map/dot_general | solution.py:20
  302.0 3.8 collective-permute-start.23
  308.0 14.0 %weight_grads.3 = bf16[2048,2048]{1,0:T(8,128)(2,1)} custom-call(f32[1]{0:T(128)} %div.35.factor_ref, bf16[1024,2048]{1,0:T(8,128)(2,1)S(1)} %copy-done.13, bf16[1024,2048]{1,0:T(8,128)(2,1)} %copy-done.6), custom_call_target="tpu_custom_call" | custom-call | flops 1048576 | bytes 65536 | tf_op jit(solution)/shard_map/weight_grads/pallas_call | solution.py:265
  322.5 4.0 add_convert_fusion.17
  328.3 5.2 collective-permute-start.25
  333.5 3.0 copy-done.9
  336.5 14.2 %weight_grads.4 = bf16[2048,2048]{1,0:T(8,128)(2,1)} custom-call(f32[1]{0:T(128)} %div.35.factor_ref, bf16[1024,2048]{1,0:T(8,128)(2,1)S(1)} %copy-done.9, bf16[1024,2048]{1,0:T(8,128)(2,1)} %copy-done.23), custom_call_target="tpu_custom_call" | custom-call | flops 1048576 | bytes 65536 | tf_op jit(solution)/shard_map/weight_grads/pallas_call | solution.py:265
  350.8 5.1 add_convert_fusion.15
  357.2 4.6 collective-permute-start.27
  361.9 3.0 convert_reduce_fusion
  364.9 10.7 %collective-permute-done.28.right_ref = bf16[256,2048]{1,0:T(8,128)(2,1)S(1)} collective-permute-done((bf16[256,2048]{1,0:T(8,128)(2,1)}, bf16[256,2048]{1,0:T(8,128)(2,1)S(1)}, u32[]{:S(2)}, u32[]{:S(2)}) %collective-permute-start.28) | collective-permute-done | bytes 1048608 | tf_op jit(solution)/shard_map/ppermute | solution.py:579
  377.6 3.3 add_convert_fusion.14
  380.9 5.3 collective-permute-start.29
  390.4 5.2 middle_back.1
  398.2 4.5 multiply_convert_fusion
  407.4 2.9 collective-permute-done.34
  416.4 3.2 add_convert_fusion.10
  419.5 2.9 add_convert_fusion.12
  422.5 7.0 %collective-permute-done.32 = bf16[256,512]{1,0:T(8,128)(2,1)S(1)} collective-permute-done((bf16[256,512]{1,0:T(8,128)(2,1)S(1)}, bf16[256,512]{1,0:T(8,128)(2,1)S(1)}, u32[]{:S(2)}, u32[]{:S(2)}) %collective-permute-start.32) | collective-permute-done | bytes 262176 | tf_op jit(solution)/shard_map/ppermute | solution.py:514
  430.2 3.2 add_convert_fusion.8
  438.4 15.8 %attend_back.1.x_ref.right_ref = bf16[1024,1536]{1,0:T(8,128)(2,1)S(1)} custom-call(bf16[1024,1536]{1,0:T(8,128)(2,1)} %fusion.7.q_ref.k_ref.v_ref, bf16[1024,1536]{1,0:T(8,128)(2,1)} %fusion.7.q_ref.k_ref.v_ref, bf16[1024,1536]{1,0:T(8,128)(2,1)} %fusion.7.q_ref.k_ref.v_ref, bf16[1024,512]{1,0:T(8,128)(2,1)S(1)} %constant_dynamic-update-slice_fusion.grad_ref, ...), custom_call_target="tpu_custom_call" | custom-call | flops 1048576 | bytes 65536 | tf_op jit(solution)/shard_map/attend_back/pallas_call | solution.py:94
  454.2 4.2 half_product.2.refs_0_
  458.4 4.0 collective-permute-done.36
  468.9 4.8 collective-permute-start.37
  473.7 4.2 half_product.3.term_ref
  478.0 4.1 gain_sums.1
  484.1 12.3 %weight_grads.5 = bf16[2048,1536]{1,0:T(8,128)(2,1)} custom-call(f32[1]{0:T(128)} %div.35.factor_ref, bf16[1024,2048]{1,0:T(8,128)(2,1)} %get-tuple-element.224.left_ref, bf16[1024,1536]{1,0:T(8,128)(2,1)S(1)} %copy-done.5), custom_call_target="tpu_custom_call" | custom-call | flops 1048576 | bytes 65536 | tf_op jit(solution)/shard_map/weight_grads/pallas_call | solution.py:265
  496.5 4.7 add_convert_fusion.5
  503.5 4.5 collective-permute-start.42
  513.5 15.2 %collective-permute-done.42 = bf16[256,2048]{1,0:T(8,128)(2,1)S(1)} collective-permute-done((bf16[256,2048]{1,0:T(8,128)(2,1)}, bf16[256,2048]{1,0:T(8,128)(2,1)S(1)}, u32[]{:S(2)}, u32[]{:S(2)}) %collective-permute-start.42) | collective-permute-done | bytes 1048608 | tf_op jit(solution)/shard_map/ppermute | solution.py:578
  534.2 4.9 collective-permute-start.44
  539.1 3.9 collective-permute-start.48
  543.0 3.6 add_convert_fusion
  549.7 2.9 copy.32
  552.6 8.8 %collective-permute-done.48 = f32[12288]{0:T(1024)S(1)} collective-permute-done((f32[12288]{0:T(1024)S(1)}, f32[12288]{0:T(1024)S(1)}, u32[]{:S(2)}, u32[]{:S(2)}) %collective-permute-start.48) | collective-permute-done | bytes 49184 | tf_op jit(solution)/shard_map/ppermute | solution.py:586
  566.0 5.1 collective-permute-start.51
  571.6 3.8 input_back.1
  575.5 10.4 %all_gather.19 = f32[8,8,1920]{2,1,0:T(8,128)} all-gather(f32[1,8,1920]{2,1,0:T(8,128)S(1)} %reshape.101), channel_id=1, replica_groups=mesh['dp'=8,'mp'=4] {'dp'}, dimensions={0}, use_global_device_ids=true | all-gather | bytes 552960 | tf_op jit(solution)/shard_map/all_gather | solution.py:873
  (354 shorter events, 146.6 us)
Async XLA Ops:
  7.2 103.8 %all-gather.5.cloned.1.call-start = ((), (), s32[]{:S(2)}) async-start(), calls=%async_computation.6 | async-start | bytes 1310720 | tf_op jit(solution)/shard_map/all_gather | solution.py:728
  7.2 27.8 %collective-permute-start = (bf16[256,2048]{1,0:T(8,128)(2,1)}, bf16[256,2048]{1,0:T(8,128)(2,1)}, u32[]{:S(2)}, u32[]{:S(2)}) collective-permute-start(bf16[256,2048]{1,0:T(8,128)(2,1)} %value_ref.1), channel_id=1, source_target_pairs={{0,1},{1,2},{2,3},{4,5},{5,6},{6,7},{8,9},{9,10},{10,11},{12,13},{... | collective-permute-start | bytes 3145736 | tf_op jit(solution)/shard_map/ppermute | solution.py:546
  13.3 26.8 %collective-permute-start.1 = (bf16[256,2048]{1,0:T(8,128)(2,1)}, bf16[256,2048]{1,0:T(8,128)(2,1)}, u32[]{:S(2)}, u32[]{:S(2)}) collective-permute-start(bf16[256,2048]{1,0:T(8,128)(2,1)} %value_ref.1), channel_id=1, source_target_pairs={{1,0},{2,1},{3,2},{5,4},{6,5},{7,6},{9,8},{10,9},{11,10},{13,12},{... | collective-permute-start | bytes 3145736 | tf_op jit(solution)/shard_map/ppermute | solution.py:547
  40.1 9.4 %collective-permute-start.2 = (bf16[256,2048]{1,0:T(8,128)(2,1)}, bf16[256,2048]{1,0:T(8,128)(2,1)S(1)}, u32[]{:S(2)}, u32[]{:S(2)}) collective-permute-start(bf16[256,2048]{1,0:T(8,128)(2,1)} %collective-permute-done), channel_id=1, source_target_pairs={{1,2},{2,3},{5,6},{6,7},{9,10},{10,11},{13,14},{14,15},{17,18},{18... | collective-permute-start | bytes 3145736 | tf_op jit(solution)/shard_map/ppermute | solution.py:546
  40.9 44.2 %collective-permute-start.3 = (bf16[256,2048]{1,0:T(8,128)(2,1)}, bf16[256,2048]{1,0:T(8,128)(2,1)}, u32[]{:S(2)}, u32[]{:S(2)}) collective-permute-start(bf16[256,2048]{1,0:T(8,128)(2,1)} %collective-permute-done.1), channel_id=1, source_target_pairs={{1,0},{2,1},{5,4},{6,5},{9,8},{10,9},{13,12},{14,13},{17,16},{18,1... | collective-permute-start | bytes 3145736 | tf_op jit(solution)/shard_map/ppermute | solution.py:547
  42.2 153.7 %all-gather.7.cloned.1.call-start = ((), (), s32[]{:S(2)}) async-start(), calls=%async_computation.7 | async-start | bytes 9437184 | tf_op jit(solution)/shard_map/all_gather | solution.py:733
  85.0 8.7 %collective-permute-start.4 = (bf16[256,2048]{1,0:T(8,128)(2,1)S(1)}, bf16[256,2048]{1,0:T(8,128)(2,1)S(1)}, u32[]{:S(2)}, u32[]{:S(2)}) collective-permute-start(bf16[256,2048]{1,0:T(8,128)(2,1)S(1)} %collective-permute-done.2), channel_id=1, source_target_pairs={{2,3},{6,7},{10,11},{14,15},{18,19},{22,23},{26,27},{30,31}} | collective-permute-start | bytes 3145736 | tf_op jit(solution)/shard_map/ppermute | solution.py:546
  85.7 24.3 %collective-permute-start.5 = (bf16[256,2048]{1,0:T(8,128)(2,1)}, bf16[256,2048]{1,0:T(8,128)(2,1)S(1)}, u32[]{:S(2)}, u32[]{:S(2)}) collective-permute-start(bf16[256,2048]{1,0:T(8,128)(2,1)} %collective-permute-done.3), channel_id=1, source_target_pairs={{1,0},{5,4},{9,8},{13,12},{17,16},{21,20},{25,24},{29,28}} | collective-permute-start | bytes 3145736 | tf_op jit(solution)/shard_map/ppermute | solution.py:547
  111.0 319.1 %reduce-scatter.4.cloned.1.call-start = ((), (), s32[]{:S(2)}) async-start(), calls=%async_computation.3 | async-start | bytes 9437184 | tf_op jit(solution)/shard_map/reduce_scatter | solution.py:794
  113.6 21.6 %collective-permute-start.6 = (bf16[256,2048]{1,0:T(8,128)(2,1)S(1)}, bf16[256,2048]{1,0:T(8,128)(2,1)}, u32[]{:S(2)}, u32[]{:S(2)}) collective-permute-start(bf16[256,2048]{1,0:T(8,128)(2,1)S(1)} %copy-done.11), channel_id=1, source_target_pairs={{0,1},{1,2},{2,3},{4,5},{5,6},{6,7},{8,9},{9,10},{10,11},{12,13},{... | collective-permute-start | bytes 3145736 | tf_op jit(solution)/shard_map/ppermute | solution.py:546
  116.1 23.0 %collective-permute-start.7 = (bf16[256,2048]{1,0:T(8,128)(2,1)S(1)}, bf16[256,2048]{1,0:T(8,128)(2,1)}, u32[]{:S(2)}, u32[]{:S(2)}) collective-permute-start(bf16[256,2048]{1,0:T(8,128)(2,1)S(1)} %copy-done.11), channel_id=1, source_target_pairs={{1,0},{2,1},{3,2},{5,4},{6,5},{7,6},{9,8},{10,9},{11,10},{13,12},{... | collective-permute-start | bytes 3145736 | tf_op jit(solution)/shard_map/ppermute | solution.py:547
  139.1 20.0 %collective-permute-start.8 = (bf16[1024,512]{1,0:T(8,128)(2,1)S(1)}, bf16[1024,512]{1,0:T(8,128)(2,1)S(1)}, u32[]{:S(2)}, u32[]{:S(2)}) collective-permute-start(bf16[1024,512]{1,0:T(8,128)(2,1)S(1)} %attend.1), channel_id=1, source_target_pairs={{0,1},{1,2},{2,3},{4,5},{5,6},{6,7},{8,9},{9,10},{10,11},{12,13},{... | collective-permute-start | bytes 3145736 | tf_op jit(solution)/shard_map/ppermute | solution.py:546
  140.6 22.2 %collective-permute-start.9 = (bf16[1024,512]{1,0:T(8,128)(2,1)S(1)}, bf16[1024,512]{1,0:T(8,128)(2,1)S(1)}, u32[]{:S(2)}, u32[]{:S(2)}) collective-permute-start(bf16[1024,512]{1,0:T(8,128)(2,1)S(1)} %attend.1), channel_id=1, source_target_pairs={{1,0},{2,1},{3,2},{5,4},{6,5},{7,6},{9,8},{10,9},{11,10},{13,12},{... | collective-permute-start | bytes 3145736 | tf_op jit(solution)/shard_map/ppermute | solution.py:547
  141.9 8.0 %collective-permute-start.10 = (f32[1]{0:T(128)}, f32[1]{0:T(128)}, u32[]{:S(2)}, u32[]{:S(2)}) collective-permute-start(f32[1]{0:T(128)} %convert_element_type.295), channel_id=1, source_target_pairs={{0,4},{4,0},{8,12},{12,8},{16,20},{20,16},{24,28},{28,24},{1,5},{5... | collective-permute-start | bytes 20 | tf_op jit(solution)/shard_map/ppermute | solution.py:586
  142.9 26.2 %slice-start.2 = ((s8[8388608]{0:T(1024)(128)(4,1)}), s8[4194304]{0:T(1024)(128)(4,1)S(1)}, s32[]{:S(2)}) async-start(s8[8388608]{0:T(1024)(128)(4,1)} %bitcast.63), calls=%async_computation.10 | async-start | bytes 8388608
  144.2 25.0 %slice-start.3 = ((s8[8388608]{0:T(1024)(128)(4,1)}), s8[4194304]{0:T(1024)(128)(4,1)S(1)}, s32[]{:S(2)}) async-start(s8[8388608]{0:T(1024)(128)(4,1)} %bitcast.63), calls=%async_computation.11 | async-start | bytes 8388608
  150.5 3.7 collective-permute-start.11
  154.7 3.7 collective-permute-start.12
  162.8 12.4 %collective-permute-start.13 = (bf16[1024,512]{1,0:T(8,128)(2,1)S(1)}, bf16[1024,512]{1,0:T(8,128)(2,1)}, u32[]{:S(2)}, u32[]{:S(2)}) collective-permute-start(bf16[1024,512]{1,0:T(8,128)(2,1)S(1)} %collective-permute-done.8), channel_id=1, source_target_pairs={{1,2},{2,3},{5,6},{6,7},{9,10},{10,11},{13,14},{14,15},{17,18},{18... | collective-permute-start | bytes 3145736 | tf_op jit(solution)/shard_map/ppermute | solution.py:546
  164.5 25.6 %collective-permute-start.14 = (bf16[1024,512]{1,0:T(8,128)(2,1)S(1)}, bf16[1024,512]{1,0:T(8,128)(2,1)}, u32[]{:S(2)}, u32[]{:S(2)}) collective-permute-start(bf16[1024,512]{1,0:T(8,128)(2,1)S(1)} %collective-permute-done.9), channel_id=1, source_target_pairs={{1,0},{2,1},{5,4},{6,5},{9,8},{10,9},{13,12},{14,13},{17,16},{18,1... | collective-permute-start | bytes 3145736 | tf_op jit(solution)/shard_map/ppermute | solution.py:547
  190.0 19.5 %collective-permute-start.15 = (bf16[1024,512]{1,0:T(8,128)(2,1)}, bf16[1024,512]{1,0:T(8,128)(2,1)}, u32[]{:S(2)}, u32[]{:S(2)}) collective-permute-start(bf16[1024,512]{1,0:T(8,128)(2,1)} %collective-permute-done.13), channel_id=1, source_target_pairs={{2,3},{6,7},{10,11},{14,15},{18,19},{22,23},{26,27},{30,31}} | collective-permute-start | bytes 3145736 | tf_op jit(solution)/shard_map/ppermute | solution.py:546
  191.7 23.6 %collective-permute-start.16 = (bf16[1024,512]{1,0:T(8,128)(2,1)}, bf16[1024,512]{1,0:T(8,128)(2,1)}, u32[]{:S(2)}, u32[]{:S(2)}) collective-permute-start(bf16[1024,512]{1,0:T(8,128)(2,1)} %collective-permute-done.14), channel_id=1, source_target_pairs={{1,0},{5,4},{9,8},{13,12},{17,16},{21,20},{25,24},{29,28}} | collective-permute-start | bytes 3145736 | tf_op jit(solution)/shard_map/ppermute | solution.py:547
  215.3 32.2 %collective-permute-start.17 = (bf16[256,2048]{1,0:T(8,128)(2,1)}, bf16[256,2048]{1,0:T(8,128)(2,1)}, u32[]{:S(2)}, u32[]{:S(2)}) collective-permute-start(bf16[256,2048]{1,0:T(8,128)(2,1)} %collective-permute-done.6), channel_id=1, source_target_pairs={{1,2},{2,3},{5,6},{6,7},{9,10},{10,11},{13,14},{14,15},{17,18},{18... | collective-permute-start | bytes 3145736 | tf_op jit(solution)/shard_map/ppermute | solution.py:546
  217.0 30.5 %collective-permute-start.18 = (bf16[256,2048]{1,0:T(8,128)(2,1)}, bf16[256,2048]{1,0:T(8,128)(2,1)}, u32[]{:S(2)}, u32[]{:S(2)}) collective-permute-start(bf16[256,2048]{1,0:T(8,128)(2,1)} %collective-permute-done.7), channel_id=1, source_target_pairs={{1,0},{2,1},{5,4},{6,5},{9,8},{10,9},{13,12},{14,13},{17,16},{18,1... | collective-permute-start | bytes 3145736 | tf_op jit(solution)/shard_map/ppermute | solution.py:547
  247.4 20.3 %collective-permute-start.19 = (bf16[256,2048]{1,0:T(8,128)(2,1)}, bf16[256,2048]{1,0:T(8,128)(2,1)S(1)}, u32[]{:S(2)}, u32[]{:S(2)}) collective-permute-start(bf16[256,2048]{1,0:T(8,128)(2,1)} %collective-permute-done.17), channel_id=1, source_target_pairs={{2,3},{6,7},{10,11},{14,15},{18,19},{22,23},{26,27},{30,31}} | collective-permute-start | bytes 3145736 | tf_op jit(solution)/shard_map/ppermute | solution.py:546
  248.2 22.6 %collective-permute-start.20 = (bf16[256,2048]{1,0:T(8,128)(2,1)}, bf16[256,2048]{1,0:T(8,128)(2,1)S(1)}, u32[]{:S(2)}, u32[]{:S(2)}) collective-permute-start(bf16[256,2048]{1,0:T(8,128)(2,1)} %collective-permute-done.18), channel_id=1, source_target_pairs={{1,0},{5,4},{9,8},{13,12},{17,16},{21,20},{25,24},{29,28}} | collective-permute-start | bytes 3145736 | tf_op jit(solution)/shard_map/ppermute | solution.py:547
  270.9 27.1 %collective-permute-start.21 = (bf16[256,2048]{1,0:T(8,128)(2,1)S(1)}, bf16[256,2048]{1,0:T(8,128)(2,1)S(1)}, u32[]{:S(2)}, u32[]{:S(2)}) collective-permute-start(bf16[256,2048]{1,0:T(8,128)(2,1)S(1)} %get-tuple-element.305), channel_id=1, source_target_pairs={{0,1},{4,5},{8,9},{12,13},{16,17},{20,21},{24,25},{28,29}} | collective-permute-start | bytes 3145736 | tf_op jit(solution)/shard_map/ppermute | solution.py:578
  272.6 25.5 %collective-permute-start.22 = (bf16[256,2048]{1,0:T(8,128)(2,1)S(1)}, bf16[256,2048]{1,0:T(8,128)(2,1)S(1)}, u32[]{:S(2)}, u32[]{:S(2)}) collective-permute-start(bf16[256,2048]{1,0:T(8,128)(2,1)S(1)} %get-tuple-element.306), channel_id=1, source_target_pairs={{3,2},{7,6},{11,10},{15,14},{19,18},{23,22},{27,26},{31,30}} | collective-permute-start | bytes 3145736 | tf_op jit(solution)/shard_map/ppermute | solution.py:579
  300.4 21.6 %collective-permute-start.24 = (bf16[256,2048]{1,0:T(8,128)(2,1)}, bf16[256,2048]{1,0:T(8,128)(2,1)}, u32[]{:S(2)}, u32[]{:S(2)}) collective-permute-start(bf16[256,2048]{1,0:T(8,128)(2,1)} %get-tuple-element.303), channel_id=1, source_target_pairs={{3,2},{7,6},{11,10},{15,14},{19,18},{23,22},{27,26},{31,30}} | collective-permute-start | bytes 3145736 | tf_op jit(solution)/shard_map/ppermute | solution.py:579
  302.0 20.5 %collective-permute-start.23 = (bf16[256,2048]{1,0:T(8,128)(2,1)S(1)}, bf16[256,2048]{1,0:T(8,128)(2,1)}, u32[]{:S(2)}, u32[]{:S(2)}) collective-permute-start(bf16[256,2048]{1,0:T(8,128)(2,1)S(1)} %get-tuple-element.304), channel_id=1, source_target_pairs={{0,1},{4,5},{8,9},{12,13},{16,17},{20,21},{24,25},{28,29}} | collective-permute-start | bytes 3145736 | tf_op jit(solution)/shard_map/ppermute | solution.py:578
  326.5 170.0 %reduce-scatter.6.cloned.1.call-start = ((), (), s32[]{:S(2)}) async-start(), calls=%async_computation.4 | async-start | bytes 9437184 | tf_op jit(solution)/shard_map/reduce_scatter | solution.py:794
  326.6 24.2 %collective-permute-start.26 = (bf16[256,2048]{1,0:T(8,128)(2,1)}, bf16[256,2048]{1,0:T(8,128)(2,1)}, u32[]{:S(2)}, u32[]{:S(2)}) collective-permute-start(bf16[256,2048]{1,0:T(8,128)(2,1)} %get-tuple-element.301), channel_id=1, source_target_pairs={{2,1},{3,2},{6,5},{7,6},{10,9},{11,10},{14,13},{15,14},{18,17},{19... | collective-permute-start | bytes 3145736 | tf_op jit(solution)/shard_map/ppermute | solution.py:579
  328.3 22.5 %collective-permute-start.25 = (bf16[256,2048]{1,0:T(8,128)(2,1)S(1)}, bf16[256,2048]{1,0:T(8,128)(2,1)}, u32[]{:S(2)}, u32[]{:S(2)}) collective-permute-start(bf16[256,2048]{1,0:T(8,128)(2,1)S(1)} %get-tuple-element.302), channel_id=1, source_target_pairs={{0,1},{1,2},{4,5},{5,6},{8,9},{9,10},{12,13},{13,14},{16,17},{17,1... | collective-permute-start | bytes 3145736 | tf_op jit(solution)/shard_map/ppermute | solution.py:578
  355.9 230.0 %reduce-scatter.8.cloned.1.call-start = ((), (), s32[]{:S(2)}) async-start(), calls=%async_computation.5 | async-start | bytes 7077888 | tf_op jit(solution)/shard_map/reduce_scatter | solution.py:794
  355.9 19.7 %collective-permute-start.28 = (bf16[256,2048]{1,0:T(8,128)(2,1)}, bf16[256,2048]{1,0:T(8,128)(2,1)S(1)}, u32[]{:S(2)}, u32[]{:S(2)}) collective-permute-start(bf16[256,2048]{1,0:T(8,128)(2,1)} %get-tuple-element.299), channel_id=1, source_target_pairs={{1,0},{2,1},{3,2},{5,4},{6,5},{7,6},{9,8},{10,9},{11,10},{13,12},{... | collective-permute-start | bytes 3145736 | tf_op jit(solution)/shard_map/ppermute | solution.py:579
  357.2 20.3 %collective-permute-start.27 = (bf16[256,2048]{1,0:T(8,128)(2,1)}, bf16[256,2048]{1,0:T(8,128)(2,1)S(1)}, u32[]{:S(2)}, u32[]{:S(2)}) collective-permute-start(bf16[256,2048]{1,0:T(8,128)(2,1)} %get-tuple-element.300), channel_id=1, source_target_pairs={{0,1},{1,2},{2,3},{4,5},{5,6},{6,7},{8,9},{9,10},{10,11},{12,13},{... | collective-permute-start | bytes 3145736 | tf_op jit(solution)/shard_map/ppermute | solution.py:578
  361.9 33.7 %slice-start = ((s8[8388608]{0:T(1024)(128)(4,1)}), s8[4194304]{0:T(1024)(128)(4,1)S(1)}, s32[]{:S(2)}) async-start(s8[8388608]{0:T(1024)(128)(4,1)} %bitcast.60), calls=%async_computation.8 | async-start | bytes 8388608
  380.9 21.8 %collective-permute-start.29 = (bf16[256,2048]{1,0:T(8,128)(2,1)S(1)}, bf16[256,2048]{1,0:T(8,128)(2,1)}, u32[]{:S(2)}, u32[]{:S(2)}) collective-permute-start(bf16[256,2048]{1,0:T(8,128)(2,1)S(1)} %get-tuple-element.297), channel_id=1, source_target_pairs={{0,1},{1,2},{4,5},{5,6},{8,9},{9,10},{12,13},{13,14},{16,17},{17,1... | collective-permute-start | bytes 3145736 | tf_op jit(solution)/shard_map/ppermute | solution.py:578
  386.2 16.5 %collective-permute-start.30 = (bf16[256,2048]{1,0:T(8,128)(2,1)S(1)}, bf16[256,2048]{1,0:T(8,128)(2,1)}, u32[]{:S(2)}, u32[]{:S(2)}) collective-permute-start(bf16[256,2048]{1,0:T(8,128)(2,1)S(1)} %get-tuple-element.298), channel_id=1, source_target_pairs={{2,1},{3,2},{6,5},{7,6},{10,9},{11,10},{14,13},{15,14},{18,17},{19... | collective-permute-start | bytes 3145736 | tf_op jit(solution)/shard_map/ppermute | solution.py:579
  402.7 7.6 %collective-permute-start.34 = (bf16[2048,1024]{1,0:T(8,128)(2,1)}, bf16[2048,1024]{1,0:T(8,128)(2,1)}, u32[]{:S(2)}, u32[]{:S(2)}) collective-permute-start(bf16[2048,1024]{1,0:T(8,128)(2,1)} %multiply_convert_fusion), channel_id=1, source_target_pairs={{0,4},{4,0},{8,12},{12,8},{16,20},{20,16},{24,28},{28,24},{1,5},{5... | collective-permute-start | bytes 12582920 | tf_op jit(solution)/shard_map/ppermute | solution.py:586
  403.0 19.4 %collective-permute-start.33 = (bf16[256,512]{1,0:T(8,128)(2,1)S(1)}, bf16[256,512]{1,0:T(8,128)(2,1)S(1)}, u32[]{:S(2)}, u32[]{:S(2)}) collective-permute-start(bf16[256,512]{1,0:T(8,128)(2,1)S(1)} %get-tuple-element.321), channel_id=1, source_target_pairs={{0,3},{1,0},{2,1},{3,2},{4,7},{5,4},{6,5},{7,6},{8,11},{9,8},{10,9... | collective-permute-start | bytes 786440 | tf_op jit(solution)/shard_map/ppermute | solution.py:514
  405.1 24.4 %collective-permute-start.32 = (bf16[256,512]{1,0:T(8,128)(2,1)S(1)}, bf16[256,512]{1,0:T(8,128)(2,1)S(1)}, u32[]{:S(2)}, u32[]{:S(2)}) collective-permute-start(bf16[256,512]{1,0:T(8,128)(2,1)S(1)} %get-tuple-element.322), channel_id=1, source_target_pairs={{0,2},{1,3},{2,0},{3,1},{4,6},{5,7},{6,4},{7,5},{8,10},{9,11},{10,... | collective-permute-start | bytes 786440 | tf_op jit(solution)/shard_map/ppermute | solution.py:514
  405.9 24.3 %collective-permute-start.31 = (bf16[256,512]{1,0:T(8,128)(2,1)S(1)}, bf16[256,512]{1,0:T(8,128)(2,1)}, u32[]{:S(2)}, u32[]{:S(2)}) collective-permute-start(bf16[256,512]{1,0:T(8,128)(2,1)S(1)} %get-tuple-element.323), channel_id=1, source_target_pairs={{0,1},{1,2},{2,3},{3,0},{4,5},{5,6},{6,7},{7,4},{8,9},{9,10},{10,1... | collective-permute-start | bytes 786440 | tf_op jit(solution)/shard_map/ppermute | solution.py:514
  433.4 25.0 %collective-permute-start.35 = (bf16[256,2048]{1,0:T(8,128)(2,1)S(1)}, bf16[256,2048]{1,0:T(8,128)(2,1)S(1)}, u32[]{:S(2)}, u32[]{:S(2)}) collective-permute-start(bf16[256,2048]{1,0:T(8,128)(2,1)S(1)} %get-tuple-element.291), channel_id=1, source_target_pairs={{0,1},{1,2},{2,3},{4,5},{5,6},{6,7},{8,9},{9,10},{10,11},{12,13},{... | collective-permute-start | bytes 3145736 | tf_op jit(solution)/shard_map/ppermute | solution.py:578
  435.1 27.3 %collective-permute-start.36 = (bf16[256,2048]{1,0:T(8,128)(2,1)S(1)}, bf16[256,2048]{1,0:T(8,128)(2,1)S(1)}, u32[]{:S(2)}, u32[]{:S(2)}) collective-permute-start(bf16[256,2048]{1,0:T(8,128)(2,1)S(1)} %get-tuple-element.292), channel_id=1, source_target_pairs={{1,0},{2,1},{3,2},{5,4},{6,5},{7,6},{9,8},{10,9},{11,10},{13,12},{... | collective-permute-start | bytes 3145736 | tf_op jit(solution)/shard_map/ppermute | solution.py:579
  462.4 34.1 %collective-permute-start.39 = (bf16[1024,512]{1,0:T(8,128)(2,1)}, bf16[1024,512]{1,0:T(8,128)(2,1)S(1)}, u32[]{:S(2)}, u32[]{:S(2)}) collective-permute-start(bf16[1024,512]{1,0:T(8,128)(2,1)} %add_convert_fusion.12), channel_id=1, source_target_pairs={{0,8},{4,12},{8,0},{12,4},{16,24},{20,28},{24,16},{28,20},{1,9},{5... | collective-permute-start | bytes 3145736 | tf_op jit(solution)/shard_map/ppermute | solution.py:586
  464.0 32.5 %collective-permute-start.40 = (bf16[1024,512]{1,0:T(8,128)(2,1)}, bf16[1024,512]{1,0:T(8,128)(2,1)}, u32[]{:S(2)}, u32[]{:S(2)}) collective-permute-start(bf16[1024,512]{1,0:T(8,128)(2,1)} %add_convert_fusion.11), channel_id=1, source_target_pairs={{0,16},{4,20},{8,24},{12,28},{16,0},{20,4},{24,8},{28,12},{1,17},{... | collective-permute-start | bytes 3145736 | tf_op jit(solution)/shard_map/ppermute | solution.py:586
  467.2 29.3 %collective-permute-start.38 = (bf16[256,2048]{1,0:T(8,128)(2,1)}, bf16[256,2048]{1,0:T(8,128)(2,1)}, u32[]{:S(2)}, u32[]{:S(2)}) collective-permute-start(bf16[256,2048]{1,0:T(8,128)(2,1)} %get-tuple-element.289), channel_id=1, source_target_pairs={{3,2},{7,6},{11,10},{15,14},{19,18},{23,22},{27,26},{31,30}} | collective-permute-start | bytes 3145736 | tf_op jit(solution)/shard_map/ppermute | solution.py:579
  468.9 27.6 %collective-permute-start.37 = (bf16[256,2048]{1,0:T(8,128)(2,1)}, bf16[256,2048]{1,0:T(8,128)(2,1)}, u32[]{:S(2)}, u32[]{:S(2)}) collective-permute-start(bf16[256,2048]{1,0:T(8,128)(2,1)} %get-tuple-element.290), channel_id=1, source_target_pairs={{0,1},{4,5},{8,9},{12,13},{16,17},{20,21},{24,25},{28,29}} | collective-permute-start | bytes 3145736 | tf_op jit(solution)/shard_map/ppermute | solution.py:578
  482.1 14.3 %collective-permute-start.41 = (f32[12288]{0:T(1024)S(1)}, f32[12288]{0:T(1024)S(1)}, u32[]{:S(2)}, u32[]{:S(2)}) collective-permute-start(f32[12288]{0:T(1024)S(1)} %mul.324), channel_id=1, source_target_pairs={{0,1},{1,0},{2,3},{3,2},{4,5},{5,4},{6,7},{7,6},{8,9},{9,8},{10,11... | collective-permute-start | bytes 147464 | tf_op jit(solution)/shard_map/ppermute | solution.py:586
  502.7 10.8 %collective-permute-start.43 = (bf16[256,2048]{1,0:T(8,128)(2,1)}, bf16[256,2048]{1,0:T(8,128)(2,1)S(1)}, u32[]{:S(2)}, u32[]{:S(2)}) collective-permute-start(bf16[256,2048]{1,0:T(8,128)(2,1)} %get-tuple-element.287), channel_id=1, source_target_pairs={{2,1},{3,2},{6,5},{7,6},{10,9},{11,10},{14,13},{15,14},{18,17},{19... | collective-permute-start | bytes 3145736 | tf_op jit(solution)/shard_map/ppermute | solution.py:579
  503.5 25.3 %collective-permute-start.42 = (bf16[256,2048]{1,0:T(8,128)(2,1)}, bf16[256,2048]{1,0:T(8,128)(2,1)S(1)}, u32[]{:S(2)}, u32[]{:S(2)}) collective-permute-start(bf16[256,2048]{1,0:T(8,128)(2,1)} %get-tuple-element.288), channel_id=1, source_target_pairs={{0,1},{1,2},{4,5},{5,6},{8,9},{9,10},{12,13},{13,14},{16,17},{17,1... | collective-permute-start | bytes 3145736 | tf_op jit(solution)/shard_map/ppermute | solution.py:578
  512.7 20.2 %copy-start.50 = (bf16[1024,512]{1,0:T(8,128)(2,1)}, bf16[1024,512]{1,0:T(8,128)(2,1)S(1)}, u32[]{:S(2)}) copy-start(bf16[1024,512]{1,0:T(8,128)(2,1)S(1)} %add_convert_fusion.4) | copy-start | bytes 3145732
  513.5 29.5 %copy-start.56 = (bf16[256,2048]{1,0:T(8,128)(2,1)S(1)}, bf16[256,2048]{1,0:T(8,128)(2,1)}, u32[]{:S(2)}) copy-start(bf16[256,2048]{1,0:T(8,128)(2,1)} %copy-done.55) | copy-start | bytes 3145732
  513.5 29.5 %copy-start.58 = (bf16[256,2048]{1,0:T(8,128)(2,1)S(1)}, bf16[256,2048]{1,0:T(8,128)(2,1)}, u32[]{:S(2)}) copy-start(bf16[256,2048]{1,0:T(8,128)(2,1)} %copy-done.57) | copy-start | bytes 3145732
  513.5 29.5 %copy-start.70 = (f32[1,2048]{1,0:T(1,128)S(1)}, f32[1,2048]{1,0:T(1,128)}, u32[]{:S(2)}) copy-start(f32[1,2048]{1,0:T(1,128)} %get-tuple-element.342) | copy-start | bytes 24580
  528.8 32.7 %collective-permute-start.46 = (bf16[1024,256]{1,0:T(8,128)(2,1)}, bf16[1024,256]{1,0:T(8,128)(2,1)}, u32[]{:S(2)}, u32[]{:S(2)}) collective-permute-start(bf16[1024,256]{1,0:T(8,128)(2,1)} %fusion.83), channel_id=1, source_target_pairs={{0,16},{4,20},{8,24},{12,28},{16,0},{20,4},{24,8},{28,12},{1,17},{... | collective-permute-start | bytes 1572872 | tf_op jit(solution)/shard_map/ppermute | solution.py:586
  530.1 31.4 %collective-permute-start.47 = (bf16[1024,256]{1,0:T(8,128)(2,1)}, bf16[1024,256]{1,0:T(8,128)(2,1)}, u32[]{:S(2)}, u32[]{:S(2)}) collective-permute-start(bf16[1024,256]{1,0:T(8,128)(2,1)} %fusion.82), channel_id=1, source_target_pairs={{0,8},{4,12},{8,0},{12,4},{16,24},{20,28},{24,16},{28,20},{1,9},{5... | collective-permute-start | bytes 1572872 | tf_op jit(solution)/shard_map/ppermute | solution.py:586
  532.9 28.6 %collective-permute-start.45 = (bf16[256,2048]{1,0:T(8,128)(2,1)}, bf16[256,2048]{1,0:T(8,128)(2,1)S(1)}, u32[]{:S(2)}, u32[]{:S(2)}) collective-permute-start(bf16[256,2048]{1,0:T(8,128)(2,1)} %get-tuple-element.285), channel_id=1, source_target_pairs={{1,0},{2,1},{3,2},{5,4},{6,5},{7,6},{9,8},{10,9},{11,10},{13,12},{... | collective-permute-start | bytes 3145736 | tf_op jit(solution)/shard_map/ppermute | solution.py:579
  534.2 27.3 %collective-permute-start.44 = (bf16[256,2048]{1,0:T(8,128)(2,1)}, bf16[256,2048]{1,0:T(8,128)(2,1)S(1)}, u32[]{:S(2)}, u32[]{:S(2)}) collective-permute-start(bf16[256,2048]{1,0:T(8,128)(2,1)} %get-tuple-element.286), channel_id=1, source_target_pairs={{0,1},{1,2},{2,3},{4,5},{5,6},{6,7},{8,9},{9,10},{10,11},{12,13},{... | collective-permute-start | bytes 3145736 | tf_op jit(solution)/shard_map/ppermute | solution.py:578
  539.1 22.3 %collective-permute-start.48 = (f32[12288]{0:T(1024)S(1)}, f32[12288]{0:T(1024)S(1)}, u32[]{:S(2)}, u32[]{:S(2)}) collective-permute-start(f32[12288]{0:T(1024)S(1)} %add.601), channel_id=1, source_target_pairs={{0,2},{1,3},{2,0},{3,1},{4,6},{5,7},{6,4},{7,5},{8,10},{9,11},{10,... | collective-permute-start | bytes 147464 | tf_op jit(solution)/shard_map/ppermute | solution.py:586
  566.0 22.6 %collective-permute-start.51 = (bf16[512,256]{1,0:T(8,128)(2,1)}, bf16[512,256]{1,0:T(8,128)(2,1)S(1)}, u32[]{:S(2)}, u32[]{:S(2)}) collective-permute-start(bf16[512,256]{1,0:T(8,128)(2,1)} %get-tuple-element.310), channel_id=1, source_target_pairs={{0,3},{1,0},{2,1},{3,2},{4,7},{5,4},{6,5},{7,6},{8,11},{9,8},{10,9... | collective-permute-start | bytes 786440 | tf_op jit(solution)/shard_map/ppermute | solution.py:525
  571.1 18.9 %collective-permute-start.50 = (bf16[512,256]{1,0:T(8,128)(2,1)}, bf16[512,256]{1,0:T(8,128)(2,1)}, u32[]{:S(2)}, u32[]{:S(2)}) collective-permute-start(bf16[512,256]{1,0:T(8,128)(2,1)} %get-tuple-element.311), channel_id=1, source_target_pairs={{0,2},{1,3},{2,0},{3,1},{4,6},{5,7},{6,4},{7,5},{8,10},{9,11},{10,... | collective-permute-start | bytes 786440 | tf_op jit(solution)/shard_map/ppermute | solution.py:525
  571.1 18.9 %collective-permute-start.49 = (bf16[512,256]{1,0:T(8,128)(2,1)}, bf16[512,256]{1,0:T(8,128)(2,1)}, u32[]{:S(2)}, u32[]{:S(2)}) collective-permute-start(bf16[512,256]{1,0:T(8,128)(2,1)} %get-tuple-element.312), channel_id=1, source_target_pairs={{0,1},{1,2},{2,3},{3,0},{4,5},{5,6},{6,7},{7,4},{8,9},{9,10},{10,1... | collective-permute-start | bytes 786440 | tf_op jit(solution)/shard_map/ppermute | solution.py:525
  (73 other events, 398.1 us)
Sparse Core Ops, SparseCore 0:
  42.3 41.1 all-gather.4
  111.1 52.6 all-gather.6
  326.6 71.5 reduce-scatter.3
  401.9 80.4 reduce-scatter.5
  501.4 71.8 reduce-scatter.7
